TPU v7x, 32 devices: a whole 2x2x4 slice. The times are simulated.
32 devices in a mesh: rows: 4 (over y, core), cols: 8 (over z, x).
Axes of the slice: x: 2, y: 2, z: 4, core: 2. Of those that a mesh axis runs over, the one named last changes fastest.
Arguments:
- kernel: float32 [4096, 16384], P('rows', 'cols'), may hold values from -0.09375 to 0.09375
- slip_delta: float32 [64, 32, 128], P('cols', 'rows'), may hold values from -6 to 6
- block_list: int32 [64, 32], P('cols', 'rows'), may hold values from 0 to 127, as said below
- live_count: int32 [64], P('cols'), may hold values from 1 to 32, 1024 in all
- direct_effect: float32 [4096], P(('rows', 'cols')), may hold values from 0.5 to 2
- load_rate: float32 [4096], P(('rows', 'cols')), may hold values from 0.02 to 0.2
- time_before: float32 [4096], P(('rows', 'cols')), may hold values from 1 to 50
Outputs:
- stress_change: float32 [4096, 64], P(('rows', 'cols'))
- log_time: float32 [4096, 64], P(('rows', 'cols'))
Inputs may be any that keep to these rules, and one draw needn't show every extreme that they name: The first live_count[e] entries of row e of block_list are distinct block numbers; the rest of the row are padding.
All inputs are finite; a program needn't handle non-finite values. No bound on the sum of `live_count` on one device may be relied on, other than what follows from the above.
Results may differ from a plain program's by a relative error of at most 0.00007.
Values sent between devices are 32-bit elements; how exact they have to be, the bound alone decides.
No kernel may reach another device: no remote copies, remote signals or barrier semaphores. Data moves between devices by JAX's collectives and lax.ppermute only.
A program may use at most 64 MiB of HBM per device.

v0:
```python
import jax
import jax.numpy as jnp
from jax import lax
from jax.sharding import PartitionSpec as P

BLOCK = 128


def per_device(kernel, slip_delta, block_list, live_count, direct_effect, load_rate, time_before):
    slip_rows, list_rows = (
        lax.all_gather(slip_delta, "rows", axis=1, tiled=True),
        lax.all_gather(block_list, "rows", axis=1, tiled=True),
    )
    blocks_here = kernel.shape[1] // BLOCK
    my_column = lax.axis_index("cols")
    width = lax.axis_size("cols")
    all_slip, all_list, all_count = (
        lax.all_gather(slip_rows, "cols", axis=0, tiled=True),
        lax.all_gather(list_rows, "cols", axis=0, tiled=True),
        lax.all_gather(live_count, "cols", axis=0, tiled=True),
    )
    offset_index = all_list - my_column * blocks_here
    live_mask = jnp.arange(all_list.shape[1], dtype=jnp.int32)[None, :] < all_count[:, None]
    onehot = (
        (offset_index[:, :, None] == jnp.arange(blocks_here, dtype=jnp.int32)[None, None, :])
        & live_mask[:, :, None]
    ).astype(jnp.float32)
    dense_slip = jnp.einsum("ebj,ebc->ejc", onehot, all_slip, precision=lax.Precision.HIGHEST)
    dense_slip = dense_slip.reshape(all_slip.shape[0], blocks_here * BLOCK)
    share_rows = kernel.shape[0] // width
    partial_sum = lax.dot_general(
        kernel,
        dense_slip,
        (((1,), (1,)), ((), ())),
        precision=lax.Precision.HIGHEST,
        preferred_element_type=jnp.float32,
    )
    summed = lax.psum(partial_sum, "cols")
    stress_change = lax.dynamic_slice_in_dim(summed, my_column * share_rows, share_rows, 0)
    scale = direct_effect[:, None]
    growth = jnp.expm1(load_rate * time_before / direct_effect)[:, None]
    log_time = jnp.log(scale / load_rate[:, None]) + jnp.log(
        jnp.log1p(jnp.exp(-stress_change / scale) * growth)
    )
    return (stress_change, log_time)


def solution(mesh):
    in_specs = (
        P("rows", "cols"),
        P("cols", "rows", None),
        P("cols", "rows"),
        P("cols"),
        P(("rows", "cols")),
        P(("rows", "cols")),
        P(("rows", "cols")),
    )
    out_specs = (P(("rows", "cols"), None), P(("rows", "cols"), None))
    return jax.shard_map(
        per_device, mesh=mesh, in_specs=in_specs, out_specs=out_specs, check_vma=False
    )
```

profile of v0, /device:TPU:0, one launch (start us, length us, event | category | flops | bytes accessed | tf_op | source)
XLA Modules:
  0.0 156.4 jit_solution(1746615377204307877)
XLA Ops:
  7.2 0.0 copy-start
  7.2 0.0 copy-start.1
  7.2 0.0 copy-start.2
  7.2 0.0 all-gather.2.cloned.1.call-start
  7.2 8.4 %all_gather.18 = f32[8,32,128]{2,1,0:T(8,128)} all-gather(f32[8,8,128]{2,1,0:T(8,128)} %param.8), channel_id=1, replica_groups=mesh['rows'=4,'cols'=8] {'rows'}, dimensions={1}, use_global_device_ids=true | all-gather | bytes 163840 | tf_op jit(solution)/shard_map/all_gather | solution.py:11
  15.7 0.0 all-gather.2.cloned.1.call-update
  15.7 0.0 all-reduce.3.cloned.1.call-start
  15.7 0.8 copy.11
  16.5 5.2 %all_gather.15 = s32[8,32]{0,1:T(8,128)S(1)} all-gather(s32[8,8]{0,1:T(8,128)S(1)} %copy.11), channel_id=1, replica_groups=mesh['rows'=4,'cols'=8] {'rows'}, dimensions={1}, use_global_device_ids=true | all-gather | bytes 1280 | tf_op jit(solution)/shard_map/all_gather | solution.py:12
  21.7 0.1 copy.12
  21.7 1.2 dynamic-slice
  23.6 0.9 dynamic-update-slice
  24.5 11.8 %all-reduce = s32[64]{0:T(128)S(1)} all-reduce(s32[64]{0:T(128)S(1)} %dynamic-update-slice), channel_id=1, replica_groups=mesh['rows'=4,'cols'=8] {'cols'}, use_global_device_ids=true, to_apply=%add | all-reduce | flops 64 | bytes 512
  36.3 30.5 %all_gather.16 = s32[64,32]{1,0:T(8,128)S(1)} all-gather(s32[8,32]{1,0:T(8,128)S(1)} %copy.12), channel_id=1, replica_groups=mesh['rows'=4,'cols'=8] {'cols'}, dimensions={0}, use_global_device_ids=true | all-gather | bytes 9216 | tf_op jit(solution)/shard_map/all_gather | solution.py:19
  66.8 0.1 iota_compare_fusion.1
  66.9 0.0 all-gather.2.cloned.1.call-done
  66.9 1.9 %fusion.3 = f32[64,16,128]{2,1,0:T(8,128)S(1)} fusion(f32[64,32,128]{2,1,0:T(8,128)} %all-gather.2.cloned.1.call-done, s32[64,32]{1,0:T(8,128)S(1)} %broadcast_subtract_fusion, pred[64,32]{1,0:T(8,128)(4,1)S(1)} %iota_compare_fusion.1), kind=kOutput, calls=%fused_computation.5 | convolution fusion | flops 50397184 | bytes 1583104 | tf_op jit(solution)/shard_map/ebj,ebc->ejc/dot_general | solution.py:28
  68.8 11.2 %convolution_bitcast_fusion = f32[1024,64]{0,1:T(8,128)} fusion(f32[1024,2048]{1,0:T(8,128)} %param.7, f32[8,8,16,128]{3,2,1,0:T(8,128)S(1)} %bitcast.9), kind=kOutput, calls=%fused_computation | convolution fusion | flops 1610612736 | bytes 9175040 | tf_op jit(solution)/shard_map/dot_general | solution.py:31
  80.0 0.0 all-reduce.3.cloned.1.call-update
  80.0 0.0 copy-done
  80.0 0.0 copy-done.1
  80.0 0.0 copy-done.2
  80.1 68.0 %all-reduce.3.cloned.1.call-done = f32[1024,64]{0,1:T(8,128)} async-done(((f32[1024,64]{0,1:T(8,128)}), f32[1024,64]{0,1:T(8,128)}) %all-reduce.3.cloned.1.call-update) | async-done | bytes 262160 | tf_op jit(solution)/shard_map/psum | solution.py:38
  148.1 1.4 log_add_fusion
  (3 shorter events, 0.0 us)
Async XLA Ops:
  7.2 72.8 %copy-start = (f32[128]{0:T(128)S(1)}, f32[128]{0:T(128)}, u32[]{:S(2)}) copy-start(f32[128]{0:T(128)} %param.11) | copy-start | bytes 1540
  7.2 72.8 %copy-start.1 = (f32[128]{0:T(128)S(1)}, f32[128]{0:T(128)}, u32[]{:S(2)}) copy-start(f32[128]{0:T(128)} %param.12) | copy-start | bytes 1540
  7.2 72.8 %copy-start.2 = (f32[128]{0:T(128)S(1)}, f32[128]{0:T(128)}, u32[]{:S(2)}) copy-start(f32[128]{0:T(128)} %param.13) | copy-start | bytes 1540
  7.2 59.7 %all-gather.2.cloned.1.call-start = ((), (), s32[]{:S(2)}) async-start(), calls=%async_computation | async-start | bytes 1179648 | tf_op jit(solution)/shard_map/all_gather | solution.py:18
  15.7 132.4 %all-reduce.3.cloned.1.call-start = ((), (), s32[]{:S(2)}) async-start(), calls=%async_computation.1 | async-start | bytes 524288 | tf_op jit(solution)/shard_map/psum | solution.py:38
Sparse Core Ops, SparseCore 0:
  15.8 40.5 all-gather.1
  80.1 67.9 all-reduce.2
where the time goes:
time: 157 us; the launch traced here: 156 us
  waiting for transfers between devices  68.1 us (43%)
  blocking collectives  55.9 us (36%)
  between operations  14.8 us (9%)
  matrix products  13.1 us (8%)
  local copies, waits for them, and re-layouts  2.94 us (2%)
    psum x1, waiting for transfers between devices, per_device(): summed = lax.psum(partial_sum, 'cols')  68 us
    all_gather x1, blocking collectives, per_device(): lax.all_gather(list_rows, 'cols', axis=0, tiled=True)  30.5 us
    unnamed x1, blocking collectives  11.8 us
    dot_general x1, matrix products, per_device(): lax.dot_general(kernel, dense_slip, (((1,), (1,)), ((), ())), precision=l...  11.2 us
    all_gather x1, blocking collectives, per_device(): lax.all_gather(slip_delta, 'rows', axis=1, tiled=True)  8.42 us
    all_gather x1, blocking collectives, per_device(): lax.all_gather(block_list, 'rows', axis=1, tiled=True)  5.17 us
  transfers between devices with their start and end apart: 2, of which 1 were waited for; matrix products, arithmetic and copies ran while one was open for 2% of the time, Pallas kernels for 0%

commit v1 on v0

v1 whole, which is shorter than its diff:
```python
import math

import jax
import jax.numpy as jnp
import numpy as np
from jax import lax
from jax.sharding import PartitionSpec as P

BLOCK = 128


def gather_rows(block, width):
    held = block[None]
    step = width // 2
    while step:
        other = lax.ppermute(held, "rows", [(r, r ^ step) for r in range(width)])
        held = jnp.concatenate([held, other], axis=0)
        step //= 2
    bits = width.bit_length() - 1
    slot = np.array([int(f"{k:0{bits}b}"[::-1], 2) for k in range(width)], np.int32)
    mine = lax.axis_index("rows")
    return jnp.take(held, jnp.asarray(slot)[mine ^ jnp.arange(width, dtype=jnp.int32)], axis=0)


def per_device(kernel, slip_delta, block_list, live_count, direct_effect, load_rate, time_before):
    width = lax.axis_size("cols")
    height = lax.axis_size("rows")
    my_row = lax.axis_index("rows")
    events_here, entries_here = block_list.shape
    blocks_here = kernel.shape[1] // BLOCK
    split = math.gcd(events_here, height)
    parts = height // split
    blocks_part = blocks_here // parts
    group = events_here // split

    entry = my_row * entries_here + jnp.arange(entries_here, dtype=jnp.int32)
    ids = jnp.where(entry[None, :] < live_count[:, None], block_list, -1).astype(jnp.float32)
    ids = jnp.pad(ids, ((0, 0), (0, BLOCK - entries_here)))
    packed = jnp.concatenate(
        [
            slip_delta.reshape(split, group * entries_here, BLOCK),
            ids.reshape(split, group, BLOCK),
        ],
        axis=1,
    )
    packed = jnp.repeat(packed, parts, axis=0)
    packed = lax.all_to_all(packed, "rows", 0, 0, tiled=True)
    slips = packed[:, : group * entries_here].reshape(height, group, entries_here, BLOCK)
    ids = packed[:, group * entries_here :, :entries_here]
    block = jnp.arange(width * blocks_here, dtype=jnp.float32)
    onehot = (ids[..., None] == block).astype(jnp.float32)
    dense = jnp.einsum("hgbj,hgbc->jgc", onehot, slips, precision=lax.Precision.HIGHEST)
    dense = dense.reshape(width, parts, blocks_part, group, BLOCK)
    if parts > 1:
        dense = lax.dynamic_index_in_dim(dense, my_row % parts, 1, keepdims=True)
    dense = dense.reshape(width, blocks_part, group, BLOCK)
    dense = lax.all_to_all(dense, "cols", 0, 0, tiled=True)
    held = gather_rows(dense, height)
    held = held.reshape(split, parts, width, blocks_part, group, BLOCK)
    held = held.transpose(2, 0, 4, 1, 3, 5).reshape(width * events_here, blocks_here * BLOCK)
    partial_sum = lax.dot_general(
        held,
        kernel,
        (((1,), (1,)), ((), ())),
        precision=lax.Precision.HIGH,
        preferred_element_type=jnp.float32,
    )
    share_rows = kernel.shape[0] // width
    partial_sum = partial_sum.reshape(held.shape[0], width, share_rows).transpose(1, 0, 2)
    stress_change = jnp.sum(lax.all_to_all(partial_sum, "cols", 0, 0, tiled=True), axis=0)
    scale = direct_effect[None, :]
    growth = jnp.expm1(load_rate * time_before / direct_effect)[None, :]
    log_time = jnp.log(scale / load_rate[None, :]) + jnp.log(
        jnp.log1p(jnp.exp(-stress_change / scale) * growth)
    )
    return (stress_change.T, log_time.T)


def solution(mesh):
    in_specs = (
        P("rows", "cols"),
        P("cols", "rows", None),
        P("cols", "rows"),
        P("cols"),
        P(("rows", "cols")),
        P(("rows", "cols")),
        P(("rows", "cols")),
    )
    out_specs = (P(("rows", "cols"), None), P(("rows", "cols"), None))
    return jax.shard_map(
        per_device, mesh=mesh, in_specs=in_specs, out_specs=out_specs, check_vma=False
    )
```

time: 157 us -> 52.9 us (0.34)
  blocking collectives: 55.9 us -> 8.06 us
  waiting for transfers between devices: 68.1 us -> 21.8 us
  between operations: 14.8 us -> 0.78 us
  starting transfers between devices: 0.08 us -> 9.37 us
  matrix products: 13.1 us -> 7.31 us
    psum x1 -> x0, waiting for transfers between devices: 68 us -> none  [per_device(): summed = lax.psum(partial_sum, 'cols')]
    all_gather x3 -> x0, blocking collectives: 44.1 us -> none  [the longest x1 30.5 us: per_device(): lax.all_gather(list_rows, 'cols', axis=0, tiled=True)]
    all_to_all x0 -> x2, waiting for transfers between devices: none -> 15.4 us  [the longest x1 9.39 us: per_device(): lax.all_to_all(partial_sum, 'cols', 0, 0, tiled=True)]
    unnamed x1 -> x0, blocking collectives: 11.8 us -> none
    all_to_all x0 -> x2, starting transfers between devices: none -> 9.22 us  [the longest x1 5.81 us: per_device(): dense = lax.all_to_all(dense, 'cols', 0, 0, tiled=True)]
    all_to_all x0 -> x1, blocking collectives: none -> 8.06 us  [per_device(): packed = lax.all_to_all(packed, 'rows', 0, 0, tiled=True)]
    ppermute x0 -> x2, waiting for transfers between devices: none -> 6.38 us  [gather_rows(): other = lax.ppermute(held, 'rows', [(r, r ^ step) for r in range(width)])]
    dot_general x2, matrix products: 13.1 us -> 7.31 us  [the longest x1 6.96 us: per_device(): lax.dot_general(held, kernel, (((1,), (1,)), ((), ())), precision=lax.Pre...]
  transfers between devices with their start and end apart: 2 -> 4, of which waited for: 1 -> 4; matrix products, arithmetic and copies ran while one was open for 2% -> 3% of each run, Pallas kernels for 0% -> 0%
where the time goes in v1:
time: 52.9 us; the launch traced here: 52.4 us
  waiting for transfers between devices  21.8 us (41%)
  starting transfers between devices  9.37 us (18%)
  blocking collectives  8.06 us (15%)
  matrix products  7.31 us (14%)
  local copies, waits for them, and re-layouts  2.69 us (5%)
  other arithmetic  2.42 us (5%)
  between operations  0.78 us (1%)
    all_to_all x1, waiting for transfers between devices, per_device(): lax.all_to_all(partial_sum, 'cols', 0, 0, tiled=True)  9.39 us
    all_to_all x1, blocking collectives, per_device(): packed = lax.all_to_all(packed, 'rows', 0, 0, tiled=True)  8.06 us
    dot_general x1, matrix products, per_device(): lax.dot_general(held, kernel, (((1,), (1,)), ((), ())), precision=lax.Pre...  6.96 us
    ppermute x2, waiting for transfers between devices, gather_rows(): other = lax.ppermute(held, 'rows', [(r, r ^ step) for r in range(width)])  6.38 us
    all_to_all x1, waiting for transfers between devices, per_device(): dense = lax.all_to_all(dense, 'cols', 0, 0, tiled=True)  6.03 us
    all_to_all x1, starting transfers between devices, per_device(): dense = lax.all_to_all(dense, 'cols', 0, 0, tiled=True)  5.81 us
    all_to_all x1, starting transfers between devices, per_device(): lax.all_to_all(partial_sum, 'cols', 0, 0, tiled=True)  3.41 us
    gather x1, local copies, waits for them, and re-layouts, gather_rows(): jnp.asarray(slot)[mine ^ jnp.arange(width, dtype=jnp.int32)]  1.3 us
  transfers between devices with their start and end apart: 4, of which 4 were waited for; matrix products, arithmetic and copies ran while one was open for 3% of the time, Pallas kernels for 0%

profile of v1, /device:TPU:0, one launch (start us, length us, event | category | flops | bytes accessed | tf_op | source)
XLA Modules:
  0.0 52.4 jit_solution(217760861589282323)
XLA Ops:
  0.6 0.8 %select_convert_fusion = f32[8,8]{1,0:T(8,128)S(1)} fusion(s32[8,8]{1,0:T(8,128)} %param.10, s32[8]{0:T(128)S(1)} %iota_add_fusion, s32[8]{0:T(128)} %param.11), kind=kLoop, calls=%fused_computation.15 | loop fusion | flops 192 | bytes 576 | tf_op jit(solution)/shard_map/convert_element_type | solution.py:37
  1.4 0.8 %pad_maximum_fusion.2 = f32[4,18,128]{2,1,0:T(8,128)S(1)} fusion(f32[4,2,128]{2,1,0:T(2,128)S(1)} %bitcast.41, f32[4,16,128]{2,1,0:T(8,128)} %bitcast.40), kind=kLoop, calls=%fused_computation.7 | loop fusion | flops 9216 | bytes 73728 | tf_op jit(solution)/shard_map/concatenate | solution.py:39
  2.2 8.1 %all_to_all.15 = f32[4,18,128]{2,1,0:T(8,128)S(1)} all-to-all(f32[4,18,128]{2,1,0:T(8,128)S(1)} %pad_maximum_fusion.2), channel_id=1, replica_groups=mesh['rows'=4,'cols'=8] {'rows'}, dimensions={0} | all-to-all | bytes 73728 | tf_op jit(solution)/shard_map/all_to_all | solution.py:47
  10.2 0.0 copy-start.1
  10.2 0.0 copy-start.2
  10.2 0.0 copy-start.3
  10.3 0.4 fusion.1
  10.6 0.7 %copy.16 = f32[8,16,2,128]{3,1,2,0:T(8,128)} copy(f32[8,16,2,128]{3,1,0,2:T(8,128)S(1)} %bitcast.39) | data formatting | bytes 262144 | tf_op jit(solution)/shard_map/reshape;reshape | solution.py:56
  11.3 5.8 %all-to-all-start.1 = ((f32[8,16,2,128]{3,1,2,0:T(8,128)}), f32[8,16,2,128]{3,1,2,0:T(8,128)S(1)}, u32[]{:S(2)}, u32[]{:S(2)}) async-start(f32[8,16,2,128]{3,1,2,0:T(8,128)} %copy.16), calls=%async_computation.1 | async-start | bytes 262144 | tf_op jit(solution)/shard_map/all_to_all | solution.py:57
  17.1 1.3 %gather_fusion = s32[4]{0:T(128)S(1)} fusion(s32[4]{0:T(128)} %constant.33.clone, s32[1024]{0:T(1024)S(1)} %pad_clamp_fusion.1), kind=kCustom, calls=%fused_computation | custom fusion | bytes 48 | tf_op jit(solution)/shard_map/gather | solution.py:22
  18.4 6.0 %all-to-all-done.1 = f32[8,16,2,128]{3,1,2,0:T(8,128)S(1)} async-done(((f32[8,16,2,128]{3,1,2,0:T(8,128)}), f32[8,16,2,128]{3,1,2,0:T(8,128)S(1)}, u32[]{:S(2)}, u32[]{:S(2)}) %all-to-all-start.1) | async-done | bytes 131104 | tf_op jit(solution)/shard_map/all_to_all | solution.py:57
  24.4 0.1 collective-permute-start
  24.5 4.9 %collective-permute-done = f32[1,8,16,2,128]{4,2,3,1,0:T(8,128)S(1)} collective-permute-done((f32[1,8,16,2,128]{4,2,3,1,0:T(8,128)S(1)}, f32[1,8,16,2,128]{4,2,3,1,0:T(8,128)S(1)}, u32[]{:S(2)}, u32[]{:S(2)}) %collective-permute-start) | collective-permute-done | bytes 131104 | tf_op jit(solution)/shard_map/ppermute | solution.py:16
  29.4 0.1 collective-permute-start.1
  29.5 1.5 %collective-permute-done.1 = f32[2,8,16,2,128]{4,2,3,1,0:T(8,128)S(1)} collective-permute-done((f32[2,8,16,2,128]{4,2,3,1,0:T(8,128)S(1)}, f32[2,8,16,2,128]{4,2,3,1,0:T(8,128)S(1)}, u32[]{:S(2)}, u32[]{:S(2)}) %collective-permute-start.1) | collective-permute-done | bytes 262176 | tf_op jit(solution)/shard_map/ppermute | solution.py:16
  31.1 0.6 %gather_fusion.1 = f32[4,8,16,2,128]{4,2,3,1,0:T(8,128)S(1)} fusion(f32[4,8,16,2,128]{4,2,3,1,0:T(8,128)S(1)} %pad_maximum_fusion, s32[1024]{0:T(1024)S(1)} %pad_clamp_fusion), kind=kCustom, calls=%fused_computation.1 | custom fusion | bytes 1048592 | tf_op jit(solution)/shard_map/jit(_take)/gather | solution.py:22
  31.6 0.1 fusion
  31.8 0.1 reshape.92
  31.9 7.0 %convolution_bitcast_fusion = f32[8,64,128]{2,1,0:T(8,128)} fusion(f32[64,2048,1]{1,0,2:T(8,128)S(1)} %reshape.92, f32[8,128,2048]{2,1,0:T(8,128)} %bitcast.34), kind=kOutput, calls=%fused_computation.2 | convolution fusion | flops 805306368 | bytes 9175040 | tf_op jit(solution)/shard_map/dot_general | solution.py:61
  38.9 3.4 %all-to-all-start.2 = ((f32[8,64,128]{2,1,0:T(8,128)}), f32[8,64,128]{2,1,0:T(8,128)S(1)}, u32[]{:S(2)}, u32[]{:S(2)}) async-start(f32[8,64,128]{2,1,0:T(8,128)} %convolution_bitcast_fusion), calls=%async_computation.2 | async-start | bytes 524288 | tf_op jit(solution)/shard_map/all_to_all | solution.py:70
  42.3 0.0 copy-done.1
  42.3 0.0 copy-done.2
  42.3 0.0 copy-done.3
  42.3 9.4 %all-to-all-done.2 = f32[8,64,128]{2,1,0:T(8,128)S(1)} async-done(((f32[8,64,128]{2,1,0:T(8,128)}), f32[8,64,128]{2,1,0:T(8,128)S(1)}, u32[]{:S(2)}, u32[]{:S(2)}) %all-to-all-start.2) | async-done | bytes 262176 | tf_op jit(solution)/shard_map/all_to_all | solution.py:70
  51.7 0.0 copy-start
  51.8 0.7 %log_add_fusion = f32[128,64]{0,1:T(8,128)} fusion(f32[128]{0:T(128)S(1)} %get-tuple-element.3, f32[128]{0:T(128)S(1)} %copy-done.1, f32[128]{0:T(128)S(1)} %get-tuple-element.2, f32[64,128]{1,0:T(8,128)S(1)} %reduce_sum.9), kind=kLoop, calls=%fused_computation.10 | loop fusion | flops 32768 | bytes 67072 | tf_op jit(solution)/shard_map/add | solution.py:73
  52.4 0.0 copy-done
  (13 shorter events, 0.2 us)
Async XLA Ops:
  10.2 32.0 %copy-start.1 = (f32[128]{0:T(128)S(1)}, f32[128]{0:T(128)}, u32[]{:S(2)}) copy-start(f32[128]{0:T(128)} %param.12) | copy-start | bytes 1540
  10.2 32.1 %copy-start.2 = (f32[128]{0:T(128)S(1)}, f32[128]{0:T(128)}, u32[]{:S(2)}) copy-start(f32[128]{0:T(128)} %param.13) | copy-start | bytes 1540
  10.2 32.1 %copy-start.3 = (f32[128]{0:T(128)S(1)}, f32[128]{0:T(128)}, u32[]{:S(2)}) copy-start(f32[128]{0:T(128)} %param.14) | copy-start | bytes 1540
  11.3 13.1 %all-to-all-start.1 = ((f32[8,16,2,128]{3,1,2,0:T(8,128)}), f32[8,16,2,128]{3,1,2,0:T(8,128)S(1)}, u32[]{:S(2)}, u32[]{:S(2)}) async-start(f32[8,16,2,128]{3,1,2,0:T(8,128)} %copy.16), calls=%async_computation.1 | async-start | bytes 262144 | tf_op jit(solution)/shard_map/all_to_all | solution.py:57
  24.4 5.0 %collective-permute-start = (f32[1,8,16,2,128]{4,2,3,1,0:T(8,128)S(1)}, f32[1,8,16,2,128]{4,2,3,1,0:T(8,128)S(1)}, u32[]{:S(2)}, u32[]{:S(2)}) collective-permute-start(f32[1,8,16,2,128]{4,2,3,1,0:T(8,128)S(1)} %bitcast.35), channel_id=1, source_target_pairs={{0,16},{8,24},{16,0},{24,8},{1,17},{9,25},{17,1},{25,9},{2,18},{10... | collective-permute-start | bytes 393224 | tf_op jit(solution)/shard_map/ppermute | solution.py:16
  29.4 1.6 %collective-permute-start.1 = (f32[2,8,16,2,128]{4,2,3,1,0:T(8,128)S(1)}, f32[2,8,16,2,128]{4,2,3,1,0:T(8,128)S(1)}, u32[]{:S(2)}, u32[]{:S(2)}) collective-permute-start(f32[2,8,16,2,128]{4,2,3,1,0:T(8,128)S(1)} %pad_maximum_fusion.1), channel_id=1, source_target_pairs={{0,8},{8,0},{16,24},{24,16},{1,9},{9,1},{17,25},{25,17},{2,10},{10... | collective-permute-start | bytes 786440 | tf_op jit(solution)/shard_map/ppermute | solution.py:16
  38.9 12.9 %all-to-all-start.2 = ((f32[8,64,128]{2,1,0:T(8,128)}), f32[8,64,128]{2,1,0:T(8,128)S(1)}, u32[]{:S(2)}, u32[]{:S(2)}) async-start(f32[8,64,128]{2,1,0:T(8,128)} %convolution_bitcast_fusion), calls=%async_computation.2 | async-start | bytes 524288 | tf_op jit(solution)/shard_map/all_to_all | solution.py:70
  51.7 0.7 %copy-start = (f32[64,128]{1,0:T(8,128)}, f32[64,128]{1,0:T(8,128)S(1)}, u32[]{:S(2)}) copy-start(f32[64,128]{1,0:T(8,128)S(1)} %reduce_sum.9) | copy-start | bytes 98308

commit v2 on v0

v2 whole, which is shorter than its diff:
```python
import functools
import math

import jax
import jax.numpy as jnp
from jax import lax
from jax.experimental import pallas as pl
from jax.experimental.pallas import tpu as pltpu
from jax.sharding import PartitionSpec as P

BLOCK = 128
SUB = 8
VMEM_SPEC = pl.BlockSpec(memory_space=pltpu.VMEM)
SMEM_SPEC = pl.BlockSpec(memory_space=pltpu.SMEM)
MIB = 1024 * 1024


def f32(*shape):
    return jax.ShapeDtypeStruct(shape, jnp.float32)


def send_xor(block, axis, width, k):
    return lax.ppermute(block, axis, [(r, r ^ k) for r in range(width)])


def pack_body(height, parts, group, me_ref, slip_ref, list_ref, count_ref, *refs):
    out_refs, ids = refs[:height], refs[height]
    events, entries = list_ref.shape
    row = me_ref[0]
    lane = lax.broadcasted_iota(jnp.int32, (events, entries), 1) + row * entries
    event = lax.broadcasted_iota(jnp.int32, (events, entries), 0)
    count = jnp.zeros((events, entries), jnp.int32)
    for e in range(events):
        count = jnp.where(event == e, count_ref[e], count)
    ids[...] = jnp.full(ids.shape, -1.0, jnp.float32)
    ids[0:events, 0:entries] = jnp.where(lane < count, list_ref[...], -1).astype(jnp.float32)
    placed = pltpu.roll(ids[...], row * entries, 1)
    ids[...] = placed
    for k in range(height):
        first = ((row ^ k) // parts) * group
        for i in range(group):
            out_refs[k][i, 0:entries, :] = slip_ref[first + i]
            out_refs[k][i, SUB : 2 * SUB, :] = jnp.broadcast_to(ids[pl.ds(first + i, 1), :], (SUB, BLOCK))


def densify_body(height, width, parts, blocks_here, entries, me_ref, *refs):
    ins, outs, dense = refs[:height], refs[height : height + width], refs[-1]
    group = ins[0].shape[0]
    row, col = me_ref[0], me_ref[1]
    blocks_part = blocks_here // parts
    blocks = width * blocks_here
    for i in range(group):
        ids = ins[0][i, SUB : 2 * SUB, :]
        for k in range(1, height):
            ids = jnp.maximum(ids, ins[k][i, SUB : 2 * SUB, :])
        ids = jnp.concatenate([ids] * (blocks // SUB), axis=0)[:, : height * entries]
        number = lax.broadcasted_iota(jnp.int32, ids.shape, 0).astype(jnp.float32)
        onehot = (ids == number).astype(jnp.bfloat16)
        slips = dense.at[i, 0 : height * entries, :]
        for k in range(height):
            slips[pl.ds(pl.multiple_of((row ^ k) * entries, entries), entries), :] = ins[k][i, 0:entries, :]
        slip = slips[...]
        total = jnp.zeros((blocks, BLOCK), jnp.float32)
        for _ in range(3):
            piece = slip.astype(jnp.bfloat16)
            slip = slip - piece.astype(jnp.float32)
            total = total + jnp.dot(onehot, piece, preferred_element_type=jnp.float32)
        dense[i] = total
        part = (row % parts) * blocks_part
        for k in range(width):
            start = pl.multiple_of((col ^ k) * blocks_here + part, blocks_part)
            outs[k][i] = dense[i, pl.ds(start, blocks_part), :]


def stress_body(height, width, parts, me_ref, *refs):
    slips, (kernel_ref, out_ref, dense, stacked) = refs[:-4], refs[-4:]
    events, blocks_here, _ = dense.shape
    row, col = me_ref[0], me_ref[1]
    group, blocks_part = slips[0].shape[1], slips[0].shape[2]
    split = height // parts

    @pl.when(pl.program_id(0) == 0)
    def _():
        for kr in range(height):
            source = row ^ kr
            for kc in range(width):
                first = (col ^ kc) * (events // width) + (source // parts) * group
                for i in range(group):
                    where = pl.ds(pl.multiple_of((source % parts) * blocks_part, blocks_part), blocks_part)
                    if parts == 1:
                        where = slice(None)
                    dense[first + i, where, :] = slips[kr][kc, i]
        flat = dense.reshape(events * blocks_here, BLOCK)
        for t in range(events // SUB):
            for b in range(blocks_here):
                stacked[t * SUB : (t + 1) * SUB, b * BLOCK : (b + 1) * BLOCK] = flat[
                    pl.ds(t * SUB * blocks_here + b, SUB, stride=blocks_here), :
                ]

    slip = stacked[...]
    slip_hi = slip.astype(jnp.bfloat16)
    slip_lo = (slip - slip_hi.astype(jnp.float32)).astype(jnp.bfloat16)
    both = jnp.concatenate([slip_hi, slip_lo], axis=0)
    block = kernel_ref[...]
    block_hi = block.astype(jnp.bfloat16)
    block_lo = (block - block_hi.astype(jnp.float32)).astype(jnp.bfloat16)
    dims = (((1,), (1,)), ((), ()))
    first = lax.dot_general(both, block_hi, dims, preferred_element_type=jnp.float32)
    second = lax.dot_general(slip_hi, block_lo, dims, preferred_element_type=jnp.float32)
    total = first[:events] + first[events:] + second
    share = out_ref.shape[2]
    for j in range(out_ref.shape[0]):
        out_ref[j] = total[:, j * share : (j + 1) * share]


def per_device(kernel, slip_delta, block_list, live_count, direct_effect, load_rate, time_before):
    width = lax.axis_size("cols")
    height = lax.axis_size("rows")
    events_here, entries = block_list.shape
    events = events_here * width
    receivers, sources = kernel.shape
    blocks_here = sources // BLOCK
    split = math.gcd(events_here, height)
    parts = height // split
    group = events_here // split
    blocks_part = blocks_here // parts
    me = jnp.stack([lax.axis_index("rows"), lax.axis_index("cols")]).astype(jnp.int32)

    message = f32(group, 2 * SUB, BLOCK)
    packed = pl.pallas_call(
        functools.partial(pack_body, height, parts, group),
        out_shape=[message] * height,
        in_specs=[SMEM_SPEC, VMEM_SPEC, VMEM_SPEC, SMEM_SPEC],
        out_specs=[VMEM_SPEC] * height,
        scratch_shapes=[pltpu.VMEM((SUB, BLOCK), jnp.float32)],
        compiler_params=pltpu.CompilerParams(vmem_limit_bytes=8 * MIB),
        name="pack",
    )(me, slip_delta, block_list, live_count)
    packed = [packed[0]] + [send_xor(packed[k], "rows", height, k) for k in range(1, height)]

    dense = pl.pallas_call(
        functools.partial(densify_body, height, width, parts, blocks_here, entries),
        out_shape=[f32(group, blocks_part, BLOCK)] * width,
        in_specs=[SMEM_SPEC] + [VMEM_SPEC] * height,
        out_specs=[VMEM_SPEC] * width,
        scratch_shapes=[pltpu.VMEM((group, width * blocks_here, BLOCK), jnp.float32)],
        compiler_params=pltpu.CompilerParams(vmem_limit_bytes=8 * MIB),
        name="densify",
    )(me, *packed)
    dense = [dense[0]] + [send_xor(dense[k], "cols", width, k) for k in range(1, width)]

    held = [jnp.stack(dense)]
    step = height // 2
    while step:
        sent = jnp.stack(held) if len(held) > 1 else held[0][None]
        came = send_xor(sent, "rows", height, step)
        held = [x for j in range(len(held)) for x in (held[j], came[j])]
        step //= 2

    steps = 4
    share = receivers // width
    per_step = width // steps
    partial_sum = pl.pallas_call(
        functools.partial(stress_body, height, width, parts),
        out_shape=f32(width, events, share),
        grid=(steps,),
        in_specs=[SMEM_SPEC]
        + [pl.BlockSpec(h.shape, lambda s: (0, 0, 0, 0)) for h in held]
        + [pl.BlockSpec((receivers // steps, sources), lambda s: (s, 0))],
        out_specs=pl.BlockSpec((per_step, events, share), lambda s: (s, 0, 0)),
        scratch_shapes=[
            pltpu.VMEM((events, blocks_here, BLOCK), jnp.float32),
            pltpu.VMEM((events, sources), jnp.float32),
        ],
        compiler_params=pltpu.CompilerParams(vmem_limit_bytes=32 * MIB),
        cost_estimate=pl.CostEstimate(
            flops=6 * receivers * sources * events,
            bytes_accessed=4 * receivers * sources,
            transcendentals=0,
        ),
        name="stress",
    )(me, *held, kernel)

    col = lax.axis_index("cols")
    stress_change = lax.dynamic_index_in_dim(partial_sum, col, 0, keepdims=False)
    for k in range(1, width):
        mine = lax.dynamic_index_in_dim(partial_sum, col ^ k, 0, keepdims=False)
        stress_change = stress_change + send_xor(mine, "cols", width, k)
    scale = direct_effect[None, :]
    growth = jnp.expm1(load_rate * time_before / direct_effect)[None, :]
    log_time = jnp.log(scale / load_rate[None, :]) + jnp.log(
        jnp.log1p(jnp.exp(-stress_change / scale) * growth)
    )
    return (stress_change.T, log_time.T)


def solution(mesh):
    in_specs = (
        P("rows", "cols"),
        P("cols", "rows", None),
        P("cols", "rows"),
        P("cols"),
        P(("rows", "cols")),
        P(("rows", "cols")),
        P(("rows", "cols")),
    )
    out_specs = (P(("rows", "cols"), None), P(("rows", "cols"), None))
    return jax.shard_map(
        per_device, mesh=mesh, in_specs=in_specs, out_specs=out_specs, check_vma=False
    )
```

time: 157 us -> 56.4 us (0.36)
  blocking collectives: 55.9 us -> 0 us
  waiting for transfers between devices: 68.1 us -> 17.3 us
  starting transfers between devices: 0.08 us -> 26.3 us
  between operations: 14.8 us -> 0.82 us
  matrix products: 13.1 us -> 0 us
  Pallas kernels: 0 us -> 5.45 us
  local copies, waits for them, and re-layouts: 2.94 us -> 5.56 us
    psum x1 -> x0, waiting for transfers between devices: 68 us -> none  [per_device(): summed = lax.psum(partial_sum, 'cols')]
    all_gather x3 -> x0, blocking collectives: 44.1 us -> none  [the longest x1 30.5 us: per_device(): lax.all_gather(list_rows, 'cols', axis=0, tiled=True)]
    ppermute x0 -> x19, starting transfers between devices: none -> 26.3 us  [send_xor(): return lax.ppermute(block, axis, [(r, r ^ k) for r in range(width)])]
    ppermute x0 -> x19, waiting for transfers between devices: none -> 17.3 us  [send_xor(): return lax.ppermute(block, axis, [(r, r ^ k) for r in range(width)])]
    dot_general x2 -> x0, matrix products: 13.1 us -> none  [the longest x1 11.2 us: per_device(): lax.dot_general(kernel, dense_slip, (((1,), (1,)), ((), ())), precision=l...]
    unnamed x1 -> x0, blocking collectives: 11.8 us -> none
    pallas_call x0 -> x3, Pallas kernels: none -> 5.45 us  [the longest x1 3.91 us: per_device(): pl.pallas_call(functools.partial(stress_body, height, width, parts), out_...]
    unnamed x10 -> x21, local copies, waits for them, and re-layouts: 2.87 us -> 5.5 us
  transfers between devices with their start and end apart: 2 -> 19, of which waited for: 1 -> 9; matrix products, arithmetic and copies ran while one was open for 2% -> 0% of each run, Pallas kernels for 0% -> 0%
where the time goes in v2:
time: 56.4 us; the launch traced here: 56.1 us
  starting transfers between devices  26.3 us (47%)
  waiting for transfers between devices  17.3 us (31%)
  local copies, waits for them, and re-layouts  5.56 us (10%)
  Pallas kernels  5.45 us (10%)
  between operations  0.82 us (1%)
  other arithmetic  0.77 us (1%)
    ppermute x19, starting transfers between devices, send_xor(): return lax.ppermute(block, axis, [(r, r ^ k) for r in range(width)])  26.3 us
    ppermute x19, waiting for transfers between devices, send_xor(): return lax.ppermute(block, axis, [(r, r ^ k) for r in range(width)])  17.3 us
    unnamed x21, local copies, waits for them, and re-layouts  5.5 us
    pallas_call x1, Pallas kernels, per_device(): pl.pallas_call(functools.partial(stress_body, height, width, parts), out_...  3.91 us
  transfers between devices with their start and end apart: 19, of which 9 were waited for; matrix products, arithmetic and copies ran while one was open for 0% of the time, Pallas kernels for 0%

profile of v2, /device:TPU:0, one launch (start us, length us, event | category | flops | bytes accessed | tf_op | source)
XLA Modules:
  0.0 56.1 jit_solution(6563123291030480215)
XLA Ops:
  0.6 0.0 copy-start.4
  0.6 0.0 copy-start.5
  0.7 0.0 copy-start.6
  0.7 0.1 pad_add_fusion.me_ref
  0.7 0.0 copy-start.1
  0.7 0.8 %copy-done.1 = f32[8,8,128]{2,1,0:T(8,128)S(1)} copy-done((f32[8,8,128]{2,1,0:T(8,128)S(1)}, f32[8,8,128]{2,1,0:T(8,128)}, u32[]{:S(2)}) %copy-start.1) | copy-done | bytes 32792
  1.5 0.0 copy-start.2
  1.5 0.7 %copy-done.2 = s32[8,8]{1,0:T(8,128)S(1)} copy-done((s32[8,8]{1,0:T(8,128)S(1)}, s32[8,8]{1,0:T(8,128)}, u32[]{:S(2)}) %copy-start.2) | copy-done | bytes 280
  2.2 0.0 copy-start.3
  2.2 0.7 %copy-done.3 = s32[8]{0:T(128)S(1)} copy-done((s32[8]{0:T(128)S(1)}, s32[8]{0:T(128)}, u32[]{:S(2)}) %copy-start.3) | copy-done | bytes 56
  2.8 0.6 %pack.1 = (f32[2,16,128]{2,1,0:T(8,128)S(1)}, f32[2,16,128]{2,1,0:T(8,128)S(1)}, f32[2,16,128]{2,1,0:T(8,128)S(1)}, f32[2,16,128]{2,1,0:T(8,128)S(1)}) custom-call(s32[2]{0:T(128)S(1)} %pad_add_fusion.me_ref, f32[8,8,128]{2,1,0:T(8,128)S(1)} %copy-done.1, s32[8,8]{1,0:T(8,128)S(1)} %copy-done.2, s32[8]{0:T(128)S(1)} %copy-done.3), custom_call_target="tpu_custom_call" | custom-call | tf_op jit(solution)/shard_map/pack/pallas_call | solution.py:130
  3.5 0.5 collective-permute-start
  3.9 2.6 %collective-permute-start.1 = (f32[2,16,128]{2,1,0:T(8,128)S(1)}, f32[2,16,128]{2,1,0:T(8,128)S(1)}, u32[]{:S(2)}, u32[]{:S(2)}) collective-permute-start(f32[2,16,128]{2,1,0:T(8,128)S(1)} %get-tuple-element.16), channel_id=1, source_target_pairs={{0,16},{8,24},{16,0},{24,8},{1,17},{9,25},{17,1},{25,9},{2,18},{10... | collective-permute-start | bytes 49160 | tf_op jit(solution)/shard_map/ppermute | solution.py:23
  6.5 0.1 collective-permute-start.2
  6.6 0.0 collective-permute-done.refs_1_
  6.6 1.6 %collective-permute-done.1.refs_2_ = f32[2,16,128]{2,1,0:T(8,128)S(1)} collective-permute-done((f32[2,16,128]{2,1,0:T(8,128)S(1)}, f32[2,16,128]{2,1,0:T(8,128)S(1)}, u32[]{:S(2)}, u32[]{:S(2)}) %collective-permute-start.1) | collective-permute-done | bytes 16416 | tf_op jit(solution)/shard_map/ppermute | solution.py:23
  8.2 1.4 %collective-permute-done.2.refs_3_ = f32[2,16,128]{2,1,0:T(8,128)S(1)} collective-permute-done((f32[2,16,128]{2,1,0:T(8,128)S(1)}, f32[2,16,128]{2,1,0:T(8,128)S(1)}, u32[]{:S(2)}, u32[]{:S(2)}) %collective-permute-start.2) | collective-permute-done | bytes 16416 | tf_op jit(solution)/shard_map/ppermute | solution.py:23
  9.7 0.9 %densify.1 = (f32[2,16,128]{2,1,0:T(8,128)S(1)}, f32[2,16,128]{2,1,0:T(8,128)S(1)}, f32[2,16,128]{2,1,0:T(8,128)S(1)}, f32[2,16,128]{2,1,0:T(8,128)S(1)}, f32[2,...) custom-call(s32[2]{0:T(128)S(1)} %pad_add_fusion.me_ref, ...), custom_call_target="tpu_custom_call" | custom-call | tf_op jit(solution)/shard_map/densify/pallas_call | solution.py:141
  10.6 1.6 %collective-permute-start.3 = (f32[2,16,128]{2,1,0:T(8,128)S(1)}, f32[2,16,128]{2,1,0:T(8,128)S(1)}, u32[]{:S(2)}, u32[]{:S(2)}) collective-permute-start(f32[2,16,128]{2,1,0:T(8,128)S(1)} %get-tuple-element.19), channel_id=1, source_target_pairs={{0,1},{1,0},{2,3},{3,2},{4,5},{5,4},{6,7},{7,6},{8,9},{9,8},{10,11... | collective-permute-start | bytes 49160 | tf_op jit(solution)/shard_map/ppermute | solution.py:23
  12.2 1.6 %collective-permute-start.4 = (f32[2,16,128]{2,1,0:T(8,128)S(1)}, f32[2,16,128]{2,1,0:T(8,128)S(1)}, u32[]{:S(2)}, u32[]{:S(2)}) collective-permute-start(f32[2,16,128]{2,1,0:T(8,128)S(1)} %get-tuple-element.20), channel_id=1, source_target_pairs={{0,2},{1,3},{2,0},{3,1},{4,6},{5,7},{6,4},{7,5},{8,10},{9,11},{10,... | collective-permute-start | bytes 49160 | tf_op jit(solution)/shard_map/ppermute | solution.py:23
  13.7 0.4 collective-permute-start.5
  14.2 2.6 %collective-permute-start.6 = (f32[2,16,128]{2,1,0:T(8,128)S(1)}, f32[2,16,128]{2,1,0:T(8,128)S(1)}, u32[]{:S(2)}, u32[]{:S(2)}) collective-permute-start(f32[2,16,128]{2,1,0:T(8,128)S(1)} %get-tuple-element.22), channel_id=1, source_target_pairs={{0,4},{1,5},{2,6},{3,7},{4,0},{5,1},{6,2},{7,3},{8,12},{9,13},{10,... | collective-permute-start | bytes 49160 | tf_op jit(solution)/shard_map/ppermute | solution.py:23
  16.8 1.3 %collective-permute-start.7 = (f32[2,16,128]{2,1,0:T(8,128)S(1)}, f32[2,16,128]{2,1,0:T(8,128)S(1)}, u32[]{:S(2)}, u32[]{:S(2)}) collective-permute-start(f32[2,16,128]{2,1,0:T(8,128)S(1)} %get-tuple-element.23), channel_id=1, source_target_pairs={{0,5},{1,4},{2,7},{3,6},{4,1},{5,0},{6,3},{7,2},{8,13},{9,12},{10,... | collective-permute-start | bytes 49160 | tf_op jit(solution)/shard_map/ppermute | solution.py:23
  18.0 0.0 collective-permute-done.3
  18.0 3.6 %collective-permute-start.8 = (f32[2,16,128]{2,1,0:T(8,128)S(1)}, f32[2,16,128]{2,1,0:T(8,128)S(1)}, u32[]{:S(2)}, u32[]{:S(2)}) collective-permute-start(f32[2,16,128]{2,1,0:T(8,128)S(1)} %get-tuple-element.24), channel_id=1, source_target_pairs={{0,6},{1,7},{2,4},{3,5},{4,2},{5,3},{6,0},{7,1},{8,14},{9,15},{10,... | collective-permute-start | bytes 49160 | tf_op jit(solution)/shard_map/ppermute | solution.py:23
  21.6 0.0 collective-permute-done.4
  21.6 0.2 collective-permute-start.9
  21.8 0.0 collective-permute-done.5
  21.8 0.0 collective-permute-done.6
  21.9 0.4 collective-permute-done.7
  22.3 1.3 %collective-permute-done.8 = f32[2,16,128]{2,1,0:T(8,128)S(1)} collective-permute-done((f32[2,16,128]{2,1,0:T(8,128)S(1)}, f32[2,16,128]{2,1,0:T(8,128)S(1)}, u32[]{:S(2)}, u32[]{:S(2)}) %collective-permute-start.8) | collective-permute-done | bytes 16416 | tf_op jit(solution)/shard_map/ppermute | solution.py:23
  23.6 4.5 %collective-permute-done.9 = f32[2,16,128]{2,1,0:T(8,128)S(1)} collective-permute-done((f32[2,16,128]{2,1,0:T(8,128)S(1)}, f32[2,16,128]{2,1,0:T(8,128)S(1)}, u32[]{:S(2)}, u32[]{:S(2)}) %collective-permute-start.9) | collective-permute-done | bytes 16416 | tf_op jit(solution)/shard_map/ppermute | solution.py:23
  28.1 0.7 %collective-permute-start.10 = (f32[1,8,2,16,128]{4,3,2,1,0:T(8,128)S(1)}, f32[1,8,2,16,128]{4,3,2,1,0:T(8,128)S(1)}, u32[]{:S(2)}, u32[]{:S(2)}) collective-permute-start(f32[1,8,2,16,128]{4,3,2,1,0:T(8,128)S(1)} %bitcast.56), channel_id=1, source_target_pairs={{0,16},{8,24},{16,0},{24,8},{1,17},{9,25},{17,1},{25,9},{2,18},{10... | collective-permute-start | bytes 393224 | tf_op jit(solution)/shard_map/ppermute | solution.py:23
  28.8 4.3 %collective-permute-done.10 = f32[1,8,2,16,128]{4,3,2,1,0:T(8,128)S(1)} collective-permute-done((f32[1,8,2,16,128]{4,3,2,1,0:T(8,128)S(1)}, f32[1,8,2,16,128]{4,3,2,1,0:T(8,128)S(1)}, u32[]{:S(2)}, u32[]{:S(2)}) %collective-permute-start.10) | collective-permute-done | bytes 131104 | tf_op jit(solution)/shard_map/ppermute | solution.py:23
  33.1 0.1 collective-permute-start.11
  33.2 1.5 %collective-permute-done.11 = f32[2,8,2,16,128]{4,3,2,1,0:T(8,128)S(1)} collective-permute-done((f32[2,8,2,16,128]{4,3,2,1,0:T(8,128)S(1)}, f32[2,8,2,16,128]{4,3,2,1,0:T(8,128)S(1)}, u32[]{:S(2)}, u32[]{:S(2)}) %collective-permute-start.11) | collective-permute-done | bytes 262176 | tf_op jit(solution)/shard_map/ppermute | solution.py:23
  34.7 0.0 copy-start
  34.7 3.4 %copy-done = f32[1024,2048]{1,0:T(8,128)S(1)} copy-done((f32[1024,2048]{1,0:T(8,128)S(1)}, f32[1024,2048]{1,0:T(8,128)}, u32[]{:S(2)}) %copy-start) | copy-done | bytes 8388632
  38.1 3.9 %stress.1 = f32[8,64,128]{2,1,0:T(8,128)S(1)} custom-call(s32[2]{0:T(128)S(1)} %pad_add_fusion.me_ref, f32[8,2,16,128]{3,2,1,0:T(8,128)S(1)} %constant_dynamic-update-slice_fusion.refs_0_, f32[8,2,16,128]{3,2,1,0:T(8,128)S(1)} %get-tuple-element.36.refs_1_, f32[8,2,16,128]{3,2,1,0:T(8,128)S(1)} %bitcast.58, f32[8,2,16,128]{3,2,1,0:T(8,128)S(1)} %get-tuple-element.35.refs_3_, ...), custom_call_target="tpu_custom_call" | custom-call | flops 805306368 | bytes 8388608 | tf_op jit(solution)/shard_map/stress/pallas_call | solution.py:163
  42.0 0.6 %collective-permute-start.12 = (f32[64,128]{1,0:T(8,128)S(1)}, f32[64,128]{1,0:T(8,128)S(1)}, u32[]{:S(2)}, u32[]{:S(2)}) collective-permute-start(f32[64,128]{1,0:T(8,128)S(1)} %get-tuple-element.28), channel_id=1, source_target_pairs={{0,1},{1,0},{2,3},{3,2},{4,5},{5,4},{6,7},{7,6},{8,9},{9,8},{10,11... | collective-permute-start | bytes 98312 | tf_op jit(solution)/shard_map/ppermute | solution.py:23
  42.6 0.0 collective-permute-start.13
  42.6 3.0 %collective-permute-start.14 = (f32[64,128]{1,0:T(8,128)S(1)}, f32[64,128]{1,0:T(8,128)S(1)}, u32[]{:S(2)}, u32[]{:S(2)}) collective-permute-start(f32[64,128]{1,0:T(8,128)S(1)} %get-tuple-element.33), channel_id=1, source_target_pairs={{0,3},{1,2},{2,1},{3,0},{4,7},{5,6},{6,5},{7,4},{8,11},{9,10},{10,... | collective-permute-start | bytes 98312 | tf_op jit(solution)/shard_map/ppermute | solution.py:23
  45.6 0.0 collective-permute-start.15
  45.6 2.9 %collective-permute-start.16 = (f32[64,128]{1,0:T(8,128)S(1)}, f32[64,128]{1,0:T(8,128)S(1)}, u32[]{:S(2)}, u32[]{:S(2)}) collective-permute-start(f32[64,128]{1,0:T(8,128)S(1)} %get-tuple-element.31), channel_id=1, source_target_pairs={{0,5},{1,4},{2,7},{3,6},{4,1},{5,0},{6,3},{7,2},{8,13},{9,12},{10,... | collective-permute-start | bytes 98312 | tf_op jit(solution)/shard_map/ppermute | solution.py:23
  48.5 0.0 collective-permute-done.12
  48.5 0.2 collective-permute-start.17
  48.7 0.0 collective-permute-done.13
  48.7 4.5 %collective-permute-start.18 = (f32[64,128]{1,0:T(8,128)S(1)}, f32[64,128]{1,0:T(8,128)S(1)}, u32[]{:S(2)}, u32[]{:S(2)}) collective-permute-start(f32[64,128]{1,0:T(8,128)S(1)} %get-tuple-element.29), channel_id=1, source_target_pairs={{0,7},{1,6},{2,5},{3,4},{4,3},{5,2},{6,1},{7,0},{8,15},{9,14},{10,... | collective-permute-start | bytes 98312 | tf_op jit(solution)/shard_map/ppermute | solution.py:23
  53.2 0.0 copy-done.4
  53.2 0.0 copy-done.5
  53.2 0.0 copy-done.6
  53.3 0.0 collective-permute-done.14
  53.3 0.0 collective-permute-done.15
  53.3 0.0 collective-permute-done.16
  53.3 0.9 %collective-permute-done.17 = f32[64,128]{1,0:T(8,128)S(1)} collective-permute-done((f32[64,128]{1,0:T(8,128)S(1)}, f32[64,128]{1,0:T(8,128)S(1)}, u32[]{:S(2)}, u32[]{:S(2)}) %collective-permute-start.17) | collective-permute-done | bytes 32800 | tf_op jit(solution)/shard_map/ppermute | solution.py:23
  54.2 1.3 %collective-permute-done.18 = f32[64,128]{1,0:T(8,128)S(1)} collective-permute-done((f32[64,128]{1,0:T(8,128)S(1)}, f32[64,128]{1,0:T(8,128)S(1)}, u32[]{:S(2)}, u32[]{:S(2)}) %collective-permute-start.18) | collective-permute-done | bytes 32800 | tf_op jit(solution)/shard_map/ppermute | solution.py:23
  55.5 0.7 %add_bitcast_fusion = (f32[128,64]{0,1:T(8,128)}, f32[64,128]{1,0:T(8,128)}) fusion(f32[128]{0:T(128)S(1)} %get-tuple-element.38, f32[128]{0:T(128)S(1)} %copy-done.4, f32[128]{0:T(128)S(1)} %get-tuple-element.37, f32[64,128]{1,0:T(8,128)S(1)} %collective-permute-done.18, f32[64,128]{1,0:T(8,128)S(1)} %collective-permute-done.17, ...), kind=kLoop, calls=%fused_computation.10 | loop fusion | flops 90112 | bytes 329220 | tf_op jit(solution)/shard_map/transpose | solution.py:194
  (12 shorter events, 0.1 us)
Async XLA Ops:
  0.6 52.6 %copy-start.4 = (f32[128]{0:T(128)S(1)}, f32[128]{0:T(128)}, u32[]{:S(2)}) copy-start(f32[128]{0:T(128)} %param.11) | copy-start | bytes 1540
  0.6 52.6 %copy-start.5 = (f32[128]{0:T(128)S(1)}, f32[128]{0:T(128)}, u32[]{:S(2)}) copy-start(f32[128]{0:T(128)} %param.12) | copy-start | bytes 1540
  0.7 52.6 %copy-start.6 = (f32[128]{0:T(128)S(1)}, f32[128]{0:T(128)}, u32[]{:S(2)}) copy-start(f32[128]{0:T(128)} %param.13) | copy-start | bytes 1540
  0.7 0.8 %copy-start.1 = (f32[8,8,128]{2,1,0:T(8,128)S(1)}, f32[8,8,128]{2,1,0:T(8,128)}, u32[]{:S(2)}) copy-start(f32[8,8,128]{2,1,0:T(8,128)} %slip_ref.1) | copy-start | bytes 98308
  1.5 0.7 %copy-start.2 = (s32[8,8]{1,0:T(8,128)S(1)}, s32[8,8]{1,0:T(8,128)}, u32[]{:S(2)}) copy-start(s32[8,8]{1,0:T(8,128)} %list_ref.1) | copy-start | bytes 772
  2.2 0.7 %copy-start.3 = (s32[8]{0:T(128)S(1)}, s32[8]{0:T(128)}, u32[]{:S(2)}) copy-start(s32[8]{0:T(128)} %count_ref.1) | copy-start | bytes 100
  3.5 3.1 %collective-permute-start = (f32[2,16,128]{2,1,0:T(8,128)S(1)}, f32[2,16,128]{2,1,0:T(8,128)S(1)}, u32[]{:S(2)}, u32[]{:S(2)}) collective-permute-start(f32[2,16,128]{2,1,0:T(8,128)S(1)} %get-tuple-element.15), channel_id=1, source_target_pairs={{0,8},{8,0},{16,24},{24,16},{1,9},{9,1},{17,25},{25,17},{2,10},{10... | collective-permute-start | bytes 49160 | tf_op jit(solution)/shard_map/ppermute | solution.py:23
  3.9 4.3 %collective-permute-start.1 = (f32[2,16,128]{2,1,0:T(8,128)S(1)}, f32[2,16,128]{2,1,0:T(8,128)S(1)}, u32[]{:S(2)}, u32[]{:S(2)}) collective-permute-start(f32[2,16,128]{2,1,0:T(8,128)S(1)} %get-tuple-element.16), channel_id=1, source_target_pairs={{0,16},{8,24},{16,0},{24,8},{1,17},{9,25},{17,1},{25,9},{2,18},{10... | collective-permute-start | bytes 49160 | tf_op jit(solution)/shard_map/ppermute | solution.py:23
  6.5 3.2 %collective-permute-start.2 = (f32[2,16,128]{2,1,0:T(8,128)S(1)}, f32[2,16,128]{2,1,0:T(8,128)S(1)}, u32[]{:S(2)}, u32[]{:S(2)}) collective-permute-start(f32[2,16,128]{2,1,0:T(8,128)S(1)} %get-tuple-element.17), channel_id=1, source_target_pairs={{0,24},{8,16},{16,8},{24,0},{1,25},{9,17},{17,9},{25,1},{2,26},{10... | collective-permute-start | bytes 49160 | tf_op jit(solution)/shard_map/ppermute | solution.py:23
  10.6 7.4 %collective-permute-start.3 = (f32[2,16,128]{2,1,0:T(8,128)S(1)}, f32[2,16,128]{2,1,0:T(8,128)S(1)}, u32[]{:S(2)}, u32[]{:S(2)}) collective-permute-start(f32[2,16,128]{2,1,0:T(8,128)S(1)} %get-tuple-element.19), channel_id=1, source_target_pairs={{0,1},{1,0},{2,3},{3,2},{4,5},{5,4},{6,7},{7,6},{8,9},{9,8},{10,11... | collective-permute-start | bytes 49160 | tf_op jit(solution)/shard_map/ppermute | solution.py:23
  12.2 9.5 %collective-permute-start.4 = (f32[2,16,128]{2,1,0:T(8,128)S(1)}, f32[2,16,128]{2,1,0:T(8,128)S(1)}, u32[]{:S(2)}, u32[]{:S(2)}) collective-permute-start(f32[2,16,128]{2,1,0:T(8,128)S(1)} %get-tuple-element.20), channel_id=1, source_target_pairs={{0,2},{1,3},{2,0},{3,1},{4,6},{5,7},{6,4},{7,5},{8,10},{9,11},{10,... | collective-permute-start | bytes 49160 | tf_op jit(solution)/shard_map/ppermute | solution.py:23
  13.7 8.1 %collective-permute-start.5 = (f32[2,16,128]{2,1,0:T(8,128)S(1)}, f32[2,16,128]{2,1,0:T(8,128)S(1)}, u32[]{:S(2)}, u32[]{:S(2)}) collective-permute-start(f32[2,16,128]{2,1,0:T(8,128)S(1)} %get-tuple-element.21), channel_id=1, source_target_pairs={{0,3},{1,2},{2,1},{3,0},{4,7},{5,6},{6,5},{7,4},{8,11},{9,10},{10,... | collective-permute-start | bytes 49160 | tf_op jit(solution)/shard_map/ppermute | solution.py:23
  14.2 7.7 %collective-permute-start.6 = (f32[2,16,128]{2,1,0:T(8,128)S(1)}, f32[2,16,128]{2,1,0:T(8,128)S(1)}, u32[]{:S(2)}, u32[]{:S(2)}) collective-permute-start(f32[2,16,128]{2,1,0:T(8,128)S(1)} %get-tuple-element.22), channel_id=1, source_target_pairs={{0,4},{1,5},{2,6},{3,7},{4,0},{5,1},{6,2},{7,3},{8,12},{9,13},{10,... | collective-permute-start | bytes 49160 | tf_op jit(solution)/shard_map/ppermute | solution.py:23
  16.8 5.5 %collective-permute-start.7 = (f32[2,16,128]{2,1,0:T(8,128)S(1)}, f32[2,16,128]{2,1,0:T(8,128)S(1)}, u32[]{:S(2)}, u32[]{:S(2)}) collective-permute-start(f32[2,16,128]{2,1,0:T(8,128)S(1)} %get-tuple-element.23), channel_id=1, source_target_pairs={{0,5},{1,4},{2,7},{3,6},{4,1},{5,0},{6,3},{7,2},{8,13},{9,12},{10,... | collective-permute-start | bytes 49160 | tf_op jit(solution)/shard_map/ppermute | solution.py:23
  18.0 5.5 %collective-permute-start.8 = (f32[2,16,128]{2,1,0:T(8,128)S(1)}, f32[2,16,128]{2,1,0:T(8,128)S(1)}, u32[]{:S(2)}, u32[]{:S(2)}) collective-permute-start(f32[2,16,128]{2,1,0:T(8,128)S(1)} %get-tuple-element.24), channel_id=1, source_target_pairs={{0,6},{1,7},{2,4},{3,5},{4,2},{5,3},{6,0},{7,1},{8,14},{9,15},{10,... | collective-permute-start | bytes 49160 | tf_op jit(solution)/shard_map/ppermute | solution.py:23
  21.6 6.4 %collective-permute-start.9 = (f32[2,16,128]{2,1,0:T(8,128)S(1)}, f32[2,16,128]{2,1,0:T(8,128)S(1)}, u32[]{:S(2)}, u32[]{:S(2)}) collective-permute-start(f32[2,16,128]{2,1,0:T(8,128)S(1)} %get-tuple-element.25), channel_id=1, source_target_pairs={{0,7},{1,6},{2,5},{3,4},{4,3},{5,2},{6,1},{7,0},{8,15},{9,14},{10,... | collective-permute-start | bytes 49160 | tf_op jit(solution)/shard_map/ppermute | solution.py:23
  28.1 5.0 %collective-permute-start.10 = (f32[1,8,2,16,128]{4,3,2,1,0:T(8,128)S(1)}, f32[1,8,2,16,128]{4,3,2,1,0:T(8,128)S(1)}, u32[]{:S(2)}, u32[]{:S(2)}) collective-permute-start(f32[1,8,2,16,128]{4,3,2,1,0:T(8,128)S(1)} %bitcast.56), channel_id=1, source_target_pairs={{0,16},{8,24},{16,0},{24,8},{1,17},{9,25},{17,1},{25,9},{2,18},{10... | collective-permute-start | bytes 393224 | tf_op jit(solution)/shard_map/ppermute | solution.py:23
  33.1 1.6 %collective-permute-start.11 = (f32[2,8,2,16,128]{4,3,2,1,0:T(8,128)S(1)}, f32[2,8,2,16,128]{4,3,2,1,0:T(8,128)S(1)}, u32[]{:S(2)}, u32[]{:S(2)}) collective-permute-start(f32[2,8,2,16,128]{4,3,2,1,0:T(8,128)S(1)} %pad_maximum_fusion), channel_id=1, source_target_pairs={{0,8},{8,0},{16,24},{24,16},{1,9},{9,1},{17,25},{25,17},{2,10},{10... | collective-permute-start | bytes 786440 | tf_op jit(solution)/shard_map/ppermute | solution.py:23
  34.7 3.4 %copy-start = (f32[1024,2048]{1,0:T(8,128)S(1)}, f32[1024,2048]{1,0:T(8,128)}, u32[]{:S(2)}) copy-start(f32[1024,2048]{1,0:T(8,128)} %refs_4_.1) | copy-start | bytes 25165828
  42.0 6.5 %collective-permute-start.12 = (f32[64,128]{1,0:T(8,128)S(1)}, f32[64,128]{1,0:T(8,128)S(1)}, u32[]{:S(2)}, u32[]{:S(2)}) collective-permute-start(f32[64,128]{1,0:T(8,128)S(1)} %get-tuple-element.28), channel_id=1, source_target_pairs={{0,1},{1,0},{2,3},{3,2},{4,5},{5,4},{6,7},{7,6},{8,9},{9,8},{10,11... | collective-permute-start | bytes 98312 | tf_op jit(solution)/shard_map/ppermute | solution.py:23
  42.6 6.1 %collective-permute-start.13 = (f32[64,128]{1,0:T(8,128)S(1)}, f32[64,128]{1,0:T(8,128)S(1)}, u32[]{:S(2)}, u32[]{:S(2)}) collective-permute-start(f32[64,128]{1,0:T(8,128)S(1)} %get-tuple-element.34), channel_id=1, source_target_pairs={{0,2},{1,3},{2,0},{3,1},{4,6},{5,7},{6,4},{7,5},{8,10},{9,11},{10,... | collective-permute-start | bytes 98312 | tf_op jit(solution)/shard_map/ppermute | solution.py:23
  42.6 10.6 %collective-permute-start.14 = (f32[64,128]{1,0:T(8,128)S(1)}, f32[64,128]{1,0:T(8,128)S(1)}, u32[]{:S(2)}, u32[]{:S(2)}) collective-permute-start(f32[64,128]{1,0:T(8,128)S(1)} %get-tuple-element.33), channel_id=1, source_target_pairs={{0,3},{1,2},{2,1},{3,0},{4,7},{5,6},{6,5},{7,4},{8,11},{9,10},{10,... | collective-permute-start | bytes 98312 | tf_op jit(solution)/shard_map/ppermute | solution.py:23
  45.6 7.7 %collective-permute-start.15 = (f32[64,128]{1,0:T(8,128)S(1)}, f32[64,128]{1,0:T(8,128)S(1)}, u32[]{:S(2)}, u32[]{:S(2)}) collective-permute-start(f32[64,128]{1,0:T(8,128)S(1)} %get-tuple-element.32), channel_id=1, source_target_pairs={{0,4},{1,5},{2,6},{3,7},{4,0},{5,1},{6,2},{7,3},{8,12},{9,13},{10,... | collective-permute-start | bytes 98312 | tf_op jit(solution)/shard_map/ppermute | solution.py:23
  45.6 7.7 %collective-permute-start.16 = (f32[64,128]{1,0:T(8,128)S(1)}, f32[64,128]{1,0:T(8,128)S(1)}, u32[]{:S(2)}, u32[]{:S(2)}) collective-permute-start(f32[64,128]{1,0:T(8,128)S(1)} %get-tuple-element.31), channel_id=1, source_target_pairs={{0,5},{1,4},{2,7},{3,6},{4,1},{5,0},{6,3},{7,2},{8,13},{9,12},{10,... | collective-permute-start | bytes 98312 | tf_op jit(solution)/shard_map/ppermute | solution.py:23
  48.5 5.7 %collective-permute-start.17 = (f32[64,128]{1,0:T(8,128)S(1)}, f32[64,128]{1,0:T(8,128)S(1)}, u32[]{:S(2)}, u32[]{:S(2)}) collective-permute-start(f32[64,128]{1,0:T(8,128)S(1)} %get-tuple-element.30), channel_id=1, source_target_pairs={{0,6},{1,7},{2,4},{3,5},{4,2},{5,3},{6,0},{7,1},{8,14},{9,15},{10,... | collective-permute-start | bytes 98312 | tf_op jit(solution)/shard_map/ppermute | solution.py:23
  48.7 6.8 %collective-permute-start.18 = (f32[64,128]{1,0:T(8,128)S(1)}, f32[64,128]{1,0:T(8,128)S(1)}, u32[]{:S(2)}, u32[]{:S(2)}) collective-permute-start(f32[64,128]{1,0:T(8,128)S(1)} %get-tuple-element.29), channel_id=1, source_target_pairs={{0,7},{1,6},{2,5},{3,4},{4,3},{5,2},{6,1},{7,0},{8,15},{9,14},{10,... | collective-permute-start | bytes 98312 | tf_op jit(solution)/shard_map/ppermute | solution.py:23

commit v3 on v0

v3 whole, which is shorter than its diff:
```python
import functools

import jax
import jax.numpy as jnp
from jax import lax
from jax.experimental import pallas as pl
from jax.experimental.pallas import tpu as pltpu
from jax.sharding import PartitionSpec as P

BLOCK = 128
SUB = 8
VMEM_SPEC = pl.BlockSpec(memory_space=pltpu.VMEM)
SMEM_SPEC = pl.BlockSpec(memory_space=pltpu.SMEM)
HBM_SPEC = pl.BlockSpec(memory_space=pltpu.HBM)
MIB = 1024 * 1024
NT = (((1,), (1,)), ((), ()))


def f32(*shape):
    return jax.ShapeDtypeStruct(shape, jnp.float32)


def bf16(*shape):
    return jax.ShapeDtypeStruct(shape, jnp.bfloat16)


def params(mib):
    return pltpu.CompilerParams(vmem_limit_bytes=mib * MIB)


def send_xor(block, axis, k):
    return lax.ppermute(block, axis, [(r, r ^ k) for r in range(lax.axis_size(axis))])


def pack_body(me_ref, slip_hbm, list_hbm, count_hbm, out_ref, slip_ref, list_ref, count_ref, ids, sems):
    copies = [
        pltpu.make_async_copy(src, dst, sems.at[j])
        for j, (src, dst) in enumerate(((slip_hbm, slip_ref), (list_hbm, list_ref), (count_hbm, count_ref)))
    ]
    for copy in copies:
        copy.start()
    for copy in copies:
        copy.wait()
    events, entries = list_ref.shape
    half = events // 2
    row = me_ref[0]
    entry = lax.broadcasted_iota(jnp.int32, (events, entries), 1) + row * entries
    event = lax.broadcasted_iota(jnp.int32, (events, entries), 0)
    count = jnp.zeros((events, entries), jnp.int32)
    for e in range(events):
        count = jnp.where(event == e, count_ref[e], count)
    ids[...] = jnp.full(ids.shape, -1.0, jnp.float32)
    ids[0:events, 0:entries] = jnp.where(entry < count, list_ref[...], -1).astype(jnp.float32)
    ids[...] = pltpu.roll(ids[...], row * entries, 1)
    for h in range(2):
        first = ((row % 2) ^ h) * half
        for i in range(half):
            out_ref[h, i, 0:entries, :] = slip_ref[first + i]
            out_ref[h, half, i : i + 1, :] = ids[pl.ds(first + i, 1), :]


def densify_body(entries, me_ref, own_ref, came_ref, out_ref, slips):
    halves, half = own_ref.shape[0], own_ref.shape[1] - 1
    width, _, blocks_here, _ = out_ref.shape
    blocks = width * blocks_here
    live = 2 * halves * entries
    row = me_ref[0]
    for i in range(half):
        ids = jnp.full((1, BLOCK), -1.0, jnp.float32)
        for ref in (own_ref, came_ref):
            for j in range(halves):
                ids = jnp.maximum(ids, ref[j, half, i : i + 1, :])
        ids = jnp.broadcast_to(ids, (blocks, BLOCK))[:, :live]
        number = lax.broadcasted_iota(jnp.int32, ids.shape, 0).astype(jnp.float32)
        onehot = (ids == number).astype(jnp.bfloat16)
        for core, ref in enumerate((own_ref, came_ref)):
            for j in range(halves):
                source = row ^ (2 * j + core)
                slips[i, pl.ds(pl.multiple_of(source * entries, entries), entries), :] = ref[j, i, 0:entries, :]
        slip = slips[i]
        total = jnp.zeros((blocks, BLOCK), jnp.float32)
        for _ in range(3):
            piece = slip.astype(jnp.bfloat16)
            slip = slip - piece.astype(jnp.float32)
            total = total + jnp.dot(onehot, piece, preferred_element_type=jnp.float32)
        out_ref[:, i] = total.reshape(width, blocks_here, BLOCK)


def split_body(kernel_hbm, hi_ref, lo_ref, held, sems):
    steps = held.shape[0]
    rows = held.shape[1]
    copies = [
        pltpu.make_async_copy(kernel_hbm.at[pl.ds(s * rows, rows)], held.at[s], sems.at[s]) for s in range(steps)
    ]
    for copy in copies:
        copy.start()
    for s, copy in enumerate(copies):
        copy.wait()
        block = held[s]
        hi = block.astype(jnp.bfloat16)
        hi_ref[s * rows : (s + 1) * rows, :] = hi
        lo_ref[s * rows : (s + 1) * rows, :] = (block - hi.astype(jnp.float32)).astype(jnp.bfloat16)


def assemble_body(me_ref, own_ref, came_ref, out_ref, dense):
    width, half, blocks_here, _ = own_ref.shape
    events = dense.shape[0]
    core = me_ref[0] % 2
    for c in range(width):
        for other, ref in enumerate((own_ref, came_ref)):
            for i in range(half):
                dense[(2 * c + (core ^ other)) * half + i] = ref[c, i]
    flat = dense.reshape(events * blocks_here, BLOCK)
    for t in range(events // (2 * SUB)):
        for b in range(blocks_here):
            rows = [
                flat[pl.ds((2 * t + u) * SUB * blocks_here + b, SUB, stride=blocks_here), :] for u in range(2)
            ]
            slip = jnp.concatenate(rows, axis=0)
            hi = slip.astype(jnp.bfloat16)
            lo = (slip - hi.astype(jnp.float32)).astype(jnp.bfloat16)
            where = slice(b * BLOCK, (b + 1) * BLOCK)
            out_ref[2 * t * SUB : 2 * (t + 1) * SUB, where] = hi
            out_ref[events + 2 * t * SUB : events + 2 * (t + 1) * SUB, where] = lo


def stress_body(targets, me_ref, slip_ref, hi_ref, lo_ref, out_ref):
    events = slip_ref.shape[0] // 2
    share = out_ref.shape[2]
    col = me_ref[1]
    for j, k in enumerate(targets):
        rows = pl.ds(pl.multiple_of((col ^ k) * share, share), share)
        first = lax.dot_general(slip_ref[...], hi_ref[rows, :], NT, preferred_element_type=jnp.float32)
        second = lax.dot_general(slip_ref[:events, :], lo_ref[rows, :], NT, preferred_element_type=jnp.float32)
        out_ref[j] = first[:events] + first[events:] + second


def halving_order(width):
    bits = width.bit_length() - 1
    return [int(f"{k:0{bits}b}"[::-1], 2) for k in range(width)]


def per_device(kernel, slip_delta, block_list, live_count, direct_effect, load_rate, time_before):
    width = lax.axis_size("cols")
    height = lax.axis_size("rows")
    events_here, entries = block_list.shape
    half = events_here // 2
    events = events_here * width
    receivers, sources = kernel.shape
    blocks_here = sources // BLOCK
    me = jnp.stack([lax.axis_index("rows"), lax.axis_index("cols")]).astype(jnp.int32)

    packed = pl.pallas_call(
        pack_body,
        out_shape=f32(2, half + 1, SUB, BLOCK),
        in_specs=[SMEM_SPEC, HBM_SPEC, HBM_SPEC, HBM_SPEC],
        out_specs=VMEM_SPEC,
        scratch_shapes=[
            pltpu.VMEM(slip_delta.shape, jnp.float32),
            pltpu.VMEM(block_list.shape, jnp.int32),
            pltpu.SMEM(live_count.shape, jnp.int32),
            pltpu.VMEM((SUB, BLOCK), jnp.float32),
            pltpu.SemaphoreType.DMA((3,)),
        ],
        compiler_params=params(4),
        name="pack",
    )(me, slip_delta, block_list, live_count)
    held = packed[None]
    step = 2
    while step < height:
        held = jnp.concatenate([held, send_xor(held, "rows", step)], axis=0)
        step *= 2
    came = send_xor(held[:, 1], "rows", 1)

    dense = pl.pallas_call(
        functools.partial(densify_body, entries),
        out_shape=f32(width, half, blocks_here, BLOCK),
        in_specs=[SMEM_SPEC, VMEM_SPEC, VMEM_SPEC],
        out_specs=VMEM_SPEC,
        scratch_shapes=[pltpu.VMEM((half, height * entries, BLOCK), jnp.float32)],
        compiler_params=params(8),
        name="densify",
    )(me, held[:, 0], came)
    mine = lax.all_to_all(dense, "cols", 0, 0, tiled=True)

    steps = 8
    hi, lo = pl.pallas_call(
        split_body,
        out_shape=[bf16(receivers, sources)] * 2,
        in_specs=[HBM_SPEC],
        out_specs=[VMEM_SPEC] * 2,
        scratch_shapes=[
            pltpu.VMEM((steps, receivers // steps, sources), jnp.float32),
            pltpu.SemaphoreType.DMA((steps,)),
        ],
        compiler_params=params(24),
        cost_estimate=pl.CostEstimate(
            flops=3 * receivers * sources, bytes_accessed=8 * receivers * sources, transcendentals=0
        ),
        name="split",
    )(kernel)

    slips = pl.pallas_call(
        assemble_body,
        out_shape=bf16(2 * events, sources),
        in_specs=[SMEM_SPEC, VMEM_SPEC, VMEM_SPEC],
        out_specs=VMEM_SPEC,
        scratch_shapes=[pltpu.VMEM((events, blocks_here, BLOCK), jnp.float32)],
        compiler_params=params(8),
        name="assemble",
    )(me, mine, send_xor(mine, "rows", 1))

    share = receivers // width

    def stress(targets):
        return pl.pallas_call(
            functools.partial(stress_body, targets),
            out_shape=f32(len(targets), events, share),
            in_specs=[SMEM_SPEC] + [VMEM_SPEC] * 3,
            out_specs=VMEM_SPEC,
            compiler_params=params(8),
            cost_estimate=pl.CostEstimate(
                flops=6 * len(targets) * share * sources * events,
                bytes_accessed=4 * len(targets) * share * sources,
                transcendentals=0,
            ),
            name="stress",
        )(me, slips, hi, lo)

    order = halving_order(width)
    sent = stress(order[width // 2 :])
    came = send_xor(sent, "cols", 1)
    total = stress(order[: width // 2]) + came
    step = 2
    while step < width:
        keep = total.shape[0] // 2
        total = total[:keep] + send_xor(total[keep:], "cols", step)
        step *= 2
    stress_change = total[0]
    scale = direct_effect[None, :]
    growth = jnp.expm1(load_rate * time_before / direct_effect)[None, :]
    log_time = jnp.log(scale / load_rate[None, :]) + jnp.log(
        jnp.log1p(jnp.exp(-stress_change / scale) * growth)
    )
    return (stress_change.T, log_time.T)


def solution(mesh):
    in_specs = (
        P("rows", "cols"),
        P("cols", "rows", None),
        P("cols", "rows"),
        P("cols"),
        P(("rows", "cols")),
        P(("rows", "cols")),
        P(("rows", "cols")),
    )
    out_specs = (P(("rows", "cols"), None), P(("rows", "cols"), None))
    return jax.shard_map(
        per_device, mesh=mesh, in_specs=in_specs, out_specs=out_specs, check_vma=False
    )
```

time: 157 us -> 51.3 us (0.33)
  waiting for transfers between devices: 68.1 us -> 12.6 us
  blocking collectives: 55.9 us -> 15.3 us
  between operations: 14.8 us -> 0.74 us
  matrix products: 13.1 us -> 0 us
  Pallas kernels: 0 us -> 8.56 us
  starting transfers between devices: 0.08 us -> 6.77 us
  local copies, waits for them, and re-layouts: 2.94 us -> 5.51 us
    psum x1 -> x0, waiting for transfers between devices: 68 us -> none  [per_device(): summed = lax.psum(partial_sum, 'cols')]
    all_gather x3 -> x0, blocking collectives: 44.1 us -> none  [the longest x1 30.5 us: per_device(): lax.all_gather(list_rows, 'cols', axis=0, tiled=True)]
    all_to_all x0 -> x1, blocking collectives: none -> 15.3 us  [per_device(): mine = lax.all_to_all(dense, 'cols', 0, 0, tiled=True)]
    dot_general x2 -> x0, matrix products: 13.1 us -> none  [the longest x1 11.2 us: per_device(): lax.dot_general(kernel, dense_slip, (((1,), (1,)), ((), ())), precision=l...]
    ppermute x0 -> x6, waiting for transfers between devices: none -> 12.6 us  [send_xor(): lax.ppermute(block, axis, [(r, r ^ k) for r in range(lax.axis_size(axis))])]
    unnamed x1 -> x0, blocking collectives: 11.8 us -> none
    pallas_call x0 -> x6, Pallas kernels: none -> 8.56 us  [the longest x2 3.95 us: stress(): pl.pallas_call(functools.partial(stress_body, targets), out_shape=f32(len...]
    ppermute x0 -> x6, starting transfers between devices: none -> 6.77 us  [send_xor(): lax.ppermute(block, axis, [(r, r ^ k) for r in range(lax.axis_size(axis))])]
  transfers between devices with their start and end apart: 2 -> 6, of which waited for: 1 -> 5; matrix products, arithmetic and copies ran while one was open for 2% -> 0% of each run, Pallas kernels for 0% -> 7%
where the time goes in v3:
time: 51.3 us; the launch traced here: 51 us
  blocking collectives  15.3 us (30%)
  waiting for transfers between devices  12.6 us (25%)
  Pallas kernels  8.56 us (17%)
  starting transfers between devices  6.77 us (13%)
  local copies, waits for them, and re-layouts  5.51 us (11%)
  other arithmetic  1.4 us (3%)
  between operations  0.74 us (1%)
    all_to_all x1, blocking collectives, per_device(): mine = lax.all_to_all(dense, 'cols', 0, 0, tiled=True)  15.3 us
    ppermute x6, waiting for transfers between devices, send_xor(): lax.ppermute(block, axis, [(r, r ^ k) for r in range(lax.axis_size(axis))])  12.6 us
    ppermute x6, starting transfers between devices, send_xor(): lax.ppermute(block, axis, [(r, r ^ k) for r in range(lax.axis_size(axis))])  6.77 us
    unnamed x14, local copies, waits for them, and re-layouts  5.5 us
    pallas_call x2, Pallas kernels, stress(): pl.pallas_call(functools.partial(stress_body, targets), out_shape=f32(len...  3.95 us
    pallas_call x1, Pallas kernels, per_device(): pl.pallas_call(split_body, out_shape=[bf16(receivers, sources)] * 2, in_s...  1.78 us
    transpose x2, other arithmetic, per_device(): return (stress_change.T, log_time.T)  1.28 us
    pallas_call x1, Pallas kernels, per_device(): pl.pallas_call(pack_body, out_shape=f32(2, half + 1, SUB, BLOCK), in_spec...  1.24 us
  transfers between devices with their start and end apart: 6, of which 5 were waited for; matrix products, arithmetic and copies ran while one was open for 0% of the time, Pallas kernels for 7%

profile of v3, /device:TPU:0, one launch (start us, length us, event | category | flops | bytes accessed | tf_op | source)
XLA Modules:
  0.0 51.0 jit_solution(2565320543640195179)
XLA Ops:
  0.6 0.1 pad_add_fusion.me_ref
  0.7 0.0 copy-start.1
  0.7 0.8 %copy-done.1 = f32[8,8,128]{2,1,0:T(8,128)S(1)} copy-done((f32[8,8,128]{2,1,0:T(8,128)S(1)}, f32[8,8,128]{2,1,0:T(8,128)}, u32[]{:S(2)}) %copy-start.1) | copy-done | bytes 32792
  1.5 0.0 copy-start.2
  1.5 0.7 %copy-done.2 = s32[8,8]{1,0:T(8,128)S(1)} copy-done((s32[8,8]{1,0:T(8,128)S(1)}, s32[8,8]{1,0:T(8,128)}, u32[]{:S(2)}) %copy-start.2) | copy-done | bytes 280
  2.2 0.0 copy-start.3
  2.2 0.7 %copy-done.3 = s32[8]{0:T(128)S(1)} copy-done((s32[8]{0:T(128)S(1)}, s32[8]{0:T(128)}, u32[]{:S(2)}) %copy-start.3) | copy-done | bytes 56
  2.8 1.2 %pack.1 = f32[2,5,8,128]{3,2,1,0:T(8,128)S(1)} custom-call(s32[2]{0:T(128)S(1)} %pad_add_fusion.me_ref, f32[8,8,128]{2,1,0:T(8,128)S(1)} %copy-done.1, s32[8,8]{1,0:T(8,128)S(1)} %copy-done.2, s32[8]{0:T(128)S(1)} %copy-done.3), custom_call_target="tpu_custom_call" | custom-call | tf_op jit(solution)/shard_map/pack/pallas_call | solution.py:153
  4.1 3.0 %collective-permute-start = (f32[1,2,5,8,128]{4,3,2,0,1:T(8,128)S(1)}, f32[1,2,5,8,128]{4,3,2,0,1:T(8,128)S(1)}, u32[]{:S(2)}, u32[]{:S(2)}) collective-permute-start(f32[1,2,5,8,128]{4,3,2,0,1:T(8,128)S(1)} %bitcast.28), channel_id=1, source_target_pairs={{0,16},{8,24},{16,0},{24,8},{1,17},{9,25},{17,1},{25,9},{2,18},{10... | collective-permute-start | bytes 122888 | tf_op jit(solution)/shard_map/ppermute | solution.py:32
  7.1 2.0 %collective-permute-done = f32[1,2,5,8,128]{4,3,2,0,1:T(8,128)S(1)} collective-permute-done((f32[1,2,5,8,128]{4,3,2,0,1:T(8,128)S(1)}, f32[1,2,5,8,128]{4,3,2,0,1:T(8,128)S(1)}, u32[]{:S(2)}, u32[]{:S(2)}) %collective-permute-start) | collective-permute-done | bytes 40992 | tf_op jit(solution)/shard_map/ppermute | solution.py:32
  9.1 0.0 collective-permute-start.1
  9.1 1.2 %collective-permute-done.1.came_ref = f32[2,5,8,128]{3,2,1,0:T(8,128)S(1)} collective-permute-done((f32[2,5,8,128]{3,2,1,0:T(8,128)S(1)}, f32[2,5,8,128]{3,2,1,0:T(8,128)S(1)}, u32[]{:S(2)}, u32[]{:S(2)}) %collective-permute-start.1) | collective-permute-done | bytes 40992 | tf_op jit(solution)/shard_map/ppermute | solution.py:32
  10.3 0.8 %densify.1 = f32[8,4,16,128]{3,2,1,0:T(8,128)S(1)} custom-call(s32[2]{0:T(128)S(1)} %pad_add_fusion.me_ref, f32[2,5,8,128]{3,2,1,0:T(8,128)S(1)} %get-tuple-element.7.own_ref, f32[2,5,8,128]{3,2,1,0:T(8,128)S(1)} %collective-permute-done.1.came_ref), custom_call_target="tpu_custom_call" | custom-call | tf_op jit(solution)/shard_map/densify/pallas_call | solution.py:175
  11.1 15.3 %all_to_all.5.own_ref = f32[8,4,16,128]{3,2,1,0:T(8,128)S(1)} all-to-all(f32[8,4,16,128]{3,2,1,0:T(8,128)S(1)} %densify.1), channel_id=1, replica_groups=mesh['rows'=4,'cols'=8] {'cols'}, dimensions={0} | all-to-all | bytes 524288 | tf_op jit(solution)/shard_map/all_to_all | solution.py:184
  26.5 0.0 collective-permute-start.2
  26.5 0.0 copy-start
  26.5 3.4 %copy-done = f32[1024,2048]{1,0:T(8,128)S(1)} copy-done((f32[1024,2048]{1,0:T(8,128)S(1)}, f32[1024,2048]{1,0:T(8,128)}, u32[]{:S(2)}) %copy-start) | copy-done | bytes 8388632
  29.8 1.8 %split.1 = (bf16[1024,2048]{1,0:T(8,128)(2,1)S(1)}, bf16[1024,2048]{1,0:T(8,128)(2,1)S(1)}) custom-call(f32[1024,2048]{1,0:T(8,128)S(1)} %copy-done), custom_call_target="tpu_custom_call" | custom-call | flops 6291456 | bytes 16777216 | tf_op jit(solution)/shard_map/split/pallas_call | solution.py:187
  31.6 0.0 collective-permute-done.2.came_ref
  31.6 0.8 %assemble.1.slip_ref = bf16[128,2048]{1,0:T(8,128)(2,1)S(1)} custom-call(s32[2]{0:T(128)S(1)} %pad_add_fusion.me_ref, f32[8,4,16,128]{3,2,1,0:T(8,128)S(1)} %all_to_all.5.own_ref, f32[8,4,16,128]{3,2,1,0:T(8,128)S(1)} %collective-permute-done.2.came_ref), custom_call_target="tpu_custom_call" | custom-call | tf_op jit(solution)/shard_map/assemble/pallas_call | solution.py:203
  32.4 2.0 %stress.3 = f32[4,64,128]{2,1,0:T(8,128)S(1)} custom-call(s32[2]{0:T(128)S(1)} %pad_add_fusion.me_ref, bf16[128,2048]{1,0:T(8,128)(2,1)S(1)} %assemble.1.slip_ref, bf16[1024,2048]{1,0:T(8,128)(2,1)S(1)} %get-tuple-element.4.hi_ref, bf16[1024,2048]{1,0:T(8,128)(2,1)S(1)} %get-tuple-element.5.lo_ref), custom_call_target="tpu_custom_call" | custom-call | flops 402653184 | bytes 4194304 | tf_op jit(solution)/shard_map/stress/pallas_call | solution.py:216
  34.4 0.0 copy-start.4
  34.4 0.0 copy-start.5
  34.4 0.0 copy-start.6
  34.4 1.5 %collective-permute-start.3 = (f32[4,64,128]{2,1,0:T(8,128)S(1)}, f32[4,64,128]{2,1,0:T(8,128)S(1)}, u32[]{:S(2)}, u32[]{:S(2)}) collective-permute-start(f32[4,64,128]{2,1,0:T(8,128)S(1)} %stress.3), channel_id=1, source_target_pairs={{0,1},{1,0},{2,3},{3,2},{4,5},{5,4},{6,7},{7,6},{8,9},{9,8},{10,11... | collective-permute-start | bytes 393224 | tf_op jit(solution)/shard_map/ppermute | solution.py:32
  35.9 2.0 %stress.2 = f32[4,64,128]{2,1,0:T(8,128)S(1)} custom-call(s32[2]{0:T(128)S(1)} %pad_add_fusion.me_ref, bf16[128,2048]{1,0:T(8,128)(2,1)S(1)} %assemble.1.slip_ref, bf16[1024,2048]{1,0:T(8,128)(2,1)S(1)} %get-tuple-element.4.hi_ref, bf16[1024,2048]{1,0:T(8,128)(2,1)S(1)} %get-tuple-element.5.lo_ref), custom_call_target="tpu_custom_call" | custom-call | flops 402653184 | bytes 4194304 | tf_op jit(solution)/shard_map/stress/pallas_call | solution.py:216
  37.9 2.5 %collective-permute-done.3 = f32[4,64,128]{2,1,0:T(8,128)S(1)} collective-permute-done((f32[4,64,128]{2,1,0:T(8,128)S(1)}, f32[4,64,128]{2,1,0:T(8,128)S(1)}, u32[]{:S(2)}, u32[]{:S(2)}) %collective-permute-start.3) | collective-permute-done | bytes 131104 | tf_op jit(solution)/shard_map/ppermute | solution.py:32
  40.5 1.1 %collective-permute-start.4 = (f32[2,64,128]{2,1,0:T(8,128)S(1)}, f32[2,64,128]{2,1,0:T(8,128)S(1)}, u32[]{:S(2)}, u32[]{:S(2)}) collective-permute-start(f32[2,64,128]{2,1,0:T(8,128)S(1)} %slice.27), channel_id=1, source_target_pairs={{0,2},{1,3},{2,0},{3,1},{4,6},{5,7},{6,4},{7,5},{8,10},{9,11},{10,... | collective-permute-start | bytes 196616 | tf_op jit(solution)/shard_map/ppermute | solution.py:32
  41.6 3.2 %collective-permute-done.4 = f32[2,64,128]{2,1,0:T(8,128)S(1)} collective-permute-done((f32[2,64,128]{2,1,0:T(8,128)S(1)}, f32[2,64,128]{2,1,0:T(8,128)S(1)}, u32[]{:S(2)}, u32[]{:S(2)}) %collective-permute-start.4) | collective-permute-done | bytes 65568 | tf_op jit(solution)/shard_map/ppermute | solution.py:32
  44.8 1.1 %collective-permute-start.5 = (f32[1,64,128]{2,1,0:T(8,128)S(1)}, f32[1,64,128]{2,1,0:T(8,128)S(1)}, u32[]{:S(2)}, u32[]{:S(2)}) collective-permute-start(f32[1,64,128]{2,1,0:T(8,128)S(1)} %slice.29), channel_id=1, source_target_pairs={{0,4},{1,5},{2,6},{3,7},{4,0},{5,1},{6,2},{7,3},{8,12},{9,13},{10,... | collective-permute-start | bytes 98312 | tf_op jit(solution)/shard_map/ppermute | solution.py:32
  45.9 0.0 copy-done.4
  45.9 0.0 copy-done.5
  45.9 0.0 copy-done.6
  46.0 3.7 %collective-permute-done.5 = f32[1,64,128]{2,1,0:T(8,128)S(1)} collective-permute-done((f32[1,64,128]{2,1,0:T(8,128)S(1)}, f32[1,64,128]{2,1,0:T(8,128)S(1)}, u32[]{:S(2)}, u32[]{:S(2)}) %collective-permute-start.5) | collective-permute-done | bytes 32800 | tf_op jit(solution)/shard_map/ppermute | solution.py:32
  49.7 0.6 %fusion.10 = f32[128,64]{0,1:T(8,128)} fusion(f32[1,64,128]{2,1,0:T(8,128)S(1)} %collective-permute-done.5, f32[2,64,128]{2,1,0:T(8,128)S(1)} %slice_add_fusion), kind=kLoop, calls=%fused_computation.16 | loop fusion | flops 8192 | bytes 98304 | tf_op jit(solution)/shard_map/transpose | solution.py:245
  50.3 0.7 %fusion.9 = f32[128,64]{0,1:T(8,128)} fusion(f32[128]{0:T(128)S(1)} %get-tuple-element.9, f32[128]{0:T(128)S(1)} %copy-done.4, f32[128]{0:T(128)S(1)} %get-tuple-element.8, f32[1,64,128]{2,1,0:T(8,128)S(1)} %collective-permute-done.5, f32[2,64,128]{2,1,0:T(8,128)S(1)} %slice_add_fusion), kind=kLoop, calls=%fused_computation.15 | loop fusion | flops 40960 | bytes 99840 | tf_op jit(solution)/shard_map/transpose | solution.py:245
  (6 shorter events, 0.1 us)
Async XLA Ops:
  0.7 0.8 %copy-start.1 = (f32[8,8,128]{2,1,0:T(8,128)S(1)}, f32[8,8,128]{2,1,0:T(8,128)}, u32[]{:S(2)}) copy-start(f32[8,8,128]{2,1,0:T(8,128)} %slip_hbm.1) | copy-start | bytes 98308
  1.5 0.7 %copy-start.2 = (s32[8,8]{1,0:T(8,128)S(1)}, s32[8,8]{1,0:T(8,128)}, u32[]{:S(2)}) copy-start(s32[8,8]{1,0:T(8,128)} %list_hbm.1) | copy-start | bytes 772
  2.2 0.7 %copy-start.3 = (s32[8]{0:T(128)S(1)}, s32[8]{0:T(128)}, u32[]{:S(2)}) copy-start(s32[8]{0:T(128)} %count_hbm.1) | copy-start | bytes 100
  4.1 5.0 %collective-permute-start = (f32[1,2,5,8,128]{4,3,2,0,1:T(8,128)S(1)}, f32[1,2,5,8,128]{4,3,2,0,1:T(8,128)S(1)}, u32[]{:S(2)}, u32[]{:S(2)}) collective-permute-start(f32[1,2,5,8,128]{4,3,2,0,1:T(8,128)S(1)} %bitcast.28), channel_id=1, source_target_pairs={{0,16},{8,24},{16,0},{24,8},{1,17},{9,25},{17,1},{25,9},{2,18},{10... | collective-permute-start | bytes 122888 | tf_op jit(solution)/shard_map/ppermute | solution.py:32
  9.1 1.2 %collective-permute-start.1 = (f32[2,5,8,128]{3,2,1,0:T(8,128)S(1)}, f32[2,5,8,128]{3,2,1,0:T(8,128)S(1)}, u32[]{:S(2)}, u32[]{:S(2)}) collective-permute-start(f32[2,5,8,128]{3,2,1,0:T(8,128)S(1)} %get-tuple-element.6), channel_id=1, source_target_pairs={{0,8},{8,0},{16,24},{24,16},{1,9},{9,1},{17,25},{25,17},{2,10},{10... | collective-permute-start | bytes 122888 | tf_op jit(solution)/shard_map/ppermute | solution.py:32
  26.5 5.2 %collective-permute-start.2 = (f32[8,4,16,128]{3,2,1,0:T(8,128)S(1)}, f32[8,4,16,128]{3,2,1,0:T(8,128)S(1)}, u32[]{:S(2)}, u32[]{:S(2)}) collective-permute-start(f32[8,4,16,128]{3,2,1,0:T(8,128)S(1)} %all_to_all.5.own_ref), channel_id=1, source_target_pairs={{0,8},{8,0},{16,24},{24,16},{1,9},{9,1},{17,25},{25,17},{2,10},{10... | collective-permute-start | bytes 786440 | tf_op jit(solution)/shard_map/ppermute | solution.py:32
  26.5 3.4 %copy-start = (f32[1024,2048]{1,0:T(8,128)S(1)}, f32[1024,2048]{1,0:T(8,128)}, u32[]{:S(2)}) copy-start(f32[1024,2048]{1,0:T(8,128)} %kernel_hbm.1) | copy-start | bytes 25165828
  34.4 11.5 %copy-start.4 = (f32[128]{0:T(128)S(1)}, f32[128]{0:T(128)}, u32[]{:S(2)}) copy-start(f32[128]{0:T(128)} %param.11) | copy-start | bytes 1540
  34.4 11.5 %copy-start.5 = (f32[128]{0:T(128)S(1)}, f32[128]{0:T(128)}, u32[]{:S(2)}) copy-start(f32[128]{0:T(128)} %param.12) | copy-start | bytes 1540
  34.4 11.5 %copy-start.6 = (f32[128]{0:T(128)S(1)}, f32[128]{0:T(128)}, u32[]{:S(2)}) copy-start(f32[128]{0:T(128)} %param.13) | copy-start | bytes 1540
  34.4 6.0 %collective-permute-start.3 = (f32[4,64,128]{2,1,0:T(8,128)S(1)}, f32[4,64,128]{2,1,0:T(8,128)S(1)}, u32[]{:S(2)}, u32[]{:S(2)}) collective-permute-start(f32[4,64,128]{2,1,0:T(8,128)S(1)} %stress.3), channel_id=1, source_target_pairs={{0,1},{1,0},{2,3},{3,2},{4,5},{5,4},{6,7},{7,6},{8,9},{9,8},{10,11... | collective-permute-start | bytes 393224 | tf_op jit(solution)/shard_map/ppermute | solution.py:32
  40.5 4.3 %collective-permute-start.4 = (f32[2,64,128]{2,1,0:T(8,128)S(1)}, f32[2,64,128]{2,1,0:T(8,128)S(1)}, u32[]{:S(2)}, u32[]{:S(2)}) collective-permute-start(f32[2,64,128]{2,1,0:T(8,128)S(1)} %slice.27), channel_id=1, source_target_pairs={{0,2},{1,3},{2,0},{3,1},{4,6},{5,7},{6,4},{7,5},{8,10},{9,11},{10,... | collective-permute-start | bytes 196616 | tf_op jit(solution)/shard_map/ppermute | solution.py:32
  44.8 4.9 %collective-permute-start.5 = (f32[1,64,128]{2,1,0:T(8,128)S(1)}, f32[1,64,128]{2,1,0:T(8,128)S(1)}, u32[]{:S(2)}, u32[]{:S(2)}) collective-permute-start(f32[1,64,128]{2,1,0:T(8,128)S(1)} %slice.29), channel_id=1, source_target_pairs={{0,4},{1,5},{2,6},{3,7},{4,0},{5,1},{6,2},{7,3},{8,12},{9,13},{10,... | collective-permute-start | bytes 98312 | tf_op jit(solution)/shard_map/ppermute | solution.py:32

commit v4 on v3

v4 whole, which is shorter than its diff:
```python
import functools

import jax
import jax.numpy as jnp
from jax import lax
from jax.experimental import pallas as pl
from jax.experimental.pallas import tpu as pltpu
from jax.sharding import PartitionSpec as P

BLOCK = 128
SUB = 8
VMEM_SPEC = pl.BlockSpec(memory_space=pltpu.VMEM)
SMEM_SPEC = pl.BlockSpec(memory_space=pltpu.SMEM)
HBM_SPEC = pl.BlockSpec(memory_space=pltpu.HBM)
MIB = 1024 * 1024
NT = (((1,), (1,)), ((), ()))


def f32(*shape):
    return jax.ShapeDtypeStruct(shape, jnp.float32)


def bf16(*shape):
    return jax.ShapeDtypeStruct(shape, jnp.bfloat16)


def params(mib):
    return pltpu.CompilerParams(vmem_limit_bytes=mib * MIB)


def send_xor(block, axis, k):
    return lax.ppermute(block, axis, [(r, r ^ k) for r in range(lax.axis_size(axis))])


def fetch(targets, col, kernel_hbm, out_ref, sems):
    share = out_ref.shape[1]
    copies = [
        pltpu.make_async_copy(
            kernel_hbm.at[pl.ds(pl.multiple_of((col ^ k) * share, share), share), :], out_ref.at[j], sems.at[j]
        )
        for j, k in enumerate(targets)
    ]
    for copy in copies:
        copy.start()
    return copies


def wait(copies):
    for copy in copies:
        copy.wait()


def pack_body(
    targets, me_ref, slip_hbm, list_hbm, count_hbm, kernel_hbm, out_ref, held_ref,
    slip_ref, list_ref, count_ref, ids, sems, held_sems,
):
    copies = [
        pltpu.make_async_copy(src, dst, sems.at[j])
        for j, (src, dst) in enumerate(((list_hbm, list_ref), (count_hbm, count_ref), (slip_hbm, slip_ref)))
    ]
    for copy in copies:
        copy.start()
    held = fetch(targets, me_ref[1], kernel_hbm, held_ref, held_sems)
    events, entries = list_ref.shape
    half = events // 2
    row = me_ref[0]
    entry = lax.broadcasted_iota(jnp.int32, (events, entries), 1) + row * entries
    event = lax.broadcasted_iota(jnp.int32, (events, entries), 0)
    ids[...] = jnp.full(ids.shape, -1.0, jnp.float32)
    wait(copies)
    count = jnp.zeros((events, entries), jnp.int32)
    for e in range(events):
        count = jnp.where(event == e, count_ref[e], count)
    ids[0:events, 0:entries] = jnp.where(entry < count, list_ref[...], -1).astype(jnp.float32)
    ids[...] = pltpu.roll(ids[...], row * entries, 1)
    for h in range(2):
        first = ((row % 2) ^ h) * half
        for i in range(half):
            out_ref[h, i, 0:entries, :] = slip_ref[first + i]
            out_ref[h, half, i : i + 1, :] = ids[pl.ds(first + i, 1), :]
    wait(held)


def densify_body(targets, entries, me_ref, own_ref, came_ref, kernel_hbm, out_ref, held_ref, slips, held_sems):
    held = fetch(targets, me_ref[1], kernel_hbm, held_ref, held_sems)
    halves, half = own_ref.shape[0], own_ref.shape[1] - 1
    width, _, blocks_here, _ = out_ref.shape
    blocks = width * blocks_here
    live = 2 * halves * entries
    row = me_ref[0]
    for i in range(half):
        ids = jnp.full((1, BLOCK), -1.0, jnp.float32)
        for ref in (own_ref, came_ref):
            for j in range(halves):
                ids = jnp.maximum(ids, ref[j, half, i : i + 1, :])
        ids = jnp.broadcast_to(ids, (blocks, BLOCK))[:, :live]
        number = lax.broadcasted_iota(jnp.int32, ids.shape, 0).astype(jnp.float32)
        onehot = (ids == number).astype(jnp.bfloat16)
        for core, ref in enumerate((own_ref, came_ref)):
            for j in range(halves):
                source = row ^ (2 * j + core)
                slips[i, pl.ds(pl.multiple_of(source * entries, entries), entries), :] = ref[j, i, 0:entries, :]
        slip = slips[i]
        total = jnp.zeros((blocks, BLOCK), jnp.float32)
        for _ in range(3):
            piece = slip.astype(jnp.bfloat16)
            slip = slip - piece.astype(jnp.float32)
            total = total + jnp.dot(onehot, piece, preferred_element_type=jnp.float32)
        out_ref[:, i] = total.reshape(width, blocks_here, BLOCK)
    wait(held)


def assemble(row, own_ref, came_ref, out_ref, dense):
    width, half, blocks_here, _ = own_ref.shape
    events = dense.shape[0]
    core = row % 2
    for c in range(width):
        for other, ref in enumerate((own_ref, came_ref)):
            for i in range(half):
                dense[(2 * c + (core ^ other)) * half + i] = ref[c, i]
    flat = dense.reshape(events * blocks_here, BLOCK)
    for t in range(events // (2 * SUB)):
        for b in range(blocks_here):
            rows = [
                flat[pl.ds((2 * t + u) * SUB * blocks_here + b, SUB, stride=blocks_here), :] for u in range(2)
            ]
            slip = jnp.concatenate(rows, axis=0)
            hi = slip.astype(jnp.bfloat16)
            lo = (slip - hi.astype(jnp.float32)).astype(jnp.bfloat16)
            where = slice(b * BLOCK, (b + 1) * BLOCK)
            out_ref[2 * t * SUB : 2 * (t + 1) * SUB, where] = hi
            out_ref[events + 2 * t * SUB : events + 2 * (t + 1) * SUB, where] = lo


def stress(slip_ref, kernel_ref, out_ref):
    events = slip_ref.shape[0] // 2
    for j in range(out_ref.shape[0]):
        block = kernel_ref[j]
        hi = block.astype(jnp.bfloat16)
        lo = (block - hi.astype(jnp.float32)).astype(jnp.bfloat16)
        first = lax.dot_general(slip_ref[...], hi, NT, preferred_element_type=jnp.float32)
        second = lax.dot_general(slip_ref[:events, :], lo, NT, preferred_element_type=jnp.float32)
        out_ref[j] = first[:events] + first[events:] + second


def first_body(
    targets, me_ref, own_ref, came_ref, kernel_ref, kernel_hbm, slip_ref, out_ref, *refs
):
    held_refs, dense, held_sems = refs[:-2], refs[-2], refs[-1]
    held = [
        fetch(t, me_ref[1], kernel_hbm, ref, held_sems.at[j]) for j, (t, ref) in enumerate(zip(targets, held_refs))
    ]
    assemble(me_ref[0], own_ref, came_ref, slip_ref, dense)
    stress(slip_ref, kernel_ref, out_ref)
    for copies in held:
        wait(copies)


def halving_order(width):
    bits = width.bit_length() - 1
    return [int(f"{k:0{bits}b}"[::-1], 2) for k in range(width)]


def per_device(kernel, slip_delta, block_list, live_count, direct_effect, load_rate, time_before):
    width = lax.axis_size("cols")
    height = lax.axis_size("rows")
    events_here, entries = block_list.shape
    half = events_here // 2
    events = events_here * width
    receivers, sources = kernel.shape
    blocks_here = sources // BLOCK
    me = jnp.stack([lax.axis_index("rows"), lax.axis_index("cols")]).astype(jnp.int32)

    order = halving_order(width)
    share = receivers // width
    quarter = width // 4
    near_keep, far_keep = order[0 : 2 * quarter : 2], order[1 : 2 * quarter : 2]
    near_send, far_send = order[2 * quarter :: 2], order[2 * quarter + 1 :: 2]
    held_shape = pltpu.VMEM((quarter, share, sources), jnp.float32)
    held_sems = pltpu.SemaphoreType.DMA((quarter,))
    in_hbm, in_vmem = (
        functools.partial(pltpu.with_memory_space_constraint, memory_space=m) for m in (pltpu.HBM, pltpu.VMEM)
    )
    packed, far_send_kernel = pl.pallas_call(
        functools.partial(pack_body, far_send),
        out_shape=[f32(2, half + 1, SUB, BLOCK), held_shape],
        in_specs=[SMEM_SPEC] + [HBM_SPEC] * 4,
        out_specs=[VMEM_SPEC] * 2,
        scratch_shapes=[
            pltpu.VMEM(slip_delta.shape, jnp.float32),
            pltpu.VMEM(block_list.shape, jnp.int32),
            pltpu.SMEM(live_count.shape, jnp.int32),
            pltpu.VMEM((SUB, BLOCK), jnp.float32),
            pltpu.SemaphoreType.DMA((3,)),
            held_sems,
        ],
        compiler_params=params(4),
        name="pack",
    )(me, in_hbm(slip_delta), in_hbm(block_list), in_hbm(live_count), in_hbm(kernel))
    held = packed[None]
    step = 2
    while step < height:
        held = jnp.concatenate([held, send_xor(held, "rows", step)], axis=0)
        step *= 2
    came = send_xor(held[:, 1], "rows", 1)

    dense, near_send_kernel = pl.pallas_call(
        functools.partial(densify_body, near_send, entries),
        out_shape=[f32(width, half, blocks_here, BLOCK), held_shape],
        in_specs=[SMEM_SPEC, VMEM_SPEC, VMEM_SPEC, HBM_SPEC],
        out_specs=[VMEM_SPEC] * 2,
        scratch_shapes=[pltpu.VMEM((half, height * entries, BLOCK), jnp.float32), held_sems],
        compiler_params=params(8),
        name="densify",
    )(me, held[:, 0], came, in_hbm(kernel))
    mine = lax.all_to_all(dense, "cols", 0, 0, tiled=True)

    cost = pl.CostEstimate(
        flops=6 * quarter * share * sources * events,
        bytes_accessed=4 * quarter * share * sources,
        transcendentals=0,
    )
    slips, far_sent, far_keep_kernel, near_keep_kernel = pl.pallas_call(
        functools.partial(first_body, (far_keep, near_keep)),
        out_shape=[bf16(2 * events, sources), f32(quarter, events, share), held_shape, held_shape],
        in_specs=[SMEM_SPEC, VMEM_SPEC, VMEM_SPEC, VMEM_SPEC, HBM_SPEC],
        out_specs=[VMEM_SPEC] * 4,
        scratch_shapes=[
            pltpu.VMEM((events, blocks_here, BLOCK), jnp.float32),
            pltpu.SemaphoreType.DMA((2, quarter)),
        ],
        compiler_params=params(8),
        cost_estimate=cost,
        name="first_stress",
    )(me, mine, send_xor(mine, "rows", 1), in_vmem(far_send_kernel), in_hbm(kernel))

    def later(held):
        return pl.pallas_call(
            stress,
            out_shape=f32(quarter, events, share),
            in_specs=[VMEM_SPEC, VMEM_SPEC],
            out_specs=VMEM_SPEC,
            compiler_params=params(8),
            cost_estimate=cost,
            name="stress",
        )(slips, in_vmem(held))

    far_came = send_xor(far_sent, "cols", 1)
    near_came = send_xor(later(near_send_kernel), "cols", 1)
    far = later(far_keep_kernel) + far_came
    near = later(near_keep_kernel) + near_came
    step = 2
    while step < width // 2:
        keep = far.shape[0] // 2
        far = far[:keep] + send_xor(far[keep:], "cols", step)
        near = near[:keep] + send_xor(near[keep:], "cols", step)
        step *= 2
    total = near + send_xor(far, "cols", step)
    stress_change = total[0]
    scale = direct_effect[None, :]
    growth = jnp.expm1(load_rate * time_before / direct_effect)[None, :]
    log_time = jnp.log(scale / load_rate[None, :]) + jnp.log(
        jnp.log1p(jnp.exp(-stress_change / scale) * growth)
    )
    return (stress_change.T, log_time.T)


def solution(mesh):
    in_specs = (
        P("rows", "cols"),
        P("cols", "rows", None),
        P("cols", "rows"),
        P("cols"),
        P(("rows", "cols")),
        P(("rows", "cols")),
        P(("rows", "cols")),
    )
    out_specs = (P(("rows", "cols"), None), P(("rows", "cols"), None))
    return jax.shard_map(
        per_device, mesh=mesh, in_specs=in_specs, out_specs=out_specs, check_vma=False
    )
```

time: 51.3 us -> 46.7 us (0.910)
  local copies, waits for them, and re-layouts: 5.51 us -> 0.03 us
  waiting for transfers between devices: 12.6 us -> 10 us
  starting transfers between devices: 6.77 us -> 8.75 us
  Pallas kernels: 8.56 us -> 10.2 us
    unnamed x14 -> x6, local copies, waits for them, and re-layouts: 5.5 us -> 0.02 us
    ppermute x6 -> x8, waiting for transfers between devices: 12.6 us -> 10 us  [send_xor(): lax.ppermute(block, axis, [(r, r ^ k) for r in range(lax.axis_size(axis))])]
    ppermute x6 -> x8, starting transfers between devices: 6.77 us -> 8.75 us  [send_xor(): lax.ppermute(block, axis, [(r, r ^ k) for r in range(lax.axis_size(axis))])]
    pallas_call x6, Pallas kernels: 8.56 us -> 10.2 us  [the longest x1 3.56 us: per_device(): pl.pallas_call(functools.partial(first_body, (far_keep, near_keep)), out_...]
  transfers between devices with their start and end apart: 6 -> 8, of which waited for: 5 -> 7; matrix products, arithmetic and copies ran while one was open for 0% -> 0% of each run, Pallas kernels for 7% -> 5%
where the time goes in v4:
time: 46.7 us; the launch traced here: 46.5 us
  blocking collectives  15.3 us (33%)
  Pallas kernels  10.2 us (22%)
  waiting for transfers between devices  10 us (21%)
  starting transfers between devices  8.75 us (19%)
  other arithmetic  1.4 us (3%)
  between operations  0.76 us (2%)
    all_to_all x1, blocking collectives, per_device(): mine = lax.all_to_all(dense, 'cols', 0, 0, tiled=True)  15.3 us
    ppermute x8, waiting for transfers between devices, send_xor(): lax.ppermute(block, axis, [(r, r ^ k) for r in range(lax.axis_size(axis))])  10 us
    ppermute x8, starting transfers between devices, send_xor(): lax.ppermute(block, axis, [(r, r ^ k) for r in range(lax.axis_size(axis))])  8.75 us
    pallas_call x1, Pallas kernels, per_device(): pl.pallas_call(functools.partial(first_body, (far_keep, near_keep)), out_...  3.56 us
    pallas_call x3, Pallas kernels, later(): pl.pallas_call(stress, out_shape=f32(quarter, events, share), in_specs=[V...  2.32 us
    pallas_call x1, Pallas kernels, per_device(): pl.pallas_call(functools.partial(pack_body, far_send), out_shape=[f32(2,...  2.16 us
    pallas_call x1, Pallas kernels, per_device(): pl.pallas_call(functools.partial(densify_body, near_send, entries), out_s...  2.13 us
    transpose x2, other arithmetic, per_device(): return (stress_change.T, log_time.T)  1.28 us
  transfers between devices with their start and end apart: 8, of which 7 were waited for; matrix products, arithmetic and copies ran while one was open for 0% of the time, Pallas kernels for 5%

profile of v4, /device:TPU:0, one launch (start us, length us, event | category | flops | bytes accessed | tf_op | source)
XLA Modules:
  0.0 46.5 jit_solution(874955133641706050)
XLA Ops:
  0.6 0.1 pad_add_fusion.me_ref
  0.7 2.2 %pack.1 = (f32[2,5,8,128]{3,2,1,0:T(8,128)S(1)}, f32[2,128,2048]{2,1,0:T(8,128)S(1)}) custom-call(s32[2]{0:T(128)S(1)} %pad_add_fusion.me_ref, f32[8,8,128]{2,1,0:T(8,128)} %slip_hbm.1, s32[8,8]{1,0:T(8,128)} %list_hbm.1, s32[8]{0:T(128)} %count_hbm.1, f32[1024,2048]{1,0:T(8,128)} %kernel_hbm.5), custom_call_target="tpu_custom_call" | custom-call | tf_op jit(solution)/shard_map/pack/pallas_call | solution.py:184
  2.9 3.0 %collective-permute-start = (f32[1,2,5,8,128]{4,3,2,0,1:T(8,128)S(1)}, f32[1,2,5,8,128]{4,3,2,0,1:T(8,128)S(1)}, u32[]{:S(2)}, u32[]{:S(2)}) collective-permute-start(f32[1,2,5,8,128]{4,3,2,0,1:T(8,128)S(1)} %bitcast.28), channel_id=1, source_target_pairs={{0,16},{8,24},{16,0},{24,8},{1,17},{9,25},{17,1},{25,9},{2,18},{10... | collective-permute-start | bytes 122888 | tf_op jit(solution)/shard_map/ppermute | solution.py:32
  5.9 2.0 %collective-permute-done = f32[1,2,5,8,128]{4,3,2,0,1:T(8,128)S(1)} collective-permute-done((f32[1,2,5,8,128]{4,3,2,0,1:T(8,128)S(1)}, f32[1,2,5,8,128]{4,3,2,0,1:T(8,128)S(1)}, u32[]{:S(2)}, u32[]{:S(2)}) %collective-permute-start) | collective-permute-done | bytes 40992 | tf_op jit(solution)/shard_map/ppermute | solution.py:32
  7.9 0.0 collective-permute-start.1
  7.9 1.2 %collective-permute-done.1.came_ref = f32[2,5,8,128]{3,2,1,0:T(8,128)S(1)} collective-permute-done((f32[2,5,8,128]{3,2,1,0:T(8,128)S(1)}, f32[2,5,8,128]{3,2,1,0:T(8,128)S(1)}, u32[]{:S(2)}, u32[]{:S(2)}) %collective-permute-start.1) | collective-permute-done | bytes 40992 | tf_op jit(solution)/shard_map/ppermute | solution.py:32
  9.1 2.1 %densify.1 = (f32[8,4,16,128]{3,2,1,0:T(8,128)S(1)}, f32[2,128,2048]{2,1,0:T(8,128)S(1)}) custom-call(s32[2]{0:T(128)S(1)} %pad_add_fusion.me_ref, f32[2,5,8,128]{3,2,1,0:T(8,128)S(1)} %get-tuple-element.19.own_ref, f32[2,5,8,128]{3,2,1,0:T(8,128)S(1)} %collective-permute-done.1.came_ref, f32[1024,2048]{1,0:T(8,128)} %kernel_hbm.5), custom_call_target="tpu_custom_call" | custom-call | tf_op jit(solution)/shard_map/densify/pallas_call | solution.py:207
  11.3 15.3 %all_to_all.5.own_ref = f32[8,4,16,128]{3,2,1,0:T(8,128)S(1)} all-to-all(f32[8,4,16,128]{3,2,1,0:T(8,128)S(1)} %get-tuple-element.11), channel_id=1, replica_groups=mesh['rows'=4,'cols'=8] {'cols'}, dimensions={0} | all-to-all | bytes 524288 | tf_op jit(solution)/shard_map/all_to_all | solution.py:216
  26.6 0.0 collective-permute-start.2
  26.6 1.5 %collective-permute-done.2.came_ref = f32[8,4,16,128]{3,2,1,0:T(8,128)S(1)} collective-permute-done((f32[8,4,16,128]{3,2,1,0:T(8,128)S(1)}, f32[8,4,16,128]{3,2,1,0:T(8,128)S(1)}, u32[]{:S(2)}, u32[]{:S(2)}) %collective-permute-start.2) | collective-permute-done | bytes 262176 | tf_op jit(solution)/shard_map/ppermute | solution.py:32
  28.1 3.6 %first_stress.1 = (bf16[128,2048]{1,0:T(8,128)(2,1)S(1)}, f32[2,64,128]{2,1,0:T(8,128)S(1)}, f32[2,128,2048]{2,1,0:T(8,128)S(1)}, f32[2,128,2048]{2,1,0:T(8,128)S(1)}) custom-call(s32[2]{0:T(128)S(1)} %pad_add_fusion.me_ref, f32[8,4,16,128]{3,2,1,0:T(8,128)S(1)} %all_to_all.5.own_ref, f32[8,4,16,128]{3,2,1,0:T(8,128)S(1)} %collective-permute-done.2.came_ref, ...), custom_call_target="tpu_custom_call" | custom-call | flops 201326592 | bytes 2097152 | tf_op jit(solution)/shard_map/first_stress/pallas_call | solution.py:223
  31.7 1.5 %collective-permute-start.5 = (f32[2,64,128]{2,1,0:T(8,128)S(1)}, f32[2,64,128]{2,1,0:T(8,128)S(1)}, u32[]{:S(2)}, u32[]{:S(2)}) collective-permute-start(f32[2,64,128]{2,1,0:T(8,128)S(1)} %get-tuple-element.17), channel_id=1, source_target_pairs={{0,1},{1,0},{2,3},{3,2},{4,5},{5,4},{6,7},{7,6},{8,9},{9,8},{10,11... | collective-permute-start | bytes 196616 | tf_op jit(solution)/shard_map/ppermute | solution.py:32
  33.2 0.8 %stress.4 = f32[2,64,128]{2,1,0:T(8,128)S(1)} custom-call(bf16[128,2048]{1,0:T(8,128)(2,1)S(1)} %get-tuple-element.13.slip_ref, f32[2,128,2048]{2,1,0:T(8,128)S(1)} %get-tuple-element.15.kernel_ref), custom_call_target="tpu_custom_call" | custom-call | flops 201326592 | bytes 2097152 | tf_op jit(solution)/shard_map/stress/pallas_call | solution.py:238
  34.0 0.7 %collective-permute-start.3 = (f32[2,64,128]{2,1,0:T(8,128)S(1)}, f32[2,64,128]{2,1,0:T(8,128)S(1)}, u32[]{:S(2)}, u32[]{:S(2)}) collective-permute-start(f32[2,64,128]{2,1,0:T(8,128)S(1)} %stress.4), channel_id=1, source_target_pairs={{0,1},{1,0},{2,3},{3,2},{4,5},{5,4},{6,7},{7,6},{8,9},{9,8},{10,11... | collective-permute-start | bytes 196616 | tf_op jit(solution)/shard_map/ppermute | solution.py:32
  34.6 0.8 %stress.5 = f32[2,64,128]{2,1,0:T(8,128)S(1)} custom-call(bf16[128,2048]{1,0:T(8,128)(2,1)S(1)} %get-tuple-element.13.slip_ref, f32[2,128,2048]{2,1,0:T(8,128)S(1)} %get-tuple-element.16.kernel_ref), custom_call_target="tpu_custom_call" | custom-call | flops 201326592 | bytes 2097152 | tf_op jit(solution)/shard_map/stress/pallas_call | solution.py:238
  35.4 0.0 copy-start
  35.4 0.0 copy-start.1
  35.5 0.0 copy-start.2
  35.5 0.6 %collective-permute-done.5 = f32[2,64,128]{2,1,0:T(8,128)S(1)} collective-permute-done((f32[2,64,128]{2,1,0:T(8,128)S(1)}, f32[2,64,128]{2,1,0:T(8,128)S(1)}, u32[]{:S(2)}, u32[]{:S(2)}) %collective-permute-start.5) | collective-permute-done | bytes 65568 | tf_op jit(solution)/shard_map/ppermute | solution.py:32
  36.1 1.7 %collective-permute-start.6 = (f32[1,64,128]{2,1,0:T(8,128)S(1)}, f32[1,64,128]{2,1,0:T(8,128)S(1)}, u32[]{:S(2)}, u32[]{:S(2)}) collective-permute-start(f32[1,64,128]{2,1,0:T(8,128)S(1)} %slice.29), channel_id=1, source_target_pairs={{0,2},{1,3},{2,0},{3,1},{4,6},{5,7},{6,4},{7,5},{8,10},{9,11},{10,... | collective-permute-start | bytes 98312 | tf_op jit(solution)/shard_map/ppermute | solution.py:32
  37.7 0.8 %stress.3 = f32[2,64,128]{2,1,0:T(8,128)S(1)} custom-call(bf16[128,2048]{1,0:T(8,128)(2,1)S(1)} %get-tuple-element.13.slip_ref, f32[2,128,2048]{2,1,0:T(8,128)S(1)} %get-tuple-element.14.kernel_ref), custom_call_target="tpu_custom_call" | custom-call | flops 201326592 | bytes 2097152 | tf_op jit(solution)/shard_map/stress/pallas_call | solution.py:238
  38.5 0.0 collective-permute-done.3
  38.6 0.5 %collective-permute-start.4 = (f32[1,64,128]{2,1,0:T(8,128)S(1)}, f32[1,64,128]{2,1,0:T(8,128)S(1)}, u32[]{:S(2)}, u32[]{:S(2)}) collective-permute-start(f32[1,64,128]{2,1,0:T(8,128)S(1)} %slice.27), channel_id=1, source_target_pairs={{0,2},{1,3},{2,0},{3,1},{4,6},{5,7},{6,4},{7,5},{8,10},{9,11},{10,... | collective-permute-start | bytes 98312 | tf_op jit(solution)/shard_map/ppermute | solution.py:32
  39.0 1.3 %collective-permute-done.6 = f32[1,64,128]{2,1,0:T(8,128)S(1)} collective-permute-done((f32[1,64,128]{2,1,0:T(8,128)S(1)}, f32[1,64,128]{2,1,0:T(8,128)S(1)}, u32[]{:S(2)}, u32[]{:S(2)}) %collective-permute-start.6) | collective-permute-done | bytes 32800 | tf_op jit(solution)/shard_map/ppermute | solution.py:32
  40.4 1.4 %collective-permute-start.7 = (f32[1,64,128]{2,1,0:T(8,128)S(1)}, f32[1,64,128]{2,1,0:T(8,128)S(1)}, u32[]{:S(2)}, u32[]{:S(2)}) collective-permute-start(f32[1,64,128]{2,1,0:T(8,128)S(1)} %slice_add_fusion), channel_id=1, source_target_pairs={{0,4},{1,5},{2,6},{3,7},{4,0},{5,1},{6,2},{7,3},{8,12},{9,13},{10,... | collective-permute-start | bytes 98312 | tf_op jit(solution)/shard_map/ppermute | solution.py:32
  41.8 0.0 copy-done
  41.8 0.0 copy-done.1
  41.8 0.0 copy-done.2
  41.8 0.7 %collective-permute-done.4 = f32[1,64,128]{2,1,0:T(8,128)S(1)} collective-permute-done((f32[1,64,128]{2,1,0:T(8,128)S(1)}, f32[1,64,128]{2,1,0:T(8,128)S(1)}, u32[]{:S(2)}, u32[]{:S(2)}) %collective-permute-start.4) | collective-permute-done | bytes 32800 | tf_op jit(solution)/shard_map/ppermute | solution.py:32
  42.5 2.7 %collective-permute-done.7 = f32[1,64,128]{2,1,0:T(8,128)S(1)} collective-permute-done((f32[1,64,128]{2,1,0:T(8,128)S(1)}, f32[1,64,128]{2,1,0:T(8,128)S(1)}, u32[]{:S(2)}, u32[]{:S(2)}) %collective-permute-start.7) | collective-permute-done | bytes 32800 | tf_op jit(solution)/shard_map/ppermute | solution.py:32
  45.2 0.6 %fusion.12 = f32[128,64]{0,1:T(8,128)} fusion(f32[1,64,128]{2,1,0:T(8,128)S(1)} %collective-permute-done.7, f32[1,64,128]{2,1,0:T(8,128)S(1)} %collective-permute-done.4, f32[2,64,128]{2,1,0:T(8,128)S(1)} %add.23), kind=kLoop, calls=%fused_computation.21 | loop fusion | flops 16384 | bytes 131072 | tf_op jit(solution)/shard_map/transpose | solution.py:265
  45.8 0.7 %fusion.10 = f32[128,64]{0,1:T(8,128)} fusion(f32[128]{0:T(128)S(1)} %get-tuple-element.21, f32[128]{0:T(128)S(1)} %copy-done, f32[128]{0:T(128)S(1)} %get-tuple-element.20, f32[1,64,128]{2,1,0:T(8,128)S(1)} %collective-permute-done.7, f32[1,64,128]{2,1,0:T(8,128)S(1)} %collective-permute-done.4, f32[2,64,128]{2,1,0:T(8,128)S(1)} %add.23), kind=kLoop, calls=%fused_computation.16 | loop fusion | flops 49152 | bytes 132608 | tf_op jit(solution)/shard_map/transpose | solution.py:265
  (7 shorter events, 0.1 us)
Async XLA Ops:
  2.9 5.0 %collective-permute-start = (f32[1,2,5,8,128]{4,3,2,0,1:T(8,128)S(1)}, f32[1,2,5,8,128]{4,3,2,0,1:T(8,128)S(1)}, u32[]{:S(2)}, u32[]{:S(2)}) collective-permute-start(f32[1,2,5,8,128]{4,3,2,0,1:T(8,128)S(1)} %bitcast.28), channel_id=1, source_target_pairs={{0,16},{8,24},{16,0},{24,8},{1,17},{9,25},{17,1},{25,9},{2,18},{10... | collective-permute-start | bytes 122888 | tf_op jit(solution)/shard_map/ppermute | solution.py:32
  7.9 1.2 %collective-permute-start.1 = (f32[2,5,8,128]{3,2,1,0:T(8,128)S(1)}, f32[2,5,8,128]{3,2,1,0:T(8,128)S(1)}, u32[]{:S(2)}, u32[]{:S(2)}) collective-permute-start(f32[2,5,8,128]{3,2,1,0:T(8,128)S(1)} %get-tuple-element.18), channel_id=1, source_target_pairs={{0,8},{8,0},{16,24},{24,16},{1,9},{9,1},{17,25},{25,17},{2,10},{10... | collective-permute-start | bytes 122888 | tf_op jit(solution)/shard_map/ppermute | solution.py:32
  26.6 1.5 %collective-permute-start.2 = (f32[8,4,16,128]{3,2,1,0:T(8,128)S(1)}, f32[8,4,16,128]{3,2,1,0:T(8,128)S(1)}, u32[]{:S(2)}, u32[]{:S(2)}) collective-permute-start(f32[8,4,16,128]{3,2,1,0:T(8,128)S(1)} %all_to_all.5.own_ref), channel_id=1, source_target_pairs={{0,8},{8,0},{16,24},{24,16},{1,9},{9,1},{17,25},{25,17},{2,10},{10... | collective-permute-start | bytes 786440 | tf_op jit(solution)/shard_map/ppermute | solution.py:32
  31.7 4.3 %collective-permute-start.5 = (f32[2,64,128]{2,1,0:T(8,128)S(1)}, f32[2,64,128]{2,1,0:T(8,128)S(1)}, u32[]{:S(2)}, u32[]{:S(2)}) collective-permute-start(f32[2,64,128]{2,1,0:T(8,128)S(1)} %get-tuple-element.17), channel_id=1, source_target_pairs={{0,1},{1,0},{2,3},{3,2},{4,5},{5,4},{6,7},{7,6},{8,9},{9,8},{10,11... | collective-permute-start | bytes 196616 | tf_op jit(solution)/shard_map/ppermute | solution.py:32
  34.0 4.5 %collective-permute-start.3 = (f32[2,64,128]{2,1,0:T(8,128)S(1)}, f32[2,64,128]{2,1,0:T(8,128)S(1)}, u32[]{:S(2)}, u32[]{:S(2)}) collective-permute-start(f32[2,64,128]{2,1,0:T(8,128)S(1)} %stress.4), channel_id=1, source_target_pairs={{0,1},{1,0},{2,3},{3,2},{4,5},{5,4},{6,7},{7,6},{8,9},{9,8},{10,11... | collective-permute-start | bytes 196616 | tf_op jit(solution)/shard_map/ppermute | solution.py:32
  35.4 6.4 %copy-start = (f32[128]{0:T(128)S(1)}, f32[128]{0:T(128)}, u32[]{:S(2)}) copy-start(f32[128]{0:T(128)} %param.11) | copy-start | bytes 1540
  35.4 6.4 %copy-start.1 = (f32[128]{0:T(128)S(1)}, f32[128]{0:T(128)}, u32[]{:S(2)}) copy-start(f32[128]{0:T(128)} %param.12) | copy-start | bytes 1540
  35.5 6.4 %copy-start.2 = (f32[128]{0:T(128)S(1)}, f32[128]{0:T(128)}, u32[]{:S(2)}) copy-start(f32[128]{0:T(128)} %param.13) | copy-start | bytes 1540
  36.1 4.3 %collective-permute-start.6 = (f32[1,64,128]{2,1,0:T(8,128)S(1)}, f32[1,64,128]{2,1,0:T(8,128)S(1)}, u32[]{:S(2)}, u32[]{:S(2)}) collective-permute-start(f32[1,64,128]{2,1,0:T(8,128)S(1)} %slice.29), channel_id=1, source_target_pairs={{0,2},{1,3},{2,0},{3,1},{4,6},{5,7},{6,4},{7,5},{8,10},{9,11},{10,... | collective-permute-start | bytes 98312 | tf_op jit(solution)/shard_map/ppermute | solution.py:32
  38.6 4.0 %collective-permute-start.4 = (f32[1,64,128]{2,1,0:T(8,128)S(1)}, f32[1,64,128]{2,1,0:T(8,128)S(1)}, u32[]{:S(2)}, u32[]{:S(2)}) collective-permute-start(f32[1,64,128]{2,1,0:T(8,128)S(1)} %slice.27), channel_id=1, source_target_pairs={{0,2},{1,3},{2,0},{3,1},{4,6},{5,7},{6,4},{7,5},{8,10},{9,11},{10,... | collective-permute-start | bytes 98312 | tf_op jit(solution)/shard_map/ppermute | solution.py:32
  40.4 4.8 %collective-permute-start.7 = (f32[1,64,128]{2,1,0:T(8,128)S(1)}, f32[1,64,128]{2,1,0:T(8,128)S(1)}, u32[]{:S(2)}, u32[]{:S(2)}) collective-permute-start(f32[1,64,128]{2,1,0:T(8,128)S(1)} %slice_add_fusion), channel_id=1, source_target_pairs={{0,4},{1,5},{2,6},{3,7},{4,0},{5,1},{6,2},{7,3},{8,12},{9,13},{10,... | collective-permute-start | bytes 98312 | tf_op jit(solution)/shard_map/ppermute | solution.py:32

commit v5 on v4

--- a/solution.py
+++ b/solution.py
@@ -9,6 +9,7 @@
 
 BLOCK = 128
 SUB = 8
+PIECES = 4
 VMEM_SPEC = pl.BlockSpec(memory_space=pltpu.VMEM)
 SMEM_SPEC = pl.BlockSpec(memory_space=pltpu.SMEM)
 HBM_SPEC = pl.BlockSpec(memory_space=pltpu.HBM)
@@ -34,12 +35,18 @@
 
 def fetch(targets, col, kernel_hbm, out_ref, sems):
     share = out_ref.shape[1]
-    copies = [
-        pltpu.make_async_copy(
-            kernel_hbm.at[pl.ds(pl.multiple_of((col ^ k) * share, share), share), :], out_ref.at[j], sems.at[j]
-        )
-        for j, k in enumerate(targets)
-    ]
+    rows = share // PIECES
+    copies = []
+    for j, k in enumerate(targets):
+        for p in range(PIECES):
+            start = pl.multiple_of((col ^ k) * share + p * rows, rows)
+            copies.append(
+                pltpu.make_async_copy(
+                    kernel_hbm.at[pl.ds(start, rows), :],
+                    out_ref.at[j, pl.ds(p * rows, rows), :],
+                    sems.at[j, p],
+                )
+            )
     for copy in copies:
         copy.start()
     return copies
@@ -177,7 +184,7 @@
     near_keep, far_keep = order[0 : 2 * quarter : 2], order[1 : 2 * quarter : 2]
     near_send, far_send = order[2 * quarter :: 2], order[2 * quarter + 1 :: 2]
     held_shape = pltpu.VMEM((quarter, share, sources), jnp.float32)
-    held_sems = pltpu.SemaphoreType.DMA((quarter,))
+    held_sems = pltpu.SemaphoreType.DMA((quarter, PIECES))
     in_hbm, in_vmem = (
         functools.partial(pltpu.with_memory_space_constraint, memory_space=m) for m in (pltpu.HBM, pltpu.VMEM)
     )
@@ -227,7 +234,7 @@
         out_specs=[VMEM_SPEC] * 4,
         scratch_shapes=[
             pltpu.VMEM((events, blocks_here, BLOCK), jnp.float32),
-            pltpu.SemaphoreType.DMA((2, quarter)),
+            pltpu.SemaphoreType.DMA((2, quarter, PIECES)),
         ],
         compiler_params=params(8),
         cost_estimate=cost,
@@ -255,8 +262,7 @@
         far = far[:keep] + send_xor(far[keep:], "cols", step)
         near = near[:keep] + send_xor(near[keep:], "cols", step)
         step *= 2
-    total = near + send_xor(far, "cols", step)
-    stress_change = total[0]
+    stress_change = near[0] + send_xor(far[0], "cols", step)
     scale = direct_effect[None, :]
     growth = jnp.expm1(load_rate * time_before / direct_effect)[None, :]
     log_time = jnp.log(scale / load_rate[None, :]) + jnp.log(

time: 46.7 us -> 46.2 us (0.989)
  other arithmetic: 1.4 us -> 0.78 us
    transpose x2 -> x1, other arithmetic: 1.28 us -> 0.66 us  [per_device(): return (stress_change.T, log_time.T)]
where the time goes in v5:
time: 46.2 us; the launch traced here: 46 us
  blocking collectives  15.3 us (33%)
  Pallas kernels  10.3 us (22%)
  waiting for transfers between devices  10 us (22%)
  starting transfers between devices  8.74 us (19%)
  other arithmetic  0.78 us (2%)
  between operations  0.76 us (2%)
    all_to_all x1, blocking collectives, per_device(): mine = lax.all_to_all(dense, 'cols', 0, 0, tiled=True)  15.3 us
    ppermute x8, waiting for transfers between devices, send_xor(): lax.ppermute(block, axis, [(r, r ^ k) for r in range(lax.axis_size(axis))])  10 us
    ppermute x8, starting transfers between devices, send_xor(): lax.ppermute(block, axis, [(r, r ^ k) for r in range(lax.axis_size(axis))])  8.74 us
    pallas_call x1, Pallas kernels, per_device(): pl.pallas_call(functools.partial(first_body, (far_keep, near_keep)), out_...  3.62 us
    pallas_call x3, Pallas kernels, later(): pl.pallas_call(stress, out_shape=f32(quarter, events, share), in_specs=[V...  2.33 us
    pallas_call x1, Pallas kernels, per_device(): pl.pallas_call(functools.partial(pack_body, far_send), out_shape=[f32(2,...  2.17 us
    pallas_call x1, Pallas kernels, per_device(): pl.pallas_call(functools.partial(densify_body, near_send, entries), out_s...  2.15 us
  transfers between devices with their start and end apart: 8, of which 7 were waited for; matrix products, arithmetic and copies ran while one was open for 0% of the time, Pallas kernels for 5%

profile of v5, /device:TPU:0, one launch (start us, length us, event | category | flops | bytes accessed | tf_op | source)
XLA Modules:
  0.0 46.0 jit_solution(144021879824138517)
XLA Ops:
  0.6 0.1 pad_add_fusion.me_ref
  0.7 2.2 %pack.1 = (f32[2,5,8,128]{3,2,1,0:T(8,128)S(1)}, f32[2,128,2048]{2,1,0:T(8,128)S(1)}) custom-call(s32[2]{0:T(128)S(1)} %pad_add_fusion.me_ref, f32[8,8,128]{2,1,0:T(8,128)} %slip_hbm.1, s32[8,8]{1,0:T(8,128)} %list_hbm.1, s32[8]{0:T(128)} %count_hbm.1, f32[1024,2048]{1,0:T(8,128)} %kernel_hbm.5), custom_call_target="tpu_custom_call" | custom-call | tf_op jit(solution)/shard_map/pack/pallas_call | solution.py:191
  2.9 3.0 %collective-permute-start = (f32[1,2,5,8,128]{4,3,2,0,1:T(8,128)S(1)}, f32[1,2,5,8,128]{4,3,2,0,1:T(8,128)S(1)}, u32[]{:S(2)}, u32[]{:S(2)}) collective-permute-start(f32[1,2,5,8,128]{4,3,2,0,1:T(8,128)S(1)} %bitcast.21), channel_id=1, source_target_pairs={{0,16},{8,24},{16,0},{24,8},{1,17},{9,25},{17,1},{25,9},{2,18},{10... | collective-permute-start | bytes 122888 | tf_op jit(solution)/shard_map/ppermute | solution.py:33
  5.9 2.0 %collective-permute-done = f32[1,2,5,8,128]{4,3,2,0,1:T(8,128)S(1)} collective-permute-done((f32[1,2,5,8,128]{4,3,2,0,1:T(8,128)S(1)}, f32[1,2,5,8,128]{4,3,2,0,1:T(8,128)S(1)}, u32[]{:S(2)}, u32[]{:S(2)}) %collective-permute-start) | collective-permute-done | bytes 40992 | tf_op jit(solution)/shard_map/ppermute | solution.py:33
  7.9 0.0 collective-permute-start.1
  7.9 1.2 %collective-permute-done.1.came_ref = f32[2,5,8,128]{3,2,1,0:T(8,128)S(1)} collective-permute-done((f32[2,5,8,128]{3,2,1,0:T(8,128)S(1)}, f32[2,5,8,128]{3,2,1,0:T(8,128)S(1)}, u32[]{:S(2)}, u32[]{:S(2)}) %collective-permute-start.1) | collective-permute-done | bytes 40992 | tf_op jit(solution)/shard_map/ppermute | solution.py:33
  9.1 2.2 %densify.1 = (f32[8,4,16,128]{3,2,1,0:T(8,128)S(1)}, f32[2,128,2048]{2,1,0:T(8,128)S(1)}) custom-call(s32[2]{0:T(128)S(1)} %pad_add_fusion.me_ref, f32[2,5,8,128]{3,2,1,0:T(8,128)S(1)} %get-tuple-element.21.own_ref, f32[2,5,8,128]{3,2,1,0:T(8,128)S(1)} %collective-permute-done.1.came_ref, f32[1024,2048]{1,0:T(8,128)} %kernel_hbm.5), custom_call_target="tpu_custom_call" | custom-call | tf_op jit(solution)/shard_map/densify/pallas_call | solution.py:214
  11.3 15.3 %all_to_all.5.own_ref = f32[8,4,16,128]{3,2,1,0:T(8,128)S(1)} all-to-all(f32[8,4,16,128]{3,2,1,0:T(8,128)S(1)} %get-tuple-element.11), channel_id=1, replica_groups=mesh['rows'=4,'cols'=8] {'cols'}, dimensions={0} | all-to-all | bytes 524288 | tf_op jit(solution)/shard_map/all_to_all | solution.py:223
  26.6 0.0 collective-permute-start.2
  26.6 1.5 %collective-permute-done.2.came_ref = f32[8,4,16,128]{3,2,1,0:T(8,128)S(1)} collective-permute-done((f32[8,4,16,128]{3,2,1,0:T(8,128)S(1)}, f32[8,4,16,128]{3,2,1,0:T(8,128)S(1)}, u32[]{:S(2)}, u32[]{:S(2)}) %collective-permute-start.2) | collective-permute-done | bytes 262176 | tf_op jit(solution)/shard_map/ppermute | solution.py:33
  28.2 3.6 %first_stress.1 = (bf16[128,2048]{1,0:T(8,128)(2,1)S(1)}, f32[2,64,128]{2,1,0:T(8,128)S(1)}, f32[2,128,2048]{2,1,0:T(8,128)S(1)}, f32[2,128,2048]{2,1,0:T(8,128)S(1)}) custom-call(s32[2]{0:T(128)S(1)} %pad_add_fusion.me_ref, f32[8,4,16,128]{3,2,1,0:T(8,128)S(1)} %all_to_all.5.own_ref, f32[8,4,16,128]{3,2,1,0:T(8,128)S(1)} %collective-permute-done.2.came_ref, ...), custom_call_target="tpu_custom_call" | custom-call | flops 201326592 | bytes 2097152 | tf_op jit(solution)/shard_map/first_stress/pallas_call | solution.py:230
  31.8 1.5 %collective-permute-start.5 = (f32[2,64,128]{2,1,0:T(8,128)S(1)}, f32[2,64,128]{2,1,0:T(8,128)S(1)}, u32[]{:S(2)}, u32[]{:S(2)}) collective-permute-start(f32[2,64,128]{2,1,0:T(8,128)S(1)} %get-tuple-element.17), channel_id=1, source_target_pairs={{0,1},{1,0},{2,3},{3,2},{4,5},{5,4},{6,7},{7,6},{8,9},{9,8},{10,11... | collective-permute-start | bytes 196616 | tf_op jit(solution)/shard_map/ppermute | solution.py:33
  33.3 0.8 %stress.4 = f32[2,64,128]{2,1,0:T(8,128)S(1)} custom-call(bf16[128,2048]{1,0:T(8,128)(2,1)S(1)} %get-tuple-element.13.slip_ref, f32[2,128,2048]{2,1,0:T(8,128)S(1)} %get-tuple-element.15.kernel_ref), custom_call_target="tpu_custom_call" | custom-call | flops 201326592 | bytes 2097152 | tf_op jit(solution)/shard_map/stress/pallas_call | solution.py:245
  34.1 0.7 %collective-permute-start.3 = (f32[2,64,128]{2,1,0:T(8,128)S(1)}, f32[2,64,128]{2,1,0:T(8,128)S(1)}, u32[]{:S(2)}, u32[]{:S(2)}) collective-permute-start(f32[2,64,128]{2,1,0:T(8,128)S(1)} %stress.4), channel_id=1, source_target_pairs={{0,1},{1,0},{2,3},{3,2},{4,5},{5,4},{6,7},{7,6},{8,9},{9,8},{10,11... | collective-permute-start | bytes 196616 | tf_op jit(solution)/shard_map/ppermute | solution.py:33
  34.7 0.8 %stress.5 = f32[2,64,128]{2,1,0:T(8,128)S(1)} custom-call(bf16[128,2048]{1,0:T(8,128)(2,1)S(1)} %get-tuple-element.13.slip_ref, f32[2,128,2048]{2,1,0:T(8,128)S(1)} %get-tuple-element.16.kernel_ref), custom_call_target="tpu_custom_call" | custom-call | flops 201326592 | bytes 2097152 | tf_op jit(solution)/shard_map/stress/pallas_call | solution.py:245
  35.5 0.0 copy-start
  35.5 0.0 copy-start.1
  35.6 0.0 copy-start.2
  35.6 0.6 %collective-permute-done.5 = f32[2,64,128]{2,1,0:T(8,128)S(1)} collective-permute-done((f32[2,64,128]{2,1,0:T(8,128)S(1)}, f32[2,64,128]{2,1,0:T(8,128)S(1)}, u32[]{:S(2)}, u32[]{:S(2)}) %collective-permute-start.5) | collective-permute-done | bytes 65568 | tf_op jit(solution)/shard_map/ppermute | solution.py:33
  36.2 1.7 %collective-permute-start.6 = (f32[1,64,128]{2,1,0:T(8,128)S(1)}, f32[1,64,128]{2,1,0:T(8,128)S(1)}, u32[]{:S(2)}, u32[]{:S(2)}) collective-permute-start(f32[1,64,128]{2,1,0:T(8,128)S(1)} %slice.29), channel_id=1, source_target_pairs={{0,2},{1,3},{2,0},{3,1},{4,6},{5,7},{6,4},{7,5},{8,10},{9,11},{10,... | collective-permute-start | bytes 98312 | tf_op jit(solution)/shard_map/ppermute | solution.py:33
  37.9 0.8 %stress.3 = f32[2,64,128]{2,1,0:T(8,128)S(1)} custom-call(bf16[128,2048]{1,0:T(8,128)(2,1)S(1)} %get-tuple-element.13.slip_ref, f32[2,128,2048]{2,1,0:T(8,128)S(1)} %get-tuple-element.14.kernel_ref), custom_call_target="tpu_custom_call" | custom-call | flops 201326592 | bytes 2097152 | tf_op jit(solution)/shard_map/stress/pallas_call | solution.py:245
  38.7 0.0 collective-permute-done.3
  38.7 0.4 collective-permute-start.4
  39.1 1.3 %collective-permute-done.6 = f32[1,64,128]{2,1,0:T(8,128)S(1)} collective-permute-done((f32[1,64,128]{2,1,0:T(8,128)S(1)}, f32[1,64,128]{2,1,0:T(8,128)S(1)}, u32[]{:S(2)}, u32[]{:S(2)}) %collective-permute-start.6) | collective-permute-done | bytes 32800 | tf_op jit(solution)/shard_map/ppermute | solution.py:33
  40.5 1.4 %collective-permute-start.7 = (f32[64,128]{1,0:T(8,128)S(1)}, f32[64,128]{1,0:T(8,128)S(1)}, u32[]{:S(2)}, u32[]{:S(2)}) collective-permute-start(f32[64,128]{1,0:T(8,128)S(1)} %fusion.3), channel_id=1, source_target_pairs={{0,4},{1,5},{2,6},{3,7},{4,0},{5,1},{6,2},{7,3},{8,12},{9,13},{10,... | collective-permute-start | bytes 98312 | tf_op jit(solution)/shard_map/ppermute | solution.py:33
  41.9 0.0 copy-done
  41.9 0.0 copy-done.1
  41.9 0.0 copy-done.2
  41.9 0.8 %collective-permute-done.4 = f32[1,64,128]{2,1,0:T(8,128)S(1)} collective-permute-done((f32[1,64,128]{2,1,0:T(8,128)S(1)}, f32[1,64,128]{2,1,0:T(8,128)S(1)}, u32[]{:S(2)}, u32[]{:S(2)}) %collective-permute-start.4) | collective-permute-done | bytes 32800 | tf_op jit(solution)/shard_map/ppermute | solution.py:33
  42.7 2.6 %collective-permute-done.7 = f32[64,128]{1,0:T(8,128)S(1)} collective-permute-done((f32[64,128]{1,0:T(8,128)S(1)}, f32[64,128]{1,0:T(8,128)S(1)}, u32[]{:S(2)}, u32[]{:S(2)}) %collective-permute-start.7) | collective-permute-done | bytes 32800 | tf_op jit(solution)/shard_map/ppermute | solution.py:33
  45.3 0.7 %add_bitcast_fusion = (f32[128,64]{0,1:T(8,128)}, f32[128,64]{0,1:T(8,128)}) fusion(f32[128]{0:T(128)S(1)} %get-tuple-element.23, f32[128]{0:T(128)S(1)} %copy-done, f32[128]{0:T(128)S(1)} %get-tuple-element.22, f32[64,128]{1,0:T(8,128)S(1)} %collective-permute-done.7, f32[1,64,128]{2,1,0:T(8,128)S(1)} %collective-permute-done.4, f32[2,64,128]{2,1,0:T(8,128)S(1)} %add.23), kind=kLoop, calls=%fused_computation.11 | loop fusion | flops 49152 | bytes 165376 | tf_op jit(solution)/shard_map/transpose | solution.py:271
  (7 shorter events, 0.1 us)
Async XLA Ops:
  2.9 5.0 %collective-permute-start = (f32[1,2,5,8,128]{4,3,2,0,1:T(8,128)S(1)}, f32[1,2,5,8,128]{4,3,2,0,1:T(8,128)S(1)}, u32[]{:S(2)}, u32[]{:S(2)}) collective-permute-start(f32[1,2,5,8,128]{4,3,2,0,1:T(8,128)S(1)} %bitcast.21), channel_id=1, source_target_pairs={{0,16},{8,24},{16,0},{24,8},{1,17},{9,25},{17,1},{25,9},{2,18},{10... | collective-permute-start | bytes 122888 | tf_op jit(solution)/shard_map/ppermute | solution.py:33
  7.9 1.2 %collective-permute-start.1 = (f32[2,5,8,128]{3,2,1,0:T(8,128)S(1)}, f32[2,5,8,128]{3,2,1,0:T(8,128)S(1)}, u32[]{:S(2)}, u32[]{:S(2)}) collective-permute-start(f32[2,5,8,128]{3,2,1,0:T(8,128)S(1)} %get-tuple-element.20), channel_id=1, source_target_pairs={{0,8},{8,0},{16,24},{24,16},{1,9},{9,1},{17,25},{25,17},{2,10},{10... | collective-permute-start | bytes 122888 | tf_op jit(solution)/shard_map/ppermute | solution.py:33
  26.6 1.5 %collective-permute-start.2 = (f32[8,4,16,128]{3,2,1,0:T(8,128)S(1)}, f32[8,4,16,128]{3,2,1,0:T(8,128)S(1)}, u32[]{:S(2)}, u32[]{:S(2)}) collective-permute-start(f32[8,4,16,128]{3,2,1,0:T(8,128)S(1)} %all_to_all.5.own_ref), channel_id=1, source_target_pairs={{0,8},{8,0},{16,24},{24,16},{1,9},{9,1},{17,25},{25,17},{2,10},{10... | collective-permute-start | bytes 786440 | tf_op jit(solution)/shard_map/ppermute | solution.py:33
  31.8 4.3 %collective-permute-start.5 = (f32[2,64,128]{2,1,0:T(8,128)S(1)}, f32[2,64,128]{2,1,0:T(8,128)S(1)}, u32[]{:S(2)}, u32[]{:S(2)}) collective-permute-start(f32[2,64,128]{2,1,0:T(8,128)S(1)} %get-tuple-element.17), channel_id=1, source_target_pairs={{0,1},{1,0},{2,3},{3,2},{4,5},{5,4},{6,7},{7,6},{8,9},{9,8},{10,11... | collective-permute-start | bytes 196616 | tf_op jit(solution)/shard_map/ppermute | solution.py:33
  34.1 4.6 %collective-permute-start.3 = (f32[2,64,128]{2,1,0:T(8,128)S(1)}, f32[2,64,128]{2,1,0:T(8,128)S(1)}, u32[]{:S(2)}, u32[]{:S(2)}) collective-permute-start(f32[2,64,128]{2,1,0:T(8,128)S(1)} %stress.4), channel_id=1, source_target_pairs={{0,1},{1,0},{2,3},{3,2},{4,5},{5,4},{6,7},{7,6},{8,9},{9,8},{10,11... | collective-permute-start | bytes 196616 | tf_op jit(solution)/shard_map/ppermute | solution.py:33
  35.5 6.4 %copy-start = (f32[128]{0:T(128)S(1)}, f32[128]{0:T(128)}, u32[]{:S(2)}) copy-start(f32[128]{0:T(128)} %param.11) | copy-start | bytes 1540
  35.5 6.4 %copy-start.1 = (f32[128]{0:T(128)S(1)}, f32[128]{0:T(128)}, u32[]{:S(2)}) copy-start(f32[128]{0:T(128)} %param.12) | copy-start | bytes 1540
  35.6 6.3 %copy-start.2 = (f32[128]{0:T(128)S(1)}, f32[128]{0:T(128)}, u32[]{:S(2)}) copy-start(f32[128]{0:T(128)} %param.13) | copy-start | bytes 1540
  36.2 4.3 %collective-permute-start.6 = (f32[1,64,128]{2,1,0:T(8,128)S(1)}, f32[1,64,128]{2,1,0:T(8,128)S(1)}, u32[]{:S(2)}, u32[]{:S(2)}) collective-permute-start(f32[1,64,128]{2,1,0:T(8,128)S(1)} %slice.29), channel_id=1, source_target_pairs={{0,2},{1,3},{2,0},{3,1},{4,6},{5,7},{6,4},{7,5},{8,10},{9,11},{10,... | collective-permute-start | bytes 98312 | tf_op jit(solution)/shard_map/ppermute | solution.py:33
  38.7 4.0 %collective-permute-start.4 = (f32[1,64,128]{2,1,0:T(8,128)S(1)}, f32[1,64,128]{2,1,0:T(8,128)S(1)}, u32[]{:S(2)}, u32[]{:S(2)}) collective-permute-start(f32[1,64,128]{2,1,0:T(8,128)S(1)} %slice.27), channel_id=1, source_target_pairs={{0,2},{1,3},{2,0},{3,1},{4,6},{5,7},{6,4},{7,5},{8,10},{9,11},{10,... | collective-permute-start | bytes 98312 | tf_op jit(solution)/shard_map/ppermute | solution.py:33
  40.5 4.8 %collective-permute-start.7 = (f32[64,128]{1,0:T(8,128)S(1)}, f32[64,128]{1,0:T(8,128)S(1)}, u32[]{:S(2)}, u32[]{:S(2)}) collective-permute-start(f32[64,128]{1,0:T(8,128)S(1)} %fusion.3), channel_id=1, source_target_pairs={{0,4},{1,5},{2,6},{3,7},{4,0},{5,1},{6,2},{7,3},{8,12},{9,13},{10,... | collective-permute-start | bytes 98312 | tf_op jit(solution)/shard_map/ppermute | solution.py:33

commit v6 on v5

--- a/solution.py
+++ b/solution.py
@@ -47,8 +47,8 @@
                     sems.at[j, p],
                 )
             )
-    for copy in copies:
-        copy.start()
+    for n, copy in enumerate(copies):
+        copy.start(priority=n % 2)
     return copies
 
 

time: 46.2 us -> 46.2 us (level)
  no operation moved by 1% of the time
where the time goes in v6:
time: 46.2 us; the launch traced here: 46 us
  blocking collectives  15.3 us (33%)
  Pallas kernels  10.3 us (22%)
  waiting for transfers between devices  10.1 us (22%)
  starting transfers between devices  8.73 us (19%)
  other arithmetic  0.78 us (2%)
  between operations  0.76 us (2%)
    all_to_all x1, blocking collectives, per_device(): mine = lax.all_to_all(dense, 'cols', 0, 0, tiled=True)  15.3 us
    ppermute x8, waiting for transfers between devices, send_xor(): lax.ppermute(block, axis, [(r, r ^ k) for r in range(lax.axis_size(axis))])  10.1 us
    ppermute x8, starting transfers between devices, send_xor(): lax.ppermute(block, axis, [(r, r ^ k) for r in range(lax.axis_size(axis))])  8.73 us
    pallas_call x1, Pallas kernels, per_device(): pl.pallas_call(functools.partial(first_body, (far_keep, near_keep)), out_...  3.62 us
    pallas_call x3, Pallas kernels, later(): pl.pallas_call(stress, out_shape=f32(quarter, events, share), in_specs=[V...  2.33 us
    pallas_call x1, Pallas kernels, per_device(): pl.pallas_call(functools.partial(pack_body, far_send), out_shape=[f32(2,...  2.17 us
    pallas_call x1, Pallas kernels, per_device(): pl.pallas_call(functools.partial(densify_body, near_send, entries), out_s...  2.14 us
  transfers between devices with their start and end apart: 8, of which 7 were waited for; matrix products, arithmetic and copies ran while one was open for 0% of the time, Pallas kernels for 5%

profile of v6, /device:TPU:0, one launch (start us, length us, event | category | flops | bytes accessed | tf_op | source)
XLA Modules:
  0.0 46.0 jit_solution(16051270765951018070)
XLA Ops:
  0.6 0.1 pad_add_fusion.me_ref
  0.7 2.2 %pack.1 = (f32[2,5,8,128]{3,2,1,0:T(8,128)S(1)}, f32[2,128,2048]{2,1,0:T(8,128)S(1)}) custom-call(s32[2]{0:T(128)S(1)} %pad_add_fusion.me_ref, f32[8,8,128]{2,1,0:T(8,128)} %slip_hbm.1, s32[8,8]{1,0:T(8,128)} %list_hbm.1, s32[8]{0:T(128)} %count_hbm.1, f32[1024,2048]{1,0:T(8,128)} %kernel_hbm.5), custom_call_target="tpu_custom_call" | custom-call | tf_op jit(solution)/shard_map/pack/pallas_call | solution.py:191
  2.9 3.0 %collective-permute-start = (f32[1,2,5,8,128]{4,3,2,0,1:T(8,128)S(1)}, f32[1,2,5,8,128]{4,3,2,0,1:T(8,128)S(1)}, u32[]{:S(2)}, u32[]{:S(2)}) collective-permute-start(f32[1,2,5,8,128]{4,3,2,0,1:T(8,128)S(1)} %bitcast.21), channel_id=1, source_target_pairs={{0,16},{8,24},{16,0},{24,8},{1,17},{9,25},{17,1},{25,9},{2,18},{10... | collective-permute-start | bytes 122888 | tf_op jit(solution)/shard_map/ppermute | solution.py:33
  5.9 2.0 %collective-permute-done = f32[1,2,5,8,128]{4,3,2,0,1:T(8,128)S(1)} collective-permute-done((f32[1,2,5,8,128]{4,3,2,0,1:T(8,128)S(1)}, f32[1,2,5,8,128]{4,3,2,0,1:T(8,128)S(1)}, u32[]{:S(2)}, u32[]{:S(2)}) %collective-permute-start) | collective-permute-done | bytes 40992 | tf_op jit(solution)/shard_map/ppermute | solution.py:33
  7.9 0.0 collective-permute-start.1
  7.9 1.2 %collective-permute-done.1.came_ref = f32[2,5,8,128]{3,2,1,0:T(8,128)S(1)} collective-permute-done((f32[2,5,8,128]{3,2,1,0:T(8,128)S(1)}, f32[2,5,8,128]{3,2,1,0:T(8,128)S(1)}, u32[]{:S(2)}, u32[]{:S(2)}) %collective-permute-start.1) | collective-permute-done | bytes 40992 | tf_op jit(solution)/shard_map/ppermute | solution.py:33
  9.1 2.1 %densify.1 = (f32[8,4,16,128]{3,2,1,0:T(8,128)S(1)}, f32[2,128,2048]{2,1,0:T(8,128)S(1)}) custom-call(s32[2]{0:T(128)S(1)} %pad_add_fusion.me_ref, f32[2,5,8,128]{3,2,1,0:T(8,128)S(1)} %get-tuple-element.21.own_ref, f32[2,5,8,128]{3,2,1,0:T(8,128)S(1)} %collective-permute-done.1.came_ref, f32[1024,2048]{1,0:T(8,128)} %kernel_hbm.5), custom_call_target="tpu_custom_call" | custom-call | tf_op jit(solution)/shard_map/densify/pallas_call | solution.py:214
  11.3 15.3 %all_to_all.5.own_ref = f32[8,4,16,128]{3,2,1,0:T(8,128)S(1)} all-to-all(f32[8,4,16,128]{3,2,1,0:T(8,128)S(1)} %get-tuple-element.11), channel_id=1, replica_groups=mesh['rows'=4,'cols'=8] {'cols'}, dimensions={0} | all-to-all | bytes 524288 | tf_op jit(solution)/shard_map/all_to_all | solution.py:223
  26.6 0.0 collective-permute-start.2
  26.6 1.5 %collective-permute-done.2.came_ref = f32[8,4,16,128]{3,2,1,0:T(8,128)S(1)} collective-permute-done((f32[8,4,16,128]{3,2,1,0:T(8,128)S(1)}, f32[8,4,16,128]{3,2,1,0:T(8,128)S(1)}, u32[]{:S(2)}, u32[]{:S(2)}) %collective-permute-start.2) | collective-permute-done | bytes 262176 | tf_op jit(solution)/shard_map/ppermute | solution.py:33
  28.2 3.6 %first_stress.1 = (bf16[128,2048]{1,0:T(8,128)(2,1)S(1)}, f32[2,64,128]{2,1,0:T(8,128)S(1)}, f32[2,128,2048]{2,1,0:T(8,128)S(1)}, f32[2,128,2048]{2,1,0:T(8,128)S(1)}) custom-call(s32[2]{0:T(128)S(1)} %pad_add_fusion.me_ref, f32[8,4,16,128]{3,2,1,0:T(8,128)S(1)} %all_to_all.5.own_ref, f32[8,4,16,128]{3,2,1,0:T(8,128)S(1)} %collective-permute-done.2.came_ref, ...), custom_call_target="tpu_custom_call" | custom-call | flops 201326592 | bytes 2097152 | tf_op jit(solution)/shard_map/first_stress/pallas_call | solution.py:230
  31.8 1.5 %collective-permute-start.5 = (f32[2,64,128]{2,1,0:T(8,128)S(1)}, f32[2,64,128]{2,1,0:T(8,128)S(1)}, u32[]{:S(2)}, u32[]{:S(2)}) collective-permute-start(f32[2,64,128]{2,1,0:T(8,128)S(1)} %get-tuple-element.17), channel_id=1, source_target_pairs={{0,1},{1,0},{2,3},{3,2},{4,5},{5,4},{6,7},{7,6},{8,9},{9,8},{10,11... | collective-permute-start | bytes 196616 | tf_op jit(solution)/shard_map/ppermute | solution.py:33
  33.3 0.8 %stress.4 = f32[2,64,128]{2,1,0:T(8,128)S(1)} custom-call(bf16[128,2048]{1,0:T(8,128)(2,1)S(1)} %get-tuple-element.13.slip_ref, f32[2,128,2048]{2,1,0:T(8,128)S(1)} %get-tuple-element.15.kernel_ref), custom_call_target="tpu_custom_call" | custom-call | flops 201326592 | bytes 2097152 | tf_op jit(solution)/shard_map/stress/pallas_call | solution.py:245
  34.1 0.7 %collective-permute-start.3 = (f32[2,64,128]{2,1,0:T(8,128)S(1)}, f32[2,64,128]{2,1,0:T(8,128)S(1)}, u32[]{:S(2)}, u32[]{:S(2)}) collective-permute-start(f32[2,64,128]{2,1,0:T(8,128)S(1)} %stress.4), channel_id=1, source_target_pairs={{0,1},{1,0},{2,3},{3,2},{4,5},{5,4},{6,7},{7,6},{8,9},{9,8},{10,11... | collective-permute-start | bytes 196616 | tf_op jit(solution)/shard_map/ppermute | solution.py:33
  34.7 0.8 %stress.5 = f32[2,64,128]{2,1,0:T(8,128)S(1)} custom-call(bf16[128,2048]{1,0:T(8,128)(2,1)S(1)} %get-tuple-element.13.slip_ref, f32[2,128,2048]{2,1,0:T(8,128)S(1)} %get-tuple-element.16.kernel_ref), custom_call_target="tpu_custom_call" | custom-call | flops 201326592 | bytes 2097152 | tf_op jit(solution)/shard_map/stress/pallas_call | solution.py:245
  35.5 0.0 copy-start
  35.5 0.0 copy-start.1
  35.5 0.0 copy-start.2
  35.6 0.6 %collective-permute-done.5 = f32[2,64,128]{2,1,0:T(8,128)S(1)} collective-permute-done((f32[2,64,128]{2,1,0:T(8,128)S(1)}, f32[2,64,128]{2,1,0:T(8,128)S(1)}, u32[]{:S(2)}, u32[]{:S(2)}) %collective-permute-start.5) | collective-permute-done | bytes 65568 | tf_op jit(solution)/shard_map/ppermute | solution.py:33
  36.1 1.7 %collective-permute-start.6 = (f32[1,64,128]{2,1,0:T(8,128)S(1)}, f32[1,64,128]{2,1,0:T(8,128)S(1)}, u32[]{:S(2)}, u32[]{:S(2)}) collective-permute-start(f32[1,64,128]{2,1,0:T(8,128)S(1)} %slice.29), channel_id=1, source_target_pairs={{0,2},{1,3},{2,0},{3,1},{4,6},{5,7},{6,4},{7,5},{8,10},{9,11},{10,... | collective-permute-start | bytes 98312 | tf_op jit(solution)/shard_map/ppermute | solution.py:33
  37.8 0.8 %stress.3 = f32[2,64,128]{2,1,0:T(8,128)S(1)} custom-call(bf16[128,2048]{1,0:T(8,128)(2,1)S(1)} %get-tuple-element.13.slip_ref, f32[2,128,2048]{2,1,0:T(8,128)S(1)} %get-tuple-element.14.kernel_ref), custom_call_target="tpu_custom_call" | custom-call | flops 201326592 | bytes 2097152 | tf_op jit(solution)/shard_map/stress/pallas_call | solution.py:245
  38.6 0.0 collective-permute-done.3
  38.7 0.5 collective-permute-start.4
  39.1 1.4 %collective-permute-done.6 = f32[1,64,128]{2,1,0:T(8,128)S(1)} collective-permute-done((f32[1,64,128]{2,1,0:T(8,128)S(1)}, f32[1,64,128]{2,1,0:T(8,128)S(1)}, u32[]{:S(2)}, u32[]{:S(2)}) %collective-permute-start.6) | collective-permute-done | bytes 32800 | tf_op jit(solution)/shard_map/ppermute | solution.py:33
  40.5 1.4 %collective-permute-start.7 = (f32[64,128]{1,0:T(8,128)S(1)}, f32[64,128]{1,0:T(8,128)S(1)}, u32[]{:S(2)}, u32[]{:S(2)}) collective-permute-start(f32[64,128]{1,0:T(8,128)S(1)} %fusion.3), channel_id=1, source_target_pairs={{0,4},{1,5},{2,6},{3,7},{4,0},{5,1},{6,2},{7,3},{8,12},{9,13},{10,... | collective-permute-start | bytes 98312 | tf_op jit(solution)/shard_map/ppermute | solution.py:33
  41.9 0.0 copy-done
  41.9 0.0 copy-done.1
  41.9 0.0 copy-done.2
  41.9 0.8 %collective-permute-done.4 = f32[1,64,128]{2,1,0:T(8,128)S(1)} collective-permute-done((f32[1,64,128]{2,1,0:T(8,128)S(1)}, f32[1,64,128]{2,1,0:T(8,128)S(1)}, u32[]{:S(2)}, u32[]{:S(2)}) %collective-permute-start.4) | collective-permute-done | bytes 32800 | tf_op jit(solution)/shard_map/ppermute | solution.py:33
  42.7 2.6 %collective-permute-done.7 = f32[64,128]{1,0:T(8,128)S(1)} collective-permute-done((f32[64,128]{1,0:T(8,128)S(1)}, f32[64,128]{1,0:T(8,128)S(1)}, u32[]{:S(2)}, u32[]{:S(2)}) %collective-permute-start.7) | collective-permute-done | bytes 32800 | tf_op jit(solution)/shard_map/ppermute | solution.py:33
  45.3 0.7 %add_bitcast_fusion = (f32[128,64]{0,1:T(8,128)}, f32[128,64]{0,1:T(8,128)}) fusion(f32[128]{0:T(128)S(1)} %get-tuple-element.23, f32[128]{0:T(128)S(1)} %copy-done, f32[128]{0:T(128)S(1)} %get-tuple-element.22, f32[64,128]{1,0:T(8,128)S(1)} %collective-permute-done.7, f32[1,64,128]{2,1,0:T(8,128)S(1)} %collective-permute-done.4, f32[2,64,128]{2,1,0:T(8,128)S(1)} %add.23), kind=kLoop, calls=%fused_computation.11 | loop fusion | flops 49152 | bytes 165376 | tf_op jit(solution)/shard_map/transpose | solution.py:271
  (7 shorter events, 0.1 us)
Async XLA Ops:
  2.9 5.0 %collective-permute-start = (f32[1,2,5,8,128]{4,3,2,0,1:T(8,128)S(1)}, f32[1,2,5,8,128]{4,3,2,0,1:T(8,128)S(1)}, u32[]{:S(2)}, u32[]{:S(2)}) collective-permute-start(f32[1,2,5,8,128]{4,3,2,0,1:T(8,128)S(1)} %bitcast.21), channel_id=1, source_target_pairs={{0,16},{8,24},{16,0},{24,8},{1,17},{9,25},{17,1},{25,9},{2,18},{10... | collective-permute-start | bytes 122888 | tf_op jit(solution)/shard_map/ppermute | solution.py:33
  7.9 1.2 %collective-permute-start.1 = (f32[2,5,8,128]{3,2,1,0:T(8,128)S(1)}, f32[2,5,8,128]{3,2,1,0:T(8,128)S(1)}, u32[]{:S(2)}, u32[]{:S(2)}) collective-permute-start(f32[2,5,8,128]{3,2,1,0:T(8,128)S(1)} %get-tuple-element.20), channel_id=1, source_target_pairs={{0,8},{8,0},{16,24},{24,16},{1,9},{9,1},{17,25},{25,17},{2,10},{10... | collective-permute-start | bytes 122888 | tf_op jit(solution)/shard_map/ppermute | solution.py:33
  26.6 1.5 %collective-permute-start.2 = (f32[8,4,16,128]{3,2,1,0:T(8,128)S(1)}, f32[8,4,16,128]{3,2,1,0:T(8,128)S(1)}, u32[]{:S(2)}, u32[]{:S(2)}) collective-permute-start(f32[8,4,16,128]{3,2,1,0:T(8,128)S(1)} %all_to_all.5.own_ref), channel_id=1, source_target_pairs={{0,8},{8,0},{16,24},{24,16},{1,9},{9,1},{17,25},{25,17},{2,10},{10... | collective-permute-start | bytes 786440 | tf_op jit(solution)/shard_map/ppermute | solution.py:33
  31.8 4.3 %collective-permute-start.5 = (f32[2,64,128]{2,1,0:T(8,128)S(1)}, f32[2,64,128]{2,1,0:T(8,128)S(1)}, u32[]{:S(2)}, u32[]{:S(2)}) collective-permute-start(f32[2,64,128]{2,1,0:T(8,128)S(1)} %get-tuple-element.17), channel_id=1, source_target_pairs={{0,1},{1,0},{2,3},{3,2},{4,5},{5,4},{6,7},{7,6},{8,9},{9,8},{10,11... | collective-permute-start | bytes 196616 | tf_op jit(solution)/shard_map/ppermute | solution.py:33
  34.1 4.6 %collective-permute-start.3 = (f32[2,64,128]{2,1,0:T(8,128)S(1)}, f32[2,64,128]{2,1,0:T(8,128)S(1)}, u32[]{:S(2)}, u32[]{:S(2)}) collective-permute-start(f32[2,64,128]{2,1,0:T(8,128)S(1)} %stress.4), channel_id=1, source_target_pairs={{0,1},{1,0},{2,3},{3,2},{4,5},{5,4},{6,7},{7,6},{8,9},{9,8},{10,11... | collective-permute-start | bytes 196616 | tf_op jit(solution)/shard_map/ppermute | solution.py:33
  35.5 6.3 %copy-start = (f32[128]{0:T(128)S(1)}, f32[128]{0:T(128)}, u32[]{:S(2)}) copy-start(f32[128]{0:T(128)} %param.11) | copy-start | bytes 1540
  35.5 6.3 %copy-start.1 = (f32[128]{0:T(128)S(1)}, f32[128]{0:T(128)}, u32[]{:S(2)}) copy-start(f32[128]{0:T(128)} %param.12) | copy-start | bytes 1540
  35.5 6.3 %copy-start.2 = (f32[128]{0:T(128)S(1)}, f32[128]{0:T(128)}, u32[]{:S(2)}) copy-start(f32[128]{0:T(128)} %param.13) | copy-start | bytes 1540
  36.1 4.3 %collective-permute-start.6 = (f32[1,64,128]{2,1,0:T(8,128)S(1)}, f32[1,64,128]{2,1,0:T(8,128)S(1)}, u32[]{:S(2)}, u32[]{:S(2)}) collective-permute-start(f32[1,64,128]{2,1,0:T(8,128)S(1)} %slice.29), channel_id=1, source_target_pairs={{0,2},{1,3},{2,0},{3,1},{4,6},{5,7},{6,4},{7,5},{8,10},{9,11},{10,... | collective-permute-start | bytes 98312 | tf_op jit(solution)/shard_map/ppermute | solution.py:33
  38.7 4.0 %collective-permute-start.4 = (f32[1,64,128]{2,1,0:T(8,128)S(1)}, f32[1,64,128]{2,1,0:T(8,128)S(1)}, u32[]{:S(2)}, u32[]{:S(2)}) collective-permute-start(f32[1,64,128]{2,1,0:T(8,128)S(1)} %slice.27), channel_id=1, source_target_pairs={{0,2},{1,3},{2,0},{3,1},{4,6},{5,7},{6,4},{7,5},{8,10},{9,11},{10,... | collective-permute-start | bytes 98312 | tf_op jit(solution)/shard_map/ppermute | solution.py:33
  40.5 4.8 %collective-permute-start.7 = (f32[64,128]{1,0:T(8,128)S(1)}, f32[64,128]{1,0:T(8,128)S(1)}, u32[]{:S(2)}, u32[]{:S(2)}) collective-permute-start(f32[64,128]{1,0:T(8,128)S(1)} %fusion.3), channel_id=1, source_target_pairs={{0,4},{1,5},{2,6},{3,7},{4,0},{5,1},{6,2},{7,3},{8,12},{9,13},{10,... | collective-permute-start | bytes 98312 | tf_op jit(solution)/shard_map/ppermute | solution.py:33

commit v7 on v6

--- a/solution.py
+++ b/solution.py
@@ -57,17 +57,13 @@
         copy.wait()
 
 
-def pack_body(
-    targets, me_ref, slip_hbm, list_hbm, count_hbm, kernel_hbm, out_ref, held_ref,
-    slip_ref, list_ref, count_ref, ids, sems, held_sems,
-):
+def pack_body(me_ref, slip_hbm, list_hbm, count_hbm, out_ref, slip_ref, list_ref, count_ref, ids, sems):
     copies = [
         pltpu.make_async_copy(src, dst, sems.at[j])
         for j, (src, dst) in enumerate(((list_hbm, list_ref), (count_hbm, count_ref), (slip_hbm, slip_ref)))
     ]
     for copy in copies:
         copy.start()
-    held = fetch(targets, me_ref[1], kernel_hbm, held_ref, held_sems)
     events, entries = list_ref.shape
     half = events // 2
     row = me_ref[0]
@@ -85,11 +81,9 @@
         for i in range(half):
             out_ref[h, i, 0:entries, :] = slip_ref[first + i]
             out_ref[h, half, i : i + 1, :] = ids[pl.ds(first + i, 1), :]
-    wait(held)
-
-
-def densify_body(targets, entries, me_ref, own_ref, came_ref, kernel_hbm, out_ref, held_ref, slips, held_sems):
-    held = fetch(targets, me_ref[1], kernel_hbm, held_ref, held_sems)
+
+
+def densify_body(entries, me_ref, own_ref, came_ref, out_hbm, out_ref, slips, sem):
     halves, half = own_ref.shape[0], own_ref.shape[1] - 1
     width, _, blocks_here, _ = out_ref.shape
     blocks = width * blocks_here
@@ -114,7 +108,18 @@
             slip = slip - piece.astype(jnp.float32)
             total = total + jnp.dot(onehot, piece, preferred_element_type=jnp.float32)
         out_ref[:, i] = total.reshape(width, blocks_here, BLOCK)
-    wait(held)
+    copy = pltpu.make_async_copy(out_ref, out_hbm, sem)
+    copy.start()
+    copy.wait()
+
+
+def fetch_body(targets, me_ref, kernel_hbm, *refs):
+    held_refs, held_sems = refs[:-1], refs[-1]
+    held = [
+        fetch(t, me_ref[1], kernel_hbm, ref, held_sems.at[j]) for j, (t, ref) in enumerate(zip(targets, held_refs))
+    ]
+    for copies in held:
+        wait(copies)
 
 
 def assemble(row, own_ref, came_ref, out_ref, dense):
@@ -184,26 +189,24 @@
     near_keep, far_keep = order[0 : 2 * quarter : 2], order[1 : 2 * quarter : 2]
     near_send, far_send = order[2 * quarter :: 2], order[2 * quarter + 1 :: 2]
     held_shape = pltpu.VMEM((quarter, share, sources), jnp.float32)
-    held_sems = pltpu.SemaphoreType.DMA((quarter, PIECES))
     in_hbm, in_vmem = (
         functools.partial(pltpu.with_memory_space_constraint, memory_space=m) for m in (pltpu.HBM, pltpu.VMEM)
     )
-    packed, far_send_kernel = pl.pallas_call(
-        functools.partial(pack_body, far_send),
-        out_shape=[f32(2, half + 1, SUB, BLOCK), held_shape],
-        in_specs=[SMEM_SPEC] + [HBM_SPEC] * 4,
-        out_specs=[VMEM_SPEC] * 2,
+    packed = pl.pallas_call(
+        pack_body,
+        out_shape=f32(2, half + 1, SUB, BLOCK),
+        in_specs=[SMEM_SPEC] + [HBM_SPEC] * 3,
+        out_specs=VMEM_SPEC,
         scratch_shapes=[
             pltpu.VMEM(slip_delta.shape, jnp.float32),
             pltpu.VMEM(block_list.shape, jnp.int32),
             pltpu.SMEM(live_count.shape, jnp.int32),
             pltpu.VMEM((SUB, BLOCK), jnp.float32),
             pltpu.SemaphoreType.DMA((3,)),
-            held_sems,
         ],
         compiler_params=params(4),
         name="pack",
-    )(me, in_hbm(slip_delta), in_hbm(block_list), in_hbm(live_count), in_hbm(kernel))
+    )(me, in_hbm(slip_delta), in_hbm(block_list), in_hbm(live_count))
     held = packed[None]
     step = 2
     while step < height:
@@ -211,30 +214,50 @@
         step *= 2
     came = send_xor(held[:, 1], "rows", 1)
 
-    dense, near_send_kernel = pl.pallas_call(
-        functools.partial(densify_body, near_send, entries),
-        out_shape=[f32(width, half, blocks_here, BLOCK), held_shape],
-        in_specs=[SMEM_SPEC, VMEM_SPEC, VMEM_SPEC, HBM_SPEC],
-        out_specs=[VMEM_SPEC] * 2,
-        scratch_shapes=[pltpu.VMEM((half, height * entries, BLOCK), jnp.float32), held_sems],
+    dense = pl.pallas_call(
+        functools.partial(densify_body, entries),
+        out_shape=pltpu.HBM((width, half, blocks_here, BLOCK), jnp.float32),
+        in_specs=[SMEM_SPEC, VMEM_SPEC, VMEM_SPEC],
+        out_specs=HBM_SPEC,
+        scratch_shapes=[
+            pltpu.VMEM((width, half, blocks_here, BLOCK), jnp.float32),
+            pltpu.VMEM((half, height * entries, BLOCK), jnp.float32),
+            pltpu.SemaphoreType.DMA,
+        ],
         compiler_params=params(8),
         name="densify",
-    )(me, held[:, 0], came, in_hbm(kernel))
+    )(me, held[:, 0], came)
+    dense, after = lax.optimization_barrier((dense, me))
     mine = lax.all_to_all(dense, "cols", 0, 0, tiled=True)
+    far_send_kernel, near_send_kernel, far_keep_kernel = pl.pallas_call(
+        functools.partial(fetch_body, (far_send, near_send, far_keep)),
+        out_shape=[held_shape] * 3,
+        in_specs=[SMEM_SPEC, HBM_SPEC],
+        out_specs=[VMEM_SPEC] * 3,
+        scratch_shapes=[pltpu.SemaphoreType.DMA((3, quarter, PIECES))],
+        compiler_params=params(4),
+        cost_estimate=pl.CostEstimate(
+            flops=0, bytes_accessed=6 * receivers * sources, transcendentals=0
+        ),
+        name="fetch",
+    )(after, in_hbm(kernel))
+    mine, far_send_kernel, near_send_kernel, far_keep_kernel = lax.optimization_barrier(
+        (mine, far_send_kernel, near_send_kernel, far_keep_kernel)
+    )
 
     cost = pl.CostEstimate(
         flops=6 * quarter * share * sources * events,
         bytes_accessed=4 * quarter * share * sources,
         transcendentals=0,
     )
-    slips, far_sent, far_keep_kernel, near_keep_kernel = pl.pallas_call(
-        functools.partial(first_body, (far_keep, near_keep)),
-        out_shape=[bf16(2 * events, sources), f32(quarter, events, share), held_shape, held_shape],
+    slips, far_sent, near_keep_kernel = pl.pallas_call(
+        functools.partial(first_body, (near_keep,)),
+        out_shape=[bf16(2 * events, sources), f32(quarter, events, share), held_shape],
         in_specs=[SMEM_SPEC, VMEM_SPEC, VMEM_SPEC, VMEM_SPEC, HBM_SPEC],
-        out_specs=[VMEM_SPEC] * 4,
+        out_specs=[VMEM_SPEC] * 3,
         scratch_shapes=[
             pltpu.VMEM((events, blocks_here, BLOCK), jnp.float32),
-            pltpu.SemaphoreType.DMA((2, quarter, PIECES)),
+            pltpu.SemaphoreType.DMA((1, quarter, PIECES)),
         ],
         compiler_params=params(8),
         cost_estimate=cost,

time: 46.2 us -> 46 us (level)
  blocking collectives: 15.3 us -> 0 us
  starting transfers between devices: 8.73 us -> 15 us
  local copies, waits for them, and re-layouts: 0.03 us -> 4.25 us
  waiting for transfers between devices: 10.1 us -> 13.1 us
  Pallas kernels: 10.3 us -> 11.7 us
    all_to_all x1 -> x0, blocking collectives: 15.3 us -> none  [per_device(): mine = lax.all_to_all(dense, 'cols', 0, 0, tiled=True)]
    all_to_all x0 -> x1, starting transfers between devices: none -> 6.32 us  [per_device(): mine = lax.all_to_all(dense, 'cols', 0, 0, tiled=True)]
    unnamed x6 -> x14, local copies, waits for them, and re-layouts: 0.02 us -> 4.24 us
    all_to_all x0 -> x1, waiting for transfers between devices: none -> 3.09 us  [per_device(): mine = lax.all_to_all(dense, 'cols', 0, 0, tiled=True)]
    pallas_call x3 -> x4, Pallas kernels: 7.93 us -> 9.37 us  [the longest x1 3.51 us: per_device(): pl.pallas_call(functools.partial(fetch_body, (far_send, near_send, far_ke...]
  transfers between devices with their start and end apart: 8 -> 9, of which waited for: 7 -> 8; matrix products, arithmetic and copies ran while one was open for 0% -> 0% of each run, Pallas kernels for 5% -> 13%
where the time goes in v7:
time: 46 us; the launch traced here: 45.7 us
  starting transfers between devices  15 us (33%)
  waiting for transfers between devices  13.1 us (28%)
  Pallas kernels  11.7 us (25%)
  local copies, waits for them, and re-layouts  4.25 us (9%)
  other arithmetic  0.78 us (2%)
  between operations  0.78 us (2%)
    ppermute x8, waiting for transfers between devices, send_xor(): lax.ppermute(block, axis, [(r, r ^ k) for r in range(lax.axis_size(axis))])  10 us
    ppermute x8, starting transfers between devices, send_xor(): lax.ppermute(block, axis, [(r, r ^ k) for r in range(lax.axis_size(axis))])  8.72 us
    all_to_all x1, starting transfers between devices, per_device(): mine = lax.all_to_all(dense, 'cols', 0, 0, tiled=True)  6.32 us
    unnamed x14, local copies, waits for them, and re-layouts  4.24 us
    pallas_call x1, Pallas kernels, per_device(): pl.pallas_call(functools.partial(fetch_body, (far_send, near_send, far_ke...  3.51 us
    all_to_all x1, waiting for transfers between devices, per_device(): mine = lax.all_to_all(dense, 'cols', 0, 0, tiled=True)  3.09 us
    pallas_call x1, Pallas kernels, per_device(): pl.pallas_call(functools.partial(first_body, (near_keep,)), out_shape=[bf...  2.88 us
    pallas_call x3, Pallas kernels, later(): pl.pallas_call(stress, out_shape=f32(quarter, events, share), in_specs=[V...  2.34 us
  transfers between devices with their start and end apart: 9, of which 8 were waited for; matrix products, arithmetic and copies ran while one was open for 0% of the time, Pallas kernels for 13%

profile of v7, /device:TPU:0, one launch (start us, length us, event | category | flops | bytes accessed | tf_op | source)
XLA Modules:
  0.0 45.7 jit_solution(6659788584272166906)
XLA Ops:
  0.6 0.1 pad_add_fusion.me_ref
  0.7 1.5 %pack.1 = f32[2,5,8,128]{3,2,1,0:T(8,128)S(1)} custom-call(s32[2]{0:T(128)S(1)} %pad_add_fusion.me_ref, f32[8,8,128]{2,1,0:T(8,128)} %slip_hbm.1, s32[8,8]{1,0:T(8,128)} %list_hbm.1, s32[8]{0:T(128)} %count_hbm.1), custom_call_target="tpu_custom_call" | custom-call | tf_op jit(solution)/shard_map/pack/pallas_call | solution.py:195
  2.2 3.0 %collective-permute-start = (f32[1,2,5,8,128]{4,3,2,0,1:T(8,128)S(1)}, f32[1,2,5,8,128]{4,3,2,0,1:T(8,128)S(1)}, u32[]{:S(2)}, u32[]{:S(2)}) collective-permute-start(f32[1,2,5,8,128]{4,3,2,0,1:T(8,128)S(1)} %bitcast.21), channel_id=1, source_target_pairs={{0,16},{8,24},{16,0},{24,8},{1,17},{9,25},{17,1},{25,9},{2,18},{10... | collective-permute-start | bytes 122888 | tf_op jit(solution)/shard_map/ppermute | solution.py:33
  5.2 2.0 %collective-permute-done = f32[1,2,5,8,128]{4,3,2,0,1:T(8,128)S(1)} collective-permute-done((f32[1,2,5,8,128]{4,3,2,0,1:T(8,128)S(1)}, f32[1,2,5,8,128]{4,3,2,0,1:T(8,128)S(1)}, u32[]{:S(2)}, u32[]{:S(2)}) %collective-permute-start) | collective-permute-done | bytes 40992 | tf_op jit(solution)/shard_map/ppermute | solution.py:33
  7.2 0.0 collective-permute-start.1
  7.2 1.2 %collective-permute-done.1.came_ref = f32[2,5,8,128]{3,2,1,0:T(8,128)S(1)} collective-permute-done((f32[2,5,8,128]{3,2,1,0:T(8,128)S(1)}, f32[2,5,8,128]{3,2,1,0:T(8,128)S(1)}, u32[]{:S(2)}, u32[]{:S(2)}) %collective-permute-start.1) | collective-permute-done | bytes 40992 | tf_op jit(solution)/shard_map/ppermute | solution.py:33
  8.4 1.5 %densify.1 = f32[8,4,16,128]{3,2,1,0:T(8,128)} custom-call(s32[2]{0:T(128)S(1)} %pad_add_fusion.me_ref, f32[2,5,8,128]{3,2,1,0:T(8,128)S(1)} %get-tuple-element.29.own_ref, f32[2,5,8,128]{3,2,1,0:T(8,128)S(1)} %collective-permute-done.1.came_ref), custom_call_target="tpu_custom_call" | custom-call | tf_op jit(solution)/shard_map/densify/pallas_call | solution.py:217
  10.0 6.3 %all-to-all-start = ((f32[8,4,16,128]{3,2,1,0:T(8,128)}), f32[8,4,16,128]{3,2,1,0:T(8,128)S(1)}, u32[]{:S(2)}, u32[]{:S(2)}) async-start(f32[8,4,16,128]{3,2,1,0:T(8,128)} %densify.1), calls=%async_computation | async-start | bytes 524288 | tf_op jit(solution)/shard_map/all_to_all | solution.py:231
  16.3 3.5 %fetch.1 = (f32[2,128,2048]{2,1,0:T(8,128)S(1)}, f32[2,128,2048]{2,1,0:T(8,128)S(1)}, f32[2,128,2048]{2,1,0:T(8,128)S(1)}) custom-call(s32[2]{0:T(128)S(1)} %pad_add_fusion.me_ref, f32[1024,2048]{1,0:T(8,128)} %kernel_hbm.3), custom_call_target="tpu_custom_call" | custom-call | bytes 12582912 | tf_op jit(solution)/shard_map/fetch/pallas_call | solution.py:232
  19.8 0.0 copy-start
  19.8 1.3 %copy-done = f32[2,128,2048]{2,1,0:T(8,128)} copy-done((f32[2,128,2048]{2,1,0:T(8,128)}, f32[2,128,2048]{2,1,0:T(8,128)S(1)}, u32[]{:S(2)}) %copy-start) | copy-done | bytes 2097176
  21.1 0.0 copy-start.2
  21.1 1.3 %copy-done.2 = f32[2,128,2048]{2,1,0:T(8,128)} copy-done((f32[2,128,2048]{2,1,0:T(8,128)}, f32[2,128,2048]{2,1,0:T(8,128)S(1)}, u32[]{:S(2)}) %copy-start.2) | copy-done | bytes 2097176
  22.4 3.1 %all-to-all-done.own_ref = f32[8,4,16,128]{3,2,1,0:T(8,128)S(1)} async-done(((f32[8,4,16,128]{3,2,1,0:T(8,128)}), f32[8,4,16,128]{3,2,1,0:T(8,128)S(1)}, u32[]{:S(2)}, u32[]{:S(2)}) %all-to-all-start) | async-done | bytes 262176 | tf_op jit(solution)/shard_map/all_to_all | solution.py:231
  25.5 0.0 copy-start.1
  25.5 0.0 collective-permute-start.2
  25.5 1.5 %collective-permute-done.2.came_ref = f32[8,4,16,128]{3,2,1,0:T(8,128)S(1)} collective-permute-done((f32[8,4,16,128]{3,2,1,0:T(8,128)S(1)}, f32[8,4,16,128]{3,2,1,0:T(8,128)S(1)}, u32[]{:S(2)}, u32[]{:S(2)}) %collective-permute-start.2) | collective-permute-done | bytes 262176 | tf_op jit(solution)/shard_map/ppermute | solution.py:33
  27.1 0.0 copy-start.3
  27.1 1.6 %copy-done.3 = f32[2,128,2048]{2,1,0:T(8,128)S(1)} copy-done((f32[2,128,2048]{2,1,0:T(8,128)S(1)}, f32[2,128,2048]{2,1,0:T(8,128)}, u32[]{:S(2)}) %copy-start.3) | copy-done | bytes 2097176
  28.7 2.9 %first_stress.1 = (bf16[128,2048]{1,0:T(8,128)(2,1)S(1)}, f32[2,64,128]{2,1,0:T(8,128)S(1)}, f32[2,128,2048]{2,1,0:T(8,128)S(1)}) custom-call(s32[2]{0:T(128)S(1)} %pad_add_fusion.me_ref, f32[8,4,16,128]{3,2,1,0:T(8,128)S(1)} %all-to-all-done.own_ref, f32[8,4,16,128]{3,2,1,0:T(8,128)S(1)} %collective-permute-done.2.came_ref, f32[2,128,2048]{2,1,0:T(8,128)S(1)} %copy-done.3, ...), custom_call_target="tpu_custom_call" | custom-call | flops 201326592 | bytes 2097152 | tf_op jit(solution)/shard_map/first_stress/pallas_call | solution.py:253
  31.5 1.5 %collective-permute-start.5 = (f32[2,64,128]{2,1,0:T(8,128)S(1)}, f32[2,64,128]{2,1,0:T(8,128)S(1)}, u32[]{:S(2)}, u32[]{:S(2)}) collective-permute-start(f32[2,64,128]{2,1,0:T(8,128)S(1)} %get-tuple-element.25), channel_id=1, source_target_pairs={{0,1},{1,0},{2,3},{3,2},{4,5},{5,4},{6,7},{7,6},{8,9},{9,8},{10,11... | collective-permute-start | bytes 196616 | tf_op jit(solution)/shard_map/ppermute | solution.py:33
  33.0 0.0 copy-done.1
  33.0 0.8 %stress.4 = f32[2,64,128]{2,1,0:T(8,128)S(1)} custom-call(bf16[128,2048]{1,0:T(8,128)(2,1)S(1)} %get-tuple-element.21.slip_ref, f32[2,128,2048]{2,1,0:T(8,128)S(1)} %copy-done.1), custom_call_target="tpu_custom_call" | custom-call | flops 201326592 | bytes 2097152 | tf_op jit(solution)/shard_map/stress/pallas_call | solution.py:268
  33.8 0.7 %collective-permute-start.3 = (f32[2,64,128]{2,1,0:T(8,128)S(1)}, f32[2,64,128]{2,1,0:T(8,128)S(1)}, u32[]{:S(2)}, u32[]{:S(2)}) collective-permute-start(f32[2,64,128]{2,1,0:T(8,128)S(1)} %stress.4), channel_id=1, source_target_pairs={{0,1},{1,0},{2,3},{3,2},{4,5},{5,4},{6,7},{7,6},{8,9},{9,8},{10,11... | collective-permute-start | bytes 196616 | tf_op jit(solution)/shard_map/ppermute | solution.py:33
  34.5 0.8 %stress.5 = f32[2,64,128]{2,1,0:T(8,128)S(1)} custom-call(bf16[128,2048]{1,0:T(8,128)(2,1)S(1)} %get-tuple-element.21.slip_ref, f32[2,128,2048]{2,1,0:T(8,128)S(1)} %get-tuple-element.24.kernel_ref), custom_call_target="tpu_custom_call" | custom-call | flops 201326592 | bytes 2097152 | tf_op jit(solution)/shard_map/stress/pallas_call | solution.py:268
  35.3 0.0 copy-start.4
  35.3 0.0 copy-start.5
  35.3 0.0 copy-start.6
  35.3 0.5 %collective-permute-done.5 = f32[2,64,128]{2,1,0:T(8,128)S(1)} collective-permute-done((f32[2,64,128]{2,1,0:T(8,128)S(1)}, f32[2,64,128]{2,1,0:T(8,128)S(1)}, u32[]{:S(2)}, u32[]{:S(2)}) %collective-permute-start.5) | collective-permute-done | bytes 65568 | tf_op jit(solution)/shard_map/ppermute | solution.py:33
  35.9 1.7 %collective-permute-start.6 = (f32[1,64,128]{2,1,0:T(8,128)S(1)}, f32[1,64,128]{2,1,0:T(8,128)S(1)}, u32[]{:S(2)}, u32[]{:S(2)}) collective-permute-start(f32[1,64,128]{2,1,0:T(8,128)S(1)} %slice.29), channel_id=1, source_target_pairs={{0,2},{1,3},{2,0},{3,1},{4,6},{5,7},{6,4},{7,5},{8,10},{9,11},{10,... | collective-permute-start | bytes 98312 | tf_op jit(solution)/shard_map/ppermute | solution.py:33
  37.6 0.8 %stress.3 = f32[2,64,128]{2,1,0:T(8,128)S(1)} custom-call(bf16[128,2048]{1,0:T(8,128)(2,1)S(1)} %get-tuple-element.21.slip_ref, f32[2,128,2048]{2,1,0:T(8,128)S(1)} %get-tuple-element.22.kernel_ref), custom_call_target="tpu_custom_call" | custom-call | flops 201326592 | bytes 2097152 | tf_op jit(solution)/shard_map/stress/pallas_call | solution.py:268
  38.3 0.0 collective-permute-done.3
  38.4 0.5 %collective-permute-start.4 = (f32[1,64,128]{2,1,0:T(8,128)S(1)}, f32[1,64,128]{2,1,0:T(8,128)S(1)}, u32[]{:S(2)}, u32[]{:S(2)}) collective-permute-start(f32[1,64,128]{2,1,0:T(8,128)S(1)} %slice.27), channel_id=1, source_target_pairs={{0,2},{1,3},{2,0},{3,1},{4,6},{5,7},{6,4},{7,5},{8,10},{9,11},{10,... | collective-permute-start | bytes 98312 | tf_op jit(solution)/shard_map/ppermute | solution.py:33
  38.9 1.3 %collective-permute-done.6 = f32[1,64,128]{2,1,0:T(8,128)S(1)} collective-permute-done((f32[1,64,128]{2,1,0:T(8,128)S(1)}, f32[1,64,128]{2,1,0:T(8,128)S(1)}, u32[]{:S(2)}, u32[]{:S(2)}) %collective-permute-start.6) | collective-permute-done | bytes 32800 | tf_op jit(solution)/shard_map/ppermute | solution.py:33
  40.2 1.4 %collective-permute-start.7 = (f32[64,128]{1,0:T(8,128)S(1)}, f32[64,128]{1,0:T(8,128)S(1)}, u32[]{:S(2)}, u32[]{:S(2)}) collective-permute-start(f32[64,128]{1,0:T(8,128)S(1)} %fusion.3), channel_id=1, source_target_pairs={{0,4},{1,5},{2,6},{3,7},{4,0},{5,1},{6,2},{7,3},{8,12},{9,13},{10,... | collective-permute-start | bytes 98312 | tf_op jit(solution)/shard_map/ppermute | solution.py:33
  41.6 0.0 copy-done.4
  41.6 0.0 copy-done.5
  41.6 0.0 copy-done.6
  41.6 0.8 %collective-permute-done.4 = f32[1,64,128]{2,1,0:T(8,128)S(1)} collective-permute-done((f32[1,64,128]{2,1,0:T(8,128)S(1)}, f32[1,64,128]{2,1,0:T(8,128)S(1)}, u32[]{:S(2)}, u32[]{:S(2)}) %collective-permute-start.4) | collective-permute-done | bytes 32800 | tf_op jit(solution)/shard_map/ppermute | solution.py:33
  42.4 2.7 %collective-permute-done.7 = f32[64,128]{1,0:T(8,128)S(1)} collective-permute-done((f32[64,128]{1,0:T(8,128)S(1)}, f32[64,128]{1,0:T(8,128)S(1)}, u32[]{:S(2)}, u32[]{:S(2)}) %collective-permute-start.7) | collective-permute-done | bytes 32800 | tf_op jit(solution)/shard_map/ppermute | solution.py:33
  45.0 0.7 %add_bitcast_fusion = (f32[128,64]{0,1:T(8,128)}, f32[128,64]{0,1:T(8,128)}) fusion(f32[128]{0:T(128)S(1)} %get-tuple-element.31, f32[128]{0:T(128)S(1)} %copy-done.4, f32[128]{0:T(128)S(1)} %get-tuple-element.30, f32[64,128]{1,0:T(8,128)S(1)} %collective-permute-done.7, f32[1,64,128]{2,1,0:T(8,128)S(1)} %collective-permute-done.4, f32[2,64,128]{2,1,0:T(8,128)S(1)} %add.23), kind=kLoop, calls=%fused_computation.11 | loop fusion | flops 49152 | bytes 165376 | tf_op jit(solution)/shard_map/transpose | solution.py:294
  (7 shorter events, 0.1 us)
Async XLA Ops:
  2.2 5.0 %collective-permute-start = (f32[1,2,5,8,128]{4,3,2,0,1:T(8,128)S(1)}, f32[1,2,5,8,128]{4,3,2,0,1:T(8,128)S(1)}, u32[]{:S(2)}, u32[]{:S(2)}) collective-permute-start(f32[1,2,5,8,128]{4,3,2,0,1:T(8,128)S(1)} %bitcast.21), channel_id=1, source_target_pairs={{0,16},{8,24},{16,0},{24,8},{1,17},{9,25},{17,1},{25,9},{2,18},{10... | collective-permute-start | bytes 122888 | tf_op jit(solution)/shard_map/ppermute | solution.py:33
  7.2 1.2 %collective-permute-start.1 = (f32[2,5,8,128]{3,2,1,0:T(8,128)S(1)}, f32[2,5,8,128]{3,2,1,0:T(8,128)S(1)}, u32[]{:S(2)}, u32[]{:S(2)}) collective-permute-start(f32[2,5,8,128]{3,2,1,0:T(8,128)S(1)} %get-tuple-element.28), channel_id=1, source_target_pairs={{0,8},{8,0},{16,24},{24,16},{1,9},{9,1},{17,25},{25,17},{2,10},{10... | collective-permute-start | bytes 122888 | tf_op jit(solution)/shard_map/ppermute | solution.py:33
  10.0 15.6 %all-to-all-start = ((f32[8,4,16,128]{3,2,1,0:T(8,128)}), f32[8,4,16,128]{3,2,1,0:T(8,128)S(1)}, u32[]{:S(2)}, u32[]{:S(2)}) async-start(f32[8,4,16,128]{3,2,1,0:T(8,128)} %densify.1), calls=%async_computation | async-start | bytes 524288 | tf_op jit(solution)/shard_map/all_to_all | solution.py:231
  19.8 1.3 %copy-start = (f32[2,128,2048]{2,1,0:T(8,128)}, f32[2,128,2048]{2,1,0:T(8,128)S(1)}, u32[]{:S(2)}) copy-start(f32[2,128,2048]{2,1,0:T(8,128)S(1)} %get-tuple-element.23.kernel_ref) | copy-start | bytes 6291460
  21.1 1.3 %copy-start.2 = (f32[2,128,2048]{2,1,0:T(8,128)}, f32[2,128,2048]{2,1,0:T(8,128)S(1)}, u32[]{:S(2)}) copy-start(f32[2,128,2048]{2,1,0:T(8,128)S(1)} %get-tuple-element.20.kernel_ref) | copy-start | bytes 6291460
  25.5 7.5 %copy-start.1 = (f32[2,128,2048]{2,1,0:T(8,128)S(1)}, f32[2,128,2048]{2,1,0:T(8,128)}, u32[]{:S(2)}) copy-start(f32[2,128,2048]{2,1,0:T(8,128)} %copy-done) | copy-start | bytes 6291460
  25.5 1.5 %collective-permute-start.2 = (f32[8,4,16,128]{3,2,1,0:T(8,128)S(1)}, f32[8,4,16,128]{3,2,1,0:T(8,128)S(1)}, u32[]{:S(2)}, u32[]{:S(2)}) collective-permute-start(f32[8,4,16,128]{3,2,1,0:T(8,128)S(1)} %all-to-all-done.own_ref), channel_id=1, source_target_pairs={{0,8},{8,0},{16,24},{24,16},{1,9},{9,1},{17,25},{25,17},{2,10},{10... | collective-permute-start | bytes 786440 | tf_op jit(solution)/shard_map/ppermute | solution.py:33
  27.1 1.6 %copy-start.3 = (f32[2,128,2048]{2,1,0:T(8,128)S(1)}, f32[2,128,2048]{2,1,0:T(8,128)}, u32[]{:S(2)}) copy-start(f32[2,128,2048]{2,1,0:T(8,128)} %copy-done.2) | copy-start | bytes 6291460
  31.5 4.3 %collective-permute-start.5 = (f32[2,64,128]{2,1,0:T(8,128)S(1)}, f32[2,64,128]{2,1,0:T(8,128)S(1)}, u32[]{:S(2)}, u32[]{:S(2)}) collective-permute-start(f32[2,64,128]{2,1,0:T(8,128)S(1)} %get-tuple-element.25), channel_id=1, source_target_pairs={{0,1},{1,0},{2,3},{3,2},{4,5},{5,4},{6,7},{7,6},{8,9},{9,8},{10,11... | collective-permute-start | bytes 196616 | tf_op jit(solution)/shard_map/ppermute | solution.py:33
  33.8 4.5 %collective-permute-start.3 = (f32[2,64,128]{2,1,0:T(8,128)S(1)}, f32[2,64,128]{2,1,0:T(8,128)S(1)}, u32[]{:S(2)}, u32[]{:S(2)}) collective-permute-start(f32[2,64,128]{2,1,0:T(8,128)S(1)} %stress.4), channel_id=1, source_target_pairs={{0,1},{1,0},{2,3},{3,2},{4,5},{5,4},{6,7},{7,6},{8,9},{9,8},{10,11... | collective-permute-start | bytes 196616 | tf_op jit(solution)/shard_map/ppermute | solution.py:33
  35.3 6.3 %copy-start.4 = (f32[128]{0:T(128)S(1)}, f32[128]{0:T(128)}, u32[]{:S(2)}) copy-start(f32[128]{0:T(128)} %param.11) | copy-start | bytes 1540
  35.3 6.3 %copy-start.5 = (f32[128]{0:T(128)S(1)}, f32[128]{0:T(128)}, u32[]{:S(2)}) copy-start(f32[128]{0:T(128)} %param.12) | copy-start | bytes 1540
  35.3 6.3 %copy-start.6 = (f32[128]{0:T(128)S(1)}, f32[128]{0:T(128)}, u32[]{:S(2)}) copy-start(f32[128]{0:T(128)} %param.13) | copy-start | bytes 1540
  35.9 4.3 %collective-permute-start.6 = (f32[1,64,128]{2,1,0:T(8,128)S(1)}, f32[1,64,128]{2,1,0:T(8,128)S(1)}, u32[]{:S(2)}, u32[]{:S(2)}) collective-permute-start(f32[1,64,128]{2,1,0:T(8,128)S(1)} %slice.29), channel_id=1, source_target_pairs={{0,2},{1,3},{2,0},{3,1},{4,6},{5,7},{6,4},{7,5},{8,10},{9,11},{10,... | collective-permute-start | bytes 98312 | tf_op jit(solution)/shard_map/ppermute | solution.py:33
  38.4 4.0 %collective-permute-start.4 = (f32[1,64,128]{2,1,0:T(8,128)S(1)}, f32[1,64,128]{2,1,0:T(8,128)S(1)}, u32[]{:S(2)}, u32[]{:S(2)}) collective-permute-start(f32[1,64,128]{2,1,0:T(8,128)S(1)} %slice.27), channel_id=1, source_target_pairs={{0,2},{1,3},{2,0},{3,1},{4,6},{5,7},{6,4},{7,5},{8,10},{9,11},{10,... | collective-permute-start | bytes 98312 | tf_op jit(solution)/shard_map/ppermute | solution.py:33
  40.2 4.8 %collective-permute-start.7 = (f32[64,128]{1,0:T(8,128)S(1)}, f32[64,128]{1,0:T(8,128)S(1)}, u32[]{:S(2)}, u32[]{:S(2)}) collective-permute-start(f32[64,128]{1,0:T(8,128)S(1)} %fusion.3), channel_id=1, source_target_pairs={{0,4},{1,5},{2,6},{3,7},{4,0},{5,1},{6,2},{7,3},{8,12},{9,13},{10,... | collective-permute-start | bytes 98312 | tf_op jit(solution)/shard_map/ppermute | solution.py:33

commit v8 on v7

--- a/solution.py
+++ b/solution.py
@@ -83,7 +83,7 @@
             out_ref[h, half, i : i + 1, :] = ids[pl.ds(first + i, 1), :]
 
 
-def densify_body(entries, me_ref, own_ref, came_ref, out_hbm, out_ref, slips, sem):
+def densify_body(entries, me_ref, own_ref, came_ref, out_ref, slips):
     halves, half = own_ref.shape[0], own_ref.shape[1] - 1
     width, _, blocks_here, _ = out_ref.shape
     blocks = width * blocks_here
@@ -108,13 +108,11 @@
             slip = slip - piece.astype(jnp.float32)
             total = total + jnp.dot(onehot, piece, preferred_element_type=jnp.float32)
         out_ref[:, i] = total.reshape(width, blocks_here, BLOCK)
-    copy = pltpu.make_async_copy(out_ref, out_hbm, sem)
-    copy.start()
-    copy.wait()
-
-
-def fetch_body(targets, me_ref, kernel_hbm, *refs):
+
+
+def fetch_body(targets, me_ref, kernel_hbm, mark_ref, *refs):
     held_refs, held_sems = refs[:-1], refs[-1]
+    mark_ref[...] = jnp.zeros(mark_ref.shape, jnp.float32)
     held = [
         fetch(t, me_ref[1], kernel_hbm, ref, held_sems.at[j]) for j, (t, ref) in enumerate(zip(targets, held_refs))
     ]
@@ -155,17 +153,9 @@
         out_ref[j] = first[:events] + first[events:] + second
 
 
-def first_body(
-    targets, me_ref, own_ref, came_ref, kernel_ref, kernel_hbm, slip_ref, out_ref, *refs
-):
-    held_refs, dense, held_sems = refs[:-2], refs[-2], refs[-1]
-    held = [
-        fetch(t, me_ref[1], kernel_hbm, ref, held_sems.at[j]) for j, (t, ref) in enumerate(zip(targets, held_refs))
-    ]
+def first_body(me_ref, own_ref, came_ref, kernel_ref, mark_ref, slip_ref, out_ref, dense):
     assemble(me_ref[0], own_ref, came_ref, slip_ref, dense)
     stress(slip_ref, kernel_ref, out_ref)
-    for copies in held:
-        wait(copies)
 
 
 def halving_order(width):
@@ -216,53 +206,42 @@
 
     dense = pl.pallas_call(
         functools.partial(densify_body, entries),
-        out_shape=pltpu.HBM((width, half, blocks_here, BLOCK), jnp.float32),
+        out_shape=f32(width, half, blocks_here, BLOCK),
         in_specs=[SMEM_SPEC, VMEM_SPEC, VMEM_SPEC],
-        out_specs=HBM_SPEC,
-        scratch_shapes=[
-            pltpu.VMEM((width, half, blocks_here, BLOCK), jnp.float32),
-            pltpu.VMEM((half, height * entries, BLOCK), jnp.float32),
-            pltpu.SemaphoreType.DMA,
-        ],
+        out_specs=VMEM_SPEC,
+        scratch_shapes=[pltpu.VMEM((half, height * entries, BLOCK), jnp.float32)],
         compiler_params=params(8),
         name="densify",
     )(me, held[:, 0], came)
     dense, after = lax.optimization_barrier((dense, me))
     mine = lax.all_to_all(dense, "cols", 0, 0, tiled=True)
-    far_send_kernel, near_send_kernel, far_keep_kernel = pl.pallas_call(
-        functools.partial(fetch_body, (far_send, near_send, far_keep)),
-        out_shape=[held_shape] * 3,
+    mark, far_send_kernel, near_send_kernel, far_keep_kernel, near_keep_kernel = pl.pallas_call(
+        functools.partial(fetch_body, (far_send, near_send, far_keep, near_keep)),
+        out_shape=[f32(SUB, BLOCK)] + [held_shape] * 4,
         in_specs=[SMEM_SPEC, HBM_SPEC],
-        out_specs=[VMEM_SPEC] * 3,
-        scratch_shapes=[pltpu.SemaphoreType.DMA((3, quarter, PIECES))],
+        out_specs=[VMEM_SPEC] * 5,
+        scratch_shapes=[pltpu.SemaphoreType.DMA((4, quarter, PIECES))],
         compiler_params=params(4),
-        cost_estimate=pl.CostEstimate(
-            flops=0, bytes_accessed=6 * receivers * sources, transcendentals=0
-        ),
+        cost_estimate=pl.CostEstimate(flops=0, bytes_accessed=8 * receivers * sources, transcendentals=0),
         name="fetch",
     )(after, in_hbm(kernel))
-    mine, far_send_kernel, near_send_kernel, far_keep_kernel = lax.optimization_barrier(
-        (mine, far_send_kernel, near_send_kernel, far_keep_kernel)
-    )
+    mine, mark = lax.optimization_barrier((mine, mark))
 
     cost = pl.CostEstimate(
         flops=6 * quarter * share * sources * events,
         bytes_accessed=4 * quarter * share * sources,
         transcendentals=0,
     )
-    slips, far_sent, near_keep_kernel = pl.pallas_call(
-        functools.partial(first_body, (near_keep,)),
-        out_shape=[bf16(2 * events, sources), f32(quarter, events, share), held_shape],
-        in_specs=[SMEM_SPEC, VMEM_SPEC, VMEM_SPEC, VMEM_SPEC, HBM_SPEC],
-        out_specs=[VMEM_SPEC] * 3,
-        scratch_shapes=[
-            pltpu.VMEM((events, blocks_here, BLOCK), jnp.float32),
-            pltpu.SemaphoreType.DMA((1, quarter, PIECES)),
-        ],
+    slips, far_sent = pl.pallas_call(
+        first_body,
+        out_shape=[bf16(2 * events, sources), f32(quarter, events, share)],
+        in_specs=[SMEM_SPEC] + [VMEM_SPEC] * 4,
+        out_specs=[VMEM_SPEC] * 2,
+        scratch_shapes=[pltpu.VMEM((events, blocks_here, BLOCK), jnp.float32)],
         compiler_params=params(8),
         cost_estimate=cost,
         name="first_stress",
-    )(me, mine, send_xor(mine, "rows", 1), in_vmem(far_send_kernel), in_hbm(kernel))
+    )(me, mine, send_xor(mine, "rows", 1), in_vmem(far_send_kernel), mark)
 
     def later(held):
         return pl.pallas_call(

time: 46 us -> 44.5 us (0.967)
  waiting for transfers between devices: 13.1 us -> 10.7 us
  local copies, waits for them, and re-layouts: 4.25 us -> 5.58 us
  Pallas kernels: 11.7 us -> 11 us
    all_to_all x1, waiting for transfers between devices: 3.09 us -> 1.06 us  [per_device(): mine = lax.all_to_all(dense, 'cols', 0, 0, tiled=True)]
    pallas_call x2, Pallas kernels: 4.41 us -> 2.96 us  [the longest x1 1.52 us: per_device(): pl.pallas_call(functools.partial(densify_body, entries), out_shape=f32(wi...]
    unnamed x14 -> x18, local copies, waits for them, and re-layouts: 4.24 us -> 5.57 us
    pallas_call x1, Pallas kernels: 3.51 us -> 4.21 us  [per_device(): pl.pallas_call(functools.partial(fetch_body, (far_send, near_send, far_ke...]
  transfers between devices with their start and end apart: 9 -> 9, of which waited for: 8 -> 9; matrix products, arithmetic and copies ran while one was open for 0% -> 0% of each run, Pallas kernels for 13% -> 15%
where the time goes in v8:
time: 44.5 us; the launch traced here: 44.2 us
  starting transfers between devices  15.4 us (35%)
  Pallas kernels  11 us (25%)
  waiting for transfers between devices  10.7 us (24%)
  local copies, waits for them, and re-layouts  5.58 us (13%)
  other arithmetic  0.78 us (2%)
  between operations  0.75 us (2%)
    ppermute x8, waiting for transfers between devices, send_xor(): lax.ppermute(block, axis, [(r, r ^ k) for r in range(lax.axis_size(axis))])  9.65 us
    ppermute x8, starting transfers between devices, send_xor(): lax.ppermute(block, axis, [(r, r ^ k) for r in range(lax.axis_size(axis))])  9.13 us
    all_to_all x1, starting transfers between devices, per_device(): mine = lax.all_to_all(dense, 'cols', 0, 0, tiled=True)  6.31 us
    unnamed x18, local copies, waits for them, and re-layouts  5.57 us
    pallas_call x1, Pallas kernels, per_device(): pl.pallas_call(functools.partial(fetch_body, (far_send, near_send, far_ke...  4.21 us
    pallas_call x3, Pallas kernels, later(): pl.pallas_call(stress, out_shape=f32(quarter, events, share), in_specs=[V...  2.34 us
    pallas_call x1, Pallas kernels, per_device(): pl.pallas_call(functools.partial(densify_body, entries), out_shape=f32(wi...  1.52 us
    pallas_call x1, Pallas kernels, per_device(): pl.pallas_call(pack_body, out_shape=f32(2, half + 1, SUB, BLOCK), in_spec...  1.45 us
  transfers between devices with their start and end apart: 9, of which 9 were waited for; matrix products, arithmetic and copies ran while one was open for 0% of the time, Pallas kernels for 15%

profile of v8, /device:TPU:0, one launch (start us, length us, event | category | flops | bytes accessed | tf_op | source)
XLA Modules:
  0.0 44.2 jit_solution(17430942273017608059)
XLA Ops:
  0.6 0.1 pad_add_fusion.me_ref
  0.7 1.5 %pack.1 = f32[2,5,8,128]{3,2,1,0:T(8,128)S(1)} custom-call(s32[2]{0:T(128)S(1)} %pad_add_fusion.me_ref, f32[8,8,128]{2,1,0:T(8,128)} %slip_hbm.1, s32[8,8]{1,0:T(8,128)} %list_hbm.1, s32[8]{0:T(128)} %count_hbm.1), custom_call_target="tpu_custom_call" | custom-call | tf_op jit(solution)/shard_map/pack/pallas_call | solution.py:185
  2.2 3.0 %collective-permute-start = (f32[1,2,5,8,128]{4,3,2,0,1:T(8,128)S(1)}, f32[1,2,5,8,128]{4,3,2,0,1:T(8,128)S(1)}, u32[]{:S(2)}, u32[]{:S(2)}) collective-permute-start(f32[1,2,5,8,128]{4,3,2,0,1:T(8,128)S(1)} %bitcast.21), channel_id=1, source_target_pairs={{0,16},{8,24},{16,0},{24,8},{1,17},{9,25},{17,1},{25,9},{2,18},{10... | collective-permute-start | bytes 122888 | tf_op jit(solution)/shard_map/ppermute | solution.py:33
  5.2 2.0 %collective-permute-done = f32[1,2,5,8,128]{4,3,2,0,1:T(8,128)S(1)} collective-permute-done((f32[1,2,5,8,128]{4,3,2,0,1:T(8,128)S(1)}, f32[1,2,5,8,128]{4,3,2,0,1:T(8,128)S(1)}, u32[]{:S(2)}, u32[]{:S(2)}) %collective-permute-start) | collective-permute-done | bytes 40992 | tf_op jit(solution)/shard_map/ppermute | solution.py:33
  7.2 0.0 collective-permute-start.1
  7.2 1.2 %collective-permute-done.1.came_ref = f32[2,5,8,128]{3,2,1,0:T(8,128)S(1)} collective-permute-done((f32[2,5,8,128]{3,2,1,0:T(8,128)S(1)}, f32[2,5,8,128]{3,2,1,0:T(8,128)S(1)}, u32[]{:S(2)}, u32[]{:S(2)}) %collective-permute-start.1) | collective-permute-done | bytes 40992 | tf_op jit(solution)/shard_map/ppermute | solution.py:33
  8.4 1.5 %densify.1 = f32[8,4,16,128]{3,2,1,0:T(8,128)} custom-call(s32[2]{0:T(128)S(1)} %pad_add_fusion.me_ref, f32[2,5,8,128]{3,2,1,0:T(8,128)S(1)} %get-tuple-element.27.own_ref, f32[2,5,8,128]{3,2,1,0:T(8,128)S(1)} %collective-permute-done.1.came_ref), custom_call_target="tpu_custom_call" | custom-call | tf_op jit(solution)/shard_map/densify/pallas_call | solution.py:207
  9.9 6.3 %all-to-all-start = ((f32[8,4,16,128]{3,2,1,0:T(8,128)}), f32[8,4,16,128]{3,2,1,0:T(8,128)S(1)}, u32[]{:S(2)}, u32[]{:S(2)}) async-start(f32[8,4,16,128]{3,2,1,0:T(8,128)} %densify.1), calls=%async_computation | async-start | bytes 524288 | tf_op jit(solution)/shard_map/all_to_all | solution.py:217
  16.2 4.2 %fetch.1 = (f32[8,128]{1,0:T(8,128)S(1)}, f32[2,128,2048]{2,1,0:T(8,128)S(1)}, f32[2,128,2048]{2,1,0:T(8,128)S(1)}, f32[2,128,2048]{2,1,0:T(8,128)S(1)}, f32[2,128,2048]{2,1,0:T(8,128)S(1)}) custom-call(s32[2]{0:T(128)S(1)} %pad_add_fusion.me_ref, f32[1024,2048]{1,0:T(8,128)} %kernel_hbm.1), custom_call_target="tpu_custom_call" | custom-call | bytes 16777216 | tf_op jit(solution)/shard_map/fetch/pallas_call | solution.py:218
  20.5 0.0 copy-start
  20.5 1.3 %copy-done = f32[2,128,2048]{2,1,0:T(8,128)} copy-done((f32[2,128,2048]{2,1,0:T(8,128)}, f32[2,128,2048]{2,1,0:T(8,128)S(1)}, u32[]{:S(2)}) %copy-start) | copy-done | bytes 2097176
  21.8 0.0 copy-start.2
  21.8 1.3 %copy-done.2 = f32[2,128,2048]{2,1,0:T(8,128)} copy-done((f32[2,128,2048]{2,1,0:T(8,128)}, f32[2,128,2048]{2,1,0:T(8,128)S(1)}, u32[]{:S(2)}) %copy-start.2) | copy-done | bytes 2097176
  23.1 0.0 copy-start.4
  23.1 1.3 %copy-done.4 = f32[2,128,2048]{2,1,0:T(8,128)} copy-done((f32[2,128,2048]{2,1,0:T(8,128)}, f32[2,128,2048]{2,1,0:T(8,128)S(1)}, u32[]{:S(2)}) %copy-start.4) | copy-done | bytes 2097176
  24.4 1.1 %all-to-all-done.own_ref = f32[8,4,16,128]{3,2,1,0:T(8,128)S(1)} async-done(((f32[8,4,16,128]{3,2,1,0:T(8,128)}), f32[8,4,16,128]{3,2,1,0:T(8,128)S(1)}, u32[]{:S(2)}, u32[]{:S(2)}) %all-to-all-start) | async-done | bytes 262176 | tf_op jit(solution)/shard_map/all_to_all | solution.py:217
  25.5 0.0 copy-start.3
  25.5 0.0 collective-permute-start.2
  25.5 1.5 %collective-permute-done.2.came_ref = f32[8,4,16,128]{3,2,1,0:T(8,128)S(1)} collective-permute-done((f32[8,4,16,128]{3,2,1,0:T(8,128)S(1)}, f32[8,4,16,128]{3,2,1,0:T(8,128)S(1)}, u32[]{:S(2)}, u32[]{:S(2)}) %collective-permute-start.2) | collective-permute-done | bytes 262176 | tf_op jit(solution)/shard_map/ppermute | solution.py:33
  27.0 0.0 copy-start.5
  27.0 1.6 %copy-done.5 = f32[2,128,2048]{2,1,0:T(8,128)S(1)} copy-done((f32[2,128,2048]{2,1,0:T(8,128)S(1)}, f32[2,128,2048]{2,1,0:T(8,128)}, u32[]{:S(2)}) %copy-start.5) | copy-done | bytes 2097176
  28.6 0.0 copy-start.1
  28.6 1.4 %first_stress.1 = (bf16[128,2048]{1,0:T(8,128)(2,1)S(1)}, f32[2,64,128]{2,1,0:T(8,128)S(1)}) custom-call(s32[2]{0:T(128)S(1)} %pad_add_fusion.me_ref, f32[8,4,16,128]{3,2,1,0:T(8,128)S(1)} %all-to-all-done.own_ref, f32[8,4,16,128]{3,2,1,0:T(8,128)S(1)} %collective-permute-done.2.came_ref, f32[2,128,2048]{2,1,0:T(8,128)S(1)} %copy-done.5, ...), custom_call_target="tpu_custom_call" | custom-call | flops 201326592 | bytes 2097152 | tf_op jit(solution)/shard_map/first_stress/pallas_call | solution.py:235
  30.1 1.5 %collective-permute-start.5 = (f32[2,64,128]{2,1,0:T(8,128)S(1)}, f32[2,64,128]{2,1,0:T(8,128)S(1)}, u32[]{:S(2)}, u32[]{:S(2)}) collective-permute-start(f32[2,64,128]{2,1,0:T(8,128)S(1)} %get-tuple-element.23), channel_id=1, source_target_pairs={{0,1},{1,0},{2,3},{3,2},{4,5},{5,4},{6,7},{7,6},{8,9},{9,8},{10,11... | collective-permute-start | bytes 196616 | tf_op jit(solution)/shard_map/ppermute | solution.py:33
  31.5 0.0 copy-done.3
  31.5 0.8 %stress.4 = f32[2,64,128]{2,1,0:T(8,128)S(1)} custom-call(bf16[128,2048]{1,0:T(8,128)(2,1)S(1)} %get-tuple-element.19.slip_ref, f32[2,128,2048]{2,1,0:T(8,128)S(1)} %copy-done.3), custom_call_target="tpu_custom_call" | custom-call | flops 201326592 | bytes 2097152 | tf_op jit(solution)/shard_map/stress/pallas_call | solution.py:247
  32.3 0.7 %collective-permute-start.3 = (f32[2,64,128]{2,1,0:T(8,128)S(1)}, f32[2,64,128]{2,1,0:T(8,128)S(1)}, u32[]{:S(2)}, u32[]{:S(2)}) collective-permute-start(f32[2,64,128]{2,1,0:T(8,128)S(1)} %stress.4), channel_id=1, source_target_pairs={{0,1},{1,0},{2,3},{3,2},{4,5},{5,4},{6,7},{7,6},{8,9},{9,8},{10,11... | collective-permute-start | bytes 196616 | tf_op jit(solution)/shard_map/ppermute | solution.py:33
  33.0 0.0 copy-done.1
  33.0 0.8 %stress.5 = f32[2,64,128]{2,1,0:T(8,128)S(1)} custom-call(bf16[128,2048]{1,0:T(8,128)(2,1)S(1)} %get-tuple-element.19.slip_ref, f32[2,128,2048]{2,1,0:T(8,128)S(1)} %copy-done.1), custom_call_target="tpu_custom_call" | custom-call | flops 201326592 | bytes 2097152 | tf_op jit(solution)/shard_map/stress/pallas_call | solution.py:247
  33.8 0.0 copy-start.6
  33.8 0.0 copy-start.7
  33.8 0.0 copy-start.8
  33.8 0.6 %collective-permute-done.5 = f32[2,64,128]{2,1,0:T(8,128)S(1)} collective-permute-done((f32[2,64,128]{2,1,0:T(8,128)S(1)}, f32[2,64,128]{2,1,0:T(8,128)S(1)}, u32[]{:S(2)}, u32[]{:S(2)}) %collective-permute-start.5) | collective-permute-done | bytes 65568 | tf_op jit(solution)/shard_map/ppermute | solution.py:33
  34.4 1.1 %collective-permute-start.6 = (f32[1,64,128]{2,1,0:T(8,128)S(1)}, f32[1,64,128]{2,1,0:T(8,128)S(1)}, u32[]{:S(2)}, u32[]{:S(2)}) collective-permute-start(f32[1,64,128]{2,1,0:T(8,128)S(1)} %slice.29), channel_id=1, source_target_pairs={{0,2},{1,3},{2,0},{3,1},{4,6},{5,7},{6,4},{7,5},{8,10},{9,11},{10,... | collective-permute-start | bytes 98312 | tf_op jit(solution)/shard_map/ppermute | solution.py:33
  35.6 0.8 %stress.3 = f32[2,64,128]{2,1,0:T(8,128)S(1)} custom-call(bf16[128,2048]{1,0:T(8,128)(2,1)S(1)} %get-tuple-element.19.slip_ref, f32[2,128,2048]{2,1,0:T(8,128)S(1)} %get-tuple-element.20.kernel_ref), custom_call_target="tpu_custom_call" | custom-call | flops 201326592 | bytes 2097152 | tf_op jit(solution)/shard_map/stress/pallas_call | solution.py:247
  36.3 0.3 collective-permute-done.3
  36.7 1.1 %collective-permute-start.4 = (f32[1,64,128]{2,1,0:T(8,128)S(1)}, f32[1,64,128]{2,1,0:T(8,128)S(1)}, u32[]{:S(2)}, u32[]{:S(2)}) collective-permute-start(f32[1,64,128]{2,1,0:T(8,128)S(1)} %slice.27), channel_id=1, source_target_pairs={{0,2},{1,3},{2,0},{3,1},{4,6},{5,7},{6,4},{7,5},{8,10},{9,11},{10,... | collective-permute-start | bytes 98312 | tf_op jit(solution)/shard_map/ppermute | solution.py:33
  37.8 1.0 %collective-permute-done.6 = f32[1,64,128]{2,1,0:T(8,128)S(1)} collective-permute-done((f32[1,64,128]{2,1,0:T(8,128)S(1)}, f32[1,64,128]{2,1,0:T(8,128)S(1)}, u32[]{:S(2)}, u32[]{:S(2)}) %collective-permute-start.6) | collective-permute-done | bytes 32800 | tf_op jit(solution)/shard_map/ppermute | solution.py:33
  38.8 1.7 %collective-permute-start.7 = (f32[64,128]{1,0:T(8,128)S(1)}, f32[64,128]{1,0:T(8,128)S(1)}, u32[]{:S(2)}, u32[]{:S(2)}) collective-permute-start(f32[64,128]{1,0:T(8,128)S(1)} %fusion.3), channel_id=1, source_target_pairs={{0,4},{1,5},{2,6},{3,7},{4,0},{5,1},{6,2},{7,3},{8,12},{9,13},{10,... | collective-permute-start | bytes 98312 | tf_op jit(solution)/shard_map/ppermute | solution.py:33
  40.5 0.0 copy-done.6
  40.5 0.0 copy-done.7
  40.5 0.0 copy-done.8
  40.5 0.3 collective-permute-done.4
  40.8 2.8 %collective-permute-done.7 = f32[64,128]{1,0:T(8,128)S(1)} collective-permute-done((f32[64,128]{1,0:T(8,128)S(1)}, f32[64,128]{1,0:T(8,128)S(1)}, u32[]{:S(2)}, u32[]{:S(2)}) %collective-permute-start.7) | collective-permute-done | bytes 32800 | tf_op jit(solution)/shard_map/ppermute | solution.py:33
  43.6 0.7 %add_bitcast_fusion = (f32[128,64]{0,1:T(8,128)}, f32[128,64]{0,1:T(8,128)}) fusion(f32[128]{0:T(128)S(1)} %get-tuple-element.29, f32[128]{0:T(128)S(1)} %copy-done.6, f32[128]{0:T(128)S(1)} %get-tuple-element.28, f32[64,128]{1,0:T(8,128)S(1)} %collective-permute-done.7, f32[1,64,128]{2,1,0:T(8,128)S(1)} %collective-permute-done.4, f32[2,64,128]{2,1,0:T(8,128)S(1)} %add.23), kind=kLoop, calls=%fused_computation.11 | loop fusion | flops 49152 | bytes 165376 | tf_op jit(solution)/shard_map/transpose | solution.py:273
  (7 shorter events, 0.1 us)
Async XLA Ops:
  2.2 5.0 %collective-permute-start = (f32[1,2,5,8,128]{4,3,2,0,1:T(8,128)S(1)}, f32[1,2,5,8,128]{4,3,2,0,1:T(8,128)S(1)}, u32[]{:S(2)}, u32[]{:S(2)}) collective-permute-start(f32[1,2,5,8,128]{4,3,2,0,1:T(8,128)S(1)} %bitcast.21), channel_id=1, source_target_pairs={{0,16},{8,24},{16,0},{24,8},{1,17},{9,25},{17,1},{25,9},{2,18},{10... | collective-permute-start | bytes 122888 | tf_op jit(solution)/shard_map/ppermute | solution.py:33
  7.2 1.2 %collective-permute-start.1 = (f32[2,5,8,128]{3,2,1,0:T(8,128)S(1)}, f32[2,5,8,128]{3,2,1,0:T(8,128)S(1)}, u32[]{:S(2)}, u32[]{:S(2)}) collective-permute-start(f32[2,5,8,128]{3,2,1,0:T(8,128)S(1)} %get-tuple-element.26), channel_id=1, source_target_pairs={{0,8},{8,0},{16,24},{24,16},{1,9},{9,1},{17,25},{25,17},{2,10},{10... | collective-permute-start | bytes 122888 | tf_op jit(solution)/shard_map/ppermute | solution.py:33
  9.9 15.6 %all-to-all-start = ((f32[8,4,16,128]{3,2,1,0:T(8,128)}), f32[8,4,16,128]{3,2,1,0:T(8,128)S(1)}, u32[]{:S(2)}, u32[]{:S(2)}) async-start(f32[8,4,16,128]{3,2,1,0:T(8,128)} %densify.1), calls=%async_computation | async-start | bytes 524288 | tf_op jit(solution)/shard_map/all_to_all | solution.py:217
  20.5 1.3 %copy-start = (f32[2,128,2048]{2,1,0:T(8,128)}, f32[2,128,2048]{2,1,0:T(8,128)S(1)}, u32[]{:S(2)}) copy-start(f32[2,128,2048]{2,1,0:T(8,128)S(1)} %get-tuple-element.22.kernel_ref) | copy-start | bytes 6291460
  21.8 1.3 %copy-start.2 = (f32[2,128,2048]{2,1,0:T(8,128)}, f32[2,128,2048]{2,1,0:T(8,128)S(1)}, u32[]{:S(2)}) copy-start(f32[2,128,2048]{2,1,0:T(8,128)S(1)} %get-tuple-element.21.kernel_ref) | copy-start | bytes 6291460
  23.1 1.3 %copy-start.4 = (f32[2,128,2048]{2,1,0:T(8,128)}, f32[2,128,2048]{2,1,0:T(8,128)S(1)}, u32[]{:S(2)}) copy-start(f32[2,128,2048]{2,1,0:T(8,128)S(1)} %get-tuple-element.17.kernel_ref) | copy-start | bytes 6291460
  25.5 6.1 %copy-start.3 = (f32[2,128,2048]{2,1,0:T(8,128)S(1)}, f32[2,128,2048]{2,1,0:T(8,128)}, u32[]{:S(2)}) copy-start(f32[2,128,2048]{2,1,0:T(8,128)} %copy-done.2) | copy-start | bytes 6291460
  25.5 1.5 %collective-permute-start.2 = (f32[8,4,16,128]{3,2,1,0:T(8,128)S(1)}, f32[8,4,16,128]{3,2,1,0:T(8,128)S(1)}, u32[]{:S(2)}, u32[]{:S(2)}) collective-permute-start(f32[8,4,16,128]{3,2,1,0:T(8,128)S(1)} %all-to-all-done.own_ref), channel_id=1, source_target_pairs={{0,8},{8,0},{16,24},{24,16},{1,9},{9,1},{17,25},{25,17},{2,10},{10... | collective-permute-start | bytes 786440 | tf_op jit(solution)/shard_map/ppermute | solution.py:33
  27.0 1.6 %copy-start.5 = (f32[2,128,2048]{2,1,0:T(8,128)S(1)}, f32[2,128,2048]{2,1,0:T(8,128)}, u32[]{:S(2)}) copy-start(f32[2,128,2048]{2,1,0:T(8,128)} %copy-done.4) | copy-start | bytes 6291460
  28.6 4.4 %copy-start.1 = (f32[2,128,2048]{2,1,0:T(8,128)S(1)}, f32[2,128,2048]{2,1,0:T(8,128)}, u32[]{:S(2)}) copy-start(f32[2,128,2048]{2,1,0:T(8,128)} %copy-done) | copy-start | bytes 6291460
  30.1 4.3 %collective-permute-start.5 = (f32[2,64,128]{2,1,0:T(8,128)S(1)}, f32[2,64,128]{2,1,0:T(8,128)S(1)}, u32[]{:S(2)}, u32[]{:S(2)}) collective-permute-start(f32[2,64,128]{2,1,0:T(8,128)S(1)} %get-tuple-element.23), channel_id=1, source_target_pairs={{0,1},{1,0},{2,3},{3,2},{4,5},{5,4},{6,7},{7,6},{8,9},{9,8},{10,11... | collective-permute-start | bytes 196616 | tf_op jit(solution)/shard_map/ppermute | solution.py:33
  32.3 4.3 %collective-permute-start.3 = (f32[2,64,128]{2,1,0:T(8,128)S(1)}, f32[2,64,128]{2,1,0:T(8,128)S(1)}, u32[]{:S(2)}, u32[]{:S(2)}) collective-permute-start(f32[2,64,128]{2,1,0:T(8,128)S(1)} %stress.4), channel_id=1, source_target_pairs={{0,1},{1,0},{2,3},{3,2},{4,5},{5,4},{6,7},{7,6},{8,9},{9,8},{10,11... | collective-permute-start | bytes 196616 | tf_op jit(solution)/shard_map/ppermute | solution.py:33
  33.8 6.7 %copy-start.6 = (f32[128]{0:T(128)S(1)}, f32[128]{0:T(128)}, u32[]{:S(2)}) copy-start(f32[128]{0:T(128)} %param.11) | copy-start | bytes 1540
  33.8 6.7 %copy-start.7 = (f32[128]{0:T(128)S(1)}, f32[128]{0:T(128)}, u32[]{:S(2)}) copy-start(f32[128]{0:T(128)} %param.12) | copy-start | bytes 1540
  33.8 6.7 %copy-start.8 = (f32[128]{0:T(128)S(1)}, f32[128]{0:T(128)}, u32[]{:S(2)}) copy-start(f32[128]{0:T(128)} %param.13) | copy-start | bytes 1540
  34.4 4.3 %collective-permute-start.6 = (f32[1,64,128]{2,1,0:T(8,128)S(1)}, f32[1,64,128]{2,1,0:T(8,128)S(1)}, u32[]{:S(2)}, u32[]{:S(2)}) collective-permute-start(f32[1,64,128]{2,1,0:T(8,128)S(1)} %slice.29), channel_id=1, source_target_pairs={{0,2},{1,3},{2,0},{3,1},{4,6},{5,7},{6,4},{7,5},{8,10},{9,11},{10,... | collective-permute-start | bytes 98312 | tf_op jit(solution)/shard_map/ppermute | solution.py:33
  36.7 4.1 %collective-permute-start.4 = (f32[1,64,128]{2,1,0:T(8,128)S(1)}, f32[1,64,128]{2,1,0:T(8,128)S(1)}, u32[]{:S(2)}, u32[]{:S(2)}) collective-permute-start(f32[1,64,128]{2,1,0:T(8,128)S(1)} %slice.27), channel_id=1, source_target_pairs={{0,2},{1,3},{2,0},{3,1},{4,6},{5,7},{6,4},{7,5},{8,10},{9,11},{10,... | collective-permute-start | bytes 98312 | tf_op jit(solution)/shard_map/ppermute | solution.py:33
  38.8 4.8 %collective-permute-start.7 = (f32[64,128]{1,0:T(8,128)S(1)}, f32[64,128]{1,0:T(8,128)S(1)}, u32[]{:S(2)}, u32[]{:S(2)}) collective-permute-start(f32[64,128]{1,0:T(8,128)S(1)} %fusion.3), channel_id=1, source_target_pairs={{0,4},{1,5},{2,6},{3,7},{4,0},{5,1},{6,2},{7,3},{8,12},{9,13},{10,... | collective-permute-start | bytes 98312 | tf_op jit(solution)/shard_map/ppermute | solution.py:33

commit v9 on v8

--- a/solution.py
+++ b/solution.py
@@ -9,7 +9,6 @@
 
 BLOCK = 128
 SUB = 8
-PIECES = 4
 VMEM_SPEC = pl.BlockSpec(memory_space=pltpu.VMEM)
 SMEM_SPEC = pl.BlockSpec(memory_space=pltpu.SMEM)
 HBM_SPEC = pl.BlockSpec(memory_space=pltpu.HBM)
@@ -31,30 +30,6 @@
 
 def send_xor(block, axis, k):
     return lax.ppermute(block, axis, [(r, r ^ k) for r in range(lax.axis_size(axis))])
-
-
-def fetch(targets, col, kernel_hbm, out_ref, sems):
-    share = out_ref.shape[1]
-    rows = share // PIECES
-    copies = []
-    for j, k in enumerate(targets):
-        for p in range(PIECES):
-            start = pl.multiple_of((col ^ k) * share + p * rows, rows)
-            copies.append(
-                pltpu.make_async_copy(
-                    kernel_hbm.at[pl.ds(start, rows), :],
-                    out_ref.at[j, pl.ds(p * rows, rows), :],
-                    sems.at[j, p],
-                )
-            )
-    for n, copy in enumerate(copies):
-        copy.start(priority=n % 2)
-    return copies
-
-
-def wait(copies):
-    for copy in copies:
-        copy.wait()
 
 
 def pack_body(me_ref, slip_hbm, list_hbm, count_hbm, out_ref, slip_ref, list_ref, count_ref, ids, sems):
@@ -70,7 +45,8 @@
     entry = lax.broadcasted_iota(jnp.int32, (events, entries), 1) + row * entries
     event = lax.broadcasted_iota(jnp.int32, (events, entries), 0)
     ids[...] = jnp.full(ids.shape, -1.0, jnp.float32)
-    wait(copies)
+    for copy in copies:
+        copy.wait()
     count = jnp.zeros((events, entries), jnp.int32)
     for e in range(events):
         count = jnp.where(event == e, count_ref[e], count)
@@ -83,7 +59,7 @@
             out_ref[h, half, i : i + 1, :] = ids[pl.ds(first + i, 1), :]
 
 
-def densify_body(entries, me_ref, own_ref, came_ref, out_ref, slips):
+def densify_body(entries, me_ref, own_ref, came_ref, _, out_ref, slips):
     halves, half = own_ref.shape[0], own_ref.shape[1] - 1
     width, _, blocks_here, _ = out_ref.shape
     blocks = width * blocks_here
@@ -110,16 +86,6 @@
         out_ref[:, i] = total.reshape(width, blocks_here, BLOCK)
 
 
-def fetch_body(targets, me_ref, kernel_hbm, mark_ref, *refs):
-    held_refs, held_sems = refs[:-1], refs[-1]
-    mark_ref[...] = jnp.zeros(mark_ref.shape, jnp.float32)
-    held = [
-        fetch(t, me_ref[1], kernel_hbm, ref, held_sems.at[j]) for j, (t, ref) in enumerate(zip(targets, held_refs))
-    ]
-    for copies in held:
-        wait(copies)
-
-
 def assemble(row, own_ref, came_ref, out_ref, dense):
     width, half, blocks_here, _ = own_ref.shape
     events = dense.shape[0]
@@ -142,10 +108,11 @@
             out_ref[events + 2 * t * SUB : events + 2 * (t + 1) * SUB, where] = lo
 
 
-def stress(slip_ref, kernel_ref, out_ref):
+def stress(targets, col, slip_ref, kernel_ref, out_ref):
     events = slip_ref.shape[0] // 2
-    for j in range(out_ref.shape[0]):
-        block = kernel_ref[j]
+    share = out_ref.shape[2]
+    for j, k in enumerate(targets):
+        block = kernel_ref[pl.ds(pl.multiple_of((col ^ k) * share, share), share), :]
         hi = block.astype(jnp.bfloat16)
         lo = (block - hi.astype(jnp.float32)).astype(jnp.bfloat16)
         first = lax.dot_general(slip_ref[...], hi, NT, preferred_element_type=jnp.float32)
@@ -153,9 +120,13 @@
         out_ref[j] = first[:events] + first[events:] + second
 
 
-def first_body(me_ref, own_ref, came_ref, kernel_ref, mark_ref, slip_ref, out_ref, dense):
+def first_body(targets, me_ref, own_ref, came_ref, kernel_ref, slip_ref, out_ref, dense):
     assemble(me_ref[0], own_ref, came_ref, slip_ref, dense)
-    stress(slip_ref, kernel_ref, out_ref)
+    stress(targets, me_ref[1], slip_ref, kernel_ref, out_ref)
+
+
+def later_body(targets, me_ref, slip_ref, kernel_ref, out_ref):
+    stress(targets, me_ref[1], slip_ref, kernel_ref, out_ref)
 
 
 def halving_order(width):
@@ -178,10 +149,7 @@
     quarter = width // 4
     near_keep, far_keep = order[0 : 2 * quarter : 2], order[1 : 2 * quarter : 2]
     near_send, far_send = order[2 * quarter :: 2], order[2 * quarter + 1 :: 2]
-    held_shape = pltpu.VMEM((quarter, share, sources), jnp.float32)
-    in_hbm, in_vmem = (
-        functools.partial(pltpu.with_memory_space_constraint, memory_space=m) for m in (pltpu.HBM, pltpu.VMEM)
-    )
+    in_hbm = functools.partial(pltpu.with_memory_space_constraint, memory_space=pltpu.HBM)
     packed = pl.pallas_call(
         pack_body,
         out_shape=f32(2, half + 1, SUB, BLOCK),
@@ -207,25 +175,13 @@
     dense = pl.pallas_call(
         functools.partial(densify_body, entries),
         out_shape=f32(width, half, blocks_here, BLOCK),
-        in_specs=[SMEM_SPEC, VMEM_SPEC, VMEM_SPEC],
+        in_specs=[SMEM_SPEC, VMEM_SPEC, VMEM_SPEC, HBM_SPEC],
         out_specs=VMEM_SPEC,
         scratch_shapes=[pltpu.VMEM((half, height * entries, BLOCK), jnp.float32)],
         compiler_params=params(8),
         name="densify",
-    )(me, held[:, 0], came)
-    dense, after = lax.optimization_barrier((dense, me))
+    )(me, held[:, 0], came, in_hbm(kernel))
     mine = lax.all_to_all(dense, "cols", 0, 0, tiled=True)
-    mark, far_send_kernel, near_send_kernel, far_keep_kernel, near_keep_kernel = pl.pallas_call(
-        functools.partial(fetch_body, (far_send, near_send, far_keep, near_keep)),
-        out_shape=[f32(SUB, BLOCK)] + [held_shape] * 4,
-        in_specs=[SMEM_SPEC, HBM_SPEC],
-        out_specs=[VMEM_SPEC] * 5,
-        scratch_shapes=[pltpu.SemaphoreType.DMA((4, quarter, PIECES))],
-        compiler_params=params(4),
-        cost_estimate=pl.CostEstimate(flops=0, bytes_accessed=8 * receivers * sources, transcendentals=0),
-        name="fetch",
-    )(after, in_hbm(kernel))
-    mine, mark = lax.optimization_barrier((mine, mark))
 
     cost = pl.CostEstimate(
         flops=6 * quarter * share * sources * events,
@@ -233,31 +189,31 @@
         transcendentals=0,
     )
     slips, far_sent = pl.pallas_call(
-        first_body,
+        functools.partial(first_body, far_send),
         out_shape=[bf16(2 * events, sources), f32(quarter, events, share)],
-        in_specs=[SMEM_SPEC] + [VMEM_SPEC] * 4,
+        in_specs=[SMEM_SPEC] + [VMEM_SPEC] * 3,
         out_specs=[VMEM_SPEC] * 2,
         scratch_shapes=[pltpu.VMEM((events, blocks_here, BLOCK), jnp.float32)],
         compiler_params=params(8),
         cost_estimate=cost,
         name="first_stress",
-    )(me, mine, send_xor(mine, "rows", 1), in_vmem(far_send_kernel), mark)
-
-    def later(held):
+    )(me, mine, send_xor(mine, "rows", 1), kernel)
+
+    def later(targets):
         return pl.pallas_call(
-            stress,
+            functools.partial(later_body, targets),
             out_shape=f32(quarter, events, share),
-            in_specs=[VMEM_SPEC, VMEM_SPEC],
+            in_specs=[SMEM_SPEC, VMEM_SPEC, VMEM_SPEC],
             out_specs=VMEM_SPEC,
             compiler_params=params(8),
             cost_estimate=cost,
             name="stress",
-        )(slips, in_vmem(held))
+        )(me, slips, kernel)
 
     far_came = send_xor(far_sent, "cols", 1)
-    near_came = send_xor(later(near_send_kernel), "cols", 1)
-    far = later(far_keep_kernel) + far_came
-    near = later(near_keep_kernel) + near_came
+    near_came = send_xor(later(near_send), "cols", 1)
+    far = later(far_keep) + far_came
+    near = later(near_keep) + near_came
     step = 2
     while step < width // 2:
         keep = far.shape[0] // 2

time: 44.5 us -> 42.4 us (0.953)
  blocking collectives: 0 us -> 15.4 us
  starting transfers between devices: 15.4 us -> 8.41 us
  local copies, waits for them, and re-layouts: 5.58 us -> 0.03 us
  Pallas kernels: 11 us -> 7.93 us
  waiting for transfers between devices: 10.7 us -> 8.91 us
    all_to_all x0 -> x1, blocking collectives: none -> 15.4 us  [per_device(): mine = lax.all_to_all(dense, 'cols', 0, 0, tiled=True)]
    all_to_all x1 -> x0, starting transfers between devices: 6.31 us -> none  [per_device(): mine = lax.all_to_all(dense, 'cols', 0, 0, tiled=True)]
    unnamed x18 -> x8, local copies, waits for them, and re-layouts: 5.57 us -> 0.03 us
    pallas_call x5 -> x4, Pallas kernels: 8 us -> 5.45 us  [the longest x3 3.95 us: later(): pl.pallas_call(functools.partial(later_body, targets), out_shape=f32(quar...]
    all_to_all x1 -> x0, waiting for transfers between devices: 1.06 us -> none  [per_device(): mine = lax.all_to_all(dense, 'cols', 0, 0, tiled=True)]
    ppermute x8, waiting for transfers between devices: 9.65 us -> 8.91 us  [send_xor(): lax.ppermute(block, axis, [(r, r ^ k) for r in range(lax.axis_size(axis))])]
    pallas_call x1, Pallas kernels: 1.52 us -> 0.8 us  [per_device(): pl.pallas_call(functools.partial(densify_body, entries), out_shape=f32(wi...]
    ppermute x8, starting transfers between devices: 9.13 us -> 8.41 us  [send_xor(): lax.ppermute(block, axis, [(r, r ^ k) for r in range(lax.axis_size(axis))])]
  transfers between devices with their start and end apart: 9 -> 8, of which waited for: 9 -> 6; matrix products, arithmetic and copies ran while one was open for 0% -> 0% of each run, Pallas kernels for 15% -> 9%
where the time goes in v9:
time: 42.4 us; the launch traced here: 42.2 us
  blocking collectives  15.4 us (36%)
  waiting for transfers between devices  8.91 us (21%)
  starting transfers between devices  8.41 us (20%)
  Pallas kernels  7.93 us (19%)
  other arithmetic  0.78 us (2%)
  between operations  0.78 us (2%)
    all_to_all x1, blocking collectives, per_device(): mine = lax.all_to_all(dense, 'cols', 0, 0, tiled=True)  15.4 us
    ppermute x8, waiting for transfers between devices, send_xor(): lax.ppermute(block, axis, [(r, r ^ k) for r in range(lax.axis_size(axis))])  8.91 us
    ppermute x8, starting transfers between devices, send_xor(): lax.ppermute(block, axis, [(r, r ^ k) for r in range(lax.axis_size(axis))])  8.41 us
    pallas_call x3, Pallas kernels, later(): pl.pallas_call(functools.partial(later_body, targets), out_shape=f32(quar...  3.95 us
    pallas_call x1, Pallas kernels, per_device(): pl.pallas_call(pack_body, out_shape=f32(2, half + 1, SUB, BLOCK), in_spec...  1.68 us
    pallas_call x1, Pallas kernels, per_device(): pl.pallas_call(functools.partial(first_body, far_send), out_shape=[bf16(2...  1.5 us
  transfers between devices with their start and end apart: 8, of which 6 were waited for; matrix products, arithmetic and copies ran while one was open for 0% of the time, Pallas kernels for 9%

profile of v9, /device:TPU:0, one launch (start us, length us, event | category | flops | bytes accessed | tf_op | source)
XLA Modules:
  0.0 42.2 jit_solution(9196402129487811897)
XLA Ops:
  0.6 0.0 copy-start
  0.6 0.1 pad_add_fusion.me_ref
  0.7 1.7 %pack.1 = f32[2,5,8,128]{3,2,1,0:T(8,128)S(1)} custom-call(s32[2]{0:T(128)S(1)} %pad_add_fusion.me_ref, f32[8,8,128]{2,1,0:T(8,128)} %slip_hbm.1, s32[8,8]{1,0:T(8,128)} %list_hbm.1, s32[8]{0:T(128)} %count_hbm.1), custom_call_target="tpu_custom_call" | custom-call | tf_op jit(solution)/shard_map/pack/pallas_call | solution.py:153
  2.4 3.0 %collective-permute-start = (f32[1,2,5,8,128]{4,3,2,0,1:T(8,128)S(1)}, f32[1,2,5,8,128]{4,3,2,0,1:T(8,128)S(1)}, u32[]{:S(2)}, u32[]{:S(2)}) collective-permute-start(f32[1,2,5,8,128]{4,3,2,0,1:T(8,128)S(1)} %bitcast.21), channel_id=1, source_target_pairs={{0,16},{8,24},{16,0},{24,8},{1,17},{9,25},{17,1},{25,9},{2,18},{10... | collective-permute-start | bytes 122888 | tf_op jit(solution)/shard_map/ppermute | solution.py:32
  5.4 2.0 %collective-permute-done = f32[1,2,5,8,128]{4,3,2,0,1:T(8,128)S(1)} collective-permute-done((f32[1,2,5,8,128]{4,3,2,0,1:T(8,128)S(1)}, f32[1,2,5,8,128]{4,3,2,0,1:T(8,128)S(1)}, u32[]{:S(2)}, u32[]{:S(2)}) %collective-permute-start) | collective-permute-done | bytes 40992 | tf_op jit(solution)/shard_map/ppermute | solution.py:32
  7.4 0.0 collective-permute-start.1
  7.4 1.2 %collective-permute-done.1.came_ref = f32[2,5,8,128]{3,2,1,0:T(8,128)S(1)} collective-permute-done((f32[2,5,8,128]{3,2,1,0:T(8,128)S(1)}, f32[2,5,8,128]{3,2,1,0:T(8,128)S(1)}, u32[]{:S(2)}, u32[]{:S(2)}) %collective-permute-start.1) | collective-permute-done | bytes 40992 | tf_op jit(solution)/shard_map/ppermute | solution.py:32
  8.7 0.8 %densify.1 = f32[8,4,16,128]{3,2,1,0:T(8,128)S(1)} custom-call(s32[2]{0:T(128)S(1)} %pad_add_fusion.me_ref, f32[2,5,8,128]{3,2,1,0:T(8,128)S(1)} %get-tuple-element.9.own_ref, f32[2,5,8,128]{3,2,1,0:T(8,128)S(1)} %collective-permute-done.1.came_ref, f32[1024,2048]{1,0:T(8,128)} %kernel_ref.7), custom_call_target="tpu_custom_call" | custom-call | tf_op jit(solution)/shard_map/densify/pallas_call | solution.py:175
  9.5 15.4 %all_to_all.5.own_ref = f32[8,4,16,128]{3,2,1,0:T(8,128)S(1)} all-to-all(f32[8,4,16,128]{3,2,1,0:T(8,128)S(1)} %densify.1), channel_id=1, replica_groups=mesh['rows'=4,'cols'=8] {'cols'}, dimensions={0} | all-to-all | bytes 524288 | tf_op jit(solution)/shard_map/all_to_all | solution.py:184
  24.8 0.0 collective-permute-start.2
  24.8 1.5 %collective-permute-done.2.came_ref = f32[8,4,16,128]{3,2,1,0:T(8,128)S(1)} collective-permute-done((f32[8,4,16,128]{3,2,1,0:T(8,128)S(1)}, f32[8,4,16,128]{3,2,1,0:T(8,128)S(1)}, u32[]{:S(2)}, u32[]{:S(2)}) %collective-permute-start.2) | collective-permute-done | bytes 262176 | tf_op jit(solution)/shard_map/ppermute | solution.py:32
  26.4 0.0 copy-done
  26.4 1.5 %first_stress.1 = (bf16[128,2048]{1,0:T(8,128)(2,1)S(1)}, f32[2,64,128]{2,1,0:T(8,128)S(1)}) custom-call(s32[2]{0:T(128)S(1)} %pad_add_fusion.me_ref, f32[8,4,16,128]{3,2,1,0:T(8,128)S(1)} %all_to_all.5.own_ref, f32[8,4,16,128]{3,2,1,0:T(8,128)S(1)} %collective-permute-done.2.came_ref, f32[1024,2048]{1,0:T(8,128)S(1)} %copy-done), custom_call_target="tpu_custom_call" | custom-call | flops 201326592 | bytes 2097152 | tf_op jit(solution)/shard_map/first_stress/pallas_call | solution.py:191
  27.9 1.5 %collective-permute-start.5 = (f32[2,64,128]{2,1,0:T(8,128)S(1)}, f32[2,64,128]{2,1,0:T(8,128)S(1)}, u32[]{:S(2)}, u32[]{:S(2)}) collective-permute-start(f32[2,64,128]{2,1,0:T(8,128)S(1)} %get-tuple-element.5), channel_id=1, source_target_pairs={{0,1},{1,0},{2,3},{3,2},{4,5},{5,4},{6,7},{7,6},{8,9},{9,8},{10,11... | collective-permute-start | bytes 196616 | tf_op jit(solution)/shard_map/ppermute | solution.py:32
  29.3 1.3 %stress.4 = f32[2,64,128]{2,1,0:T(8,128)S(1)} custom-call(s32[2]{0:T(128)S(1)} %pad_add_fusion.me_ref, bf16[128,2048]{1,0:T(8,128)(2,1)S(1)} %get-tuple-element.4.slip_ref, f32[1024,2048]{1,0:T(8,128)S(1)} %copy-done), custom_call_target="tpu_custom_call" | custom-call | flops 201326592 | bytes 2097152 | tf_op jit(solution)/shard_map/stress/pallas_call | solution.py:203
  30.7 0.0 copy-start.1
  30.7 0.0 copy-start.2
  30.7 0.0 copy-start.3
  30.7 0.7 %collective-permute-start.3 = (f32[2,64,128]{2,1,0:T(8,128)S(1)}, f32[2,64,128]{2,1,0:T(8,128)S(1)}, u32[]{:S(2)}, u32[]{:S(2)}) collective-permute-start(f32[2,64,128]{2,1,0:T(8,128)S(1)} %stress.4), channel_id=1, source_target_pairs={{0,1},{1,0},{2,3},{3,2},{4,5},{5,4},{6,7},{7,6},{8,9},{9,8},{10,11... | collective-permute-start | bytes 196616 | tf_op jit(solution)/shard_map/ppermute | solution.py:32
  31.4 1.3 %stress.5 = f32[2,64,128]{2,1,0:T(8,128)S(1)} custom-call(s32[2]{0:T(128)S(1)} %pad_add_fusion.me_ref, bf16[128,2048]{1,0:T(8,128)(2,1)S(1)} %get-tuple-element.4.slip_ref, f32[1024,2048]{1,0:T(8,128)S(1)} %copy-done), custom_call_target="tpu_custom_call" | custom-call | flops 201326592 | bytes 2097152 | tf_op jit(solution)/shard_map/stress/pallas_call | solution.py:203
  32.7 0.0 collective-permute-done.5
  32.7 1.1 %collective-permute-start.6 = (f32[1,64,128]{2,1,0:T(8,128)S(1)}, f32[1,64,128]{2,1,0:T(8,128)S(1)}, u32[]{:S(2)}, u32[]{:S(2)}) collective-permute-start(f32[1,64,128]{2,1,0:T(8,128)S(1)} %slice.29), channel_id=1, source_target_pairs={{0,2},{1,3},{2,0},{3,1},{4,6},{5,7},{6,4},{7,5},{8,10},{9,11},{10,... | collective-permute-start | bytes 98312 | tf_op jit(solution)/shard_map/ppermute | solution.py:32
  33.9 1.3 %stress.3 = f32[2,64,128]{2,1,0:T(8,128)S(1)} custom-call(s32[2]{0:T(128)S(1)} %pad_add_fusion.me_ref, bf16[128,2048]{1,0:T(8,128)(2,1)S(1)} %get-tuple-element.4.slip_ref, f32[1024,2048]{1,0:T(8,128)S(1)} %copy-done), custom_call_target="tpu_custom_call" | custom-call | flops 201326592 | bytes 2097152 | tf_op jit(solution)/shard_map/stress/pallas_call | solution.py:203
  35.2 0.0 collective-permute-done.3
  35.2 1.0 %collective-permute-start.4 = (f32[1,64,128]{2,1,0:T(8,128)S(1)}, f32[1,64,128]{2,1,0:T(8,128)S(1)}, u32[]{:S(2)}, u32[]{:S(2)}) collective-permute-start(f32[1,64,128]{2,1,0:T(8,128)S(1)} %slice.27), channel_id=1, source_target_pairs={{0,2},{1,3},{2,0},{3,1},{4,6},{5,7},{6,4},{7,5},{8,10},{9,11},{10,... | collective-permute-start | bytes 98312 | tf_op jit(solution)/shard_map/ppermute | solution.py:32
  36.3 0.5 %collective-permute-done.6 = f32[1,64,128]{2,1,0:T(8,128)S(1)} collective-permute-done((f32[1,64,128]{2,1,0:T(8,128)S(1)}, f32[1,64,128]{2,1,0:T(8,128)S(1)}, u32[]{:S(2)}, u32[]{:S(2)}) %collective-permute-start.6) | collective-permute-done | bytes 32800 | tf_op jit(solution)/shard_map/ppermute | solution.py:32
  36.7 1.1 %collective-permute-start.7 = (f32[64,128]{1,0:T(8,128)S(1)}, f32[64,128]{1,0:T(8,128)S(1)}, u32[]{:S(2)}, u32[]{:S(2)}) collective-permute-start(f32[64,128]{1,0:T(8,128)S(1)} %fusion.3), channel_id=1, source_target_pairs={{0,4},{1,5},{2,6},{3,7},{4,0},{5,1},{6,2},{7,3},{8,12},{9,13},{10,... | collective-permute-start | bytes 98312 | tf_op jit(solution)/shard_map/ppermute | solution.py:32
  37.8 0.0 copy-done.1
  37.8 0.0 copy-done.2
  37.8 0.0 copy-done.3
  37.8 1.7 %collective-permute-done.4 = f32[1,64,128]{2,1,0:T(8,128)S(1)} collective-permute-done((f32[1,64,128]{2,1,0:T(8,128)S(1)}, f32[1,64,128]{2,1,0:T(8,128)S(1)}, u32[]{:S(2)}, u32[]{:S(2)}) %collective-permute-start.4) | collective-permute-done | bytes 32800 | tf_op jit(solution)/shard_map/ppermute | solution.py:32
  39.6 2.0 %collective-permute-done.7 = f32[64,128]{1,0:T(8,128)S(1)} collective-permute-done((f32[64,128]{1,0:T(8,128)S(1)}, f32[64,128]{1,0:T(8,128)S(1)}, u32[]{:S(2)}, u32[]{:S(2)}) %collective-permute-start.7) | collective-permute-done | bytes 32800 | tf_op jit(solution)/shard_map/ppermute | solution.py:32
  41.5 0.7 %add_bitcast_fusion = (f32[128,64]{0,1:T(8,128)}, f32[128,64]{0,1:T(8,128)}) fusion(f32[128]{0:T(128)S(1)} %get-tuple-element.11, f32[128]{0:T(128)S(1)} %copy-done.1, f32[128]{0:T(128)S(1)} %get-tuple-element.10, f32[64,128]{1,0:T(8,128)S(1)} %collective-permute-done.7, f32[1,64,128]{2,1,0:T(8,128)S(1)} %collective-permute-done.4, f32[2,64,128]{2,1,0:T(8,128)S(1)} %add.23), kind=kLoop, calls=%fused_computation.11 | loop fusion | flops 49152 | bytes 165376 | tf_op jit(solution)/shard_map/transpose | solution.py:229
  (7 shorter events, 0.1 us)
Async XLA Ops:
  0.6 25.7 %copy-start = (f32[1024,2048]{1,0:T(8,128)S(1)}, f32[1024,2048]{1,0:T(8,128)}, u32[]{:S(2)}) copy-start(f32[1024,2048]{1,0:T(8,128)} %kernel_ref.7) | copy-start | bytes 25165828
  2.4 5.0 %collective-permute-start = (f32[1,2,5,8,128]{4,3,2,0,1:T(8,128)S(1)}, f32[1,2,5,8,128]{4,3,2,0,1:T(8,128)S(1)}, u32[]{:S(2)}, u32[]{:S(2)}) collective-permute-start(f32[1,2,5,8,128]{4,3,2,0,1:T(8,128)S(1)} %bitcast.21), channel_id=1, source_target_pairs={{0,16},{8,24},{16,0},{24,8},{1,17},{9,25},{17,1},{25,9},{2,18},{10... | collective-permute-start | bytes 122888 | tf_op jit(solution)/shard_map/ppermute | solution.py:32
  7.4 1.2 %collective-permute-start.1 = (f32[2,5,8,128]{3,2,1,0:T(8,128)S(1)}, f32[2,5,8,128]{3,2,1,0:T(8,128)S(1)}, u32[]{:S(2)}, u32[]{:S(2)}) collective-permute-start(f32[2,5,8,128]{3,2,1,0:T(8,128)S(1)} %get-tuple-element.8), channel_id=1, source_target_pairs={{0,8},{8,0},{16,24},{24,16},{1,9},{9,1},{17,25},{25,17},{2,10},{10... | collective-permute-start | bytes 122888 | tf_op jit(solution)/shard_map/ppermute | solution.py:32
  24.8 1.5 %collective-permute-start.2 = (f32[8,4,16,128]{3,2,1,0:T(8,128)S(1)}, f32[8,4,16,128]{3,2,1,0:T(8,128)S(1)}, u32[]{:S(2)}, u32[]{:S(2)}) collective-permute-start(f32[8,4,16,128]{3,2,1,0:T(8,128)S(1)} %all_to_all.5.own_ref), channel_id=1, source_target_pairs={{0,8},{8,0},{16,24},{24,16},{1,9},{9,1},{17,25},{25,17},{2,10},{10... | collective-permute-start | bytes 786440 | tf_op jit(solution)/shard_map/ppermute | solution.py:32
  27.9 4.8 %collective-permute-start.5 = (f32[2,64,128]{2,1,0:T(8,128)S(1)}, f32[2,64,128]{2,1,0:T(8,128)S(1)}, u32[]{:S(2)}, u32[]{:S(2)}) collective-permute-start(f32[2,64,128]{2,1,0:T(8,128)S(1)} %get-tuple-element.5), channel_id=1, source_target_pairs={{0,1},{1,0},{2,3},{3,2},{4,5},{5,4},{6,7},{7,6},{8,9},{9,8},{10,11... | collective-permute-start | bytes 196616 | tf_op jit(solution)/shard_map/ppermute | solution.py:32
  30.7 7.1 %copy-start.1 = (f32[128]{0:T(128)S(1)}, f32[128]{0:T(128)}, u32[]{:S(2)}) copy-start(f32[128]{0:T(128)} %param.11) | copy-start | bytes 1540
  30.7 7.1 %copy-start.2 = (f32[128]{0:T(128)S(1)}, f32[128]{0:T(128)}, u32[]{:S(2)}) copy-start(f32[128]{0:T(128)} %param.12) | copy-start | bytes 1540
  30.7 7.1 %copy-start.3 = (f32[128]{0:T(128)S(1)}, f32[128]{0:T(128)}, u32[]{:S(2)}) copy-start(f32[128]{0:T(128)} %param.13) | copy-start | bytes 1540
  30.7 4.5 %collective-permute-start.3 = (f32[2,64,128]{2,1,0:T(8,128)S(1)}, f32[2,64,128]{2,1,0:T(8,128)S(1)}, u32[]{:S(2)}, u32[]{:S(2)}) collective-permute-start(f32[2,64,128]{2,1,0:T(8,128)S(1)} %stress.4), channel_id=1, source_target_pairs={{0,1},{1,0},{2,3},{3,2},{4,5},{5,4},{6,7},{7,6},{8,9},{9,8},{10,11... | collective-permute-start | bytes 196616 | tf_op jit(solution)/shard_map/ppermute | solution.py:32
  32.7 4.0 %collective-permute-start.6 = (f32[1,64,128]{2,1,0:T(8,128)S(1)}, f32[1,64,128]{2,1,0:T(8,128)S(1)}, u32[]{:S(2)}, u32[]{:S(2)}) collective-permute-start(f32[1,64,128]{2,1,0:T(8,128)S(1)} %slice.29), channel_id=1, source_target_pairs={{0,2},{1,3},{2,0},{3,1},{4,6},{5,7},{6,4},{7,5},{8,10},{9,11},{10,... | collective-permute-start | bytes 98312 | tf_op jit(solution)/shard_map/ppermute | solution.py:32
  35.2 4.3 %collective-permute-start.4 = (f32[1,64,128]{2,1,0:T(8,128)S(1)}, f32[1,64,128]{2,1,0:T(8,128)S(1)}, u32[]{:S(2)}, u32[]{:S(2)}) collective-permute-start(f32[1,64,128]{2,1,0:T(8,128)S(1)} %slice.27), channel_id=1, source_target_pairs={{0,2},{1,3},{2,0},{3,1},{4,6},{5,7},{6,4},{7,5},{8,10},{9,11},{10,... | collective-permute-start | bytes 98312 | tf_op jit(solution)/shard_map/ppermute | solution.py:32
  36.7 4.8 %collective-permute-start.7 = (f32[64,128]{1,0:T(8,128)S(1)}, f32[64,128]{1,0:T(8,128)S(1)}, u32[]{:S(2)}, u32[]{:S(2)}) collective-permute-start(f32[64,128]{1,0:T(8,128)S(1)} %fusion.3), channel_id=1, source_target_pairs={{0,4},{1,5},{2,6},{3,7},{4,0},{5,1},{6,2},{7,3},{8,12},{9,13},{10,... | collective-permute-start | bytes 98312 | tf_op jit(solution)/shard_map/ppermute | solution.py:32

commit v10 on v9

v10 whole, which is shorter than its diff:
```python
import functools

import jax
import jax.numpy as jnp
from jax import lax
from jax.experimental import pallas as pl
from jax.experimental.pallas import tpu as pltpu
from jax.sharding import PartitionSpec as P

BLOCK = 128
SUB = 8
VMEM_SPEC = pl.BlockSpec(memory_space=pltpu.VMEM)
SMEM_SPEC = pl.BlockSpec(memory_space=pltpu.SMEM)
HBM_SPEC = pl.BlockSpec(memory_space=pltpu.HBM)
MIB = 1024 * 1024
NT = (((1,), (1,)), ((), ()))


def f32(*shape):
    return jax.ShapeDtypeStruct(shape, jnp.float32)


def bf16(*shape):
    return jax.ShapeDtypeStruct(shape, jnp.bfloat16)


def params(mib):
    return pltpu.CompilerParams(vmem_limit_bytes=mib * MIB)


def send_xor(block, axis, k):
    return lax.ppermute(block, axis, [(r, r ^ k) for r in range(lax.axis_size(axis))])


def pack_body(me_ref, slip_hbm, list_hbm, count_hbm, out_ref, slip_ref, list_ref, count_ref, ids, sems):
    copies = [
        pltpu.make_async_copy(src, dst, sems.at[j])
        for j, (src, dst) in enumerate(((list_hbm, list_ref), (count_hbm, count_ref), (slip_hbm, slip_ref)))
    ]
    for copy in copies:
        copy.start()
    events, entries = list_ref.shape
    row = me_ref[0]
    entry = lax.broadcasted_iota(jnp.int32, (events, entries), 1) + row * entries
    event = lax.broadcasted_iota(jnp.int32, (events, entries), 0)
    ids[...] = jnp.full(ids.shape, -1.0, jnp.float32)
    for copy in copies:
        copy.wait()
    count = jnp.zeros((events, entries), jnp.int32)
    for e in range(events):
        count = jnp.where(event == e, count_ref[e], count)
    ids[0:events, 0:entries] = jnp.where(entry < count, list_ref[...], -1).astype(jnp.float32)
    out_ref[events] = pltpu.roll(ids[...], row * entries, 1)
    for e in range(events):
        out_ref[e, 0:entries, :] = slip_ref[e]


def densify_body(entries, me_ref, own_ref, came_ref, _, out_ref, slips):
    halves, events = own_ref.shape[0], own_ref.shape[1] - 1
    width, _, blocks, _ = out_ref.shape
    live = 2 * halves * entries
    row = me_ref[0]
    line = lax.broadcasted_iota(jnp.int32, (width * blocks, live), 0)
    number = ((line // blocks * 2 + row % 2) * blocks + line % blocks).astype(jnp.float32)
    for e in range(events):
        ids = jnp.full((1, BLOCK), -1.0, jnp.float32)
        for ref in (own_ref, came_ref):
            for j in range(halves):
                ids = jnp.maximum(ids, ref[j, events, e : e + 1, :])
        ids = jnp.broadcast_to(ids, (width * blocks, BLOCK))[:, :live]
        onehot = (ids == number).astype(jnp.bfloat16)
        for core, ref in enumerate((own_ref, came_ref)):
            for j in range(halves):
                source = row ^ (2 * j + core)
                slips[e, pl.ds(pl.multiple_of(source * entries, entries), entries), :] = ref[j, e, 0:entries, :]
        slip = slips[e]
        total = jnp.zeros((width * blocks, BLOCK), jnp.float32)
        for _ in range(3):
            piece = slip.astype(jnp.bfloat16)
            slip = slip - piece.astype(jnp.float32)
            total = total + jnp.dot(onehot, piece, preferred_element_type=jnp.float32)
        out_ref[:, e] = total.reshape(width, blocks, BLOCK)


def assemble(dense_ref, out_ref):
    events, blocks = out_ref.shape[0] // 2, dense_ref.shape[2]
    flat = dense_ref.reshape(events * blocks, BLOCK)
    for t in range(events // (2 * SUB)):
        for b in range(blocks):
            rows = [flat[pl.ds((2 * t + u) * SUB * blocks + b, SUB, stride=blocks), :] for u in range(2)]
            slip = jnp.concatenate(rows, axis=0)
            hi = slip.astype(jnp.bfloat16)
            lo = (slip - hi.astype(jnp.float32)).astype(jnp.bfloat16)
            where = slice(b * BLOCK, (b + 1) * BLOCK)
            out_ref[2 * t * SUB : 2 * (t + 1) * SUB, where] = hi
            out_ref[events + 2 * t * SUB : events + 2 * (t + 1) * SUB, where] = lo


def stress(k, core, col, slip_ref, kernel_ref):
    events, patches = slip_ref.shape[0] // 2, slip_ref.shape[1]
    block = kernel_ref[col ^ k, :, pl.ds(pl.multiple_of(core * patches, patches), patches)]
    hi = block.astype(jnp.bfloat16)
    lo = (block - hi.astype(jnp.float32)).astype(jnp.bfloat16)
    first = lax.dot_general(slip_ref[...], hi, NT, preferred_element_type=jnp.float32)
    second = lax.dot_general(slip_ref[:events, :], lo, NT, preferred_element_type=jnp.float32)
    return first[:events] + first[events:] + second


def own_body(targets, me_ref, dense_ref, kernel_ref, slip_ref, out_ref):
    assemble(dense_ref, slip_ref)
    for j, k in enumerate(targets):
        out_ref[j] = stress(k, me_ref[0] % 2, me_ref[1], slip_ref, kernel_ref)


def other_body(targets, me_ref, dense_ref, kernel_ref, sum_ref, slip_ref, out_ref):
    assemble(dense_ref, slip_ref)
    for j, k in enumerate(targets):
        out_ref[j] = sum_ref[j] + stress(k, 1 - me_ref[0] % 2, me_ref[1], slip_ref, kernel_ref)


def both_body(targets, me_ref, own_ref, other_ref, kernel_ref, out_ref):
    core = me_ref[0] % 2
    for j, k in enumerate(targets):
        out_ref[j] = stress(k, core, me_ref[1], own_ref, kernel_ref) + stress(
            k, 1 - core, me_ref[1], other_ref, kernel_ref
        )


def halving_order(width):
    bits = width.bit_length() - 1
    return [int(f"{k:0{bits}b}"[::-1], 2) for k in range(width)]


def per_device(kernel, slip_delta, block_list, live_count, direct_effect, load_rate, time_before):
    width = lax.axis_size("cols")
    height = lax.axis_size("rows")
    events_here, entries = block_list.shape
    events = events_here * width
    receivers, sources = kernel.shape
    blocks_here = sources // BLOCK
    me = jnp.stack([lax.axis_index("rows"), lax.axis_index("cols")]).astype(jnp.int32)

    order = halving_order(width)
    share = receivers // width
    quarter = width // 4
    near_keep, far_keep = order[0 : 2 * quarter : 2], order[1 : 2 * quarter : 2]
    near_send, far_send = order[2 * quarter :: 2], order[2 * quarter + 1 :: 2]
    in_hbm = functools.partial(pltpu.with_memory_space_constraint, memory_space=pltpu.HBM)
    kernel = kernel.reshape(width, share, sources)
    packed = pl.pallas_call(
        pack_body,
        out_shape=f32(events_here + 1, SUB, BLOCK),
        in_specs=[SMEM_SPEC] + [HBM_SPEC] * 3,
        out_specs=VMEM_SPEC,
        scratch_shapes=[
            pltpu.VMEM(slip_delta.shape, jnp.float32),
            pltpu.VMEM(block_list.shape, jnp.int32),
            pltpu.SMEM(live_count.shape, jnp.int32),
            pltpu.VMEM((SUB, BLOCK), jnp.float32),
            pltpu.SemaphoreType.DMA((3,)),
        ],
        compiler_params=params(4),
        name="pack",
    )(me, in_hbm(slip_delta), in_hbm(block_list), in_hbm(live_count))
    held = packed[None]
    step = 2
    while step < height:
        held = jnp.concatenate([held, send_xor(held, "rows", step)], axis=0)
        step *= 2

    blocks_half = blocks_here // 2
    dense = pl.pallas_call(
        functools.partial(densify_body, entries),
        out_shape=f32(width, events_here, blocks_half, BLOCK),
        in_specs=[SMEM_SPEC, VMEM_SPEC, VMEM_SPEC, HBM_SPEC],
        out_specs=VMEM_SPEC,
        scratch_shapes=[pltpu.VMEM((events_here, height * entries, BLOCK), jnp.float32)],
        compiler_params=params(8),
        name="densify",
    )(me, held, send_xor(held, "rows", 1), in_hbm(kernel))
    mine = lax.all_to_all(dense, "cols", 0, 0, tiled=True)

    def call(body, targets, outs, *args):
        return pl.pallas_call(
            functools.partial(body, targets),
            out_shape=outs,
            in_specs=[SMEM_SPEC] + [VMEM_SPEC] * len(args),
            out_specs=jax.tree.map(lambda _: VMEM_SPEC, outs),
            compiler_params=params(8),
            cost_estimate=pl.CostEstimate(
                flops=6 * quarter * share * sources * events,
                bytes_accessed=4 * quarter * share * sources,
                transcendentals=0,
            ),
            name=body.__name__.removesuffix("_body") + "_stress",
        )(me, *args)

    slips = bf16(2 * events, blocks_half * BLOCK)
    sums = f32(quarter, events, share)
    came = send_xor(mine, "rows", 1)
    own, own_sum = call(own_body, far_send, [slips, sums], mine, kernel)
    other, far_sent = call(other_body, far_send, [slips, sums], came, kernel, own_sum)

    def later(targets):
        return call(both_body, targets, sums, own, other, kernel)

    far_came = send_xor(far_sent, "cols", 1)
    near_came = send_xor(later(near_send), "cols", 1)
    far = later(far_keep) + far_came
    near = later(near_keep) + near_came
    step = 2
    while step < width // 2:
        keep = far.shape[0] // 2
        far = far[:keep] + send_xor(far[keep:], "cols", step)
        near = near[:keep] + send_xor(near[keep:], "cols", step)
        step *= 2
    stress_change = near[0] + send_xor(far[0], "cols", step)
    scale = direct_effect[None, :]
    growth = jnp.expm1(load_rate * time_before / direct_effect)[None, :]
    log_time = jnp.log(scale / load_rate[None, :]) + jnp.log(
        jnp.log1p(jnp.exp(-stress_change / scale) * growth)
    )
    return (stress_change.T, log_time.T)


def solution(mesh):
    in_specs = (
        P("rows", "cols"),
        P("cols", "rows", None),
        P("cols", "rows"),
        P("cols"),
        P(("rows", "cols")),
        P(("rows", "cols")),
        P(("rows", "cols")),
    )
    out_specs = (P(("rows", "cols"), None), P(("rows", "cols"), None))
    return jax.shard_map(
        per_device, mesh=mesh, in_specs=in_specs, out_specs=out_specs, check_vma=False
    )
```

time: 42.4 us -> 42 us (level)
  waiting for transfers between devices: 8.91 us -> 7.89 us
  Pallas kernels: 7.93 us -> 8.54 us
    ppermute x8, waiting for transfers between devices: 8.91 us -> 7.89 us  [send_xor(): lax.ppermute(block, axis, [(r, r ^ k) for r in range(lax.axis_size(axis))])]
    pallas_call x5 -> x6, Pallas kernels: 7.13 us -> 7.73 us  [the longest x5 6.05 us: call(): pl.pallas_call(functools.partial(body, targets), out_shape=outs, in_specs...]
  transfers between devices with their start and end apart: 8 -> 8, of which waited for: 6 -> 6; matrix products, arithmetic and copies ran while one was open for 0% -> 0% of each run, Pallas kernels for 9% -> 12%
where the time goes in v10:
time: 42 us; the launch traced here: 41.8 us
  blocking collectives  15.3 us (36%)
  Pallas kernels  8.54 us (20%)
  starting transfers between devices  8.41 us (20%)
  waiting for transfers between devices  7.89 us (19%)
  other arithmetic  0.79 us (2%)
  between operations  0.78 us (2%)
    all_to_all x1, blocking collectives, per_device(): mine = lax.all_to_all(dense, 'cols', 0, 0, tiled=True)  15.3 us
    ppermute x8, starting transfers between devices, send_xor(): lax.ppermute(block, axis, [(r, r ^ k) for r in range(lax.axis_size(axis))])  8.41 us
    ppermute x8, waiting for transfers between devices, send_xor(): lax.ppermute(block, axis, [(r, r ^ k) for r in range(lax.axis_size(axis))])  7.89 us
    pallas_call x5, Pallas kernels, call(): pl.pallas_call(functools.partial(body, targets), out_shape=outs, in_specs...  6.05 us
    pallas_call x1, Pallas kernels, per_device(): pl.pallas_call(pack_body, out_shape=f32(events_here + 1, SUB, BLOCK), in_...  1.68 us
  transfers between devices with their start and end apart: 8, of which 6 were waited for; matrix products, arithmetic and copies ran while one was open for 0% of the time, Pallas kernels for 12%

profile of v10, /device:TPU:0, one launch (start us, length us, event | category | flops | bytes accessed | tf_op | source)
XLA Modules:
  0.0 41.8 jit_solution(4109185582546532730)
XLA Ops:
  0.6 0.0 copy-start
  0.6 0.1 pad_add_fusion.me_ref
  0.7 1.7 %pack.1 = f32[9,8,128]{2,1,0:T(8,128)S(1)} custom-call(s32[2]{0:T(128)S(1)} %pad_add_fusion.me_ref, f32[8,8,128]{2,1,0:T(8,128)} %slip_hbm.1, s32[8,8]{1,0:T(8,128)} %list_hbm.1, s32[8]{0:T(128)} %count_hbm.1), custom_call_target="tpu_custom_call" | custom-call | tf_op jit(solution)/shard_map/pack/pallas_call | solution.py:150
  2.4 3.0 %collective-permute-start = (f32[1,9,8,128]{3,2,1,0:T(8,128)S(1)}, f32[1,9,8,128]{3,2,1,0:T(8,128)S(1)}, u32[]{:S(2)}, u32[]{:S(2)}) collective-permute-start(f32[1,9,8,128]{3,2,1,0:T(8,128)S(1)} %bitcast.24), channel_id=1, source_target_pairs={{0,16},{8,24},{16,0},{24,8},{1,17},{9,25},{17,1},{25,9},{2,18},{10... | collective-permute-start | bytes 110600 | tf_op jit(solution)/shard_map/ppermute | solution.py:32
  5.4 1.9 %collective-permute-done = f32[1,9,8,128]{3,2,1,0:T(8,128)S(1)} collective-permute-done((f32[1,9,8,128]{3,2,1,0:T(8,128)S(1)}, f32[1,9,8,128]{3,2,1,0:T(8,128)S(1)}, u32[]{:S(2)}, u32[]{:S(2)}) %collective-permute-start) | collective-permute-done | bytes 36896 | tf_op jit(solution)/shard_map/ppermute | solution.py:32
  7.4 0.0 collective-permute-start.1
  7.4 1.3 %collective-permute-done.1.came_ref = f32[2,9,8,128]{3,2,1,0:T(8,128)S(1)} collective-permute-done((f32[2,9,8,128]{3,2,1,0:T(8,128)S(1)}, f32[2,9,8,128]{3,2,1,0:T(8,128)S(1)}, u32[]{:S(2)}, u32[]{:S(2)}) %collective-permute-start.1) | collective-permute-done | bytes 73760 | tf_op jit(solution)/shard_map/ppermute | solution.py:32
  8.7 0.8 %densify.1 = f32[8,8,8,128]{3,2,1,0:T(8,128)S(1)} custom-call(s32[2]{0:T(128)S(1)} %pad_add_fusion.me_ref, f32[2,9,8,128]{3,2,1,0:T(8,128)S(1)} %pad_maximum_fusion.own_ref, f32[2,9,8,128]{3,2,1,0:T(8,128)S(1)} %collective-permute-done.1.came_ref, f32[8,128,2048]{2,1,0:T(8,128)} %bitcast.18), custom_call_target="tpu_custom_call" | custom-call | tf_op jit(solution)/shard_map/densify/pallas_call | solution.py:172
  9.5 15.3 %all_to_all.5.dense_ref = f32[8,8,8,128]{3,2,1,0:T(8,128)S(1)} all-to-all(f32[8,8,8,128]{3,2,1,0:T(8,128)S(1)} %densify.1), channel_id=1, replica_groups=mesh['rows'=4,'cols'=8] {'cols'}, dimensions={0} | all-to-all | bytes 524288 | tf_op jit(solution)/shard_map/all_to_all | solution.py:181
  24.8 0.0 collective-permute-start.2
  24.8 0.0 copy-done
  24.8 1.0 %own_stress.1 = (bf16[128,1024]{1,0:T(8,128)(2,1)S(1)}, f32[2,64,128]{2,1,0:T(8,128)S(1)}) custom-call(s32[2]{0:T(128)S(1)} %pad_add_fusion.me_ref, f32[8,8,8,128]{3,2,1,0:T(8,128)S(1)} %all_to_all.5.dense_ref, f32[8,128,2048]{2,1,0:T(8,128)S(1)} %bitcast.19), custom_call_target="tpu_custom_call" | custom-call | flops 201326592 | bytes 2097152 | tf_op jit(solution)/shard_map/own_stress/pallas_call | solution.py:184
  25.8 0.5 %collective-permute-done.2.dense_ref = f32[8,8,8,128]{3,2,1,0:T(8,128)S(1)} collective-permute-done((f32[8,8,8,128]{3,2,1,0:T(8,128)S(1)}, f32[8,8,8,128]{3,2,1,0:T(8,128)S(1)}, u32[]{:S(2)}, u32[]{:S(2)}) %collective-permute-start.2) | collective-permute-done | bytes 262176 | tf_op jit(solution)/shard_map/ppermute | solution.py:32
  26.3 1.0 %other_stress.1 = (bf16[128,1024]{1,0:T(8,128)(2,1)S(1)}, f32[2,64,128]{2,1,0:T(8,128)S(1)}) custom-call(s32[2]{0:T(128)S(1)} %pad_add_fusion.me_ref, f32[8,8,8,128]{3,2,1,0:T(8,128)S(1)} %collective-permute-done.2.dense_ref, f32[8,128,2048]{2,1,0:T(8,128)S(1)} %bitcast.20, f32[2,64,128]{2,1,0:T(8,128)S(1)} %get-tuple-element.7.sum_ref), custom_call_target="tpu_custom_call" | custom-call | flops 201326592 | bytes 2097152 | tf_op jit(solution)/shard_map/other_stress/pallas_call | solution.py:184
  27.4 1.5 %collective-permute-start.5 = (f32[2,64,128]{2,1,0:T(8,128)S(1)}, f32[2,64,128]{2,1,0:T(8,128)S(1)}, u32[]{:S(2)}, u32[]{:S(2)}) collective-permute-start(f32[2,64,128]{2,1,0:T(8,128)S(1)} %get-tuple-element.9), channel_id=1, source_target_pairs={{0,1},{1,0},{2,3},{3,2},{4,5},{5,4},{6,7},{7,6},{8,9},{9,8},{10,11... | collective-permute-start | bytes 196616 | tf_op jit(solution)/shard_map/ppermute | solution.py:32
  28.9 1.3 %both_stress.4 = f32[2,64,128]{2,1,0:T(8,128)S(1)} custom-call(s32[2]{0:T(128)S(1)} %pad_add_fusion.me_ref, bf16[128,1024]{1,0:T(8,128)(2,1)S(1)} %get-tuple-element.6.own_ref, bf16[128,1024]{1,0:T(8,128)(2,1)S(1)} %get-tuple-element.8.other_ref, f32[8,128,2048]{2,1,0:T(8,128)S(1)} %bitcast.21), custom_call_target="tpu_custom_call" | custom-call | flops 201326592 | bytes 2097152 | tf_op jit(solution)/shard_map/both_stress/pallas_call | solution.py:184
  30.2 0.0 copy-start.1
  30.2 0.0 copy-start.2
  30.2 0.0 copy-start.3
  30.3 0.7 %collective-permute-start.3 = (f32[2,64,128]{2,1,0:T(8,128)S(1)}, f32[2,64,128]{2,1,0:T(8,128)S(1)}, u32[]{:S(2)}, u32[]{:S(2)}) collective-permute-start(f32[2,64,128]{2,1,0:T(8,128)S(1)} %both_stress.4), channel_id=1, source_target_pairs={{0,1},{1,0},{2,3},{3,2},{4,5},{5,4},{6,7},{7,6},{8,9},{9,8},{10,11... | collective-permute-start | bytes 196616 | tf_op jit(solution)/shard_map/ppermute | solution.py:32
  30.9 1.3 %both_stress.5 = f32[2,64,128]{2,1,0:T(8,128)S(1)} custom-call(s32[2]{0:T(128)S(1)} %pad_add_fusion.me_ref, bf16[128,1024]{1,0:T(8,128)(2,1)S(1)} %get-tuple-element.6.own_ref, bf16[128,1024]{1,0:T(8,128)(2,1)S(1)} %get-tuple-element.8.other_ref, f32[8,128,2048]{2,1,0:T(8,128)S(1)} %bitcast.22), custom_call_target="tpu_custom_call" | custom-call | flops 201326592 | bytes 2097152 | tf_op jit(solution)/shard_map/both_stress/pallas_call | solution.py:184
  32.3 0.0 collective-permute-done.5
  32.3 1.1 %collective-permute-start.6 = (f32[1,64,128]{2,1,0:T(8,128)S(1)}, f32[1,64,128]{2,1,0:T(8,128)S(1)}, u32[]{:S(2)}, u32[]{:S(2)}) collective-permute-start(f32[1,64,128]{2,1,0:T(8,128)S(1)} %slice.19), channel_id=1, source_target_pairs={{0,2},{1,3},{2,0},{3,1},{4,6},{5,7},{6,4},{7,5},{8,10},{9,11},{10,... | collective-permute-start | bytes 98312 | tf_op jit(solution)/shard_map/ppermute | solution.py:32
  33.4 1.3 %both_stress.3 = f32[2,64,128]{2,1,0:T(8,128)S(1)} custom-call(s32[2]{0:T(128)S(1)} %pad_add_fusion.me_ref, bf16[128,1024]{1,0:T(8,128)(2,1)S(1)} %get-tuple-element.6.own_ref, bf16[128,1024]{1,0:T(8,128)(2,1)S(1)} %get-tuple-element.8.other_ref, f32[8,128,2048]{2,1,0:T(8,128)S(1)} %bitcast.23), custom_call_target="tpu_custom_call" | custom-call | flops 201326592 | bytes 2097152 | tf_op jit(solution)/shard_map/both_stress/pallas_call | solution.py:184
  34.8 0.0 collective-permute-done.3
  34.8 1.0 %collective-permute-start.4 = (f32[1,64,128]{2,1,0:T(8,128)S(1)}, f32[1,64,128]{2,1,0:T(8,128)S(1)}, u32[]{:S(2)}, u32[]{:S(2)}) collective-permute-start(f32[1,64,128]{2,1,0:T(8,128)S(1)} %slice.17), channel_id=1, source_target_pairs={{0,2},{1,3},{2,0},{3,1},{4,6},{5,7},{6,4},{7,5},{8,10},{9,11},{10,... | collective-permute-start | bytes 98312 | tf_op jit(solution)/shard_map/ppermute | solution.py:32
  35.8 0.4 %collective-permute-done.6 = f32[1,64,128]{2,1,0:T(8,128)S(1)} collective-permute-done((f32[1,64,128]{2,1,0:T(8,128)S(1)}, f32[1,64,128]{2,1,0:T(8,128)S(1)}, u32[]{:S(2)}, u32[]{:S(2)}) %collective-permute-start.6) | collective-permute-done | bytes 32800 | tf_op jit(solution)/shard_map/ppermute | solution.py:32
  36.3 1.1 %collective-permute-start.7 = (f32[64,128]{1,0:T(8,128)S(1)}, f32[64,128]{1,0:T(8,128)S(1)}, u32[]{:S(2)}, u32[]{:S(2)}) collective-permute-start(f32[64,128]{1,0:T(8,128)S(1)} %fusion), channel_id=1, source_target_pairs={{0,4},{1,5},{2,6},{3,7},{4,0},{5,1},{6,2},{7,3},{8,12},{9,13},{10,... | collective-permute-start | bytes 98312 | tf_op jit(solution)/shard_map/ppermute | solution.py:32
  37.4 0.0 copy-done.1
  37.4 0.0 copy-done.2
  37.4 0.0 copy-done.3
  37.4 1.8 %collective-permute-done.4 = f32[1,64,128]{2,1,0:T(8,128)S(1)} collective-permute-done((f32[1,64,128]{2,1,0:T(8,128)S(1)}, f32[1,64,128]{2,1,0:T(8,128)S(1)}, u32[]{:S(2)}, u32[]{:S(2)}) %collective-permute-start.4) | collective-permute-done | bytes 32800 | tf_op jit(solution)/shard_map/ppermute | solution.py:32
  39.1 2.0 %collective-permute-done.7 = f32[64,128]{1,0:T(8,128)S(1)} collective-permute-done((f32[64,128]{1,0:T(8,128)S(1)}, f32[64,128]{1,0:T(8,128)S(1)}, u32[]{:S(2)}, u32[]{:S(2)}) %collective-permute-start.7) | collective-permute-done | bytes 32800 | tf_op jit(solution)/shard_map/ppermute | solution.py:32
  41.1 0.7 %add_bitcast_fusion = (f32[128,64]{0,1:T(8,128)}, f32[128,64]{0,1:T(8,128)}) fusion(f32[128]{0:T(128)S(1)} %get-tuple-element.13, f32[128]{0:T(128)S(1)} %copy-done.1, f32[128]{0:T(128)S(1)} %get-tuple-element.12, f32[64,128]{1,0:T(8,128)S(1)} %collective-permute-done.7, f32[1,64,128]{2,1,0:T(8,128)S(1)} %collective-permute-done.4, f32[2,64,128]{2,1,0:T(8,128)S(1)} %add.23), kind=kLoop, calls=%fused_computation.6 | loop fusion | flops 49152 | bytes 165376 | tf_op jit(solution)/shard_map/transpose | solution.py:223
  (7 shorter events, 0.1 us)
Async XLA Ops:
  0.6 24.2 %copy-start = (f32[1024,2048]{1,0:T(8,128)S(1)}, f32[1024,2048]{1,0:T(8,128)}, u32[]{:S(2)}) copy-start(f32[1024,2048]{1,0:T(8,128)} %param.7) | copy-start | bytes 25165828
  2.4 5.0 %collective-permute-start = (f32[1,9,8,128]{3,2,1,0:T(8,128)S(1)}, f32[1,9,8,128]{3,2,1,0:T(8,128)S(1)}, u32[]{:S(2)}, u32[]{:S(2)}) collective-permute-start(f32[1,9,8,128]{3,2,1,0:T(8,128)S(1)} %bitcast.24), channel_id=1, source_target_pairs={{0,16},{8,24},{16,0},{24,8},{1,17},{9,25},{17,1},{25,9},{2,18},{10... | collective-permute-start | bytes 110600 | tf_op jit(solution)/shard_map/ppermute | solution.py:32
  7.4 1.3 %collective-permute-start.1 = (f32[2,9,8,128]{3,2,1,0:T(8,128)S(1)}, f32[2,9,8,128]{3,2,1,0:T(8,128)S(1)}, u32[]{:S(2)}, u32[]{:S(2)}) collective-permute-start(f32[2,9,8,128]{3,2,1,0:T(8,128)S(1)} %pad_maximum_fusion.own_ref), channel_id=1, source_target_pairs={{0,8},{8,0},{16,24},{24,16},{1,9},{9,1},{17,25},{25,17},{2,10},{10... | collective-permute-start | bytes 221192 | tf_op jit(solution)/shard_map/ppermute | solution.py:32
  24.8 1.5 %collective-permute-start.2 = (f32[8,8,8,128]{3,2,1,0:T(8,128)S(1)}, f32[8,8,8,128]{3,2,1,0:T(8,128)S(1)}, u32[]{:S(2)}, u32[]{:S(2)}) collective-permute-start(f32[8,8,8,128]{3,2,1,0:T(8,128)S(1)} %all_to_all.5.dense_ref), channel_id=1, source_target_pairs={{0,8},{8,0},{16,24},{24,16},{1,9},{9,1},{17,25},{25,17},{2,10},{10... | collective-permute-start | bytes 786440 | tf_op jit(solution)/shard_map/ppermute | solution.py:32
  27.4 4.9 %collective-permute-start.5 = (f32[2,64,128]{2,1,0:T(8,128)S(1)}, f32[2,64,128]{2,1,0:T(8,128)S(1)}, u32[]{:S(2)}, u32[]{:S(2)}) collective-permute-start(f32[2,64,128]{2,1,0:T(8,128)S(1)} %get-tuple-element.9), channel_id=1, source_target_pairs={{0,1},{1,0},{2,3},{3,2},{4,5},{5,4},{6,7},{7,6},{8,9},{9,8},{10,11... | collective-permute-start | bytes 196616 | tf_op jit(solution)/shard_map/ppermute | solution.py:32
  30.2 7.1 %copy-start.1 = (f32[128]{0:T(128)S(1)}, f32[128]{0:T(128)}, u32[]{:S(2)}) copy-start(f32[128]{0:T(128)} %param.11) | copy-start | bytes 1540
  30.2 7.1 %copy-start.2 = (f32[128]{0:T(128)S(1)}, f32[128]{0:T(128)}, u32[]{:S(2)}) copy-start(f32[128]{0:T(128)} %param.12) | copy-start | bytes 1540
  30.2 7.1 %copy-start.3 = (f32[128]{0:T(128)S(1)}, f32[128]{0:T(128)}, u32[]{:S(2)}) copy-start(f32[128]{0:T(128)} %param.13) | copy-start | bytes 1540
  30.3 4.5 %collective-permute-start.3 = (f32[2,64,128]{2,1,0:T(8,128)S(1)}, f32[2,64,128]{2,1,0:T(8,128)S(1)}, u32[]{:S(2)}, u32[]{:S(2)}) collective-permute-start(f32[2,64,128]{2,1,0:T(8,128)S(1)} %both_stress.4), channel_id=1, source_target_pairs={{0,1},{1,0},{2,3},{3,2},{4,5},{5,4},{6,7},{7,6},{8,9},{9,8},{10,11... | collective-permute-start | bytes 196616 | tf_op jit(solution)/shard_map/ppermute | solution.py:32
  32.3 4.0 %collective-permute-start.6 = (f32[1,64,128]{2,1,0:T(8,128)S(1)}, f32[1,64,128]{2,1,0:T(8,128)S(1)}, u32[]{:S(2)}, u32[]{:S(2)}) collective-permute-start(f32[1,64,128]{2,1,0:T(8,128)S(1)} %slice.19), channel_id=1, source_target_pairs={{0,2},{1,3},{2,0},{3,1},{4,6},{5,7},{6,4},{7,5},{8,10},{9,11},{10,... | collective-permute-start | bytes 98312 | tf_op jit(solution)/shard_map/ppermute | solution.py:32
  34.8 4.3 %collective-permute-start.4 = (f32[1,64,128]{2,1,0:T(8,128)S(1)}, f32[1,64,128]{2,1,0:T(8,128)S(1)}, u32[]{:S(2)}, u32[]{:S(2)}) collective-permute-start(f32[1,64,128]{2,1,0:T(8,128)S(1)} %slice.17), channel_id=1, source_target_pairs={{0,2},{1,3},{2,0},{3,1},{4,6},{5,7},{6,4},{7,5},{8,10},{9,11},{10,... | collective-permute-start | bytes 98312 | tf_op jit(solution)/shard_map/ppermute | solution.py:32
  36.3 4.8 %collective-permute-start.7 = (f32[64,128]{1,0:T(8,128)S(1)}, f32[64,128]{1,0:T(8,128)S(1)}, u32[]{:S(2)}, u32[]{:S(2)}) collective-permute-start(f32[64,128]{1,0:T(8,128)S(1)} %fusion), channel_id=1, source_target_pairs={{0,4},{1,5},{2,6},{3,7},{4,0},{5,1},{6,2},{7,3},{8,12},{9,13},{10,... | collective-permute-start | bytes 98312 | tf_op jit(solution)/shard_map/ppermute | solution.py:32

commit v11 on v10

--- a/solution.py
+++ b/solution.py
@@ -9,6 +9,7 @@
 
 BLOCK = 128
 SUB = 8
+CHUNK = 256
 VMEM_SPEC = pl.BlockSpec(memory_space=pltpu.VMEM)
 SMEM_SPEC = pl.BlockSpec(memory_space=pltpu.SMEM)
 HBM_SPEC = pl.BlockSpec(memory_space=pltpu.HBM)
@@ -98,12 +99,15 @@
 
 def stress(k, core, col, slip_ref, kernel_ref):
     events, patches = slip_ref.shape[0] // 2, slip_ref.shape[1]
-    block = kernel_ref[col ^ k, :, pl.ds(pl.multiple_of(core * patches, patches), patches)]
-    hi = block.astype(jnp.bfloat16)
-    lo = (block - hi.astype(jnp.float32)).astype(jnp.bfloat16)
-    first = lax.dot_general(slip_ref[...], hi, NT, preferred_element_type=jnp.float32)
-    second = lax.dot_general(slip_ref[:events, :], lo, NT, preferred_element_type=jnp.float32)
-    return first[:events] + first[events:] + second
+    rows = kernel_ref.at[col ^ k]
+    both = low = 0.0
+    for t in range(0, patches, CHUNK):
+        block = rows[:, pl.ds(pl.multiple_of(core * patches + t, CHUNK), CHUNK)]
+        hi = block.astype(jnp.bfloat16)
+        lo = (block - hi.astype(jnp.float32)).astype(jnp.bfloat16)
+        both += lax.dot_general(slip_ref[:, t : t + CHUNK], hi, NT, preferred_element_type=jnp.float32)
+        low += lax.dot_general(slip_ref[:events, t : t + CHUNK], lo, NT, preferred_element_type=jnp.float32)
+    return both[:events] + both[events:] + low
 
 
 def own_body(targets, me_ref, dense_ref, kernel_ref, slip_ref, out_ref):
@@ -205,8 +209,10 @@
         return call(both_body, targets, sums, own, other, kernel)
 
     far_came = send_xor(far_sent, "cols", 1)
-    near_came = send_xor(later(near_send), "cols", 1)
+    near_sent = later(near_send)
     far = later(far_keep) + far_came
+    near_sent, far = lax.optimization_barrier((near_sent, far))
+    near_came = send_xor(near_sent, "cols", 1)
     near = later(near_keep) + near_came
     step = 2
     while step < width // 2:

time: 42 us -> 43.4 us (1.033)
  waiting for transfers between devices: 7.89 us -> 9.34 us
    ppermute x8, waiting for transfers between devices: 7.89 us -> 9.34 us  [send_xor(): lax.ppermute(block, axis, [(r, r ^ k) for r in range(lax.axis_size(axis))])]
  transfers between devices with their start and end apart: 8 -> 8, of which waited for: 6 -> 8; matrix products, arithmetic and copies ran while one was open for 0% -> 0% of each run, Pallas kernels for 12% -> 12%
where the time goes in v11:
time: 43.4 us; the launch traced here: 43.3 us
  blocking collectives  15.3 us (35%)
  waiting for transfers between devices  9.34 us (22%)
  Pallas kernels  8.66 us (20%)
  starting transfers between devices  8.35 us (19%)
  other arithmetic  0.78 us (2%)
  between operations  0.76 us (2%)
    all_to_all x1, blocking collectives, per_device(): mine = lax.all_to_all(dense, 'cols', 0, 0, tiled=True)  15.3 us
    ppermute x8, waiting for transfers between devices, send_xor(): lax.ppermute(block, axis, [(r, r ^ k) for r in range(lax.axis_size(axis))])  9.34 us
    ppermute x8, starting transfers between devices, send_xor(): lax.ppermute(block, axis, [(r, r ^ k) for r in range(lax.axis_size(axis))])  8.35 us
    pallas_call x5, Pallas kernels, call(): pl.pallas_call(functools.partial(body, targets), out_shape=outs, in_specs...  6.17 us
    pallas_call x1, Pallas kernels, per_device(): pl.pallas_call(pack_body, out_shape=f32(events_here + 1, SUB, BLOCK), in_...  1.68 us
  transfers between devices with their start and end apart: 8, of which 8 were waited for; matrix products, arithmetic and copies ran while one was open for 0% of the time, Pallas kernels for 12%

profile of v11, /device:TPU:0, one launch (start us, length us, event | category | flops | bytes accessed | tf_op | source)
XLA Modules:
  0.0 43.3 jit_solution(7716326145854587476)
XLA Ops:
  0.6 0.0 copy-start
  0.6 0.1 pad_add_fusion.me_ref
  0.7 1.7 %pack.1 = f32[9,8,128]{2,1,0:T(8,128)S(1)} custom-call(s32[2]{0:T(128)S(1)} %pad_add_fusion.me_ref, f32[8,8,128]{2,1,0:T(8,128)} %slip_hbm.1, s32[8,8]{1,0:T(8,128)} %list_hbm.1, s32[8]{0:T(128)} %count_hbm.1), custom_call_target="tpu_custom_call" | custom-call | tf_op jit(solution)/shard_map/pack/pallas_call | solution.py:154
  2.4 3.0 %collective-permute-start = (f32[1,9,8,128]{3,2,1,0:T(8,128)S(1)}, f32[1,9,8,128]{3,2,1,0:T(8,128)S(1)}, u32[]{:S(2)}, u32[]{:S(2)}) collective-permute-start(f32[1,9,8,128]{3,2,1,0:T(8,128)S(1)} %bitcast.24), channel_id=1, source_target_pairs={{0,16},{8,24},{16,0},{24,8},{1,17},{9,25},{17,1},{25,9},{2,18},{10... | collective-permute-start | bytes 110600 | tf_op jit(solution)/shard_map/ppermute | solution.py:33
  5.4 1.9 %collective-permute-done = f32[1,9,8,128]{3,2,1,0:T(8,128)S(1)} collective-permute-done((f32[1,9,8,128]{3,2,1,0:T(8,128)S(1)}, f32[1,9,8,128]{3,2,1,0:T(8,128)S(1)}, u32[]{:S(2)}, u32[]{:S(2)}) %collective-permute-start) | collective-permute-done | bytes 36896 | tf_op jit(solution)/shard_map/ppermute | solution.py:33
  7.4 0.0 collective-permute-start.1
  7.4 1.3 %collective-permute-done.1.came_ref = f32[2,9,8,128]{3,2,1,0:T(8,128)S(1)} collective-permute-done((f32[2,9,8,128]{3,2,1,0:T(8,128)S(1)}, f32[2,9,8,128]{3,2,1,0:T(8,128)S(1)}, u32[]{:S(2)}, u32[]{:S(2)}) %collective-permute-start.1) | collective-permute-done | bytes 73760 | tf_op jit(solution)/shard_map/ppermute | solution.py:33
  8.7 0.8 %densify.1 = f32[8,8,8,128]{3,2,1,0:T(8,128)S(1)} custom-call(s32[2]{0:T(128)S(1)} %pad_add_fusion.me_ref, f32[2,9,8,128]{3,2,1,0:T(8,128)S(1)} %pad_maximum_fusion.own_ref, f32[2,9,8,128]{3,2,1,0:T(8,128)S(1)} %collective-permute-done.1.came_ref, f32[8,128,2048]{2,1,0:T(8,128)} %bitcast.18), custom_call_target="tpu_custom_call" | custom-call | tf_op jit(solution)/shard_map/densify/pallas_call | solution.py:176
  9.5 15.3 %all_to_all.5.dense_ref = f32[8,8,8,128]{3,2,1,0:T(8,128)S(1)} all-to-all(f32[8,8,8,128]{3,2,1,0:T(8,128)S(1)} %densify.1), channel_id=1, replica_groups=mesh['rows'=4,'cols'=8] {'cols'}, dimensions={0} | all-to-all | bytes 524288 | tf_op jit(solution)/shard_map/all_to_all | solution.py:185
  24.8 0.0 collective-permute-start.2
  24.8 0.0 copy-done
  24.8 1.0 %own_stress.1 = (bf16[128,1024]{1,0:T(8,128)(2,1)S(1)}, f32[2,64,128]{2,1,0:T(8,128)S(1)}) custom-call(s32[2]{0:T(128)S(1)} %pad_add_fusion.me_ref, f32[8,8,8,128]{3,2,1,0:T(8,128)S(1)} %all_to_all.5.dense_ref, f32[8,128,2048]{2,1,0:T(8,128)S(1)} %bitcast.19), custom_call_target="tpu_custom_call" | custom-call | flops 201326592 | bytes 2097152 | tf_op jit(solution)/shard_map/own_stress/pallas_call | solution.py:188
  25.9 0.5 %collective-permute-done.2.dense_ref = f32[8,8,8,128]{3,2,1,0:T(8,128)S(1)} collective-permute-done((f32[8,8,8,128]{3,2,1,0:T(8,128)S(1)}, f32[8,8,8,128]{3,2,1,0:T(8,128)S(1)}, u32[]{:S(2)}, u32[]{:S(2)}) %collective-permute-start.2) | collective-permute-done | bytes 262176 | tf_op jit(solution)/shard_map/ppermute | solution.py:33
  26.3 1.1 %other_stress.1 = (bf16[128,1024]{1,0:T(8,128)(2,1)S(1)}, f32[2,64,128]{2,1,0:T(8,128)S(1)}) custom-call(s32[2]{0:T(128)S(1)} %pad_add_fusion.me_ref, f32[8,8,8,128]{3,2,1,0:T(8,128)S(1)} %collective-permute-done.2.dense_ref, f32[8,128,2048]{2,1,0:T(8,128)S(1)} %bitcast.20, f32[2,64,128]{2,1,0:T(8,128)S(1)} %get-tuple-element.9.sum_ref), custom_call_target="tpu_custom_call" | custom-call | flops 201326592 | bytes 2097152 | tf_op jit(solution)/shard_map/other_stress/pallas_call | solution.py:188
  27.4 1.5 %collective-permute-start.3 = (f32[2,64,128]{2,1,0:T(8,128)S(1)}, f32[2,64,128]{2,1,0:T(8,128)S(1)}, u32[]{:S(2)}, u32[]{:S(2)}) collective-permute-start(f32[2,64,128]{2,1,0:T(8,128)S(1)} %get-tuple-element.11), channel_id=1, source_target_pairs={{0,1},{1,0},{2,3},{3,2},{4,5},{5,4},{6,7},{7,6},{8,9},{9,8},{10,11... | collective-permute-start | bytes 196616 | tf_op jit(solution)/shard_map/ppermute | solution.py:33
  28.9 1.4 %both_stress.5 = f32[2,64,128]{2,1,0:T(8,128)S(1)} custom-call(s32[2]{0:T(128)S(1)} %pad_add_fusion.me_ref, bf16[128,1024]{1,0:T(8,128)(2,1)S(1)} %get-tuple-element.8.own_ref, bf16[128,1024]{1,0:T(8,128)(2,1)S(1)} %get-tuple-element.10.other_ref, f32[8,128,2048]{2,1,0:T(8,128)S(1)} %bitcast.21), custom_call_target="tpu_custom_call" | custom-call | flops 201326592 | bytes 2097152 | tf_op jit(solution)/shard_map/both_stress/pallas_call | solution.py:188
  30.2 0.0 copy-start.1
  30.3 0.0 copy-start.2
  30.3 0.0 copy-start.3
  30.3 1.4 %both_stress.4 = f32[2,64,128]{2,1,0:T(8,128)S(1)} custom-call(s32[2]{0:T(128)S(1)} %pad_add_fusion.me_ref, bf16[128,1024]{1,0:T(8,128)(2,1)S(1)} %get-tuple-element.8.own_ref, bf16[128,1024]{1,0:T(8,128)(2,1)S(1)} %get-tuple-element.10.other_ref, f32[8,128,2048]{2,1,0:T(8,128)S(1)} %bitcast.22), custom_call_target="tpu_custom_call" | custom-call | flops 201326592 | bytes 2097152 | tf_op jit(solution)/shard_map/both_stress/pallas_call | solution.py:188
  31.7 0.1 collective-permute-done.3
  31.8 1.1 %collective-permute-start.6 = (f32[1,64,128]{2,1,0:T(8,128)S(1)}, f32[1,64,128]{2,1,0:T(8,128)S(1)}, u32[]{:S(2)}, u32[]{:S(2)}) collective-permute-start(f32[1,64,128]{2,1,0:T(8,128)S(1)} %slice.15), channel_id=1, source_target_pairs={{0,2},{1,3},{2,0},{3,1},{4,6},{5,7},{6,4},{7,5},{8,10},{9,11},{10,... | collective-permute-start | bytes 98312 | tf_op jit(solution)/shard_map/ppermute | solution.py:33
  32.9 1.4 %both_stress.3 = f32[2,64,128]{2,1,0:T(8,128)S(1)} custom-call(s32[2]{0:T(128)S(1)} %pad_add_fusion.me_ref, bf16[128,1024]{1,0:T(8,128)(2,1)S(1)} %get-tuple-element.8.own_ref, bf16[128,1024]{1,0:T(8,128)(2,1)S(1)} %get-tuple-element.10.other_ref, f32[8,128,2048]{2,1,0:T(8,128)S(1)} %bitcast.23), custom_call_target="tpu_custom_call" | custom-call | flops 201326592 | bytes 2097152 | tf_op jit(solution)/shard_map/both_stress/pallas_call | solution.py:188
  34.3 0.6 %collective-permute-start.4 = (f32[2,64,128]{2,1,0:T(8,128)S(1)}, f32[2,64,128]{2,1,0:T(8,128)S(1)}, u32[]{:S(2)}, u32[]{:S(2)}) collective-permute-start(f32[2,64,128]{2,1,0:T(8,128)S(1)} %both_stress.4), channel_id=1, source_target_pairs={{0,1},{1,0},{2,3},{3,2},{4,5},{5,4},{6,7},{7,6},{8,9},{9,8},{10,11... | collective-permute-start | bytes 196616 | tf_op jit(solution)/shard_map/ppermute | solution.py:33
  34.9 0.9 %collective-permute-done.6 = f32[1,64,128]{2,1,0:T(8,128)S(1)} collective-permute-done((f32[1,64,128]{2,1,0:T(8,128)S(1)}, f32[1,64,128]{2,1,0:T(8,128)S(1)}, u32[]{:S(2)}, u32[]{:S(2)}) %collective-permute-start.6) | collective-permute-done | bytes 32800 | tf_op jit(solution)/shard_map/ppermute | solution.py:33
  35.7 1.1 %collective-permute-start.7 = (f32[64,128]{1,0:T(8,128)S(1)}, f32[64,128]{1,0:T(8,128)S(1)}, u32[]{:S(2)}, u32[]{:S(2)}) collective-permute-start(f32[64,128]{1,0:T(8,128)S(1)} %add_bitcast_fusion.1), channel_id=1, source_target_pairs={{0,4},{1,5},{2,6},{3,7},{4,0},{5,1},{6,2},{7,3},{8,12},{9,13},{10,... | collective-permute-start | bytes 98312 | tf_op jit(solution)/shard_map/ppermute | solution.py:33
  36.8 1.8 %collective-permute-done.4 = f32[2,64,128]{2,1,0:T(8,128)S(1)} collective-permute-done((f32[2,64,128]{2,1,0:T(8,128)S(1)}, f32[2,64,128]{2,1,0:T(8,128)S(1)}, u32[]{:S(2)}, u32[]{:S(2)}) %collective-permute-start.4) | collective-permute-done | bytes 65568 | tf_op jit(solution)/shard_map/ppermute | solution.py:33
  38.6 1.0 %collective-permute-start.5 = (f32[1,64,128]{2,1,0:T(8,128)S(1)}, f32[1,64,128]{2,1,0:T(8,128)S(1)}, u32[]{:S(2)}, u32[]{:S(2)}) collective-permute-start(f32[1,64,128]{2,1,0:T(8,128)S(1)} %slice.17), channel_id=1, source_target_pairs={{0,2},{1,3},{2,0},{3,1},{4,6},{5,7},{6,4},{7,5},{8,10},{9,11},{10,... | collective-permute-start | bytes 98312 | tf_op jit(solution)/shard_map/ppermute | solution.py:33
  39.6 0.0 copy-done.1
  39.6 0.0 copy-done.2
  39.6 0.0 copy-done.3
  39.7 0.9 %collective-permute-done.7 = f32[64,128]{1,0:T(8,128)S(1)} collective-permute-done((f32[64,128]{1,0:T(8,128)S(1)}, f32[64,128]{1,0:T(8,128)S(1)}, u32[]{:S(2)}, u32[]{:S(2)}) %collective-permute-start.7) | collective-permute-done | bytes 32800 | tf_op jit(solution)/shard_map/ppermute | solution.py:33
  40.6 2.0 %collective-permute-done.5 = f32[1,64,128]{2,1,0:T(8,128)S(1)} collective-permute-done((f32[1,64,128]{2,1,0:T(8,128)S(1)}, f32[1,64,128]{2,1,0:T(8,128)S(1)}, u32[]{:S(2)}, u32[]{:S(2)}) %collective-permute-start.5) | collective-permute-done | bytes 32800 | tf_op jit(solution)/shard_map/ppermute | solution.py:33
  42.6 0.7 %add_bitcast_fusion = (f32[128,64]{0,1:T(8,128)}, f32[128,64]{0,1:T(8,128)}) fusion(f32[128]{0:T(128)S(1)} %get-tuple-element.17, f32[128]{0:T(128)S(1)} %copy-done.1, f32[128]{0:T(128)S(1)} %get-tuple-element.16, f32[64,128]{1,0:T(8,128)S(1)} %collective-permute-done.7, f32[1,64,128]{2,1,0:T(8,128)S(1)} %collective-permute-done.5, f32[2,64,128]{2,1,0:T(8,128)S(1)} %add.24), kind=kLoop, calls=%fused_computation.4 | loop fusion | flops 49152 | bytes 165376 | tf_op jit(solution)/shard_map/transpose | solution.py:229
  (7 shorter events, 0.1 us)
Async XLA Ops:
  0.6 24.2 %copy-start = (f32[1024,2048]{1,0:T(8,128)S(1)}, f32[1024,2048]{1,0:T(8,128)}, u32[]{:S(2)}) copy-start(f32[1024,2048]{1,0:T(8,128)} %param.7) | copy-start | bytes 25165828
  2.4 5.0 %collective-permute-start = (f32[1,9,8,128]{3,2,1,0:T(8,128)S(1)}, f32[1,9,8,128]{3,2,1,0:T(8,128)S(1)}, u32[]{:S(2)}, u32[]{:S(2)}) collective-permute-start(f32[1,9,8,128]{3,2,1,0:T(8,128)S(1)} %bitcast.24), channel_id=1, source_target_pairs={{0,16},{8,24},{16,0},{24,8},{1,17},{9,25},{17,1},{25,9},{2,18},{10... | collective-permute-start | bytes 110600 | tf_op jit(solution)/shard_map/ppermute | solution.py:33
  7.4 1.3 %collective-permute-start.1 = (f32[2,9,8,128]{3,2,1,0:T(8,128)S(1)}, f32[2,9,8,128]{3,2,1,0:T(8,128)S(1)}, u32[]{:S(2)}, u32[]{:S(2)}) collective-permute-start(f32[2,9,8,128]{3,2,1,0:T(8,128)S(1)} %pad_maximum_fusion.own_ref), channel_id=1, source_target_pairs={{0,8},{8,0},{16,24},{24,16},{1,9},{9,1},{17,25},{25,17},{2,10},{10... | collective-permute-start | bytes 221192 | tf_op jit(solution)/shard_map/ppermute | solution.py:33
  24.8 1.5 %collective-permute-start.2 = (f32[8,8,8,128]{3,2,1,0:T(8,128)S(1)}, f32[8,8,8,128]{3,2,1,0:T(8,128)S(1)}, u32[]{:S(2)}, u32[]{:S(2)}) collective-permute-start(f32[8,8,8,128]{3,2,1,0:T(8,128)S(1)} %all_to_all.5.dense_ref), channel_id=1, source_target_pairs={{0,8},{8,0},{16,24},{24,16},{1,9},{9,1},{17,25},{25,17},{2,10},{10... | collective-permute-start | bytes 786440 | tf_op jit(solution)/shard_map/ppermute | solution.py:33
  27.4 4.3 %collective-permute-start.3 = (f32[2,64,128]{2,1,0:T(8,128)S(1)}, f32[2,64,128]{2,1,0:T(8,128)S(1)}, u32[]{:S(2)}, u32[]{:S(2)}) collective-permute-start(f32[2,64,128]{2,1,0:T(8,128)S(1)} %get-tuple-element.11), channel_id=1, source_target_pairs={{0,1},{1,0},{2,3},{3,2},{4,5},{5,4},{6,7},{7,6},{8,9},{9,8},{10,11... | collective-permute-start | bytes 196616 | tf_op jit(solution)/shard_map/ppermute | solution.py:33
  30.2 9.4 %copy-start.1 = (f32[128]{0:T(128)S(1)}, f32[128]{0:T(128)}, u32[]{:S(2)}) copy-start(f32[128]{0:T(128)} %param.11) | copy-start | bytes 1540
  30.3 9.4 %copy-start.2 = (f32[128]{0:T(128)S(1)}, f32[128]{0:T(128)}, u32[]{:S(2)}) copy-start(f32[128]{0:T(128)} %param.12) | copy-start | bytes 1540
  30.3 9.4 %copy-start.3 = (f32[128]{0:T(128)S(1)}, f32[128]{0:T(128)}, u32[]{:S(2)}) copy-start(f32[128]{0:T(128)} %param.13) | copy-start | bytes 1540
  31.8 4.0 %collective-permute-start.6 = (f32[1,64,128]{2,1,0:T(8,128)S(1)}, f32[1,64,128]{2,1,0:T(8,128)S(1)}, u32[]{:S(2)}, u32[]{:S(2)}) collective-permute-start(f32[1,64,128]{2,1,0:T(8,128)S(1)} %slice.15), channel_id=1, source_target_pairs={{0,2},{1,3},{2,0},{3,1},{4,6},{5,7},{6,4},{7,5},{8,10},{9,11},{10,... | collective-permute-start | bytes 98312 | tf_op jit(solution)/shard_map/ppermute | solution.py:33
  34.3 4.3 %collective-permute-start.4 = (f32[2,64,128]{2,1,0:T(8,128)S(1)}, f32[2,64,128]{2,1,0:T(8,128)S(1)}, u32[]{:S(2)}, u32[]{:S(2)}) collective-permute-start(f32[2,64,128]{2,1,0:T(8,128)S(1)} %both_stress.4), channel_id=1, source_target_pairs={{0,1},{1,0},{2,3},{3,2},{4,5},{5,4},{6,7},{7,6},{8,9},{9,8},{10,11... | collective-permute-start | bytes 196616 | tf_op jit(solution)/shard_map/ppermute | solution.py:33
  35.7 4.8 %collective-permute-start.7 = (f32[64,128]{1,0:T(8,128)S(1)}, f32[64,128]{1,0:T(8,128)S(1)}, u32[]{:S(2)}, u32[]{:S(2)}) collective-permute-start(f32[64,128]{1,0:T(8,128)S(1)} %add_bitcast_fusion.1), channel_id=1, source_target_pairs={{0,4},{1,5},{2,6},{3,7},{4,0},{5,1},{6,2},{7,3},{8,12},{9,13},{10,... | collective-permute-start | bytes 98312 | tf_op jit(solution)/shard_map/ppermute | solution.py:33
  38.6 4.0 %collective-permute-start.5 = (f32[1,64,128]{2,1,0:T(8,128)S(1)}, f32[1,64,128]{2,1,0:T(8,128)S(1)}, u32[]{:S(2)}, u32[]{:S(2)}) collective-permute-start(f32[1,64,128]{2,1,0:T(8,128)S(1)} %slice.17), channel_id=1, source_target_pairs={{0,2},{1,3},{2,0},{3,1},{4,6},{5,7},{6,4},{7,5},{8,10},{9,11},{10,... | collective-permute-start | bytes 98312 | tf_op jit(solution)/shard_map/ppermute | solution.py:33

commit v12 on v11

--- a/solution.py
+++ b/solution.py
@@ -11,7 +11,6 @@
 SUB = 8
 CHUNK = 256
 VMEM_SPEC = pl.BlockSpec(memory_space=pltpu.VMEM)
-SMEM_SPEC = pl.BlockSpec(memory_space=pltpu.SMEM)
 HBM_SPEC = pl.BlockSpec(memory_space=pltpu.HBM)
 MIB = 1024 * 1024
 NT = (((1,), (1,)), ((), ()))
@@ -33,7 +32,7 @@
     return lax.ppermute(block, axis, [(r, r ^ k) for r in range(lax.axis_size(axis))])
 
 
-def pack_body(me_ref, slip_hbm, list_hbm, count_hbm, out_ref, slip_ref, list_ref, count_ref, ids, sems):
+def pack_body(slip_hbm, list_hbm, count_hbm, out_ref, slip_ref, list_ref, count_ref, ids, sems):
     copies = [
         pltpu.make_async_copy(src, dst, sems.at[j])
         for j, (src, dst) in enumerate(((list_hbm, list_ref), (count_hbm, count_ref), (slip_hbm, slip_ref)))
@@ -41,7 +40,7 @@
     for copy in copies:
         copy.start()
     events, entries = list_ref.shape
-    row = me_ref[0]
+    row = lax.axis_index("rows")
     entry = lax.broadcasted_iota(jnp.int32, (events, entries), 1) + row * entries
     event = lax.broadcasted_iota(jnp.int32, (events, entries), 0)
     ids[...] = jnp.full(ids.shape, -1.0, jnp.float32)
@@ -56,11 +55,11 @@
         out_ref[e, 0:entries, :] = slip_ref[e]
 
 
-def densify_body(entries, me_ref, own_ref, came_ref, _, out_ref, slips):
+def densify_body(entries, own_ref, came_ref, _, out_ref, slips):
     halves, events = own_ref.shape[0], own_ref.shape[1] - 1
     width, _, blocks, _ = out_ref.shape
     live = 2 * halves * entries
-    row = me_ref[0]
+    row = lax.axis_index("rows")
     line = lax.broadcasted_iota(jnp.int32, (width * blocks, live), 0)
     number = ((line // blocks * 2 + row % 2) * blocks + line % blocks).astype(jnp.float32)
     for e in range(events):
@@ -97,9 +96,10 @@
             out_ref[events + 2 * t * SUB : events + 2 * (t + 1) * SUB, where] = lo
 
 
-def stress(k, core, col, slip_ref, kernel_ref):
+def stress(k, other, slip_ref, kernel_ref):
+    core = lax.axis_index("rows") % 2 ^ other
     events, patches = slip_ref.shape[0] // 2, slip_ref.shape[1]
-    rows = kernel_ref.at[col ^ k]
+    rows = kernel_ref.at[lax.axis_index("cols") ^ k]
     both = low = 0.0
     for t in range(0, patches, CHUNK):
         block = rows[:, pl.ds(pl.multiple_of(core * patches + t, CHUNK), CHUNK)]
@@ -110,24 +110,21 @@
     return both[:events] + both[events:] + low
 
 
-def own_body(targets, me_ref, dense_ref, kernel_ref, slip_ref, out_ref):
+def own_body(targets, dense_ref, kernel_ref, slip_ref, out_ref):
     assemble(dense_ref, slip_ref)
     for j, k in enumerate(targets):
-        out_ref[j] = stress(k, me_ref[0] % 2, me_ref[1], slip_ref, kernel_ref)
-
-
-def other_body(targets, me_ref, dense_ref, kernel_ref, sum_ref, slip_ref, out_ref):
+        out_ref[j] = stress(k, 0, slip_ref, kernel_ref)
+
+
+def other_body(targets, dense_ref, kernel_ref, sum_ref, slip_ref, out_ref):
     assemble(dense_ref, slip_ref)
     for j, k in enumerate(targets):
-        out_ref[j] = sum_ref[j] + stress(k, 1 - me_ref[0] % 2, me_ref[1], slip_ref, kernel_ref)
-
-
-def both_body(targets, me_ref, own_ref, other_ref, kernel_ref, out_ref):
-    core = me_ref[0] % 2
+        out_ref[j] = sum_ref[j] + stress(k, 1, slip_ref, kernel_ref)
+
+
+def both_body(targets, own_ref, other_ref, kernel_ref, out_ref):
     for j, k in enumerate(targets):
-        out_ref[j] = stress(k, core, me_ref[1], own_ref, kernel_ref) + stress(
-            k, 1 - core, me_ref[1], other_ref, kernel_ref
-        )
+        out_ref[j] = stress(k, 0, own_ref, kernel_ref) + stress(k, 1, other_ref, kernel_ref)
 
 
 def halving_order(width):
@@ -142,7 +139,6 @@
     events = events_here * width
     receivers, sources = kernel.shape
     blocks_here = sources // BLOCK
-    me = jnp.stack([lax.axis_index("rows"), lax.axis_index("cols")]).astype(jnp.int32)
 
     order = halving_order(width)
     share = receivers // width
@@ -154,7 +150,7 @@
     packed = pl.pallas_call(
         pack_body,
         out_shape=f32(events_here + 1, SUB, BLOCK),
-        in_specs=[SMEM_SPEC] + [HBM_SPEC] * 3,
+        in_specs=[HBM_SPEC] * 3,
         out_specs=VMEM_SPEC,
         scratch_shapes=[
             pltpu.VMEM(slip_delta.shape, jnp.float32),
@@ -165,7 +161,7 @@
         ],
         compiler_params=params(4),
         name="pack",
-    )(me, in_hbm(slip_delta), in_hbm(block_list), in_hbm(live_count))
+    )(in_hbm(slip_delta), in_hbm(block_list), in_hbm(live_count))
     held = packed[None]
     step = 2
     while step < height:
@@ -176,19 +172,19 @@
     dense = pl.pallas_call(
         functools.partial(densify_body, entries),
         out_shape=f32(width, events_here, blocks_half, BLOCK),
-        in_specs=[SMEM_SPEC, VMEM_SPEC, VMEM_SPEC, HBM_SPEC],
+        in_specs=[VMEM_SPEC, VMEM_SPEC, HBM_SPEC],
         out_specs=VMEM_SPEC,
         scratch_shapes=[pltpu.VMEM((events_here, height * entries, BLOCK), jnp.float32)],
         compiler_params=params(8),
         name="densify",
-    )(me, held, send_xor(held, "rows", 1), in_hbm(kernel))
+    )(held, send_xor(held, "rows", 1), in_hbm(kernel))
     mine = lax.all_to_all(dense, "cols", 0, 0, tiled=True)
 
     def call(body, targets, outs, *args):
         return pl.pallas_call(
             functools.partial(body, targets),
             out_shape=outs,
-            in_specs=[SMEM_SPEC] + [VMEM_SPEC] * len(args),
+            in_specs=[VMEM_SPEC] * len(args),
             out_specs=jax.tree.map(lambda _: VMEM_SPEC, outs),
             compiler_params=params(8),
             cost_estimate=pl.CostEstimate(
@@ -197,7 +193,7 @@
                 transcendentals=0,
             ),
             name=body.__name__.removesuffix("_body") + "_stress",
-        )(me, *args)
+        )(*args)
 
     slips = bf16(2 * events, blocks_half * BLOCK)
     sums = f32(quarter, events, share)
@@ -209,10 +205,8 @@
         return call(both_body, targets, sums, own, other, kernel)
 
     far_came = send_xor(far_sent, "cols", 1)
-    near_sent = later(near_send)
+    near_came = send_xor(later(near_send), "cols", 1)
     far = later(far_keep) + far_came
-    near_sent, far = lax.optimization_barrier((near_sent, far))
-    near_came = send_xor(near_sent, "cols", 1)
     near = later(near_keep) + near_came
     step = 2
     while step < width // 2:

time: 43.4 us -> 39.9 us (0.919)
  Pallas kernels: 8.66 us -> 4.73 us
    pallas_call x5, Pallas kernels: 6.17 us -> 3.43 us  [call(): pl.pallas_call(functools.partial(body, targets), out_shape=outs, in_specs...]
    pallas_call x1, Pallas kernels: 1.68 us -> 1.03 us  [per_device(): pl.pallas_call(pack_body, out_shape=f32(events_here + 1, SUB, BLOCK), in_...]
    pallas_call x1, Pallas kernels: 0.81 us -> 0.26 us  [per_device(): pl.pallas_call(functools.partial(densify_body, entries), out_shape=f32(wi...]
  transfers between devices with their start and end apart: 8 -> 8, of which waited for: 8 -> 7; matrix products, arithmetic and copies ran while one was open for 0% -> 0% of each run, Pallas kernels for 12% -> 7%
where the time goes in v12:
time: 39.9 us; the launch traced here: 39.7 us
  blocking collectives  15.3 us (38%)
  waiting for transfers between devices  9.39 us (24%)
  starting transfers between devices  8.73 us (22%)
  Pallas kernels  4.73 us (12%)
  between operations  0.77 us (2%)
  other arithmetic  0.7 us (2%)
    all_to_all x1, blocking collectives, per_device(): mine = lax.all_to_all(dense, 'cols', 0, 0, tiled=True)  15.3 us
    ppermute x8, waiting for transfers between devices, send_xor(): lax.ppermute(block, axis, [(r, r ^ k) for r in range(lax.axis_size(axis))])  9.39 us
    ppermute x8, starting transfers between devices, send_xor(): lax.ppermute(block, axis, [(r, r ^ k) for r in range(lax.axis_size(axis))])  8.73 us
    pallas_call x5, Pallas kernels, call(): pl.pallas_call(functools.partial(body, targets), out_shape=outs, in_specs...  3.43 us
    pallas_call x1, Pallas kernels, per_device(): pl.pallas_call(pack_body, out_shape=f32(events_here + 1, SUB, BLOCK), in_...  1.03 us
  transfers between devices with their start and end apart: 8, of which 7 were waited for; matrix products, arithmetic and copies ran while one was open for 0% of the time, Pallas kernels for 7%

profile of v12, /device:TPU:0, one launch (start us, length us, event | category | flops | bytes accessed | tf_op | source)
XLA Modules:
  0.0 39.7 jit_solution(2532513607531237478)
XLA Ops:
  0.6 0.0 copy-start
  0.6 1.0 %pack.1 = f32[9,8,128]{2,1,0:T(8,128)S(1)} custom-call(f32[8,8,128]{2,1,0:T(8,128)} %slip_hbm.1, s32[8,8]{1,0:T(8,128)} %list_hbm.1, s32[8]{0:T(128)} %count_hbm.1), custom_call_target="tpu_custom_call" | custom-call | tf_op jit(solution)/shard_map/pack/pallas_call | solution.py:150
  1.7 3.0 %collective-permute-start = (f32[1,9,8,128]{3,2,1,0:T(8,128)S(1)}, f32[1,9,8,128]{3,2,1,0:T(8,128)S(1)}, u32[]{:S(2)}, u32[]{:S(2)}) collective-permute-start(f32[1,9,8,128]{3,2,1,0:T(8,128)S(1)} %bitcast.22), channel_id=1, source_target_pairs={{0,16},{8,24},{16,0},{24,8},{1,17},{9,25},{17,1},{25,9},{2,18},{10... | collective-permute-start | bytes 110600 | tf_op jit(solution)/shard_map/ppermute | solution.py:32
  4.7 1.9 %collective-permute-done = f32[1,9,8,128]{3,2,1,0:T(8,128)S(1)} collective-permute-done((f32[1,9,8,128]{3,2,1,0:T(8,128)S(1)}, f32[1,9,8,128]{3,2,1,0:T(8,128)S(1)}, u32[]{:S(2)}, u32[]{:S(2)}) %collective-permute-start) | collective-permute-done | bytes 36896 | tf_op jit(solution)/shard_map/ppermute | solution.py:32
  6.7 0.0 collective-permute-start.1
  6.7 1.3 %collective-permute-done.1.came_ref = f32[2,9,8,128]{3,2,1,0:T(8,128)S(1)} collective-permute-done((f32[2,9,8,128]{3,2,1,0:T(8,128)S(1)}, f32[2,9,8,128]{3,2,1,0:T(8,128)S(1)}, u32[]{:S(2)}, u32[]{:S(2)}) %collective-permute-start.1) | collective-permute-done | bytes 73760 | tf_op jit(solution)/shard_map/ppermute | solution.py:32
  7.9 0.3 densify.1
  8.2 15.3 %all_to_all.5.dense_ref = f32[8,8,8,128]{3,2,1,0:T(8,128)S(1)} all-to-all(f32[8,8,8,128]{3,2,1,0:T(8,128)S(1)} %densify.1), channel_id=1, replica_groups=mesh['rows'=4,'cols'=8] {'cols'}, dimensions={0} | all-to-all | bytes 524288 | tf_op jit(solution)/shard_map/all_to_all | solution.py:181
  23.5 0.0 collective-permute-start.2
  23.5 0.0 copy-done
  23.5 0.5 %own_stress.1 = (bf16[128,1024]{1,0:T(8,128)(2,1)S(1)}, f32[2,64,128]{2,1,0:T(8,128)S(1)}) custom-call(f32[8,8,8,128]{3,2,1,0:T(8,128)S(1)} %all_to_all.5.dense_ref, f32[8,128,2048]{2,1,0:T(8,128)S(1)} %bitcast.17), custom_call_target="tpu_custom_call" | custom-call | flops 201326592 | bytes 2097152 | tf_op jit(solution)/shard_map/own_stress/pallas_call | solution.py:184
  24.1 1.0 %collective-permute-done.2.dense_ref = f32[8,8,8,128]{3,2,1,0:T(8,128)S(1)} collective-permute-done((f32[8,8,8,128]{3,2,1,0:T(8,128)S(1)}, f32[8,8,8,128]{3,2,1,0:T(8,128)S(1)}, u32[]{:S(2)}, u32[]{:S(2)}) %collective-permute-start.2) | collective-permute-done | bytes 262176 | tf_op jit(solution)/shard_map/ppermute | solution.py:32
  25.1 0.5 %other_stress.1 = (bf16[128,1024]{1,0:T(8,128)(2,1)S(1)}, f32[2,64,128]{2,1,0:T(8,128)S(1)}) custom-call(f32[8,8,8,128]{3,2,1,0:T(8,128)S(1)} %collective-permute-done.2.dense_ref, f32[8,128,2048]{2,1,0:T(8,128)S(1)} %bitcast.18, f32[2,64,128]{2,1,0:T(8,128)S(1)} %get-tuple-element.7.sum_ref), custom_call_target="tpu_custom_call" | custom-call | flops 201326592 | bytes 2097152 | tf_op jit(solution)/shard_map/other_stress/pallas_call | solution.py:184
  25.6 1.5 %collective-permute-start.5 = (f32[2,64,128]{2,1,0:T(8,128)S(1)}, f32[2,64,128]{2,1,0:T(8,128)S(1)}, u32[]{:S(2)}, u32[]{:S(2)}) collective-permute-start(f32[2,64,128]{2,1,0:T(8,128)S(1)} %get-tuple-element.9), channel_id=1, source_target_pairs={{0,1},{1,0},{2,3},{3,2},{4,5},{5,4},{6,7},{7,6},{8,9},{9,8},{10,11... | collective-permute-start | bytes 196616 | tf_op jit(solution)/shard_map/ppermute | solution.py:32
  27.1 0.8 %both_stress.4 = f32[2,64,128]{2,1,0:T(8,128)S(1)} custom-call(bf16[128,1024]{1,0:T(8,128)(2,1)S(1)} %get-tuple-element.6.own_ref, bf16[128,1024]{1,0:T(8,128)(2,1)S(1)} %get-tuple-element.8.other_ref, f32[8,128,2048]{2,1,0:T(8,128)S(1)} %bitcast.19), custom_call_target="tpu_custom_call" | custom-call | flops 201326592 | bytes 2097152 | tf_op jit(solution)/shard_map/both_stress/pallas_call | solution.py:184
  27.9 0.0 copy-start.1
  27.9 0.0 copy-start.2
  27.9 0.0 copy-start.3
  27.9 0.7 %collective-permute-start.3 = (f32[2,64,128]{2,1,0:T(8,128)S(1)}, f32[2,64,128]{2,1,0:T(8,128)S(1)}, u32[]{:S(2)}, u32[]{:S(2)}) collective-permute-start(f32[2,64,128]{2,1,0:T(8,128)S(1)} %both_stress.4), channel_id=1, source_target_pairs={{0,1},{1,0},{2,3},{3,2},{4,5},{5,4},{6,7},{7,6},{8,9},{9,8},{10,11... | collective-permute-start | bytes 196616 | tf_op jit(solution)/shard_map/ppermute | solution.py:32
  28.6 0.8 %both_stress.5 = f32[2,64,128]{2,1,0:T(8,128)S(1)} custom-call(bf16[128,1024]{1,0:T(8,128)(2,1)S(1)} %get-tuple-element.6.own_ref, bf16[128,1024]{1,0:T(8,128)(2,1)S(1)} %get-tuple-element.8.other_ref, f32[8,128,2048]{2,1,0:T(8,128)S(1)} %bitcast.20), custom_call_target="tpu_custom_call" | custom-call | flops 201326592 | bytes 2097152 | tf_op jit(solution)/shard_map/both_stress/pallas_call | solution.py:184
  29.4 0.5 %collective-permute-done.5 = f32[2,64,128]{2,1,0:T(8,128)S(1)} collective-permute-done((f32[2,64,128]{2,1,0:T(8,128)S(1)}, f32[2,64,128]{2,1,0:T(8,128)S(1)}, u32[]{:S(2)}, u32[]{:S(2)}) %collective-permute-start.5) | collective-permute-done | bytes 65568 | tf_op jit(solution)/shard_map/ppermute | solution.py:32
  29.9 1.6 %collective-permute-start.6 = (f32[1,64,128]{2,1,0:T(8,128)S(1)}, f32[1,64,128]{2,1,0:T(8,128)S(1)}, u32[]{:S(2)}, u32[]{:S(2)}) collective-permute-start(f32[1,64,128]{2,1,0:T(8,128)S(1)} %slice.19), channel_id=1, source_target_pairs={{0,2},{1,3},{2,0},{3,1},{4,6},{5,7},{6,4},{7,5},{8,10},{9,11},{10,... | collective-permute-start | bytes 98312 | tf_op jit(solution)/shard_map/ppermute | solution.py:32
  31.6 0.8 %both_stress.3 = f32[2,64,128]{2,1,0:T(8,128)S(1)} custom-call(bf16[128,1024]{1,0:T(8,128)(2,1)S(1)} %get-tuple-element.6.own_ref, bf16[128,1024]{1,0:T(8,128)(2,1)S(1)} %get-tuple-element.8.other_ref, f32[8,128,2048]{2,1,0:T(8,128)S(1)} %bitcast.21), custom_call_target="tpu_custom_call" | custom-call | flops 201326592 | bytes 2097152 | tf_op jit(solution)/shard_map/both_stress/pallas_call | solution.py:184
  32.4 0.0 collective-permute-done.3
  32.4 0.5 %collective-permute-start.4 = (f32[1,64,128]{2,1,0:T(8,128)S(1)}, f32[1,64,128]{2,1,0:T(8,128)S(1)}, u32[]{:S(2)}, u32[]{:S(2)}) collective-permute-start(f32[1,64,128]{2,1,0:T(8,128)S(1)} %slice.17), channel_id=1, source_target_pairs={{0,2},{1,3},{2,0},{3,1},{4,6},{5,7},{6,4},{7,5},{8,10},{9,11},{10,... | collective-permute-start | bytes 98312 | tf_op jit(solution)/shard_map/ppermute | solution.py:32
  33.0 1.2 %collective-permute-done.6 = f32[1,64,128]{2,1,0:T(8,128)S(1)} collective-permute-done((f32[1,64,128]{2,1,0:T(8,128)S(1)}, f32[1,64,128]{2,1,0:T(8,128)S(1)}, u32[]{:S(2)}, u32[]{:S(2)}) %collective-permute-start.6) | collective-permute-done | bytes 32800 | tf_op jit(solution)/shard_map/ppermute | solution.py:32
  34.2 1.4 %collective-permute-start.7 = (f32[64,128]{1,0:T(8,128)S(1)}, f32[64,128]{1,0:T(8,128)S(1)}, u32[]{:S(2)}, u32[]{:S(2)}) collective-permute-start(f32[64,128]{1,0:T(8,128)S(1)} %fusion), channel_id=1, source_target_pairs={{0,4},{1,5},{2,6},{3,7},{4,0},{5,1},{6,2},{7,3},{8,12},{9,13},{10,... | collective-permute-start | bytes 98312 | tf_op jit(solution)/shard_map/ppermute | solution.py:32
  35.6 0.0 copy-done.1
  35.6 0.0 copy-done.2
  35.6 0.0 copy-done.3
  35.6 0.9 %collective-permute-done.4 = f32[1,64,128]{2,1,0:T(8,128)S(1)} collective-permute-done((f32[1,64,128]{2,1,0:T(8,128)S(1)}, f32[1,64,128]{2,1,0:T(8,128)S(1)}, u32[]{:S(2)}, u32[]{:S(2)}) %collective-permute-start.4) | collective-permute-done | bytes 32800 | tf_op jit(solution)/shard_map/ppermute | solution.py:32
  36.5 2.6 %collective-permute-done.7 = f32[64,128]{1,0:T(8,128)S(1)} collective-permute-done((f32[64,128]{1,0:T(8,128)S(1)}, f32[64,128]{1,0:T(8,128)S(1)}, u32[]{:S(2)}, u32[]{:S(2)}) %collective-permute-start.7) | collective-permute-done | bytes 32800 | tf_op jit(solution)/shard_map/ppermute | solution.py:32
  39.0 0.7 %add_bitcast_fusion = (f32[128,64]{0,1:T(8,128)}, f32[128,64]{0,1:T(8,128)}) fusion(f32[128]{0:T(128)S(1)} %get-tuple-element.13, f32[128]{0:T(128)S(1)} %copy-done.1, f32[128]{0:T(128)S(1)} %get-tuple-element.12, f32[64,128]{1,0:T(8,128)S(1)} %collective-permute-done.7, f32[1,64,128]{2,1,0:T(8,128)S(1)} %collective-permute-done.4, f32[2,64,128]{2,1,0:T(8,128)S(1)} %add.23), kind=kLoop, calls=%fused_computation.6 | loop fusion | flops 49152 | bytes 165376 | tf_op jit(solution)/shard_map/transpose | solution.py:223
  (7 shorter events, 0.1 us)
Async XLA Ops:
  0.6 22.9 %copy-start = (f32[1024,2048]{1,0:T(8,128)S(1)}, f32[1024,2048]{1,0:T(8,128)}, u32[]{:S(2)}) copy-start(f32[1024,2048]{1,0:T(8,128)} %param.7) | copy-start | bytes 25165828
  1.7 5.0 %collective-permute-start = (f32[1,9,8,128]{3,2,1,0:T(8,128)S(1)}, f32[1,9,8,128]{3,2,1,0:T(8,128)S(1)}, u32[]{:S(2)}, u32[]{:S(2)}) collective-permute-start(f32[1,9,8,128]{3,2,1,0:T(8,128)S(1)} %bitcast.22), channel_id=1, source_target_pairs={{0,16},{8,24},{16,0},{24,8},{1,17},{9,25},{17,1},{25,9},{2,18},{10... | collective-permute-start | bytes 110600 | tf_op jit(solution)/shard_map/ppermute | solution.py:32
  6.7 1.3 %collective-permute-start.1 = (f32[2,9,8,128]{3,2,1,0:T(8,128)S(1)}, f32[2,9,8,128]{3,2,1,0:T(8,128)S(1)}, u32[]{:S(2)}, u32[]{:S(2)}) collective-permute-start(f32[2,9,8,128]{3,2,1,0:T(8,128)S(1)} %pad_maximum_fusion.own_ref), channel_id=1, source_target_pairs={{0,8},{8,0},{16,24},{24,16},{1,9},{9,1},{17,25},{25,17},{2,10},{10... | collective-permute-start | bytes 221192 | tf_op jit(solution)/shard_map/ppermute | solution.py:32
  23.5 1.5 %collective-permute-start.2 = (f32[8,8,8,128]{3,2,1,0:T(8,128)S(1)}, f32[8,8,8,128]{3,2,1,0:T(8,128)S(1)}, u32[]{:S(2)}, u32[]{:S(2)}) collective-permute-start(f32[8,8,8,128]{3,2,1,0:T(8,128)S(1)} %all_to_all.5.dense_ref), channel_id=1, source_target_pairs={{0,8},{8,0},{16,24},{24,16},{1,9},{9,1},{17,25},{25,17},{2,10},{10... | collective-permute-start | bytes 786440 | tf_op jit(solution)/shard_map/ppermute | solution.py:32
  25.6 4.3 %collective-permute-start.5 = (f32[2,64,128]{2,1,0:T(8,128)S(1)}, f32[2,64,128]{2,1,0:T(8,128)S(1)}, u32[]{:S(2)}, u32[]{:S(2)}) collective-permute-start(f32[2,64,128]{2,1,0:T(8,128)S(1)} %get-tuple-element.9), channel_id=1, source_target_pairs={{0,1},{1,0},{2,3},{3,2},{4,5},{5,4},{6,7},{7,6},{8,9},{9,8},{10,11... | collective-permute-start | bytes 196616 | tf_op jit(solution)/shard_map/ppermute | solution.py:32
  27.9 7.7 %copy-start.1 = (f32[128]{0:T(128)S(1)}, f32[128]{0:T(128)}, u32[]{:S(2)}) copy-start(f32[128]{0:T(128)} %param.11) | copy-start | bytes 1540
  27.9 7.7 %copy-start.2 = (f32[128]{0:T(128)S(1)}, f32[128]{0:T(128)}, u32[]{:S(2)}) copy-start(f32[128]{0:T(128)} %param.12) | copy-start | bytes 1540
  27.9 7.7 %copy-start.3 = (f32[128]{0:T(128)S(1)}, f32[128]{0:T(128)}, u32[]{:S(2)}) copy-start(f32[128]{0:T(128)} %param.13) | copy-start | bytes 1540
  27.9 4.5 %collective-permute-start.3 = (f32[2,64,128]{2,1,0:T(8,128)S(1)}, f32[2,64,128]{2,1,0:T(8,128)S(1)}, u32[]{:S(2)}, u32[]{:S(2)}) collective-permute-start(f32[2,64,128]{2,1,0:T(8,128)S(1)} %both_stress.4), channel_id=1, source_target_pairs={{0,1},{1,0},{2,3},{3,2},{4,5},{5,4},{6,7},{7,6},{8,9},{9,8},{10,11... | collective-permute-start | bytes 196616 | tf_op jit(solution)/shard_map/ppermute | solution.py:32
  29.9 4.3 %collective-permute-start.6 = (f32[1,64,128]{2,1,0:T(8,128)S(1)}, f32[1,64,128]{2,1,0:T(8,128)S(1)}, u32[]{:S(2)}, u32[]{:S(2)}) collective-permute-start(f32[1,64,128]{2,1,0:T(8,128)S(1)} %slice.19), channel_id=1, source_target_pairs={{0,2},{1,3},{2,0},{3,1},{4,6},{5,7},{6,4},{7,5},{8,10},{9,11},{10,... | collective-permute-start | bytes 98312 | tf_op jit(solution)/shard_map/ppermute | solution.py:32
  32.4 4.0 %collective-permute-start.4 = (f32[1,64,128]{2,1,0:T(8,128)S(1)}, f32[1,64,128]{2,1,0:T(8,128)S(1)}, u32[]{:S(2)}, u32[]{:S(2)}) collective-permute-start(f32[1,64,128]{2,1,0:T(8,128)S(1)} %slice.17), channel_id=1, source_target_pairs={{0,2},{1,3},{2,0},{3,1},{4,6},{5,7},{6,4},{7,5},{8,10},{9,11},{10,... | collective-permute-start | bytes 98312 | tf_op jit(solution)/shard_map/ppermute | solution.py:32
  34.2 4.8 %collective-permute-start.7 = (f32[64,128]{1,0:T(8,128)S(1)}, f32[64,128]{1,0:T(8,128)S(1)}, u32[]{:S(2)}, u32[]{:S(2)}) collective-permute-start(f32[64,128]{1,0:T(8,128)S(1)} %fusion), channel_id=1, source_target_pairs={{0,4},{1,5},{2,6},{3,7},{4,0},{5,1},{6,2},{7,3},{8,12},{9,13},{10,... | collective-permute-start | bytes 98312 | tf_op jit(solution)/shard_map/ppermute | solution.py:32

commit v13 on v12

--- a/solution.py
+++ b/solution.py
@@ -55,24 +55,23 @@
         out_ref[e, 0:entries, :] = slip_ref[e]
 
 
-def densify_body(entries, own_ref, came_ref, _, out_ref, slips):
-    halves, events = own_ref.shape[0], own_ref.shape[1] - 1
+def densify_body(entries, *refs):
+    ins, (_, out_ref, slips) = refs[:-3], refs[-3:]
+    events = ins[0].shape[0] - 1
     width, _, blocks, _ = out_ref.shape
-    live = 2 * halves * entries
+    live = len(ins) * entries
     row = lax.axis_index("rows")
     line = lax.broadcasted_iota(jnp.int32, (width * blocks, live), 0)
     number = ((line // blocks * 2 + row % 2) * blocks + line % blocks).astype(jnp.float32)
     for e in range(events):
         ids = jnp.full((1, BLOCK), -1.0, jnp.float32)
-        for ref in (own_ref, came_ref):
-            for j in range(halves):
-                ids = jnp.maximum(ids, ref[j, events, e : e + 1, :])
+        for ref in ins:
+            ids = jnp.maximum(ids, ref[events, e : e + 1, :])
         ids = jnp.broadcast_to(ids, (width * blocks, BLOCK))[:, :live]
         onehot = (ids == number).astype(jnp.bfloat16)
-        for core, ref in enumerate((own_ref, came_ref)):
-            for j in range(halves):
-                source = row ^ (2 * j + core)
-                slips[e, pl.ds(pl.multiple_of(source * entries, entries), entries), :] = ref[j, e, 0:entries, :]
+        for k, ref in enumerate(ins):
+            where = pl.ds(pl.multiple_of((row ^ k) * entries, entries), entries)
+            slips[e, where, :] = ref[e, 0:entries, :]
         slip = slips[e]
         total = jnp.zeros((width * blocks, BLOCK), jnp.float32)
         for _ in range(3):
@@ -110,14 +109,19 @@
     return both[:events] + both[events:] + low
 
 
-def own_body(targets, dense_ref, kernel_ref, slip_ref, out_ref):
+def own_body(targets, dense_ref, kernel_ref, slip_ref, *out_refs):
     assemble(dense_ref, slip_ref)
-    for j, k in enumerate(targets):
-        out_ref[j] = stress(k, 0, slip_ref, kernel_ref)
+    for group, out_ref in zip(targets, out_refs):
+        for j, k in enumerate(group):
+            out_ref[j] = stress(k, 0, slip_ref, kernel_ref)
 
 
 def other_body(targets, dense_ref, kernel_ref, sum_ref, slip_ref, out_ref):
     assemble(dense_ref, slip_ref)
+    rest_body(targets, slip_ref, kernel_ref, sum_ref, out_ref)
+
+
+def rest_body(targets, slip_ref, kernel_ref, sum_ref, out_ref):
     for j, k in enumerate(targets):
         out_ref[j] = sum_ref[j] + stress(k, 1, slip_ref, kernel_ref)
 
@@ -162,22 +166,17 @@
         compiler_params=params(4),
         name="pack",
     )(in_hbm(slip_delta), in_hbm(block_list), in_hbm(live_count))
-    held = packed[None]
-    step = 2
-    while step < height:
-        held = jnp.concatenate([held, send_xor(held, "rows", step)], axis=0)
-        step *= 2
-
+    came = {k: send_xor(packed, "rows", k) for k in sorted(range(1, height), key=lambda k: (k < 2, k))}
     blocks_half = blocks_here // 2
     dense = pl.pallas_call(
         functools.partial(densify_body, entries),
         out_shape=f32(width, events_here, blocks_half, BLOCK),
-        in_specs=[VMEM_SPEC, VMEM_SPEC, HBM_SPEC],
+        in_specs=[VMEM_SPEC] * height + [HBM_SPEC],
         out_specs=VMEM_SPEC,
         scratch_shapes=[pltpu.VMEM((events_here, height * entries, BLOCK), jnp.float32)],
         compiler_params=params(8),
         name="densify",
-    )(held, send_xor(held, "rows", 1), in_hbm(kernel))
+    )(packed, *(came[k] for k in range(1, height)), in_hbm(kernel))
     mine = lax.all_to_all(dense, "cols", 0, 0, tiled=True)
 
     def call(body, targets, outs, *args):
@@ -198,14 +197,14 @@
     slips = bf16(2 * events, blocks_half * BLOCK)
     sums = f32(quarter, events, share)
     came = send_xor(mine, "rows", 1)
-    own, own_sum = call(own_body, far_send, [slips, sums], mine, kernel)
-    other, far_sent = call(other_body, far_send, [slips, sums], came, kernel, own_sum)
+    own, far_own, near_own = call(own_body, (far_send, near_send), [slips, sums, sums], mine, kernel)
+    other, far_sent = call(other_body, far_send, [slips, sums], came, kernel, far_own)
 
     def later(targets):
         return call(both_body, targets, sums, own, other, kernel)
 
     far_came = send_xor(far_sent, "cols", 1)
-    near_came = send_xor(later(near_send), "cols", 1)
+    near_came = send_xor(call(rest_body, near_send, sums, other, kernel, near_own), "cols", 1)
     far = later(far_keep) + far_came
     near = later(near_keep) + near_came
     step = 2

time: 39.9 us -> 39.5 us (0.990)
  blocking collectives: 15.3 us -> 14.9 us
    all_to_all x1, blocking collectives: 15.3 us -> 14.9 us  [per_device(): mine = lax.all_to_all(dense, 'cols', 0, 0, tiled=True)]
    ppermute x8 -> x9, starting transfers between devices: 8.73 us -> 9.05 us  [send_xor(): lax.ppermute(block, axis, [(r, r ^ k) for r in range(lax.axis_size(axis))])]
    ppermute x8 -> x9, waiting for transfers between devices: 9.39 us -> 9.17 us  [send_xor(): lax.ppermute(block, axis, [(r, r ^ k) for r in range(lax.axis_size(axis))])]
  transfers between devices with their start and end apart: 8 -> 9, of which waited for: 7 -> 7; matrix products, arithmetic and copies ran while one was open for 0% -> 0% of each run, Pallas kernels for 7% -> 8%
where the time goes in v13:
time: 39.5 us; the launch traced here: 39.3 us
  blocking collectives  14.9 us (38%)
  waiting for transfers between devices  9.17 us (23%)
  starting transfers between devices  9.05 us (23%)
  Pallas kernels  4.76 us (12%)
  between operations  0.74 us (2%)
  other arithmetic  0.7 us (2%)
    all_to_all x1, blocking collectives, per_device(): mine = lax.all_to_all(dense, 'cols', 0, 0, tiled=True)  14.9 us
    ppermute x9, waiting for transfers between devices, send_xor(): lax.ppermute(block, axis, [(r, r ^ k) for r in range(lax.axis_size(axis))])  9.17 us
    ppermute x9, starting transfers between devices, send_xor(): lax.ppermute(block, axis, [(r, r ^ k) for r in range(lax.axis_size(axis))])  9.05 us
    pallas_call x5, Pallas kernels, call(): pl.pallas_call(functools.partial(body, targets), out_shape=outs, in_specs...  3.46 us
    pallas_call x1, Pallas kernels, per_device(): pl.pallas_call(pack_body, out_shape=f32(events_here + 1, SUB, BLOCK), in_...  1.03 us
  transfers between devices with their start and end apart: 9, of which 7 were waited for; matrix products, arithmetic and copies ran while one was open for 0% of the time, Pallas kernels for 8%

profile of v13, /device:TPU:0, one launch (start us, length us, event | category | flops | bytes accessed | tf_op | source)
XLA Modules:
  0.0 39.3 jit_solution(12234716397173701278)
XLA Ops:
  0.6 0.0 copy-start
  0.6 1.0 %pack.1.refs_0_ = f32[9,8,128]{2,1,0:T(8,128)S(1)} custom-call(f32[8,8,128]{2,1,0:T(8,128)} %slip_hbm.1, s32[8,8]{1,0:T(8,128)} %list_hbm.1, s32[8]{0:T(128)} %count_hbm.1), custom_call_target="tpu_custom_call" | custom-call | tf_op jit(solution)/shard_map/pack/pallas_call | solution.py:154
  1.7 0.5 %collective-permute-start = (f32[9,8,128]{2,1,0:T(8,128)S(1)}, f32[9,8,128]{2,1,0:T(8,128)S(1)}, u32[]{:S(2)}, u32[]{:S(2)}) collective-permute-start(f32[9,8,128]{2,1,0:T(8,128)S(1)} %pack.1.refs_0_), channel_id=1, source_target_pairs={{0,8},{8,0},{16,24},{24,16},{1,9},{9,1},{17,25},{25,17},{2,10},{10... | collective-permute-start | bytes 110600 | tf_op jit(solution)/shard_map/ppermute | solution.py:32
  2.2 2.6 %collective-permute-start.1 = (f32[9,8,128]{2,1,0:T(8,128)S(1)}, f32[9,8,128]{2,1,0:T(8,128)S(1)}, u32[]{:S(2)}, u32[]{:S(2)}) collective-permute-start(f32[9,8,128]{2,1,0:T(8,128)S(1)} %pack.1.refs_0_), channel_id=1, source_target_pairs={{0,16},{8,24},{16,0},{24,8},{1,17},{9,25},{17,1},{25,9},{2,18},{10... | collective-permute-start | bytes 110600 | tf_op jit(solution)/shard_map/ppermute | solution.py:32
  4.8 0.1 collective-permute-start.2
  4.9 0.0 collective-permute-done.refs_1_
  4.9 2.0 %collective-permute-done.1.refs_2_ = f32[9,8,128]{2,1,0:T(8,128)S(1)} collective-permute-done((f32[9,8,128]{2,1,0:T(8,128)S(1)}, f32[9,8,128]{2,1,0:T(8,128)S(1)}, u32[]{:S(2)}, u32[]{:S(2)}) %collective-permute-start.1) | collective-permute-done | bytes 36896 | tf_op jit(solution)/shard_map/ppermute | solution.py:32
  6.9 1.4 %collective-permute-done.2.refs_3_ = f32[9,8,128]{2,1,0:T(8,128)S(1)} collective-permute-done((f32[9,8,128]{2,1,0:T(8,128)S(1)}, f32[9,8,128]{2,1,0:T(8,128)S(1)}, u32[]{:S(2)}, u32[]{:S(2)}) %collective-permute-start.2) | collective-permute-done | bytes 36896 | tf_op jit(solution)/shard_map/ppermute | solution.py:32
  8.2 0.3 densify.1
  8.5 14.9 %all_to_all.5.dense_ref = f32[8,8,8,128]{3,2,1,0:T(8,128)S(1)} all-to-all(f32[8,8,8,128]{3,2,1,0:T(8,128)S(1)} %densify.1), channel_id=1, replica_groups=mesh['rows'=4,'cols'=8] {'cols'}, dimensions={0} | all-to-all | bytes 524288 | tf_op jit(solution)/shard_map/all_to_all | solution.py:180
  23.3 0.0 collective-permute-start.3
  23.4 0.0 copy-done
  23.4 0.8 %own_stress.1 = (bf16[128,1024]{1,0:T(8,128)(2,1)S(1)}, f32[2,64,128]{2,1,0:T(8,128)S(1)}, f32[2,64,128]{2,1,0:T(8,128)S(1)}) custom-call(f32[8,8,8,128]{3,2,1,0:T(8,128)S(1)} %all_to_all.5.dense_ref, f32[8,128,2048]{2,1,0:T(8,128)S(1)} %bitcast.16), custom_call_target="tpu_custom_call" | custom-call | flops 201326592 | bytes 2097152 | tf_op jit(solution)/shard_map/own_stress/pallas_call | solution.py:183
  24.2 0.7 %collective-permute-done.3.dense_ref = f32[8,8,8,128]{3,2,1,0:T(8,128)S(1)} collective-permute-done((f32[8,8,8,128]{3,2,1,0:T(8,128)S(1)}, f32[8,8,8,128]{3,2,1,0:T(8,128)S(1)}, u32[]{:S(2)}, u32[]{:S(2)}) %collective-permute-start.3) | collective-permute-done | bytes 262176 | tf_op jit(solution)/shard_map/ppermute | solution.py:32
  24.9 0.5 %other_stress.1 = (bf16[128,1024]{1,0:T(8,128)(2,1)S(1)}, f32[2,64,128]{2,1,0:T(8,128)S(1)}) custom-call(f32[8,8,8,128]{3,2,1,0:T(8,128)S(1)} %collective-permute-done.3.dense_ref, f32[8,128,2048]{2,1,0:T(8,128)S(1)} %bitcast.17, f32[2,64,128]{2,1,0:T(8,128)S(1)} %get-tuple-element.8.sum_ref), custom_call_target="tpu_custom_call" | custom-call | flops 201326592 | bytes 2097152 | tf_op jit(solution)/shard_map/other_stress/pallas_call | solution.py:183
  25.4 1.5 %collective-permute-start.6 = (f32[2,64,128]{2,1,0:T(8,128)S(1)}, f32[2,64,128]{2,1,0:T(8,128)S(1)}, u32[]{:S(2)}, u32[]{:S(2)}) collective-permute-start(f32[2,64,128]{2,1,0:T(8,128)S(1)} %get-tuple-element.11), channel_id=1, source_target_pairs={{0,1},{1,0},{2,3},{3,2},{4,5},{5,4},{6,7},{7,6},{8,9},{9,8},{10,11... | collective-permute-start | bytes 196616 | tf_op jit(solution)/shard_map/ppermute | solution.py:32
  26.9 0.5 %rest_stress.1 = f32[2,64,128]{2,1,0:T(8,128)S(1)} custom-call(bf16[128,1024]{1,0:T(8,128)(2,1)S(1)} %get-tuple-element.9.other_ref.slip_ref, f32[8,128,2048]{2,1,0:T(8,128)S(1)} %bitcast.18, f32[2,64,128]{2,1,0:T(8,128)S(1)} %get-tuple-element.10.sum_ref), custom_call_target="tpu_custom_call" | custom-call | flops 201326592 | bytes 2097152 | tf_op jit(solution)/shard_map/rest_stress/pallas_call | solution.py:183
  27.4 0.7 %collective-permute-start.4 = (f32[2,64,128]{2,1,0:T(8,128)S(1)}, f32[2,64,128]{2,1,0:T(8,128)S(1)}, u32[]{:S(2)}, u32[]{:S(2)}) collective-permute-start(f32[2,64,128]{2,1,0:T(8,128)S(1)} %rest_stress.1), channel_id=1, source_target_pairs={{0,1},{1,0},{2,3},{3,2},{4,5},{5,4},{6,7},{7,6},{8,9},{9,8},{10,11... | collective-permute-start | bytes 196616 | tf_op jit(solution)/shard_map/ppermute | solution.py:32
  28.0 0.0 copy-start.1
  28.0 0.0 copy-start.2
  28.1 0.0 copy-start.3
  28.1 0.8 %both_stress.3 = f32[2,64,128]{2,1,0:T(8,128)S(1)} custom-call(bf16[128,1024]{1,0:T(8,128)(2,1)S(1)} %get-tuple-element.7.own_ref, bf16[128,1024]{1,0:T(8,128)(2,1)S(1)} %get-tuple-element.9.other_ref.slip_ref, f32[8,128,2048]{2,1,0:T(8,128)S(1)} %bitcast.19), custom_call_target="tpu_custom_call" | custom-call | flops 201326592 | bytes 2097152 | tf_op jit(solution)/shard_map/both_stress/pallas_call | solution.py:183
  28.9 0.9 %collective-permute-done.6 = f32[2,64,128]{2,1,0:T(8,128)S(1)} collective-permute-done((f32[2,64,128]{2,1,0:T(8,128)S(1)}, f32[2,64,128]{2,1,0:T(8,128)S(1)}, u32[]{:S(2)}, u32[]{:S(2)}) %collective-permute-start.6) | collective-permute-done | bytes 65568 | tf_op jit(solution)/shard_map/ppermute | solution.py:32
  29.8 1.7 %collective-permute-start.7 = (f32[1,64,128]{2,1,0:T(8,128)S(1)}, f32[1,64,128]{2,1,0:T(8,128)S(1)}, u32[]{:S(2)}, u32[]{:S(2)}) collective-permute-start(f32[1,64,128]{2,1,0:T(8,128)S(1)} %slice.19), channel_id=1, source_target_pairs={{0,2},{1,3},{2,0},{3,1},{4,6},{5,7},{6,4},{7,5},{8,10},{9,11},{10,... | collective-permute-start | bytes 98312 | tf_op jit(solution)/shard_map/ppermute | solution.py:32
  31.5 0.8 %both_stress.2 = f32[2,64,128]{2,1,0:T(8,128)S(1)} custom-call(bf16[128,1024]{1,0:T(8,128)(2,1)S(1)} %get-tuple-element.7.own_ref, bf16[128,1024]{1,0:T(8,128)(2,1)S(1)} %get-tuple-element.9.other_ref.slip_ref, f32[8,128,2048]{2,1,0:T(8,128)S(1)} %bitcast.20), custom_call_target="tpu_custom_call" | custom-call | flops 201326592 | bytes 2097152 | tf_op jit(solution)/shard_map/both_stress/pallas_call | solution.py:183
  32.3 0.0 collective-permute-done.4
  32.3 0.5 %collective-permute-start.5 = (f32[1,64,128]{2,1,0:T(8,128)S(1)}, f32[1,64,128]{2,1,0:T(8,128)S(1)}, u32[]{:S(2)}, u32[]{:S(2)}) collective-permute-start(f32[1,64,128]{2,1,0:T(8,128)S(1)} %slice.17), channel_id=1, source_target_pairs={{0,2},{1,3},{2,0},{3,1},{4,6},{5,7},{6,4},{7,5},{8,10},{9,11},{10,... | collective-permute-start | bytes 98312 | tf_op jit(solution)/shard_map/ppermute | solution.py:32
  32.8 1.0 %collective-permute-done.7 = f32[1,64,128]{2,1,0:T(8,128)S(1)} collective-permute-done((f32[1,64,128]{2,1,0:T(8,128)S(1)}, f32[1,64,128]{2,1,0:T(8,128)S(1)}, u32[]{:S(2)}, u32[]{:S(2)}) %collective-permute-start.7) | collective-permute-done | bytes 32800 | tf_op jit(solution)/shard_map/ppermute | solution.py:32
  33.8 1.6 %collective-permute-start.8 = (f32[64,128]{1,0:T(8,128)S(1)}, f32[64,128]{1,0:T(8,128)S(1)}, u32[]{:S(2)}, u32[]{:S(2)}) collective-permute-start(f32[64,128]{1,0:T(8,128)S(1)} %fusion), channel_id=1, source_target_pairs={{0,4},{1,5},{2,6},{3,7},{4,0},{5,1},{6,2},{7,3},{8,12},{9,13},{10,... | collective-permute-start | bytes 98312 | tf_op jit(solution)/shard_map/ppermute | solution.py:32
  35.4 0.0 copy-done.1
  35.4 0.0 copy-done.2
  35.4 0.0 copy-done.3
  35.4 0.9 %collective-permute-done.5 = f32[1,64,128]{2,1,0:T(8,128)S(1)} collective-permute-done((f32[1,64,128]{2,1,0:T(8,128)S(1)}, f32[1,64,128]{2,1,0:T(8,128)S(1)}, u32[]{:S(2)}, u32[]{:S(2)}) %collective-permute-start.5) | collective-permute-done | bytes 32800 | tf_op jit(solution)/shard_map/ppermute | solution.py:32
  36.3 2.3 %collective-permute-done.8 = f32[64,128]{1,0:T(8,128)S(1)} collective-permute-done((f32[64,128]{1,0:T(8,128)S(1)}, f32[64,128]{1,0:T(8,128)S(1)}, u32[]{:S(2)}, u32[]{:S(2)}) %collective-permute-start.8) | collective-permute-done | bytes 32800 | tf_op jit(solution)/shard_map/ppermute | solution.py:32
  38.6 0.7 %add_bitcast_fusion = (f32[128,64]{0,1:T(8,128)}, f32[128,64]{0,1:T(8,128)}) fusion(f32[128]{0:T(128)S(1)} %get-tuple-element.15, f32[128]{0:T(128)S(1)} %copy-done.1, f32[128]{0:T(128)S(1)} %get-tuple-element.14, f32[64,128]{1,0:T(8,128)S(1)} %collective-permute-done.8, f32[1,64,128]{2,1,0:T(8,128)S(1)} %collective-permute-done.5, f32[2,64,128]{2,1,0:T(8,128)S(1)} %add.23), kind=kLoop, calls=%fused_computation.5 | loop fusion | flops 49152 | bytes 165376 | tf_op jit(solution)/shard_map/transpose | solution.py:222
  (6 shorter events, 0.0 us)
Async XLA Ops:
  0.6 22.7 %copy-start = (f32[1024,2048]{1,0:T(8,128)S(1)}, f32[1024,2048]{1,0:T(8,128)}, u32[]{:S(2)}) copy-start(f32[1024,2048]{1,0:T(8,128)} %param.7) | copy-start | bytes 25165828
  1.7 3.2 %collective-permute-start = (f32[9,8,128]{2,1,0:T(8,128)S(1)}, f32[9,8,128]{2,1,0:T(8,128)S(1)}, u32[]{:S(2)}, u32[]{:S(2)}) collective-permute-start(f32[9,8,128]{2,1,0:T(8,128)S(1)} %pack.1.refs_0_), channel_id=1, source_target_pairs={{0,8},{8,0},{16,24},{24,16},{1,9},{9,1},{17,25},{25,17},{2,10},{10... | collective-permute-start | bytes 110600 | tf_op jit(solution)/shard_map/ppermute | solution.py:32
  2.2 4.7 %collective-permute-start.1 = (f32[9,8,128]{2,1,0:T(8,128)S(1)}, f32[9,8,128]{2,1,0:T(8,128)S(1)}, u32[]{:S(2)}, u32[]{:S(2)}) collective-permute-start(f32[9,8,128]{2,1,0:T(8,128)S(1)} %pack.1.refs_0_), channel_id=1, source_target_pairs={{0,16},{8,24},{16,0},{24,8},{1,17},{9,25},{17,1},{25,9},{2,18},{10... | collective-permute-start | bytes 110600 | tf_op jit(solution)/shard_map/ppermute | solution.py:32
  4.8 3.4 %collective-permute-start.2 = (f32[9,8,128]{2,1,0:T(8,128)S(1)}, f32[9,8,128]{2,1,0:T(8,128)S(1)}, u32[]{:S(2)}, u32[]{:S(2)}) collective-permute-start(f32[9,8,128]{2,1,0:T(8,128)S(1)} %pack.1.refs_0_), channel_id=1, source_target_pairs={{0,24},{8,16},{16,8},{24,0},{1,25},{9,17},{17,9},{25,1},{2,26},{10... | collective-permute-start | bytes 110600 | tf_op jit(solution)/shard_map/ppermute | solution.py:32
  23.3 1.5 %collective-permute-start.3 = (f32[8,8,8,128]{3,2,1,0:T(8,128)S(1)}, f32[8,8,8,128]{3,2,1,0:T(8,128)S(1)}, u32[]{:S(2)}, u32[]{:S(2)}) collective-permute-start(f32[8,8,8,128]{3,2,1,0:T(8,128)S(1)} %all_to_all.5.dense_ref), channel_id=1, source_target_pairs={{0,8},{8,0},{16,24},{24,16},{1,9},{9,1},{17,25},{25,17},{2,10},{10... | collective-permute-start | bytes 786440 | tf_op jit(solution)/shard_map/ppermute | solution.py:32
  25.4 4.3 %collective-permute-start.6 = (f32[2,64,128]{2,1,0:T(8,128)S(1)}, f32[2,64,128]{2,1,0:T(8,128)S(1)}, u32[]{:S(2)}, u32[]{:S(2)}) collective-permute-start(f32[2,64,128]{2,1,0:T(8,128)S(1)} %get-tuple-element.11), channel_id=1, source_target_pairs={{0,1},{1,0},{2,3},{3,2},{4,5},{5,4},{6,7},{7,6},{8,9},{9,8},{10,11... | collective-permute-start | bytes 196616 | tf_op jit(solution)/shard_map/ppermute | solution.py:32
  27.4 4.9 %collective-permute-start.4 = (f32[2,64,128]{2,1,0:T(8,128)S(1)}, f32[2,64,128]{2,1,0:T(8,128)S(1)}, u32[]{:S(2)}, u32[]{:S(2)}) collective-permute-start(f32[2,64,128]{2,1,0:T(8,128)S(1)} %rest_stress.1), channel_id=1, source_target_pairs={{0,1},{1,0},{2,3},{3,2},{4,5},{5,4},{6,7},{7,6},{8,9},{9,8},{10,11... | collective-permute-start | bytes 196616 | tf_op jit(solution)/shard_map/ppermute | solution.py:32
  28.0 7.3 %copy-start.1 = (f32[128]{0:T(128)S(1)}, f32[128]{0:T(128)}, u32[]{:S(2)}) copy-start(f32[128]{0:T(128)} %param.11) | copy-start | bytes 1540
  28.0 7.3 %copy-start.2 = (f32[128]{0:T(128)S(1)}, f32[128]{0:T(128)}, u32[]{:S(2)}) copy-start(f32[128]{0:T(128)} %param.12) | copy-start | bytes 1540
  28.1 7.3 %copy-start.3 = (f32[128]{0:T(128)S(1)}, f32[128]{0:T(128)}, u32[]{:S(2)}) copy-start(f32[128]{0:T(128)} %param.13) | copy-start | bytes 1540
  29.8 4.1 %collective-permute-start.7 = (f32[1,64,128]{2,1,0:T(8,128)S(1)}, f32[1,64,128]{2,1,0:T(8,128)S(1)}, u32[]{:S(2)}, u32[]{:S(2)}) collective-permute-start(f32[1,64,128]{2,1,0:T(8,128)S(1)} %slice.19), channel_id=1, source_target_pairs={{0,2},{1,3},{2,0},{3,1},{4,6},{5,7},{6,4},{7,5},{8,10},{9,11},{10,... | collective-permute-start | bytes 98312 | tf_op jit(solution)/shard_map/ppermute | solution.py:32
  32.3 4.0 %collective-permute-start.5 = (f32[1,64,128]{2,1,0:T(8,128)S(1)}, f32[1,64,128]{2,1,0:T(8,128)S(1)}, u32[]{:S(2)}, u32[]{:S(2)}) collective-permute-start(f32[1,64,128]{2,1,0:T(8,128)S(1)} %slice.17), channel_id=1, source_target_pairs={{0,2},{1,3},{2,0},{3,1},{4,6},{5,7},{6,4},{7,5},{8,10},{9,11},{10,... | collective-permute-start | bytes 98312 | tf_op jit(solution)/shard_map/ppermute | solution.py:32
  33.8 4.8 %collective-permute-start.8 = (f32[64,128]{1,0:T(8,128)S(1)}, f32[64,128]{1,0:T(8,128)S(1)}, u32[]{:S(2)}, u32[]{:S(2)}) collective-permute-start(f32[64,128]{1,0:T(8,128)S(1)} %fusion), channel_id=1, source_target_pairs={{0,4},{1,5},{2,6},{3,7},{4,0},{5,1},{6,2},{7,3},{8,12},{9,13},{10,... | collective-permute-start | bytes 98312 | tf_op jit(solution)/shard_map/ppermute | solution.py:32

commit v14 on v13

--- a/solution.py
+++ b/solution.py
@@ -10,6 +10,7 @@
 BLOCK = 128
 SUB = 8
 CHUNK = 256
+ROWS = 256
 VMEM_SPEC = pl.BlockSpec(memory_space=pltpu.VMEM)
 HBM_SPEC = pl.BlockSpec(memory_space=pltpu.HBM)
 MIB = 1024 * 1024
@@ -95,45 +96,39 @@
             out_ref[events + 2 * t * SUB : events + 2 * (t + 1) * SUB, where] = lo
 
 
-def stress(k, other, slip_ref, kernel_ref):
+def stress(other, slip_ref, kernel_ref, add):
+    events, patches = slip_ref.shape[0] // 2, slip_ref.shape[1]
     core = lax.axis_index("rows") % 2 ^ other
-    events, patches = slip_ref.shape[0] // 2, slip_ref.shape[1]
-    rows = kernel_ref.at[lax.axis_index("cols") ^ k]
-    both = low = 0.0
-    for t in range(0, patches, CHUNK):
-        block = rows[:, pl.ds(pl.multiple_of(core * patches + t, CHUNK), CHUNK)]
-        hi = block.astype(jnp.bfloat16)
-        lo = (block - hi.astype(jnp.float32)).astype(jnp.bfloat16)
-        both += lax.dot_general(slip_ref[:, t : t + CHUNK], hi, NT, preferred_element_type=jnp.float32)
-        low += lax.dot_general(slip_ref[:events, t : t + CHUNK], lo, NT, preferred_element_type=jnp.float32)
-    return both[:events] + both[events:] + low
-
-
-def own_body(targets, dense_ref, kernel_ref, slip_ref, *out_refs):
+    for r in range(0, kernel_ref.shape[0], ROWS):
+        both = low = 0.0
+        for t in range(0, patches, CHUNK):
+            block = kernel_ref[r : r + ROWS, pl.ds(pl.multiple_of(core * patches + t, CHUNK), CHUNK)]
+            hi = block.astype(jnp.bfloat16)
+            lo = (block - hi.astype(jnp.float32)).astype(jnp.bfloat16)
+            both += lax.dot_general(slip_ref[:, t : t + CHUNK], hi, NT, preferred_element_type=jnp.float32)
+            low += lax.dot_general(slip_ref[:events, t : t + CHUNK], lo, NT, preferred_element_type=jnp.float32)
+        add(r, both[:events] + both[events:] + low)
+
+
+def own_body(dense_ref, kernel_ref, out_ref, slip_ref):
     assemble(dense_ref, slip_ref)
-    for group, out_ref in zip(targets, out_refs):
-        for j, k in enumerate(group):
-            out_ref[j] = stress(k, 0, slip_ref, kernel_ref)
-
-
-def other_body(targets, dense_ref, kernel_ref, sum_ref, slip_ref, out_ref):
+
+    def add(r, part):
+        out_ref[:, r : r + ROWS] = part
+
+    stress(0, slip_ref, kernel_ref, add)
+
+
+def other_body(dense_ref, kernel_ref, sum_ref, out_ref, slip_ref):
     assemble(dense_ref, slip_ref)
-    rest_body(targets, slip_ref, kernel_ref, sum_ref, out_ref)
-
-
-def rest_body(targets, slip_ref, kernel_ref, sum_ref, out_ref):
-    for j, k in enumerate(targets):
-        out_ref[j] = sum_ref[j] + stress(k, 1, slip_ref, kernel_ref)
-
-
-def both_body(targets, own_ref, other_ref, kernel_ref, out_ref):
-    for j, k in enumerate(targets):
-        out_ref[j] = stress(k, 0, own_ref, kernel_ref) + stress(k, 1, other_ref, kernel_ref)
-
-
-def halving_order(width):
-    bits = width.bit_length() - 1
-    return [int(f"{k:0{bits}b}"[::-1], 2) for k in range(width)]
+    share = out_ref.shape[2]
+
+    def add(r, part):
+        total = sum_ref[:, r : r + ROWS] + part
+        for c in range(ROWS // share):
+            out_ref[r // share + c] = total[:, c * share : (c + 1) * share]
+
+    stress(1, slip_ref, kernel_ref, add)
 
 
 def per_device(kernel, slip_delta, block_list, live_count, direct_effect, load_rate, time_before):
@@ -144,13 +139,8 @@
     receivers, sources = kernel.shape
     blocks_here = sources // BLOCK
 
-    order = halving_order(width)
     share = receivers // width
-    quarter = width // 4
-    near_keep, far_keep = order[0 : 2 * quarter : 2], order[1 : 2 * quarter : 2]
-    near_send, far_send = order[2 * quarter :: 2], order[2 * quarter + 1 :: 2]
     in_hbm = functools.partial(pltpu.with_memory_space_constraint, memory_space=pltpu.HBM)
-    kernel = kernel.reshape(width, share, sources)
     packed = pl.pallas_call(
         pack_body,
         out_shape=f32(events_here + 1, SUB, BLOCK),
@@ -179,41 +169,26 @@
     )(packed, *(came[k] for k in range(1, height)), in_hbm(kernel))
     mine = lax.all_to_all(dense, "cols", 0, 0, tiled=True)
 
-    def call(body, targets, outs, *args):
+    def stress_call(body, out, *args):
         return pl.pallas_call(
-            functools.partial(body, targets),
-            out_shape=outs,
+            body,
+            out_shape=out,
             in_specs=[VMEM_SPEC] * len(args),
-            out_specs=jax.tree.map(lambda _: VMEM_SPEC, outs),
+            out_specs=VMEM_SPEC,
+            scratch_shapes=[pltpu.VMEM((2 * events, blocks_half * BLOCK), jnp.bfloat16)],
             compiler_params=params(8),
             cost_estimate=pl.CostEstimate(
-                flops=6 * quarter * share * sources * events,
-                bytes_accessed=4 * quarter * share * sources,
+                flops=3 * receivers * sources * events,
+                bytes_accessed=2 * receivers * sources,
                 transcendentals=0,
             ),
             name=body.__name__.removesuffix("_body") + "_stress",
         )(*args)
 
-    slips = bf16(2 * events, blocks_half * BLOCK)
-    sums = f32(quarter, events, share)
     came = send_xor(mine, "rows", 1)
-    own, far_own, near_own = call(own_body, (far_send, near_send), [slips, sums, sums], mine, kernel)
-    other, far_sent = call(other_body, far_send, [slips, sums], came, kernel, far_own)
-
-    def later(targets):
-        return call(both_body, targets, sums, own, other, kernel)
-
-    far_came = send_xor(far_sent, "cols", 1)
-    near_came = send_xor(call(rest_body, near_send, sums, other, kernel, near_own), "cols", 1)
-    far = later(far_keep) + far_came
-    near = later(near_keep) + near_came
-    step = 2
-    while step < width // 2:
-        keep = far.shape[0] // 2
-        far = far[:keep] + send_xor(far[keep:], "cols", step)
-        near = near[:keep] + send_xor(near[keep:], "cols", step)
-        step *= 2
-    stress_change = near[0] + send_xor(far[0], "cols", step)
+    partial_sum = stress_call(own_body, f32(events, receivers), mine, kernel)
+    partial_sum = stress_call(other_body, f32(width, events, share), came, kernel, partial_sum)
+    stress_change = jnp.sum(lax.all_to_all(partial_sum, "cols", 0, 0, tiled=True), axis=0)
     scale = direct_effect[None, :]
     growth = jnp.expm1(load_rate * time_before / direct_effect)[None, :]
     log_time = jnp.log(scale / load_rate[None, :]) + jnp.log(

time: 39.5 us -> 41.2 us (1.043)
  waiting for transfers between devices: 9.17 us -> 12.9 us
  starting transfers between devices: 9.05 us -> 6.77 us
    all_to_all x0 -> x1, waiting for transfers between devices: none -> 9.55 us  [per_device(): lax.all_to_all(partial_sum, 'cols', 0, 0, tiled=True)]
    ppermute x9 -> x4, starting transfers between devices: 9.05 us -> 3.18 us  [send_xor(): lax.ppermute(block, axis, [(r, r ^ k) for r in range(lax.axis_size(axis))])]
    ppermute x9 -> x4, waiting for transfers between devices: 9.17 us -> 3.39 us  [send_xor(): lax.ppermute(block, axis, [(r, r ^ k) for r in range(lax.axis_size(axis))])]
    all_to_all x0 -> x1, starting transfers between devices: none -> 3.59 us  [per_device(): lax.all_to_all(partial_sum, 'cols', 0, 0, tiled=True)]
    transpose x1 -> x0, other arithmetic: 0.66 us -> none  [per_device(): return (stress_change.T, log_time.T)]
    add x2 -> x1, other arithmetic: 0.02 us -> 0.66 us  [per_device(): jnp.log(scale / load_rate[None, :])]
    pallas_call x5 -> x2, Pallas kernels: 3.46 us -> 3.66 us  [stress_call(): pl.pallas_call(body, out_shape=out, in_specs=[VMEM_SPEC] * len(args), out...]
  transfers between devices with their start and end apart: 9 -> 5, of which waited for: 7 -> 3; matrix products, arithmetic and copies ran while one was open for 0% -> 0% of each run, Pallas kernels for 8% -> 4%
where the time goes in v14:
time: 41.2 us; the launch traced here: 40.9 us
  blocking collectives  14.9 us (36%)
  waiting for transfers between devices  12.9 us (31%)
  starting transfers between devices  6.77 us (16%)
  Pallas kernels  4.96 us (12%)
  between operations  0.71 us (2%)
  other arithmetic  0.69 us (2%)
    all_to_all x1, blocking collectives, per_device(): mine = lax.all_to_all(dense, 'cols', 0, 0, tiled=True)  14.9 us
    all_to_all x1, waiting for transfers between devices, per_device(): lax.all_to_all(partial_sum, 'cols', 0, 0, tiled=True)  9.55 us
    pallas_call x2, Pallas kernels, stress_call(): pl.pallas_call(body, out_shape=out, in_specs=[VMEM_SPEC] * len(args), out...  3.66 us
    all_to_all x1, starting transfers between devices, per_device(): lax.all_to_all(partial_sum, 'cols', 0, 0, tiled=True)  3.59 us
    ppermute x4, waiting for transfers between devices, send_xor(): lax.ppermute(block, axis, [(r, r ^ k) for r in range(lax.axis_size(axis))])  3.39 us
    ppermute x4, starting transfers between devices, send_xor(): lax.ppermute(block, axis, [(r, r ^ k) for r in range(lax.axis_size(axis))])  3.18 us
    pallas_call x1, Pallas kernels, per_device(): pl.pallas_call(pack_body, out_shape=f32(events_here + 1, SUB, BLOCK), in_...  1.03 us
  transfers between devices with their start and end apart: 5, of which 3 were waited for; matrix products, arithmetic and copies ran while one was open for 0% of the time, Pallas kernels for 4%

profile of v14, /device:TPU:0, one launch (start us, length us, event | category | flops | bytes accessed | tf_op | source)
XLA Modules:
  0.0 40.9 jit_solution(1197360465295009861)
XLA Ops:
  0.6 0.0 copy-start
  0.6 1.0 %pack.1.refs_0_ = f32[9,8,128]{2,1,0:T(8,128)S(1)} custom-call(f32[8,8,128]{2,1,0:T(8,128)} %slip_hbm.1, s32[8,8]{1,0:T(8,128)} %list_hbm.1, s32[8]{0:T(128)} %count_hbm.1), custom_call_target="tpu_custom_call" | custom-call | tf_op jit(solution)/shard_map/pack/pallas_call | solution.py:144
  1.7 0.5 %collective-permute-start = (f32[9,8,128]{2,1,0:T(8,128)S(1)}, f32[9,8,128]{2,1,0:T(8,128)S(1)}, u32[]{:S(2)}, u32[]{:S(2)}) collective-permute-start(f32[9,8,128]{2,1,0:T(8,128)S(1)} %pack.1.refs_0_), channel_id=1, source_target_pairs={{0,8},{8,0},{16,24},{24,16},{1,9},{9,1},{17,25},{25,17},{2,10},{10... | collective-permute-start | bytes 110600 | tf_op jit(solution)/shard_map/ppermute | solution.py:33
  2.2 2.6 %collective-permute-start.1 = (f32[9,8,128]{2,1,0:T(8,128)S(1)}, f32[9,8,128]{2,1,0:T(8,128)S(1)}, u32[]{:S(2)}, u32[]{:S(2)}) collective-permute-start(f32[9,8,128]{2,1,0:T(8,128)S(1)} %pack.1.refs_0_), channel_id=1, source_target_pairs={{0,16},{8,24},{16,0},{24,8},{1,17},{9,25},{17,1},{25,9},{2,18},{10... | collective-permute-start | bytes 110600 | tf_op jit(solution)/shard_map/ppermute | solution.py:33
  4.8 0.1 collective-permute-start.2
  4.9 0.0 collective-permute-done.refs_1_
  4.9 2.0 %collective-permute-done.1.refs_2_ = f32[9,8,128]{2,1,0:T(8,128)S(1)} collective-permute-done((f32[9,8,128]{2,1,0:T(8,128)S(1)}, f32[9,8,128]{2,1,0:T(8,128)S(1)}, u32[]{:S(2)}, u32[]{:S(2)}) %collective-permute-start.1) | collective-permute-done | bytes 36896 | tf_op jit(solution)/shard_map/ppermute | solution.py:33
  6.9 1.4 %collective-permute-done.2.refs_3_ = f32[9,8,128]{2,1,0:T(8,128)S(1)} collective-permute-done((f32[9,8,128]{2,1,0:T(8,128)S(1)}, f32[9,8,128]{2,1,0:T(8,128)S(1)}, u32[]{:S(2)}, u32[]{:S(2)}) %collective-permute-start.2) | collective-permute-done | bytes 36896 | tf_op jit(solution)/shard_map/ppermute | solution.py:33
  8.2 0.3 densify.1
  8.5 14.9 %all_to_all.10.dense_ref = f32[8,8,8,128]{3,2,1,0:T(8,128)S(1)} all-to-all(f32[8,8,8,128]{3,2,1,0:T(8,128)S(1)} %densify.1), channel_id=1, replica_groups=mesh['rows'=4,'cols'=8] {'cols'}, dimensions={0} | all-to-all | bytes 524288 | tf_op jit(solution)/shard_map/all_to_all | solution.py:170
  23.3 0.0 copy-start.2
  23.4 0.0 copy-start.3
  23.4 0.0 copy-start.4
  23.4 0.0 collective-permute-start.3
  23.4 0.0 copy-done
  23.4 1.5 %own_stress.1.sum_ref = f32[64,1024]{1,0:T(8,128)S(1)} custom-call(f32[8,8,8,128]{3,2,1,0:T(8,128)S(1)} %all_to_all.10.dense_ref, f32[1024,2048]{1,0:T(8,128)S(1)} %copy-done), custom_call_target="tpu_custom_call" | custom-call | flops 402653184 | bytes 4194304 | tf_op jit(solution)/shard_map/own_stress/pallas_call | solution.py:173
  24.9 0.0 collective-permute-done.3.dense_ref
  24.9 2.2 %other_stress.1 = f32[8,64,128]{2,1,0:T(8,128)} custom-call(f32[8,8,8,128]{3,2,1,0:T(8,128)S(1)} %collective-permute-done.3.dense_ref, f32[1024,2048]{1,0:T(8,128)S(1)} %copy-done, f32[64,1024]{1,0:T(8,128)S(1)} %own_stress.1.sum_ref), custom_call_target="tpu_custom_call" | custom-call | flops 402653184 | bytes 4194304 | tf_op jit(solution)/shard_map/other_stress/pallas_call | solution.py:173
  27.1 3.6 %all-to-all-start.1 = ((f32[8,64,128]{2,1,0:T(8,128)}), f32[8,64,128]{2,1,0:T(8,128)S(1)}, u32[]{:S(2)}, u32[]{:S(2)}) async-start(f32[8,64,128]{2,1,0:T(8,128)} %other_stress.1), calls=%async_computation.1 | async-start | bytes 524288 | tf_op jit(solution)/shard_map/all_to_all | solution.py:191
  30.7 0.0 copy-done.2
  30.7 0.0 copy-done.3
  30.7 0.0 copy-done.4
  30.7 9.6 %all-to-all-done.1 = f32[8,64,128]{2,1,0:T(8,128)S(1)} async-done(((f32[8,64,128]{2,1,0:T(8,128)}), f32[8,64,128]{2,1,0:T(8,128)S(1)}, u32[]{:S(2)}, u32[]{:S(2)}) %all-to-all-start.1) | async-done | bytes 262176 | tf_op jit(solution)/shard_map/all_to_all | solution.py:191
  40.3 0.0 copy-start.1
  40.3 0.7 %log_add_fusion = f32[128,64]{0,1:T(8,128)} fusion(f32[128]{0:T(128)S(1)} %get-tuple-element.3, f32[128]{0:T(128)S(1)} %copy-done.2, f32[128]{0:T(128)S(1)} %get-tuple-element.2, f32[64,128]{1,0:T(8,128)S(1)} %reduce_sum.9), kind=kLoop, calls=%fused_computation | loop fusion | flops 32768 | bytes 67072 | tf_op jit(solution)/shard_map/add | solution.py:194
  40.9 0.0 copy-done.1
  (2 shorter events, 0.0 us)
Async XLA Ops:
  0.6 22.7 %copy-start = (f32[1024,2048]{1,0:T(8,128)S(1)}, f32[1024,2048]{1,0:T(8,128)}, u32[]{:S(2)}) copy-start(f32[1024,2048]{1,0:T(8,128)} %kernel_ref.3) | copy-start | bytes 25165828
  1.7 3.2 %collective-permute-start = (f32[9,8,128]{2,1,0:T(8,128)S(1)}, f32[9,8,128]{2,1,0:T(8,128)S(1)}, u32[]{:S(2)}, u32[]{:S(2)}) collective-permute-start(f32[9,8,128]{2,1,0:T(8,128)S(1)} %pack.1.refs_0_), channel_id=1, source_target_pairs={{0,8},{8,0},{16,24},{24,16},{1,9},{9,1},{17,25},{25,17},{2,10},{10... | collective-permute-start | bytes 110600 | tf_op jit(solution)/shard_map/ppermute | solution.py:33
  2.2 4.7 %collective-permute-start.1 = (f32[9,8,128]{2,1,0:T(8,128)S(1)}, f32[9,8,128]{2,1,0:T(8,128)S(1)}, u32[]{:S(2)}, u32[]{:S(2)}) collective-permute-start(f32[9,8,128]{2,1,0:T(8,128)S(1)} %pack.1.refs_0_), channel_id=1, source_target_pairs={{0,16},{8,24},{16,0},{24,8},{1,17},{9,25},{17,1},{25,9},{2,18},{10... | collective-permute-start | bytes 110600 | tf_op jit(solution)/shard_map/ppermute | solution.py:33
  4.8 3.4 %collective-permute-start.2 = (f32[9,8,128]{2,1,0:T(8,128)S(1)}, f32[9,8,128]{2,1,0:T(8,128)S(1)}, u32[]{:S(2)}, u32[]{:S(2)}) collective-permute-start(f32[9,8,128]{2,1,0:T(8,128)S(1)} %pack.1.refs_0_), channel_id=1, source_target_pairs={{0,24},{8,16},{16,8},{24,0},{1,25},{9,17},{17,9},{25,1},{2,26},{10... | collective-permute-start | bytes 110600 | tf_op jit(solution)/shard_map/ppermute | solution.py:33
  23.3 7.3 %copy-start.2 = (f32[128]{0:T(128)S(1)}, f32[128]{0:T(128)}, u32[]{:S(2)}) copy-start(f32[128]{0:T(128)} %param.11) | copy-start | bytes 1540
  23.4 7.3 %copy-start.3 = (f32[128]{0:T(128)S(1)}, f32[128]{0:T(128)}, u32[]{:S(2)}) copy-start(f32[128]{0:T(128)} %param.12) | copy-start | bytes 1540
  23.4 7.3 %copy-start.4 = (f32[128]{0:T(128)S(1)}, f32[128]{0:T(128)}, u32[]{:S(2)}) copy-start(f32[128]{0:T(128)} %param.13) | copy-start | bytes 1540
  23.4 1.5 %collective-permute-start.3 = (f32[8,8,8,128]{3,2,1,0:T(8,128)S(1)}, f32[8,8,8,128]{3,2,1,0:T(8,128)S(1)}, u32[]{:S(2)}, u32[]{:S(2)}) collective-permute-start(f32[8,8,8,128]{3,2,1,0:T(8,128)S(1)} %all_to_all.10.dense_ref), channel_id=1, source_target_pairs={{0,8},{8,0},{16,24},{24,16},{1,9},{9,1},{17,25},{25,17},{2,10},{10... | collective-permute-start | bytes 786440 | tf_op jit(solution)/shard_map/ppermute | solution.py:33
  27.1 13.2 %all-to-all-start.1 = ((f32[8,64,128]{2,1,0:T(8,128)}), f32[8,64,128]{2,1,0:T(8,128)S(1)}, u32[]{:S(2)}, u32[]{:S(2)}) async-start(f32[8,64,128]{2,1,0:T(8,128)} %other_stress.1), calls=%async_computation.1 | async-start | bytes 524288 | tf_op jit(solution)/shard_map/all_to_all | solution.py:191
  40.3 0.7 %copy-start.1 = (f32[64,128]{1,0:T(8,128)}, f32[64,128]{1,0:T(8,128)S(1)}, u32[]{:S(2)}) copy-start(f32[64,128]{1,0:T(8,128)S(1)} %reduce_sum.9) | copy-start | bytes 98308

commit v15 on v14

--- a/solution.py
+++ b/solution.py
@@ -188,12 +188,12 @@
     came = send_xor(mine, "rows", 1)
     partial_sum = stress_call(own_body, f32(events, receivers), mine, kernel)
     partial_sum = stress_call(other_body, f32(width, events, share), came, kernel, partial_sum)
-    stress_change = jnp.sum(lax.all_to_all(partial_sum, "cols", 0, 0, tiled=True), axis=0)
     scale = direct_effect[None, :]
     growth = jnp.expm1(load_rate * time_before / direct_effect)[None, :]
-    log_time = jnp.log(scale / load_rate[None, :]) + jnp.log(
-        jnp.log1p(jnp.exp(-stress_change / scale) * growth)
-    )
+    base = jnp.log(scale / load_rate[None, :])
+    partial_sum, growth, base = lax.optimization_barrier((partial_sum, growth, base))
+    stress_change = jnp.sum(lax.all_to_all(partial_sum, "cols", 0, 0, tiled=True), axis=0)
+    log_time = base + jnp.log(jnp.log1p(jnp.exp(-stress_change / scale) * growth))
     return (stress_change.T, log_time.T)
 
 

time: 41.2 us -> 40.3 us (0.978)
  blocking collectives: 14.9 us -> 27.8 us
  waiting for transfers between devices: 12.9 us -> 3.36 us
  starting transfers between devices: 6.77 us -> 3.18 us
  Pallas kernels: 4.96 us -> 4.26 us
    all_to_all x0 -> x1, blocking collectives: none -> 13 us  [per_device(): lax.all_to_all(partial_sum, 'cols', 0, 0, tiled=True)]
    all_to_all x1 -> x0, waiting for transfers between devices: 9.55 us -> none  [per_device(): lax.all_to_all(partial_sum, 'cols', 0, 0, tiled=True)]
    all_to_all x1 -> x0, starting transfers between devices: 3.59 us -> none  [per_device(): lax.all_to_all(partial_sum, 'cols', 0, 0, tiled=True)]
    pallas_call x2, Pallas kernels: 3.66 us -> 2.96 us  [stress_call(): pl.pallas_call(body, out_shape=out, in_specs=[VMEM_SPEC] * len(args), out...]
  transfers between devices with their start and end apart: 5 -> 4, of which waited for: 3 -> 2; matrix products, arithmetic and copies ran while one was open for 0% -> 0% of each run, Pallas kernels for 4% -> 4%
where the time goes in v15:
time: 40.3 us; the launch traced here: 40.1 us
  blocking collectives  27.8 us (69%)
  Pallas kernels  4.26 us (11%)
  waiting for transfers between devices  3.36 us (8%)
  starting transfers between devices  3.18 us (8%)
  between operations  0.73 us (2%)
  other arithmetic  0.69 us (2%)
    all_to_all x1, blocking collectives, per_device(): mine = lax.all_to_all(dense, 'cols', 0, 0, tiled=True)  14.8 us
    all_to_all x1, blocking collectives, per_device(): lax.all_to_all(partial_sum, 'cols', 0, 0, tiled=True)  13 us
    ppermute x4, waiting for transfers between devices, send_xor(): lax.ppermute(block, axis, [(r, r ^ k) for r in range(lax.axis_size(axis))])  3.36 us
    ppermute x4, starting transfers between devices, send_xor(): lax.ppermute(block, axis, [(r, r ^ k) for r in range(lax.axis_size(axis))])  3.18 us
    pallas_call x2, Pallas kernels, stress_call(): pl.pallas_call(body, out_shape=out, in_specs=[VMEM_SPEC] * len(args), out...  2.96 us
    pallas_call x1, Pallas kernels, per_device(): pl.pallas_call(pack_body, out_shape=f32(events_here + 1, SUB, BLOCK), in_...  1.03 us
  transfers between devices with their start and end apart: 4, of which 2 were waited for; matrix products, arithmetic and copies ran while one was open for 0% of the time, Pallas kernels for 4%

profile of v15, /device:TPU:0, one launch (start us, length us, event | category | flops | bytes accessed | tf_op | source)
XLA Modules:
  0.0 40.1 jit_solution(16087140414166371769)
XLA Ops:
  0.6 0.0 copy-start
  0.6 0.0 copy-start.2
  0.7 0.0 copy-start.3
  0.7 0.0 copy-start.4
  0.7 1.0 %pack.1.refs_0_ = f32[9,8,128]{2,1,0:T(8,128)S(1)} custom-call(f32[8,8,128]{2,1,0:T(8,128)} %slip_hbm.1, s32[8,8]{1,0:T(8,128)} %list_hbm.1, s32[8]{0:T(128)} %count_hbm.1), custom_call_target="tpu_custom_call" | custom-call | tf_op jit(solution)/shard_map/pack/pallas_call | solution.py:144
  1.7 0.5 %collective-permute-start = (f32[9,8,128]{2,1,0:T(8,128)S(1)}, f32[9,8,128]{2,1,0:T(8,128)S(1)}, u32[]{:S(2)}, u32[]{:S(2)}) collective-permute-start(f32[9,8,128]{2,1,0:T(8,128)S(1)} %pack.1.refs_0_), channel_id=1, source_target_pairs={{0,8},{8,0},{16,24},{24,16},{1,9},{9,1},{17,25},{25,17},{2,10},{10... | collective-permute-start | bytes 110600 | tf_op jit(solution)/shard_map/ppermute | solution.py:33
  2.2 2.6 %collective-permute-start.1 = (f32[9,8,128]{2,1,0:T(8,128)S(1)}, f32[9,8,128]{2,1,0:T(8,128)S(1)}, u32[]{:S(2)}, u32[]{:S(2)}) collective-permute-start(f32[9,8,128]{2,1,0:T(8,128)S(1)} %pack.1.refs_0_), channel_id=1, source_target_pairs={{0,16},{8,24},{16,0},{24,8},{1,17},{9,25},{17,1},{25,9},{2,18},{10... | collective-permute-start | bytes 110600 | tf_op jit(solution)/shard_map/ppermute | solution.py:33
  4.8 0.1 collective-permute-start.2
  4.9 0.0 collective-permute-done.refs_1_
  4.9 2.0 %collective-permute-done.1.refs_2_ = f32[9,8,128]{2,1,0:T(8,128)S(1)} collective-permute-done((f32[9,8,128]{2,1,0:T(8,128)S(1)}, f32[9,8,128]{2,1,0:T(8,128)S(1)}, u32[]{:S(2)}, u32[]{:S(2)}) %collective-permute-start.1) | collective-permute-done | bytes 36896 | tf_op jit(solution)/shard_map/ppermute | solution.py:33
  6.9 1.4 %collective-permute-done.2.refs_3_ = f32[9,8,128]{2,1,0:T(8,128)S(1)} collective-permute-done((f32[9,8,128]{2,1,0:T(8,128)S(1)}, f32[9,8,128]{2,1,0:T(8,128)S(1)}, u32[]{:S(2)}, u32[]{:S(2)}) %collective-permute-start.2) | collective-permute-done | bytes 36896 | tf_op jit(solution)/shard_map/ppermute | solution.py:33
  8.3 0.3 densify.1
  8.5 14.8 %all_to_all.10.dense_ref = f32[8,8,8,128]{3,2,1,0:T(8,128)S(1)} all-to-all(f32[8,8,8,128]{3,2,1,0:T(8,128)S(1)} %densify.1), channel_id=1, replica_groups=mesh['rows'=4,'cols'=8] {'cols'}, dimensions={0} | all-to-all | bytes 524288 | tf_op jit(solution)/shard_map/all_to_all | solution.py:170
  23.4 0.0 collective-permute-start.3
  23.4 0.0 copy-done.2
  23.4 0.0 copy-done.3
  23.4 0.0 copy-done.4
  23.4 0.0 copy-done
  23.4 1.5 %own_stress.1.sum_ref = f32[64,1024]{1,0:T(8,128)S(1)} custom-call(f32[8,8,8,128]{3,2,1,0:T(8,128)S(1)} %all_to_all.10.dense_ref, f32[1024,2048]{1,0:T(8,128)S(1)} %copy-done), custom_call_target="tpu_custom_call" | custom-call | flops 402653184 | bytes 4194304 | tf_op jit(solution)/shard_map/own_stress/pallas_call | solution.py:173
  24.9 0.0 collective-permute-done.3.dense_ref
  24.9 1.5 %other_stress.1 = f32[8,64,128]{2,1,0:T(8,128)S(1)} custom-call(f32[8,8,8,128]{3,2,1,0:T(8,128)S(1)} %collective-permute-done.3.dense_ref, f32[1024,2048]{1,0:T(8,128)S(1)} %copy-done, f32[64,1024]{1,0:T(8,128)S(1)} %own_stress.1.sum_ref), custom_call_target="tpu_custom_call" | custom-call | flops 402653184 | bytes 4194304 | tf_op jit(solution)/shard_map/other_stress/pallas_call | solution.py:173
  26.4 13.0 %all_to_all.11 = f32[8,64,128]{2,1,0:T(8,128)S(1)} all-to-all(f32[8,64,128]{2,1,0:T(8,128)S(1)} %other_stress.1), channel_id=1, replica_groups=mesh['rows'=4,'cols'=8] {'cols'}, dimensions={0} | all-to-all | bytes 524288 | tf_op jit(solution)/shard_map/all_to_all | solution.py:195
  39.4 0.0 copy-start.1
  39.4 0.7 %log_add_fusion = f32[128,64]{0,1:T(8,128)} fusion(f32[128]{0:T(128)S(1)} %bitcast.10, f32[128]{0:T(128)S(1)} %copy-done.2, f32[128]{0:T(128)S(1)} %bitcast.9, f32[64,128]{1,0:T(8,128)S(1)} %reduce_sum.9), kind=kLoop, calls=%fused_computation | loop fusion | flops 32768 | bytes 67072 | tf_op jit(solution)/shard_map/add | solution.py:196
  40.1 0.0 copy-done.1
  (2 shorter events, 0.0 us)
Async XLA Ops:
  0.6 22.8 %copy-start = (f32[1024,2048]{1,0:T(8,128)S(1)}, f32[1024,2048]{1,0:T(8,128)}, u32[]{:S(2)}) copy-start(f32[1024,2048]{1,0:T(8,128)} %kernel_ref.3) | copy-start | bytes 25165828
  0.6 22.7 %copy-start.2 = (f32[128]{0:T(128)S(1)}, f32[128]{0:T(128)}, u32[]{:S(2)}) copy-start(f32[128]{0:T(128)} %param.11) | copy-start | bytes 1540
  0.7 22.7 %copy-start.3 = (f32[128]{0:T(128)S(1)}, f32[128]{0:T(128)}, u32[]{:S(2)}) copy-start(f32[128]{0:T(128)} %param.12) | copy-start | bytes 1540
  0.7 22.7 %copy-start.4 = (f32[128]{0:T(128)S(1)}, f32[128]{0:T(128)}, u32[]{:S(2)}) copy-start(f32[128]{0:T(128)} %param.13) | copy-start | bytes 1540
  1.7 3.2 %collective-permute-start = (f32[9,8,128]{2,1,0:T(8,128)S(1)}, f32[9,8,128]{2,1,0:T(8,128)S(1)}, u32[]{:S(2)}, u32[]{:S(2)}) collective-permute-start(f32[9,8,128]{2,1,0:T(8,128)S(1)} %pack.1.refs_0_), channel_id=1, source_target_pairs={{0,8},{8,0},{16,24},{24,16},{1,9},{9,1},{17,25},{25,17},{2,10},{10... | collective-permute-start | bytes 110600 | tf_op jit(solution)/shard_map/ppermute | solution.py:33
  2.2 4.7 %collective-permute-start.1 = (f32[9,8,128]{2,1,0:T(8,128)S(1)}, f32[9,8,128]{2,1,0:T(8,128)S(1)}, u32[]{:S(2)}, u32[]{:S(2)}) collective-permute-start(f32[9,8,128]{2,1,0:T(8,128)S(1)} %pack.1.refs_0_), channel_id=1, source_target_pairs={{0,16},{8,24},{16,0},{24,8},{1,17},{9,25},{17,1},{25,9},{2,18},{10... | collective-permute-start | bytes 110600 | tf_op jit(solution)/shard_map/ppermute | solution.py:33
  4.8 3.4 %collective-permute-start.2 = (f32[9,8,128]{2,1,0:T(8,128)S(1)}, f32[9,8,128]{2,1,0:T(8,128)S(1)}, u32[]{:S(2)}, u32[]{:S(2)}) collective-permute-start(f32[9,8,128]{2,1,0:T(8,128)S(1)} %pack.1.refs_0_), channel_id=1, source_target_pairs={{0,24},{8,16},{16,8},{24,0},{1,25},{9,17},{17,9},{25,1},{2,26},{10... | collective-permute-start | bytes 110600 | tf_op jit(solution)/shard_map/ppermute | solution.py:33
  23.4 1.5 %collective-permute-start.3 = (f32[8,8,8,128]{3,2,1,0:T(8,128)S(1)}, f32[8,8,8,128]{3,2,1,0:T(8,128)S(1)}, u32[]{:S(2)}, u32[]{:S(2)}) collective-permute-start(f32[8,8,8,128]{3,2,1,0:T(8,128)S(1)} %all_to_all.10.dense_ref), channel_id=1, source_target_pairs={{0,8},{8,0},{16,24},{24,16},{1,9},{9,1},{17,25},{25,17},{2,10},{10... | collective-permute-start | bytes 786440 | tf_op jit(solution)/shard_map/ppermute | solution.py:33
  39.4 0.7 %copy-start.1 = (f32[64,128]{1,0:T(8,128)}, f32[64,128]{1,0:T(8,128)S(1)}, u32[]{:S(2)}) copy-start(f32[64,128]{1,0:T(8,128)S(1)} %reduce_sum.9) | copy-start | bytes 98308

commit v16 on v13

--- a/solution.py
+++ b/solution.py
@@ -207,13 +207,9 @@
     near_came = send_xor(call(rest_body, near_send, sums, other, kernel, near_own), "cols", 1)
     far = later(far_keep) + far_came
     near = later(near_keep) + near_came
-    step = 2
-    while step < width // 2:
-        keep = far.shape[0] // 2
-        far = far[:keep] + send_xor(far[keep:], "cols", step)
-        near = near[:keep] + send_xor(near[keep:], "cols", step)
-        step *= 2
-    stress_change = near[0] + send_xor(far[0], "cols", step)
+    parts = [send_xor(far[j], "cols", k) for j, k in reversed(list(enumerate(far_keep)))]
+    parts += [send_xor(near[j], "cols", k) for j, k in enumerate(near_keep) if k]
+    stress_change = sum(parts, near[0])
     scale = direct_effect[None, :]
     growth = jnp.expm1(load_rate * time_before / direct_effect)[None, :]
     log_time = jnp.log(scale / load_rate[None, :]) + jnp.log(

time: 39.5 us -> 37.8 us (0.957)
  waiting for transfers between devices: 9.17 us -> 6.66 us
  starting transfers between devices: 9.05 us -> 9.86 us
    ppermute x9, waiting for transfers between devices: 9.17 us -> 6.66 us  [send_xor(): lax.ppermute(block, axis, [(r, r ^ k) for r in range(lax.axis_size(axis))])]
    ppermute x9, starting transfers between devices: 9.05 us -> 9.86 us  [send_xor(): lax.ppermute(block, axis, [(r, r ^ k) for r in range(lax.axis_size(axis))])]
  transfers between devices with their start and end apart: 9 -> 9, of which waited for: 7 -> 6; matrix products, arithmetic and copies ran while one was open for 0% -> 0% of each run, Pallas kernels for 8% -> 8%
where the time goes in v16:
time: 37.8 us; the launch traced here: 37.6 us
  blocking collectives  14.9 us (39%)
  starting transfers between devices  9.86 us (26%)
  waiting for transfers between devices  6.66 us (18%)
  Pallas kernels  4.76 us (13%)
  between operations  0.73 us (2%)
  other arithmetic  0.69 us (2%)
    all_to_all x1, blocking collectives, per_device(): mine = lax.all_to_all(dense, 'cols', 0, 0, tiled=True)  14.9 us
    ppermute x9, starting transfers between devices, send_xor(): lax.ppermute(block, axis, [(r, r ^ k) for r in range(lax.axis_size(axis))])  9.86 us
    ppermute x9, waiting for transfers between devices, send_xor(): lax.ppermute(block, axis, [(r, r ^ k) for r in range(lax.axis_size(axis))])  6.66 us
    pallas_call x5, Pallas kernels, call(): pl.pallas_call(functools.partial(body, targets), out_shape=outs, in_specs...  3.47 us
    pallas_call x1, Pallas kernels, per_device(): pl.pallas_call(pack_body, out_shape=f32(events_here + 1, SUB, BLOCK), in_...  1.03 us
  transfers between devices with their start and end apart: 9, of which 6 were waited for; matrix products, arithmetic and copies ran while one was open for 0% of the time, Pallas kernels for 8%

profile of v16, /device:TPU:0, one launch (start us, length us, event | category | flops | bytes accessed | tf_op | source)
XLA Modules:
  0.0 37.6 jit_solution(1561724427288866434)
XLA Ops:
  0.6 0.0 copy-start
  0.6 1.0 %pack.1.refs_0_ = f32[9,8,128]{2,1,0:T(8,128)S(1)} custom-call(f32[8,8,128]{2,1,0:T(8,128)} %slip_hbm.1, s32[8,8]{1,0:T(8,128)} %list_hbm.1, s32[8]{0:T(128)} %count_hbm.1), custom_call_target="tpu_custom_call" | custom-call | tf_op jit(solution)/shard_map/pack/pallas_call | solution.py:154
  1.7 0.5 %collective-permute-start = (f32[9,8,128]{2,1,0:T(8,128)S(1)}, f32[9,8,128]{2,1,0:T(8,128)S(1)}, u32[]{:S(2)}, u32[]{:S(2)}) collective-permute-start(f32[9,8,128]{2,1,0:T(8,128)S(1)} %pack.1.refs_0_), channel_id=1, source_target_pairs={{0,8},{8,0},{16,24},{24,16},{1,9},{9,1},{17,25},{25,17},{2,10},{10... | collective-permute-start | bytes 110600 | tf_op jit(solution)/shard_map/ppermute | solution.py:32
  2.2 2.6 %collective-permute-start.1 = (f32[9,8,128]{2,1,0:T(8,128)S(1)}, f32[9,8,128]{2,1,0:T(8,128)S(1)}, u32[]{:S(2)}, u32[]{:S(2)}) collective-permute-start(f32[9,8,128]{2,1,0:T(8,128)S(1)} %pack.1.refs_0_), channel_id=1, source_target_pairs={{0,16},{8,24},{16,0},{24,8},{1,17},{9,25},{17,1},{25,9},{2,18},{10... | collective-permute-start | bytes 110600 | tf_op jit(solution)/shard_map/ppermute | solution.py:32
  4.8 0.1 collective-permute-start.2
  4.9 0.0 collective-permute-done.refs_1_
  4.9 2.0 %collective-permute-done.1.refs_2_ = f32[9,8,128]{2,1,0:T(8,128)S(1)} collective-permute-done((f32[9,8,128]{2,1,0:T(8,128)S(1)}, f32[9,8,128]{2,1,0:T(8,128)S(1)}, u32[]{:S(2)}, u32[]{:S(2)}) %collective-permute-start.1) | collective-permute-done | bytes 36896 | tf_op jit(solution)/shard_map/ppermute | solution.py:32
  6.9 1.4 %collective-permute-done.2.refs_3_ = f32[9,8,128]{2,1,0:T(8,128)S(1)} collective-permute-done((f32[9,8,128]{2,1,0:T(8,128)S(1)}, f32[9,8,128]{2,1,0:T(8,128)S(1)}, u32[]{:S(2)}, u32[]{:S(2)}) %collective-permute-start.2) | collective-permute-done | bytes 36896 | tf_op jit(solution)/shard_map/ppermute | solution.py:32
  8.2 0.3 densify.1
  8.5 14.9 %all_to_all.5.dense_ref = f32[8,8,8,128]{3,2,1,0:T(8,128)S(1)} all-to-all(f32[8,8,8,128]{3,2,1,0:T(8,128)S(1)} %densify.1), channel_id=1, replica_groups=mesh['rows'=4,'cols'=8] {'cols'}, dimensions={0} | all-to-all | bytes 524288 | tf_op jit(solution)/shard_map/all_to_all | solution.py:180
  23.3 0.0 collective-permute-start.3
  23.4 0.0 copy-done
  23.4 0.8 %own_stress.1 = (bf16[128,1024]{1,0:T(8,128)(2,1)S(1)}, f32[2,64,128]{2,1,0:T(8,128)S(1)}, f32[2,64,128]{2,1,0:T(8,128)S(1)}) custom-call(f32[8,8,8,128]{3,2,1,0:T(8,128)S(1)} %all_to_all.5.dense_ref, f32[8,128,2048]{2,1,0:T(8,128)S(1)} %bitcast.20), custom_call_target="tpu_custom_call" | custom-call | flops 201326592 | bytes 2097152 | tf_op jit(solution)/shard_map/own_stress/pallas_call | solution.py:183
  24.2 0.7 %collective-permute-done.3.dense_ref = f32[8,8,8,128]{3,2,1,0:T(8,128)S(1)} collective-permute-done((f32[8,8,8,128]{3,2,1,0:T(8,128)S(1)}, f32[8,8,8,128]{3,2,1,0:T(8,128)S(1)}, u32[]{:S(2)}, u32[]{:S(2)}) %collective-permute-start.3) | collective-permute-done | bytes 262176 | tf_op jit(solution)/shard_map/ppermute | solution.py:32
  24.9 0.5 %other_stress.1 = (bf16[128,1024]{1,0:T(8,128)(2,1)S(1)}, f32[2,64,128]{2,1,0:T(8,128)S(1)}) custom-call(f32[8,8,8,128]{3,2,1,0:T(8,128)S(1)} %collective-permute-done.3.dense_ref, f32[8,128,2048]{2,1,0:T(8,128)S(1)} %bitcast.21, f32[2,64,128]{2,1,0:T(8,128)S(1)} %get-tuple-element.8.sum_ref), custom_call_target="tpu_custom_call" | custom-call | flops 201326592 | bytes 2097152 | tf_op jit(solution)/shard_map/other_stress/pallas_call | solution.py:183
  25.4 1.5 %collective-permute-start.5 = (f32[2,64,128]{2,1,0:T(8,128)S(1)}, f32[2,64,128]{2,1,0:T(8,128)S(1)}, u32[]{:S(2)}, u32[]{:S(2)}) collective-permute-start(f32[2,64,128]{2,1,0:T(8,128)S(1)} %get-tuple-element.11), channel_id=1, source_target_pairs={{0,1},{1,0},{2,3},{3,2},{4,5},{5,4},{6,7},{7,6},{8,9},{9,8},{10,11... | collective-permute-start | bytes 196616 | tf_op jit(solution)/shard_map/ppermute | solution.py:32
  26.9 0.5 %rest_stress.1 = f32[2,64,128]{2,1,0:T(8,128)S(1)} custom-call(bf16[128,1024]{1,0:T(8,128)(2,1)S(1)} %get-tuple-element.9.other_ref.slip_ref, f32[8,128,2048]{2,1,0:T(8,128)S(1)} %bitcast.22, f32[2,64,128]{2,1,0:T(8,128)S(1)} %get-tuple-element.10.sum_ref), custom_call_target="tpu_custom_call" | custom-call | flops 201326592 | bytes 2097152 | tf_op jit(solution)/shard_map/rest_stress/pallas_call | solution.py:183
  27.4 0.7 %collective-permute-start.4 = (f32[2,64,128]{2,1,0:T(8,128)S(1)}, f32[2,64,128]{2,1,0:T(8,128)S(1)}, u32[]{:S(2)}, u32[]{:S(2)}) collective-permute-start(f32[2,64,128]{2,1,0:T(8,128)S(1)} %rest_stress.1), channel_id=1, source_target_pairs={{0,1},{1,0},{2,3},{3,2},{4,5},{5,4},{6,7},{7,6},{8,9},{9,8},{10,11... | collective-permute-start | bytes 196616 | tf_op jit(solution)/shard_map/ppermute | solution.py:32
  28.0 0.0 copy-start.1
  28.0 0.0 copy-start.2
  28.0 0.0 copy-start.3
  28.0 0.8 %both_stress.3 = f32[2,64,128]{2,1,0:T(8,128)S(1)} custom-call(bf16[128,1024]{1,0:T(8,128)(2,1)S(1)} %get-tuple-element.7.own_ref, bf16[128,1024]{1,0:T(8,128)(2,1)S(1)} %get-tuple-element.9.other_ref.slip_ref, f32[8,128,2048]{2,1,0:T(8,128)S(1)} %bitcast.23), custom_call_target="tpu_custom_call" | custom-call | flops 201326592 | bytes 2097152 | tf_op jit(solution)/shard_map/both_stress/pallas_call | solution.py:183
  28.9 0.8 %both_stress.2 = f32[2,64,128]{2,1,0:T(8,128)S(1)} custom-call(bf16[128,1024]{1,0:T(8,128)(2,1)S(1)} %get-tuple-element.7.own_ref, bf16[128,1024]{1,0:T(8,128)(2,1)S(1)} %get-tuple-element.9.other_ref.slip_ref, f32[8,128,2048]{2,1,0:T(8,128)S(1)} %bitcast.24), custom_call_target="tpu_custom_call" | custom-call | flops 201326592 | bytes 2097152 | tf_op jit(solution)/shard_map/both_stress/pallas_call | solution.py:183
  29.7 0.0 collective-permute-done.5
  29.8 1.2 %collective-permute-start.6 = (f32[64,128]{1,0:T(8,128)S(1)}, f32[64,128]{1,0:T(8,128)S(1)}, u32[]{:S(2)}, u32[]{:S(2)}) collective-permute-start(f32[64,128]{1,0:T(8,128)S(1)} %get-tuple-element.14), channel_id=1, source_target_pairs={{0,6},{1,7},{2,4},{3,5},{4,2},{5,3},{6,0},{7,1},{8,14},{9,15},{10,... | collective-permute-start | bytes 98312 | tf_op jit(solution)/shard_map/ppermute | solution.py:32
  31.0 2.0 %collective-permute-start.7 = (f32[64,128]{1,0:T(8,128)S(1)}, f32[64,128]{1,0:T(8,128)S(1)}, u32[]{:S(2)}, u32[]{:S(2)}) collective-permute-start(f32[64,128]{1,0:T(8,128)S(1)} %get-tuple-element.15), channel_id=1, source_target_pairs={{0,4},{1,5},{2,6},{3,7},{4,0},{5,1},{6,2},{7,3},{8,12},{9,13},{10,... | collective-permute-start | bytes 98312 | tf_op jit(solution)/shard_map/ppermute | solution.py:32
  32.9 0.0 collective-permute-done.4
  32.9 1.4 %collective-permute-start.8 = (f32[64,128]{1,0:T(8,128)S(1)}, f32[64,128]{1,0:T(8,128)S(1)}, u32[]{:S(2)}, u32[]{:S(2)}) collective-permute-start(f32[64,128]{1,0:T(8,128)S(1)} %slice_bitcast_fusion), channel_id=1, source_target_pairs={{0,2},{1,3},{2,0},{3,1},{4,6},{5,7},{6,4},{7,5},{8,10},{9,11},{10,... | collective-permute-start | bytes 98312 | tf_op jit(solution)/shard_map/ppermute | solution.py:32
  34.3 0.0 copy-done.1
  34.3 0.0 copy-done.2
  34.3 0.0 copy-done.3
  34.3 1.5 %collective-permute-done.6 = f32[64,128]{1,0:T(8,128)S(1)} collective-permute-done((f32[64,128]{1,0:T(8,128)S(1)}, f32[64,128]{1,0:T(8,128)S(1)}, u32[]{:S(2)}, u32[]{:S(2)}) %collective-permute-start.6) | collective-permute-done | bytes 32800 | tf_op jit(solution)/shard_map/ppermute | solution.py:32
  35.9 0.5 %collective-permute-done.7 = f32[64,128]{1,0:T(8,128)S(1)} collective-permute-done((f32[64,128]{1,0:T(8,128)S(1)}, f32[64,128]{1,0:T(8,128)S(1)}, u32[]{:S(2)}, u32[]{:S(2)}) %collective-permute-start.7) | collective-permute-done | bytes 32800 | tf_op jit(solution)/shard_map/ppermute | solution.py:32
  36.4 0.6 %collective-permute-done.8 = f32[64,128]{1,0:T(8,128)S(1)} collective-permute-done((f32[64,128]{1,0:T(8,128)S(1)}, f32[64,128]{1,0:T(8,128)S(1)}, u32[]{:S(2)}, u32[]{:S(2)}) %collective-permute-start.8) | collective-permute-done | bytes 32800 | tf_op jit(solution)/shard_map/ppermute | solution.py:32
  36.9 0.7 %add_bitcast_fusion = (f32[128,64]{0,1:T(8,128)}, f32[64,128]{1,0:T(8,128)}) fusion(f32[128]{0:T(128)S(1)} %get-tuple-element.17, f32[128]{0:T(128)S(1)} %copy-done.1, f32[128]{0:T(128)S(1)} %get-tuple-element.16, f32[64,128]{1,0:T(8,128)S(1)} %collective-permute-done.8, f32[64,128]{1,0:T(8,128)S(1)} %collective-permute-done.7, ...), kind=kLoop, calls=%fused_computation.7 | loop fusion | flops 57344 | bytes 198144 | tf_op jit(solution)/shard_map/transpose | solution.py:218
  (5 shorter events, 0.0 us)
Async XLA Ops:
  0.6 22.7 %copy-start = (f32[1024,2048]{1,0:T(8,128)S(1)}, f32[1024,2048]{1,0:T(8,128)}, u32[]{:S(2)}) copy-start(f32[1024,2048]{1,0:T(8,128)} %param.7) | copy-start | bytes 25165828
  1.7 3.2 %collective-permute-start = (f32[9,8,128]{2,1,0:T(8,128)S(1)}, f32[9,8,128]{2,1,0:T(8,128)S(1)}, u32[]{:S(2)}, u32[]{:S(2)}) collective-permute-start(f32[9,8,128]{2,1,0:T(8,128)S(1)} %pack.1.refs_0_), channel_id=1, source_target_pairs={{0,8},{8,0},{16,24},{24,16},{1,9},{9,1},{17,25},{25,17},{2,10},{10... | collective-permute-start | bytes 110600 | tf_op jit(solution)/shard_map/ppermute | solution.py:32
  2.2 4.7 %collective-permute-start.1 = (f32[9,8,128]{2,1,0:T(8,128)S(1)}, f32[9,8,128]{2,1,0:T(8,128)S(1)}, u32[]{:S(2)}, u32[]{:S(2)}) collective-permute-start(f32[9,8,128]{2,1,0:T(8,128)S(1)} %pack.1.refs_0_), channel_id=1, source_target_pairs={{0,16},{8,24},{16,0},{24,8},{1,17},{9,25},{17,1},{25,9},{2,18},{10... | collective-permute-start | bytes 110600 | tf_op jit(solution)/shard_map/ppermute | solution.py:32
  4.8 3.4 %collective-permute-start.2 = (f32[9,8,128]{2,1,0:T(8,128)S(1)}, f32[9,8,128]{2,1,0:T(8,128)S(1)}, u32[]{:S(2)}, u32[]{:S(2)}) collective-permute-start(f32[9,8,128]{2,1,0:T(8,128)S(1)} %pack.1.refs_0_), channel_id=1, source_target_pairs={{0,24},{8,16},{16,8},{24,0},{1,25},{9,17},{17,9},{25,1},{2,26},{10... | collective-permute-start | bytes 110600 | tf_op jit(solution)/shard_map/ppermute | solution.py:32
  23.3 1.5 %collective-permute-start.3 = (f32[8,8,8,128]{3,2,1,0:T(8,128)S(1)}, f32[8,8,8,128]{3,2,1,0:T(8,128)S(1)}, u32[]{:S(2)}, u32[]{:S(2)}) collective-permute-start(f32[8,8,8,128]{3,2,1,0:T(8,128)S(1)} %all_to_all.5.dense_ref), channel_id=1, source_target_pairs={{0,8},{8,0},{16,24},{24,16},{1,9},{9,1},{17,25},{25,17},{2,10},{10... | collective-permute-start | bytes 786440 | tf_op jit(solution)/shard_map/ppermute | solution.py:32
  25.4 4.3 %collective-permute-start.5 = (f32[2,64,128]{2,1,0:T(8,128)S(1)}, f32[2,64,128]{2,1,0:T(8,128)S(1)}, u32[]{:S(2)}, u32[]{:S(2)}) collective-permute-start(f32[2,64,128]{2,1,0:T(8,128)S(1)} %get-tuple-element.11), channel_id=1, source_target_pairs={{0,1},{1,0},{2,3},{3,2},{4,5},{5,4},{6,7},{7,6},{8,9},{9,8},{10,11... | collective-permute-start | bytes 196616 | tf_op jit(solution)/shard_map/ppermute | solution.py:32
  27.4 5.6 %collective-permute-start.4 = (f32[2,64,128]{2,1,0:T(8,128)S(1)}, f32[2,64,128]{2,1,0:T(8,128)S(1)}, u32[]{:S(2)}, u32[]{:S(2)}) collective-permute-start(f32[2,64,128]{2,1,0:T(8,128)S(1)} %rest_stress.1), channel_id=1, source_target_pairs={{0,1},{1,0},{2,3},{3,2},{4,5},{5,4},{6,7},{7,6},{8,9},{9,8},{10,11... | collective-permute-start | bytes 196616 | tf_op jit(solution)/shard_map/ppermute | solution.py:32
  28.0 6.3 %copy-start.1 = (f32[128]{0:T(128)S(1)}, f32[128]{0:T(128)}, u32[]{:S(2)}) copy-start(f32[128]{0:T(128)} %param.11) | copy-start | bytes 1540
  28.0 6.3 %copy-start.2 = (f32[128]{0:T(128)S(1)}, f32[128]{0:T(128)}, u32[]{:S(2)}) copy-start(f32[128]{0:T(128)} %param.12) | copy-start | bytes 1540
  28.0 6.3 %copy-start.3 = (f32[128]{0:T(128)S(1)}, f32[128]{0:T(128)}, u32[]{:S(2)}) copy-start(f32[128]{0:T(128)} %param.13) | copy-start | bytes 1540
  29.8 6.1 %collective-permute-start.6 = (f32[64,128]{1,0:T(8,128)S(1)}, f32[64,128]{1,0:T(8,128)S(1)}, u32[]{:S(2)}, u32[]{:S(2)}) collective-permute-start(f32[64,128]{1,0:T(8,128)S(1)} %get-tuple-element.14), channel_id=1, source_target_pairs={{0,6},{1,7},{2,4},{3,5},{4,2},{5,3},{6,0},{7,1},{8,14},{9,15},{10,... | collective-permute-start | bytes 98312 | tf_op jit(solution)/shard_map/ppermute | solution.py:32
  31.0 5.4 %collective-permute-start.7 = (f32[64,128]{1,0:T(8,128)S(1)}, f32[64,128]{1,0:T(8,128)S(1)}, u32[]{:S(2)}, u32[]{:S(2)}) collective-permute-start(f32[64,128]{1,0:T(8,128)S(1)} %get-tuple-element.15), channel_id=1, source_target_pairs={{0,4},{1,5},{2,6},{3,7},{4,0},{5,1},{6,2},{7,3},{8,12},{9,13},{10,... | collective-permute-start | bytes 98312 | tf_op jit(solution)/shard_map/ppermute | solution.py:32
  32.9 4.0 %collective-permute-start.8 = (f32[64,128]{1,0:T(8,128)S(1)}, f32[64,128]{1,0:T(8,128)S(1)}, u32[]{:S(2)}, u32[]{:S(2)}) collective-permute-start(f32[64,128]{1,0:T(8,128)S(1)} %slice_bitcast_fusion), channel_id=1, source_target_pairs={{0,2},{1,3},{2,0},{3,1},{4,6},{5,7},{6,4},{7,5},{8,10},{9,11},{10,... | collective-permute-start | bytes 98312 | tf_op jit(solution)/shard_map/ppermute | solution.py:32

commit v17 on v16

--- a/solution.py
+++ b/solution.py
@@ -32,30 +32,30 @@
     return lax.ppermute(block, axis, [(r, r ^ k) for r in range(lax.axis_size(axis))])
 
 
-def pack_body(slip_hbm, list_hbm, count_hbm, out_ref, slip_ref, list_ref, count_ref, ids, sems):
+def pack_body(slip_hbm, list_hbm, count_hbm, out_ref, list_ref, count_ref, ids, sems):
+    events, entries = list_ref.shape
+    slips = out_ref.at[pl.ds(0, events), pl.ds(0, entries)]
     copies = [
         pltpu.make_async_copy(src, dst, sems.at[j])
-        for j, (src, dst) in enumerate(((list_hbm, list_ref), (count_hbm, count_ref), (slip_hbm, slip_ref)))
+        for j, (src, dst) in enumerate(((list_hbm, list_ref), (count_hbm, count_ref), (slip_hbm, slips)))
     ]
     for copy in copies:
         copy.start()
-    events, entries = list_ref.shape
     row = lax.axis_index("rows")
     entry = lax.broadcasted_iota(jnp.int32, (events, entries), 1) + row * entries
     event = lax.broadcasted_iota(jnp.int32, (events, entries), 0)
     ids[...] = jnp.full(ids.shape, -1.0, jnp.float32)
-    for copy in copies:
+    for copy in copies[:2]:
         copy.wait()
     count = jnp.zeros((events, entries), jnp.int32)
     for e in range(events):
         count = jnp.where(event == e, count_ref[e], count)
     ids[0:events, 0:entries] = jnp.where(entry < count, list_ref[...], -1).astype(jnp.float32)
     out_ref[events] = pltpu.roll(ids[...], row * entries, 1)
-    for e in range(events):
-        out_ref[e, 0:entries, :] = slip_ref[e]
-
-
-def densify_body(entries, *refs):
+    copies[2].wait()
+
+
+def densify_body(entries, sources, *refs):
     ins, (_, out_ref, slips) = refs[:-3], refs[-3:]
     events = ins[0].shape[0] - 1
     width, _, blocks, _ = out_ref.shape
@@ -69,7 +69,7 @@
             ids = jnp.maximum(ids, ref[events, e : e + 1, :])
         ids = jnp.broadcast_to(ids, (width * blocks, BLOCK))[:, :live]
         onehot = (ids == number).astype(jnp.bfloat16)
-        for k, ref in enumerate(ins):
+        for k, ref in zip(sources, ins):
             where = pl.ds(pl.multiple_of((row ^ k) * entries, entries), entries)
             slips[e, where, :] = ref[e, 0:entries, :]
         slip = slips[e]
@@ -157,7 +157,6 @@
         in_specs=[HBM_SPEC] * 3,
         out_specs=VMEM_SPEC,
         scratch_shapes=[
-            pltpu.VMEM(slip_delta.shape, jnp.float32),
             pltpu.VMEM(block_list.shape, jnp.int32),
             pltpu.SMEM(live_count.shape, jnp.int32),
             pltpu.VMEM((SUB, BLOCK), jnp.float32),
@@ -166,17 +165,18 @@
         compiler_params=params(4),
         name="pack",
     )(in_hbm(slip_delta), in_hbm(block_list), in_hbm(live_count))
-    came = {k: send_xor(packed, "rows", k) for k in sorted(range(1, height), key=lambda k: (k < 2, k))}
+    others = sorted(range(1, height), key=lambda k: (k < 2, k))
+    came = [send_xor(packed, "rows", k) for k in others]
     blocks_half = blocks_here // 2
     dense = pl.pallas_call(
-        functools.partial(densify_body, entries),
+        functools.partial(densify_body, entries, [0] + others),
         out_shape=f32(width, events_here, blocks_half, BLOCK),
         in_specs=[VMEM_SPEC] * height + [HBM_SPEC],
         out_specs=VMEM_SPEC,
         scratch_shapes=[pltpu.VMEM((events_here, height * entries, BLOCK), jnp.float32)],
         compiler_params=params(8),
         name="densify",
-    )(packed, *(came[k] for k in range(1, height)), in_hbm(kernel))
+    )(packed, *came, in_hbm(kernel))
     mine = lax.all_to_all(dense, "cols", 0, 0, tiled=True)
 
     def call(body, targets, outs, *args):

time: 37.8 us -> 37.4 us (0.989)
  blocking collectives: 14.9 us -> 14.5 us
where the time goes in v17:
time: 37.4 us; the launch traced here: 37.2 us
  blocking collectives  14.5 us (39%)
  starting transfers between devices  9.9 us (26%)
  waiting for transfers between devices  6.63 us (18%)
  Pallas kernels  4.68 us (13%)
  between operations  0.73 us (2%)
  other arithmetic  0.69 us (2%)
    all_to_all x1, blocking collectives, per_device(): mine = lax.all_to_all(dense, 'cols', 0, 0, tiled=True)  14.5 us
    ppermute x9, starting transfers between devices, send_xor(): lax.ppermute(block, axis, [(r, r ^ k) for r in range(lax.axis_size(axis))])  9.9 us
    ppermute x9, waiting for transfers between devices, send_xor(): lax.ppermute(block, axis, [(r, r ^ k) for r in range(lax.axis_size(axis))])  6.63 us
    pallas_call x5, Pallas kernels, call(): pl.pallas_call(functools.partial(body, targets), out_shape=outs, in_specs...  3.46 us
    pallas_call x1, Pallas kernels, per_device(): pl.pallas_call(pack_body, out_shape=f32(events_here + 1, SUB, BLOCK), in_...  0.96 us
  transfers between devices with their start and end apart: 9, of which 6 were waited for; matrix products, arithmetic and copies ran while one was open for 0% of the time, Pallas kernels for 8%

profile of v17, /device:TPU:0, one launch (start us, length us, event | category | flops | bytes accessed | tf_op | source)
XLA Modules:
  0.0 37.2 jit_solution(10062234602620140499)
XLA Ops:
  0.6 0.0 copy-start
  0.6 1.0 %pack.1.refs_0_ = f32[9,8,128]{2,1,0:T(8,128)S(1)} custom-call(f32[8,8,128]{2,1,0:T(8,128)} %slip_hbm.1, s32[8,8]{1,0:T(8,128)} %list_hbm.1, s32[8]{0:T(128)} %count_hbm.1), custom_call_target="tpu_custom_call" | custom-call | tf_op jit(solution)/shard_map/pack/pallas_call | solution.py:154
  1.6 3.0 %collective-permute-start = (f32[9,8,128]{2,1,0:T(8,128)S(1)}, f32[9,8,128]{2,1,0:T(8,128)S(1)}, u32[]{:S(2)}, u32[]{:S(2)}) collective-permute-start(f32[9,8,128]{2,1,0:T(8,128)S(1)} %pack.1.refs_0_), channel_id=1, source_target_pairs={{0,16},{8,24},{16,0},{24,8},{1,17},{9,25},{17,1},{25,9},{2,18},{10... | collective-permute-start | bytes 110600 | tf_op jit(solution)/shard_map/ppermute | solution.py:32
  4.6 0.0 collective-permute-start.1
  4.6 0.2 collective-permute-start.2
  4.8 1.7 %collective-permute-done.refs_1_ = f32[9,8,128]{2,1,0:T(8,128)S(1)} collective-permute-done((f32[9,8,128]{2,1,0:T(8,128)S(1)}, f32[9,8,128]{2,1,0:T(8,128)S(1)}, u32[]{:S(2)}, u32[]{:S(2)}) %collective-permute-start) | collective-permute-done | bytes 36896 | tf_op jit(solution)/shard_map/ppermute | solution.py:32
  6.6 1.6 %collective-permute-done.1.refs_2_ = f32[9,8,128]{2,1,0:T(8,128)S(1)} collective-permute-done((f32[9,8,128]{2,1,0:T(8,128)S(1)}, f32[9,8,128]{2,1,0:T(8,128)S(1)}, u32[]{:S(2)}, u32[]{:S(2)}) %collective-permute-start.1) | collective-permute-done | bytes 36896 | tf_op jit(solution)/shard_map/ppermute | solution.py:32
  8.2 0.0 collective-permute-done.2.refs_3_
  8.2 0.3 densify.1
  8.4 14.5 %all_to_all.5.dense_ref = f32[8,8,8,128]{3,2,1,0:T(8,128)S(1)} all-to-all(f32[8,8,8,128]{3,2,1,0:T(8,128)S(1)} %densify.1), channel_id=1, replica_groups=mesh['rows'=4,'cols'=8] {'cols'}, dimensions={0} | all-to-all | bytes 524288 | tf_op jit(solution)/shard_map/all_to_all | solution.py:180
  23.0 0.0 collective-permute-start.3
  23.0 0.0 copy-done
  23.0 0.8 %own_stress.1 = (bf16[128,1024]{1,0:T(8,128)(2,1)S(1)}, f32[2,64,128]{2,1,0:T(8,128)S(1)}, f32[2,64,128]{2,1,0:T(8,128)S(1)}) custom-call(f32[8,8,8,128]{3,2,1,0:T(8,128)S(1)} %all_to_all.5.dense_ref, f32[8,128,2048]{2,1,0:T(8,128)S(1)} %bitcast.20), custom_call_target="tpu_custom_call" | custom-call | flops 201326592 | bytes 2097152 | tf_op jit(solution)/shard_map/own_stress/pallas_call | solution.py:183
  23.8 0.7 %collective-permute-done.3.dense_ref = f32[8,8,8,128]{3,2,1,0:T(8,128)S(1)} collective-permute-done((f32[8,8,8,128]{3,2,1,0:T(8,128)S(1)}, f32[8,8,8,128]{3,2,1,0:T(8,128)S(1)}, u32[]{:S(2)}, u32[]{:S(2)}) %collective-permute-start.3) | collective-permute-done | bytes 262176 | tf_op jit(solution)/shard_map/ppermute | solution.py:32
  24.5 0.5 %other_stress.1 = (bf16[128,1024]{1,0:T(8,128)(2,1)S(1)}, f32[2,64,128]{2,1,0:T(8,128)S(1)}) custom-call(f32[8,8,8,128]{3,2,1,0:T(8,128)S(1)} %collective-permute-done.3.dense_ref, f32[8,128,2048]{2,1,0:T(8,128)S(1)} %bitcast.21, f32[2,64,128]{2,1,0:T(8,128)S(1)} %get-tuple-element.8.sum_ref), custom_call_target="tpu_custom_call" | custom-call | flops 201326592 | bytes 2097152 | tf_op jit(solution)/shard_map/other_stress/pallas_call | solution.py:183
  25.0 1.5 %collective-permute-start.5 = (f32[2,64,128]{2,1,0:T(8,128)S(1)}, f32[2,64,128]{2,1,0:T(8,128)S(1)}, u32[]{:S(2)}, u32[]{:S(2)}) collective-permute-start(f32[2,64,128]{2,1,0:T(8,128)S(1)} %get-tuple-element.11), channel_id=1, source_target_pairs={{0,1},{1,0},{2,3},{3,2},{4,5},{5,4},{6,7},{7,6},{8,9},{9,8},{10,11... | collective-permute-start | bytes 196616 | tf_op jit(solution)/shard_map/ppermute | solution.py:32
  26.5 0.5 %rest_stress.1 = f32[2,64,128]{2,1,0:T(8,128)S(1)} custom-call(bf16[128,1024]{1,0:T(8,128)(2,1)S(1)} %get-tuple-element.9.other_ref.slip_ref, f32[8,128,2048]{2,1,0:T(8,128)S(1)} %bitcast.22, f32[2,64,128]{2,1,0:T(8,128)S(1)} %get-tuple-element.10.sum_ref), custom_call_target="tpu_custom_call" | custom-call | flops 201326592 | bytes 2097152 | tf_op jit(solution)/shard_map/rest_stress/pallas_call | solution.py:183
  27.0 0.7 %collective-permute-start.4 = (f32[2,64,128]{2,1,0:T(8,128)S(1)}, f32[2,64,128]{2,1,0:T(8,128)S(1)}, u32[]{:S(2)}, u32[]{:S(2)}) collective-permute-start(f32[2,64,128]{2,1,0:T(8,128)S(1)} %rest_stress.1), channel_id=1, source_target_pairs={{0,1},{1,0},{2,3},{3,2},{4,5},{5,4},{6,7},{7,6},{8,9},{9,8},{10,11... | collective-permute-start | bytes 196616 | tf_op jit(solution)/shard_map/ppermute | solution.py:32
  27.6 0.0 copy-start.1
  27.6 0.0 copy-start.2
  27.7 0.0 copy-start.3
  27.7 0.8 %both_stress.3 = f32[2,64,128]{2,1,0:T(8,128)S(1)} custom-call(bf16[128,1024]{1,0:T(8,128)(2,1)S(1)} %get-tuple-element.7.own_ref, bf16[128,1024]{1,0:T(8,128)(2,1)S(1)} %get-tuple-element.9.other_ref.slip_ref, f32[8,128,2048]{2,1,0:T(8,128)S(1)} %bitcast.23), custom_call_target="tpu_custom_call" | custom-call | flops 201326592 | bytes 2097152 | tf_op jit(solution)/shard_map/both_stress/pallas_call | solution.py:183
  28.5 0.8 %both_stress.2 = f32[2,64,128]{2,1,0:T(8,128)S(1)} custom-call(bf16[128,1024]{1,0:T(8,128)(2,1)S(1)} %get-tuple-element.7.own_ref, bf16[128,1024]{1,0:T(8,128)(2,1)S(1)} %get-tuple-element.9.other_ref.slip_ref, f32[8,128,2048]{2,1,0:T(8,128)S(1)} %bitcast.24), custom_call_target="tpu_custom_call" | custom-call | flops 201326592 | bytes 2097152 | tf_op jit(solution)/shard_map/both_stress/pallas_call | solution.py:183
  29.3 0.0 collective-permute-done.5
  29.4 1.2 %collective-permute-start.6 = (f32[64,128]{1,0:T(8,128)S(1)}, f32[64,128]{1,0:T(8,128)S(1)}, u32[]{:S(2)}, u32[]{:S(2)}) collective-permute-start(f32[64,128]{1,0:T(8,128)S(1)} %get-tuple-element.14), channel_id=1, source_target_pairs={{0,6},{1,7},{2,4},{3,5},{4,2},{5,3},{6,0},{7,1},{8,14},{9,15},{10,... | collective-permute-start | bytes 98312 | tf_op jit(solution)/shard_map/ppermute | solution.py:32
  30.6 2.0 %collective-permute-start.7 = (f32[64,128]{1,0:T(8,128)S(1)}, f32[64,128]{1,0:T(8,128)S(1)}, u32[]{:S(2)}, u32[]{:S(2)}) collective-permute-start(f32[64,128]{1,0:T(8,128)S(1)} %get-tuple-element.15), channel_id=1, source_target_pairs={{0,4},{1,5},{2,6},{3,7},{4,0},{5,1},{6,2},{7,3},{8,12},{9,13},{10,... | collective-permute-start | bytes 98312 | tf_op jit(solution)/shard_map/ppermute | solution.py:32
  32.5 0.0 collective-permute-done.4
  32.6 1.4 %collective-permute-start.8 = (f32[64,128]{1,0:T(8,128)S(1)}, f32[64,128]{1,0:T(8,128)S(1)}, u32[]{:S(2)}, u32[]{:S(2)}) collective-permute-start(f32[64,128]{1,0:T(8,128)S(1)} %slice_bitcast_fusion), channel_id=1, source_target_pairs={{0,2},{1,3},{2,0},{3,1},{4,6},{5,7},{6,4},{7,5},{8,10},{9,11},{10,... | collective-permute-start | bytes 98312 | tf_op jit(solution)/shard_map/ppermute | solution.py:32
  33.9 0.0 copy-done.1
  33.9 0.0 copy-done.2
  33.9 0.0 copy-done.3
  33.9 1.5 %collective-permute-done.6 = f32[64,128]{1,0:T(8,128)S(1)} collective-permute-done((f32[64,128]{1,0:T(8,128)S(1)}, f32[64,128]{1,0:T(8,128)S(1)}, u32[]{:S(2)}, u32[]{:S(2)}) %collective-permute-start.6) | collective-permute-done | bytes 32800 | tf_op jit(solution)/shard_map/ppermute | solution.py:32
  35.5 0.5 %collective-permute-done.7 = f32[64,128]{1,0:T(8,128)S(1)} collective-permute-done((f32[64,128]{1,0:T(8,128)S(1)}, f32[64,128]{1,0:T(8,128)S(1)}, u32[]{:S(2)}, u32[]{:S(2)}) %collective-permute-start.7) | collective-permute-done | bytes 32800 | tf_op jit(solution)/shard_map/ppermute | solution.py:32
  36.0 0.6 %collective-permute-done.8 = f32[64,128]{1,0:T(8,128)S(1)} collective-permute-done((f32[64,128]{1,0:T(8,128)S(1)}, f32[64,128]{1,0:T(8,128)S(1)}, u32[]{:S(2)}, u32[]{:S(2)}) %collective-permute-start.8) | collective-permute-done | bytes 32800 | tf_op jit(solution)/shard_map/ppermute | solution.py:32
  36.5 0.7 %add_bitcast_fusion = (f32[128,64]{0,1:T(8,128)}, f32[64,128]{1,0:T(8,128)}) fusion(f32[128]{0:T(128)S(1)} %get-tuple-element.17, f32[128]{0:T(128)S(1)} %copy-done.1, f32[128]{0:T(128)S(1)} %get-tuple-element.16, f32[64,128]{1,0:T(8,128)S(1)} %collective-permute-done.8, f32[64,128]{1,0:T(8,128)S(1)} %collective-permute-done.7, ...), kind=kLoop, calls=%fused_computation.7 | loop fusion | flops 57344 | bytes 198144 | tf_op jit(solution)/shard_map/transpose | solution.py:218
  (5 shorter events, 0.0 us)
Async XLA Ops:
  0.6 22.3 %copy-start = (f32[1024,2048]{1,0:T(8,128)S(1)}, f32[1024,2048]{1,0:T(8,128)}, u32[]{:S(2)}) copy-start(f32[1024,2048]{1,0:T(8,128)} %param.7) | copy-start | bytes 25165828
  1.6 5.0 %collective-permute-start = (f32[9,8,128]{2,1,0:T(8,128)S(1)}, f32[9,8,128]{2,1,0:T(8,128)S(1)}, u32[]{:S(2)}, u32[]{:S(2)}) collective-permute-start(f32[9,8,128]{2,1,0:T(8,128)S(1)} %pack.1.refs_0_), channel_id=1, source_target_pairs={{0,16},{8,24},{16,0},{24,8},{1,17},{9,25},{17,1},{25,9},{2,18},{10... | collective-permute-start | bytes 110600 | tf_op jit(solution)/shard_map/ppermute | solution.py:32
  4.6 3.5 %collective-permute-start.1 = (f32[9,8,128]{2,1,0:T(8,128)S(1)}, f32[9,8,128]{2,1,0:T(8,128)S(1)}, u32[]{:S(2)}, u32[]{:S(2)}) collective-permute-start(f32[9,8,128]{2,1,0:T(8,128)S(1)} %pack.1.refs_0_), channel_id=1, source_target_pairs={{0,24},{8,16},{16,8},{24,0},{1,25},{9,17},{17,9},{25,1},{2,26},{10... | collective-permute-start | bytes 110600 | tf_op jit(solution)/shard_map/ppermute | solution.py:32
  4.6 3.5 %collective-permute-start.2 = (f32[9,8,128]{2,1,0:T(8,128)S(1)}, f32[9,8,128]{2,1,0:T(8,128)S(1)}, u32[]{:S(2)}, u32[]{:S(2)}) collective-permute-start(f32[9,8,128]{2,1,0:T(8,128)S(1)} %pack.1.refs_0_), channel_id=1, source_target_pairs={{0,8},{8,0},{16,24},{24,16},{1,9},{9,1},{17,25},{25,17},{2,10},{10... | collective-permute-start | bytes 110600 | tf_op jit(solution)/shard_map/ppermute | solution.py:32
  23.0 1.5 %collective-permute-start.3 = (f32[8,8,8,128]{3,2,1,0:T(8,128)S(1)}, f32[8,8,8,128]{3,2,1,0:T(8,128)S(1)}, u32[]{:S(2)}, u32[]{:S(2)}) collective-permute-start(f32[8,8,8,128]{3,2,1,0:T(8,128)S(1)} %all_to_all.5.dense_ref), channel_id=1, source_target_pairs={{0,8},{8,0},{16,24},{24,16},{1,9},{9,1},{17,25},{25,17},{2,10},{10... | collective-permute-start | bytes 786440 | tf_op jit(solution)/shard_map/ppermute | solution.py:32
  25.0 4.3 %collective-permute-start.5 = (f32[2,64,128]{2,1,0:T(8,128)S(1)}, f32[2,64,128]{2,1,0:T(8,128)S(1)}, u32[]{:S(2)}, u32[]{:S(2)}) collective-permute-start(f32[2,64,128]{2,1,0:T(8,128)S(1)} %get-tuple-element.11), channel_id=1, source_target_pairs={{0,1},{1,0},{2,3},{3,2},{4,5},{5,4},{6,7},{7,6},{8,9},{9,8},{10,11... | collective-permute-start | bytes 196616 | tf_op jit(solution)/shard_map/ppermute | solution.py:32
  27.0 5.6 %collective-permute-start.4 = (f32[2,64,128]{2,1,0:T(8,128)S(1)}, f32[2,64,128]{2,1,0:T(8,128)S(1)}, u32[]{:S(2)}, u32[]{:S(2)}) collective-permute-start(f32[2,64,128]{2,1,0:T(8,128)S(1)} %rest_stress.1), channel_id=1, source_target_pairs={{0,1},{1,0},{2,3},{3,2},{4,5},{5,4},{6,7},{7,6},{8,9},{9,8},{10,11... | collective-permute-start | bytes 196616 | tf_op jit(solution)/shard_map/ppermute | solution.py:32
  27.6 6.3 %copy-start.1 = (f32[128]{0:T(128)S(1)}, f32[128]{0:T(128)}, u32[]{:S(2)}) copy-start(f32[128]{0:T(128)} %param.11) | copy-start | bytes 1540
  27.6 6.3 %copy-start.2 = (f32[128]{0:T(128)S(1)}, f32[128]{0:T(128)}, u32[]{:S(2)}) copy-start(f32[128]{0:T(128)} %param.12) | copy-start | bytes 1540
  27.7 6.3 %copy-start.3 = (f32[128]{0:T(128)S(1)}, f32[128]{0:T(128)}, u32[]{:S(2)}) copy-start(f32[128]{0:T(128)} %param.13) | copy-start | bytes 1540
  29.4 6.1 %collective-permute-start.6 = (f32[64,128]{1,0:T(8,128)S(1)}, f32[64,128]{1,0:T(8,128)S(1)}, u32[]{:S(2)}, u32[]{:S(2)}) collective-permute-start(f32[64,128]{1,0:T(8,128)S(1)} %get-tuple-element.14), channel_id=1, source_target_pairs={{0,6},{1,7},{2,4},{3,5},{4,2},{5,3},{6,0},{7,1},{8,14},{9,15},{10,... | collective-permute-start | bytes 98312 | tf_op jit(solution)/shard_map/ppermute | solution.py:32
  30.6 5.4 %collective-permute-start.7 = (f32[64,128]{1,0:T(8,128)S(1)}, f32[64,128]{1,0:T(8,128)S(1)}, u32[]{:S(2)}, u32[]{:S(2)}) collective-permute-start(f32[64,128]{1,0:T(8,128)S(1)} %get-tuple-element.15), channel_id=1, source_target_pairs={{0,4},{1,5},{2,6},{3,7},{4,0},{5,1},{6,2},{7,3},{8,12},{9,13},{10,... | collective-permute-start | bytes 98312 | tf_op jit(solution)/shard_map/ppermute | solution.py:32
  32.6 4.0 %collective-permute-start.8 = (f32[64,128]{1,0:T(8,128)S(1)}, f32[64,128]{1,0:T(8,128)S(1)}, u32[]{:S(2)}, u32[]{:S(2)}) collective-permute-start(f32[64,128]{1,0:T(8,128)S(1)} %slice_bitcast_fusion), channel_id=1, source_target_pairs={{0,2},{1,3},{2,0},{3,1},{4,6},{5,7},{6,4},{7,5},{8,10},{9,11},{10,... | collective-permute-start | bytes 98312 | tf_op jit(solution)/shard_map/ppermute | solution.py:32

commit v18 on v17

--- a/solution.py
+++ b/solution.py
@@ -124,11 +124,6 @@
 def rest_body(targets, slip_ref, kernel_ref, sum_ref, out_ref):
     for j, k in enumerate(targets):
         out_ref[j] = sum_ref[j] + stress(k, 1, slip_ref, kernel_ref)
-
-
-def both_body(targets, own_ref, other_ref, kernel_ref, out_ref):
-    for j, k in enumerate(targets):
-        out_ref[j] = stress(k, 0, own_ref, kernel_ref) + stress(k, 1, other_ref, kernel_ref)
 
 
 def halving_order(width):
@@ -197,16 +192,17 @@
     slips = bf16(2 * events, blocks_half * BLOCK)
     sums = f32(quarter, events, share)
     came = send_xor(mine, "rows", 1)
-    own, far_own, near_own = call(own_body, (far_send, near_send), [slips, sums, sums], mine, kernel)
-    other, far_sent = call(other_body, far_send, [slips, sums], came, kernel, far_own)
-
-    def later(targets):
-        return call(both_body, targets, sums, own, other, kernel)
+    groups = (far_send, near_send, far_keep, near_keep)
+    _, *own_sums = call(own_body, groups, [slips] + [sums] * 4, mine, kernel)
+    other, far_sent = call(other_body, far_send, [slips, sums], came, kernel, own_sums[0])
+
+    def rest(g):
+        return call(rest_body, groups[g], sums, other, kernel, own_sums[g])
 
     far_came = send_xor(far_sent, "cols", 1)
-    near_came = send_xor(call(rest_body, near_send, sums, other, kernel, near_own), "cols", 1)
-    far = later(far_keep) + far_came
-    near = later(near_keep) + near_came
+    near_came = send_xor(rest(1), "cols", 1)
+    far = rest(2) + far_came
+    near = rest(3) + near_came
     parts = [send_xor(far[j], "cols", k) for j, k in reversed(list(enumerate(far_keep)))]
     parts += [send_xor(near[j], "cols", k) for j, k in enumerate(near_keep) if k]
     stress_change = sum(parts, near[0])

time: 37.4 us -> 37.8 us (1.011)
  Pallas kernels: 4.68 us -> 5.12 us
    pallas_call x5, Pallas kernels: 3.46 us -> 3.9 us  [call(): pl.pallas_call(functools.partial(body, targets), out_shape=outs, in_specs...]
  transfers between devices with their start and end apart: 9 -> 9, of which waited for: 6 -> 6; matrix products, arithmetic and copies ran while one was open for 0% -> 0% of each run, Pallas kernels for 8% -> 9%
where the time goes in v18:
time: 37.8 us; the launch traced here: 37.7 us
  blocking collectives  14.5 us (38%)
  starting transfers between devices  9.9 us (26%)
  waiting for transfers between devices  6.66 us (18%)
  Pallas kernels  5.12 us (14%)
  between operations  0.72 us (2%)
  other arithmetic  0.69 us (2%)
    all_to_all x1, blocking collectives, per_device(): mine = lax.all_to_all(dense, 'cols', 0, 0, tiled=True)  14.5 us
    ppermute x9, starting transfers between devices, send_xor(): lax.ppermute(block, axis, [(r, r ^ k) for r in range(lax.axis_size(axis))])  9.9 us
    ppermute x9, waiting for transfers between devices, send_xor(): lax.ppermute(block, axis, [(r, r ^ k) for r in range(lax.axis_size(axis))])  6.66 us
    pallas_call x5, Pallas kernels, call(): pl.pallas_call(functools.partial(body, targets), out_shape=outs, in_specs...  3.9 us
    pallas_call x1, Pallas kernels, per_device(): pl.pallas_call(pack_body, out_shape=f32(events_here + 1, SUB, BLOCK), in_...  0.96 us
  transfers between devices with their start and end apart: 9, of which 6 were waited for; matrix products, arithmetic and copies ran while one was open for 0% of the time, Pallas kernels for 9%

profile of v18, /device:TPU:0, one launch (start us, length us, event | category | flops | bytes accessed | tf_op | source)
XLA Modules:
  0.0 37.7 jit_solution(11708841416654387442)
XLA Ops:
  0.6 0.0 copy-start
  0.6 1.0 %pack.1.refs_0_ = f32[9,8,128]{2,1,0:T(8,128)S(1)} custom-call(f32[8,8,128]{2,1,0:T(8,128)} %slip_hbm.1, s32[8,8]{1,0:T(8,128)} %list_hbm.1, s32[8]{0:T(128)} %count_hbm.1), custom_call_target="tpu_custom_call" | custom-call | tf_op jit(solution)/shard_map/pack/pallas_call | solution.py:149
  1.6 3.0 %collective-permute-start = (f32[9,8,128]{2,1,0:T(8,128)S(1)}, f32[9,8,128]{2,1,0:T(8,128)S(1)}, u32[]{:S(2)}, u32[]{:S(2)}) collective-permute-start(f32[9,8,128]{2,1,0:T(8,128)S(1)} %pack.1.refs_0_), channel_id=1, source_target_pairs={{0,16},{8,24},{16,0},{24,8},{1,17},{9,25},{17,1},{25,9},{2,18},{10... | collective-permute-start | bytes 110600 | tf_op jit(solution)/shard_map/ppermute | solution.py:32
  4.6 0.0 collective-permute-start.1
  4.6 0.2 collective-permute-start.2
  4.8 1.7 %collective-permute-done.refs_1_ = f32[9,8,128]{2,1,0:T(8,128)S(1)} collective-permute-done((f32[9,8,128]{2,1,0:T(8,128)S(1)}, f32[9,8,128]{2,1,0:T(8,128)S(1)}, u32[]{:S(2)}, u32[]{:S(2)}) %collective-permute-start) | collective-permute-done | bytes 36896 | tf_op jit(solution)/shard_map/ppermute | solution.py:32
  6.6 1.6 %collective-permute-done.1.refs_2_ = f32[9,8,128]{2,1,0:T(8,128)S(1)} collective-permute-done((f32[9,8,128]{2,1,0:T(8,128)S(1)}, f32[9,8,128]{2,1,0:T(8,128)S(1)}, u32[]{:S(2)}, u32[]{:S(2)}) %collective-permute-start.1) | collective-permute-done | bytes 36896 | tf_op jit(solution)/shard_map/ppermute | solution.py:32
  8.2 0.0 collective-permute-done.2.refs_3_
  8.2 0.3 densify.1
  8.4 14.5 %all_to_all.5.dense_ref = f32[8,8,8,128]{3,2,1,0:T(8,128)S(1)} all-to-all(f32[8,8,8,128]{3,2,1,0:T(8,128)S(1)} %densify.1), channel_id=1, replica_groups=mesh['rows'=4,'cols'=8] {'cols'}, dimensions={0} | all-to-all | bytes 524288 | tf_op jit(solution)/shard_map/all_to_all | solution.py:175
  23.0 0.0 collective-permute-start.3
  23.0 0.0 copy-done
  23.0 1.9 %own_stress.1 = (bf16[128,1024]{1,0:T(8,128)(2,1)}, f32[2,64,128]{2,1,0:T(8,128)S(1)}, f32[2,64,128]{2,1,0:T(8,128)S(1)}, f32[2,64,128]{2,1,0:T(8,128)S(1)}, f32[2,64,128]{2,1,0:T(8,128)S(1)}) custom-call(f32[8,8,8,128]{3,2,1,0:T(8,128)S(1)} %all_to_all.5.dense_ref, f32[8,128,2048]{2,1,0:T(8,128)S(1)} %bitcast.20), custom_call_target="tpu_custom_call" | custom-call | flops 201326592 | bytes 2097152 | tf_op jit(solution)/shard_map/own_stress/pallas_call | solution.py:178
  24.9 0.0 collective-permute-done.3.dense_ref
  24.9 0.5 %other_stress.1 = (bf16[128,1024]{1,0:T(8,128)(2,1)S(1)}, f32[2,64,128]{2,1,0:T(8,128)S(1)}) custom-call(f32[8,8,8,128]{3,2,1,0:T(8,128)S(1)} %collective-permute-done.3.dense_ref, f32[8,128,2048]{2,1,0:T(8,128)S(1)} %bitcast.21, f32[2,64,128]{2,1,0:T(8,128)S(1)} %get-tuple-element.8.sum_ref), custom_call_target="tpu_custom_call" | custom-call | flops 201326592 | bytes 2097152 | tf_op jit(solution)/shard_map/other_stress/pallas_call | solution.py:178
  25.4 1.5 %collective-permute-start.5 = (f32[2,64,128]{2,1,0:T(8,128)S(1)}, f32[2,64,128]{2,1,0:T(8,128)S(1)}, u32[]{:S(2)}, u32[]{:S(2)}) collective-permute-start(f32[2,64,128]{2,1,0:T(8,128)S(1)} %get-tuple-element.13), channel_id=1, source_target_pairs={{0,1},{1,0},{2,3},{3,2},{4,5},{5,4},{6,7},{7,6},{8,9},{9,8},{10,11... | collective-permute-start | bytes 196616 | tf_op jit(solution)/shard_map/ppermute | solution.py:32
  26.9 0.5 %rest_stress.4 = f32[2,64,128]{2,1,0:T(8,128)S(1)} custom-call(bf16[128,1024]{1,0:T(8,128)(2,1)S(1)} %get-tuple-element.9.slip_ref, f32[8,128,2048]{2,1,0:T(8,128)S(1)} %bitcast.22, f32[2,64,128]{2,1,0:T(8,128)S(1)} %get-tuple-element.11.sum_ref), custom_call_target="tpu_custom_call" | custom-call | flops 201326592 | bytes 2097152 | tf_op jit(solution)/shard_map/rest_stress/pallas_call | solution.py:178
  27.4 0.7 %collective-permute-start.4 = (f32[2,64,128]{2,1,0:T(8,128)S(1)}, f32[2,64,128]{2,1,0:T(8,128)S(1)}, u32[]{:S(2)}, u32[]{:S(2)}) collective-permute-start(f32[2,64,128]{2,1,0:T(8,128)S(1)} %rest_stress.4), channel_id=1, source_target_pairs={{0,1},{1,0},{2,3},{3,2},{4,5},{5,4},{6,7},{7,6},{8,9},{9,8},{10,11... | collective-permute-start | bytes 196616 | tf_op jit(solution)/shard_map/ppermute | solution.py:32
  28.1 0.0 copy-start.1
  28.1 0.0 copy-start.2
  28.1 0.0 copy-start.3
  28.1 0.5 %rest_stress.5 = f32[2,64,128]{2,1,0:T(8,128)S(1)} custom-call(bf16[128,1024]{1,0:T(8,128)(2,1)S(1)} %get-tuple-element.9.slip_ref, f32[8,128,2048]{2,1,0:T(8,128)S(1)} %bitcast.23, f32[2,64,128]{2,1,0:T(8,128)S(1)} %get-tuple-element.12.sum_ref), custom_call_target="tpu_custom_call" | custom-call | flops 201326592 | bytes 2097152 | tf_op jit(solution)/shard_map/rest_stress/pallas_call | solution.py:178
  28.6 0.5 %rest_stress.3 = f32[2,64,128]{2,1,0:T(8,128)S(1)} custom-call(bf16[128,1024]{1,0:T(8,128)(2,1)S(1)} %get-tuple-element.9.slip_ref, f32[8,128,2048]{2,1,0:T(8,128)S(1)} %bitcast.24, f32[2,64,128]{2,1,0:T(8,128)S(1)} %get-tuple-element.10.sum_ref), custom_call_target="tpu_custom_call" | custom-call | flops 201326592 | bytes 2097152 | tf_op jit(solution)/shard_map/rest_stress/pallas_call | solution.py:178
  29.1 0.9 %collective-permute-done.5 = f32[2,64,128]{2,1,0:T(8,128)S(1)} collective-permute-done((f32[2,64,128]{2,1,0:T(8,128)S(1)}, f32[2,64,128]{2,1,0:T(8,128)S(1)}, u32[]{:S(2)}, u32[]{:S(2)}) %collective-permute-start.5) | collective-permute-done | bytes 65568 | tf_op jit(solution)/shard_map/ppermute | solution.py:32
  30.0 1.2 %collective-permute-start.6 = (f32[64,128]{1,0:T(8,128)S(1)}, f32[64,128]{1,0:T(8,128)S(1)}, u32[]{:S(2)}, u32[]{:S(2)}) collective-permute-start(f32[64,128]{1,0:T(8,128)S(1)} %get-tuple-element.16), channel_id=1, source_target_pairs={{0,6},{1,7},{2,4},{3,5},{4,2},{5,3},{6,0},{7,1},{8,14},{9,15},{10,... | collective-permute-start | bytes 98312 | tf_op jit(solution)/shard_map/ppermute | solution.py:32
  31.2 1.8 %collective-permute-start.7 = (f32[64,128]{1,0:T(8,128)S(1)}, f32[64,128]{1,0:T(8,128)S(1)}, u32[]{:S(2)}, u32[]{:S(2)}) collective-permute-start(f32[64,128]{1,0:T(8,128)S(1)} %get-tuple-element.17), channel_id=1, source_target_pairs={{0,4},{1,5},{2,6},{3,7},{4,0},{5,1},{6,2},{7,3},{8,12},{9,13},{10,... | collective-permute-start | bytes 98312 | tf_op jit(solution)/shard_map/ppermute | solution.py:32
  33.0 0.0 collective-permute-done.4
  33.0 1.5 %collective-permute-start.8 = (f32[64,128]{1,0:T(8,128)S(1)}, f32[64,128]{1,0:T(8,128)S(1)}, u32[]{:S(2)}, u32[]{:S(2)}) collective-permute-start(f32[64,128]{1,0:T(8,128)S(1)} %slice_bitcast_fusion), channel_id=1, source_target_pairs={{0,2},{1,3},{2,0},{3,1},{4,6},{5,7},{6,4},{7,5},{8,10},{9,11},{10,... | collective-permute-start | bytes 98312 | tf_op jit(solution)/shard_map/ppermute | solution.py:32
  34.6 0.0 copy-done.1
  34.6 0.0 copy-done.2
  34.6 0.0 copy-done.3
  34.6 1.5 %collective-permute-done.6 = f32[64,128]{1,0:T(8,128)S(1)} collective-permute-done((f32[64,128]{1,0:T(8,128)S(1)}, f32[64,128]{1,0:T(8,128)S(1)}, u32[]{:S(2)}, u32[]{:S(2)}) %collective-permute-start.6) | collective-permute-done | bytes 32800 | tf_op jit(solution)/shard_map/ppermute | solution.py:32
  36.1 0.5 %collective-permute-done.7 = f32[64,128]{1,0:T(8,128)S(1)} collective-permute-done((f32[64,128]{1,0:T(8,128)S(1)}, f32[64,128]{1,0:T(8,128)S(1)}, u32[]{:S(2)}, u32[]{:S(2)}) %collective-permute-start.7) | collective-permute-done | bytes 32800 | tf_op jit(solution)/shard_map/ppermute | solution.py:32
  36.6 0.4 %collective-permute-done.8 = f32[64,128]{1,0:T(8,128)S(1)} collective-permute-done((f32[64,128]{1,0:T(8,128)S(1)}, f32[64,128]{1,0:T(8,128)S(1)}, u32[]{:S(2)}, u32[]{:S(2)}) %collective-permute-start.8) | collective-permute-done | bytes 32800 | tf_op jit(solution)/shard_map/ppermute | solution.py:32
  37.0 0.7 %add_bitcast_fusion = (f32[128,64]{0,1:T(8,128)}, f32[64,128]{1,0:T(8,128)}) fusion(f32[128]{0:T(128)S(1)} %get-tuple-element.19, f32[128]{0:T(128)S(1)} %copy-done.1, f32[128]{0:T(128)S(1)} %get-tuple-element.18, f32[64,128]{1,0:T(8,128)S(1)} %collective-permute-done.8, f32[64,128]{1,0:T(8,128)S(1)} %collective-permute-done.7, ...), kind=kLoop, calls=%fused_computation.7 | loop fusion | flops 57344 | bytes 198144 | tf_op jit(solution)/shard_map/transpose | solution.py:214
  (5 shorter events, 0.0 us)
Async XLA Ops:
  0.6 22.3 %copy-start = (f32[1024,2048]{1,0:T(8,128)S(1)}, f32[1024,2048]{1,0:T(8,128)}, u32[]{:S(2)}) copy-start(f32[1024,2048]{1,0:T(8,128)} %param.7) | copy-start | bytes 25165828
  1.6 5.0 %collective-permute-start = (f32[9,8,128]{2,1,0:T(8,128)S(1)}, f32[9,8,128]{2,1,0:T(8,128)S(1)}, u32[]{:S(2)}, u32[]{:S(2)}) collective-permute-start(f32[9,8,128]{2,1,0:T(8,128)S(1)} %pack.1.refs_0_), channel_id=1, source_target_pairs={{0,16},{8,24},{16,0},{24,8},{1,17},{9,25},{17,1},{25,9},{2,18},{10... | collective-permute-start | bytes 110600 | tf_op jit(solution)/shard_map/ppermute | solution.py:32
  4.6 3.5 %collective-permute-start.1 = (f32[9,8,128]{2,1,0:T(8,128)S(1)}, f32[9,8,128]{2,1,0:T(8,128)S(1)}, u32[]{:S(2)}, u32[]{:S(2)}) collective-permute-start(f32[9,8,128]{2,1,0:T(8,128)S(1)} %pack.1.refs_0_), channel_id=1, source_target_pairs={{0,24},{8,16},{16,8},{24,0},{1,25},{9,17},{17,9},{25,1},{2,26},{10... | collective-permute-start | bytes 110600 | tf_op jit(solution)/shard_map/ppermute | solution.py:32
  4.6 3.5 %collective-permute-start.2 = (f32[9,8,128]{2,1,0:T(8,128)S(1)}, f32[9,8,128]{2,1,0:T(8,128)S(1)}, u32[]{:S(2)}, u32[]{:S(2)}) collective-permute-start(f32[9,8,128]{2,1,0:T(8,128)S(1)} %pack.1.refs_0_), channel_id=1, source_target_pairs={{0,8},{8,0},{16,24},{24,16},{1,9},{9,1},{17,25},{25,17},{2,10},{10... | collective-permute-start | bytes 110600 | tf_op jit(solution)/shard_map/ppermute | solution.py:32
  23.0 1.9 %collective-permute-start.3 = (f32[8,8,8,128]{3,2,1,0:T(8,128)S(1)}, f32[8,8,8,128]{3,2,1,0:T(8,128)S(1)}, u32[]{:S(2)}, u32[]{:S(2)}) collective-permute-start(f32[8,8,8,128]{3,2,1,0:T(8,128)S(1)} %all_to_all.5.dense_ref), channel_id=1, source_target_pairs={{0,8},{8,0},{16,24},{24,16},{1,9},{9,1},{17,25},{25,17},{2,10},{10... | collective-permute-start | bytes 786440 | tf_op jit(solution)/shard_map/ppermute | solution.py:32
  25.4 4.6 %collective-permute-start.5 = (f32[2,64,128]{2,1,0:T(8,128)S(1)}, f32[2,64,128]{2,1,0:T(8,128)S(1)}, u32[]{:S(2)}, u32[]{:S(2)}) collective-permute-start(f32[2,64,128]{2,1,0:T(8,128)S(1)} %get-tuple-element.13), channel_id=1, source_target_pairs={{0,1},{1,0},{2,3},{3,2},{4,5},{5,4},{6,7},{7,6},{8,9},{9,8},{10,11... | collective-permute-start | bytes 196616 | tf_op jit(solution)/shard_map/ppermute | solution.py:32
  27.4 5.6 %collective-permute-start.4 = (f32[2,64,128]{2,1,0:T(8,128)S(1)}, f32[2,64,128]{2,1,0:T(8,128)S(1)}, u32[]{:S(2)}, u32[]{:S(2)}) collective-permute-start(f32[2,64,128]{2,1,0:T(8,128)S(1)} %rest_stress.4), channel_id=1, source_target_pairs={{0,1},{1,0},{2,3},{3,2},{4,5},{5,4},{6,7},{7,6},{8,9},{9,8},{10,11... | collective-permute-start | bytes 196616 | tf_op jit(solution)/shard_map/ppermute | solution.py:32
  28.1 6.5 %copy-start.1 = (f32[128]{0:T(128)S(1)}, f32[128]{0:T(128)}, u32[]{:S(2)}) copy-start(f32[128]{0:T(128)} %param.11) | copy-start | bytes 1540
  28.1 6.5 %copy-start.2 = (f32[128]{0:T(128)S(1)}, f32[128]{0:T(128)}, u32[]{:S(2)}) copy-start(f32[128]{0:T(128)} %param.12) | copy-start | bytes 1540
  28.1 6.5 %copy-start.3 = (f32[128]{0:T(128)S(1)}, f32[128]{0:T(128)}, u32[]{:S(2)}) copy-start(f32[128]{0:T(128)} %param.13) | copy-start | bytes 1540
  30.0 6.1 %collective-permute-start.6 = (f32[64,128]{1,0:T(8,128)S(1)}, f32[64,128]{1,0:T(8,128)S(1)}, u32[]{:S(2)}, u32[]{:S(2)}) collective-permute-start(f32[64,128]{1,0:T(8,128)S(1)} %get-tuple-element.16), channel_id=1, source_target_pairs={{0,6},{1,7},{2,4},{3,5},{4,2},{5,3},{6,0},{7,1},{8,14},{9,15},{10,... | collective-permute-start | bytes 98312 | tf_op jit(solution)/shard_map/ppermute | solution.py:32
  31.2 5.4 %collective-permute-start.7 = (f32[64,128]{1,0:T(8,128)S(1)}, f32[64,128]{1,0:T(8,128)S(1)}, u32[]{:S(2)}, u32[]{:S(2)}) collective-permute-start(f32[64,128]{1,0:T(8,128)S(1)} %get-tuple-element.17), channel_id=1, source_target_pairs={{0,4},{1,5},{2,6},{3,7},{4,0},{5,1},{6,2},{7,3},{8,12},{9,13},{10,... | collective-permute-start | bytes 98312 | tf_op jit(solution)/shard_map/ppermute | solution.py:32
  33.0 4.0 %collective-permute-start.8 = (f32[64,128]{1,0:T(8,128)S(1)}, f32[64,128]{1,0:T(8,128)S(1)}, u32[]{:S(2)}, u32[]{:S(2)}) collective-permute-start(f32[64,128]{1,0:T(8,128)S(1)} %slice_bitcast_fusion), channel_id=1, source_target_pairs={{0,2},{1,3},{2,0},{3,1},{4,6},{5,7},{6,4},{7,5},{8,10},{9,11},{10,... | collective-permute-start | bytes 98312 | tf_op jit(solution)/shard_map/ppermute | solution.py:32

commit v19 on v17

--- a/solution.py
+++ b/solution.py
@@ -131,11 +131,6 @@
         out_ref[j] = stress(k, 0, own_ref, kernel_ref) + stress(k, 1, other_ref, kernel_ref)
 
 
-def halving_order(width):
-    bits = width.bit_length() - 1
-    return [int(f"{k:0{bits}b}"[::-1], 2) for k in range(width)]
-
-
 def per_device(kernel, slip_delta, block_list, live_count, direct_effect, load_rate, time_before):
     width = lax.axis_size("cols")
     height = lax.axis_size("rows")
@@ -144,11 +139,9 @@
     receivers, sources = kernel.shape
     blocks_here = sources // BLOCK
 
-    order = halving_order(width)
     share = receivers // width
-    quarter = width // 4
-    near_keep, far_keep = order[0 : 2 * quarter : 2], order[1 : 2 * quarter : 2]
-    near_send, far_send = order[2 * quarter :: 2], order[2 * quarter + 1 :: 2]
+    far_send, far_keep = [list(range(width // 2 + odd, width, 2)) for odd in (1, 0)]
+    near_keep, near_send = [0, 1], list(range(2, width // 2))
     in_hbm = functools.partial(pltpu.with_memory_space_constraint, memory_space=pltpu.HBM)
     kernel = kernel.reshape(width, share, sources)
     packed = pl.pallas_call(
@@ -187,28 +180,34 @@
             out_specs=jax.tree.map(lambda _: VMEM_SPEC, outs),
             compiler_params=params(8),
             cost_estimate=pl.CostEstimate(
-                flops=6 * quarter * share * sources * events,
-                bytes_accessed=4 * quarter * share * sources,
+                flops=3 * receivers * sources * events // 2,
+                bytes_accessed=receivers * sources,
                 transcendentals=0,
             ),
             name=body.__name__.removesuffix("_body") + "_stress",
         )(*args)
 
     slips = bf16(2 * events, blocks_half * BLOCK)
-    sums = f32(quarter, events, share)
+
+    def sums(targets):
+        return f32(len(targets), events, share)
+
     came = send_xor(mine, "rows", 1)
-    own, far_own, near_own = call(own_body, (far_send, near_send), [slips, sums, sums], mine, kernel)
-    other, far_sent = call(other_body, far_send, [slips, sums], came, kernel, far_own)
+    own, far_own, near_own = call(
+        own_body, (far_send, near_send), [slips, sums(far_send), sums(near_send)], mine, kernel
+    )
+    other, far_sent = call(other_body, far_send, [slips, sums(far_send)], came, kernel, far_own)
+    near_sent = call(rest_body, near_send, sums(near_send), other, kernel, near_own)
 
     def later(targets):
-        return call(both_body, targets, sums, own, other, kernel)
+        return call(both_body, targets, sums(targets), own, other, kernel)
 
     far_came = send_xor(far_sent, "cols", 1)
-    near_came = send_xor(call(rest_body, near_send, sums, other, kernel, near_own), "cols", 1)
+    near_came = [send_xor(near_sent[j : j + 2], "cols", near_send[j]) for j in range(0, len(near_send), 2)]
     far = later(far_keep) + far_came
-    near = later(near_keep) + near_came
+    near = sum(near_came, later(near_keep))
     parts = [send_xor(far[j], "cols", k) for j, k in reversed(list(enumerate(far_keep)))]
-    parts += [send_xor(near[j], "cols", k) for j, k in enumerate(near_keep) if k]
+    parts.append(send_xor(near[1], "cols", 1))
     stress_change = sum(parts, near[0])
     scale = direct_effect[None, :]
     growth = jnp.expm1(load_rate * time_before / direct_effect)[None, :]

time: 37.4 us -> 37.2 us (level)
  starting transfers between devices: 9.9 us -> 8.45 us
  waiting for transfers between devices: 6.63 us -> 7.86 us
    ppermute x9, starting transfers between devices: 9.9 us -> 8.45 us  [send_xor(): lax.ppermute(block, axis, [(r, r ^ k) for r in range(lax.axis_size(axis))])]
    ppermute x9, waiting for transfers between devices: 6.63 us -> 7.86 us  [send_xor(): lax.ppermute(block, axis, [(r, r ^ k) for r in range(lax.axis_size(axis))])]
  transfers between devices with their start and end apart: 9 -> 9, of which waited for: 6 -> 7; matrix products, arithmetic and copies ran while one was open for 0% -> 0% of each run, Pallas kernels for 8% -> 8%
where the time goes in v19:
time: 37.2 us; the launch traced here: 37 us
  blocking collectives  14.5 us (39%)
  starting transfers between devices  8.45 us (23%)
  waiting for transfers between devices  7.86 us (21%)
  Pallas kernels  4.68 us (13%)
  between operations  0.73 us (2%)
  other arithmetic  0.69 us (2%)
    all_to_all x1, blocking collectives, per_device(): mine = lax.all_to_all(dense, 'cols', 0, 0, tiled=True)  14.5 us
    ppermute x9, starting transfers between devices, send_xor(): lax.ppermute(block, axis, [(r, r ^ k) for r in range(lax.axis_size(axis))])  8.45 us
    ppermute x9, waiting for transfers between devices, send_xor(): lax.ppermute(block, axis, [(r, r ^ k) for r in range(lax.axis_size(axis))])  7.86 us
    pallas_call x5, Pallas kernels, call(): pl.pallas_call(functools.partial(body, targets), out_shape=outs, in_specs...  3.46 us
    pallas_call x1, Pallas kernels, per_device(): pl.pallas_call(pack_body, out_shape=f32(events_here + 1, SUB, BLOCK), in_...  0.96 us
  transfers between devices with their start and end apart: 9, of which 7 were waited for; matrix products, arithmetic and copies ran while one was open for 0% of the time, Pallas kernels for 8%

profile of v19, /device:TPU:0, one launch (start us, length us, event | category | flops | bytes accessed | tf_op | source)
XLA Modules:
  0.0 37.0 jit_solution(14093452459224105476)
XLA Ops:
  0.6 0.0 copy-start
  0.6 1.0 %pack.1.refs_0_ = f32[9,8,128]{2,1,0:T(8,128)S(1)} custom-call(f32[8,8,128]{2,1,0:T(8,128)} %slip_hbm.1, s32[8,8]{1,0:T(8,128)} %list_hbm.1, s32[8]{0:T(128)} %count_hbm.1), custom_call_target="tpu_custom_call" | custom-call | tf_op jit(solution)/shard_map/pack/pallas_call | solution.py:147
  1.6 3.0 %collective-permute-start = (f32[9,8,128]{2,1,0:T(8,128)S(1)}, f32[9,8,128]{2,1,0:T(8,128)S(1)}, u32[]{:S(2)}, u32[]{:S(2)}) collective-permute-start(f32[9,8,128]{2,1,0:T(8,128)S(1)} %pack.1.refs_0_), channel_id=1, source_target_pairs={{0,16},{8,24},{16,0},{24,8},{1,17},{9,25},{17,1},{25,9},{2,18},{10... | collective-permute-start | bytes 110600 | tf_op jit(solution)/shard_map/ppermute | solution.py:32
  4.6 0.0 collective-permute-start.1
  4.6 0.2 collective-permute-start.2
  4.8 1.7 %collective-permute-done.refs_1_ = f32[9,8,128]{2,1,0:T(8,128)S(1)} collective-permute-done((f32[9,8,128]{2,1,0:T(8,128)S(1)}, f32[9,8,128]{2,1,0:T(8,128)S(1)}, u32[]{:S(2)}, u32[]{:S(2)}) %collective-permute-start) | collective-permute-done | bytes 36896 | tf_op jit(solution)/shard_map/ppermute | solution.py:32
  6.6 1.6 %collective-permute-done.1.refs_2_ = f32[9,8,128]{2,1,0:T(8,128)S(1)} collective-permute-done((f32[9,8,128]{2,1,0:T(8,128)S(1)}, f32[9,8,128]{2,1,0:T(8,128)S(1)}, u32[]{:S(2)}, u32[]{:S(2)}) %collective-permute-start.1) | collective-permute-done | bytes 36896 | tf_op jit(solution)/shard_map/ppermute | solution.py:32
  8.2 0.0 collective-permute-done.2.refs_3_
  8.2 0.3 densify.1
  8.4 14.5 %all_to_all.5.dense_ref = f32[8,8,8,128]{3,2,1,0:T(8,128)S(1)} all-to-all(f32[8,8,8,128]{3,2,1,0:T(8,128)S(1)} %densify.1), channel_id=1, replica_groups=mesh['rows'=4,'cols'=8] {'cols'}, dimensions={0} | all-to-all | bytes 524288 | tf_op jit(solution)/shard_map/all_to_all | solution.py:173
  23.0 0.0 collective-permute-start.3
  23.0 0.0 copy-done
  23.0 0.8 %own_stress.1 = (bf16[128,1024]{1,0:T(8,128)(2,1)S(1)}, f32[2,64,128]{2,1,0:T(8,128)S(1)}, f32[2,64,128]{2,1,0:T(8,128)S(1)}) custom-call(f32[8,8,8,128]{3,2,1,0:T(8,128)S(1)} %all_to_all.5.dense_ref, f32[8,128,2048]{2,1,0:T(8,128)S(1)} %bitcast.20), custom_call_target="tpu_custom_call" | custom-call | flops 201326592 | bytes 2097152 | tf_op jit(solution)/shard_map/own_stress/pallas_call | solution.py:176
  23.8 0.7 %collective-permute-done.3.dense_ref = f32[8,8,8,128]{3,2,1,0:T(8,128)S(1)} collective-permute-done((f32[8,8,8,128]{3,2,1,0:T(8,128)S(1)}, f32[8,8,8,128]{3,2,1,0:T(8,128)S(1)}, u32[]{:S(2)}, u32[]{:S(2)}) %collective-permute-start.3) | collective-permute-done | bytes 262176 | tf_op jit(solution)/shard_map/ppermute | solution.py:32
  24.5 0.5 %other_stress.1 = (bf16[128,1024]{1,0:T(8,128)(2,1)S(1)}, f32[2,64,128]{2,1,0:T(8,128)S(1)}) custom-call(f32[8,8,8,128]{3,2,1,0:T(8,128)S(1)} %collective-permute-done.3.dense_ref, f32[8,128,2048]{2,1,0:T(8,128)S(1)} %bitcast.21, f32[2,64,128]{2,1,0:T(8,128)S(1)} %get-tuple-element.8.sum_ref), custom_call_target="tpu_custom_call" | custom-call | flops 201326592 | bytes 2097152 | tf_op jit(solution)/shard_map/other_stress/pallas_call | solution.py:176
  25.0 1.5 %collective-permute-start.5 = (f32[2,64,128]{2,1,0:T(8,128)S(1)}, f32[2,64,128]{2,1,0:T(8,128)S(1)}, u32[]{:S(2)}, u32[]{:S(2)}) collective-permute-start(f32[2,64,128]{2,1,0:T(8,128)S(1)} %get-tuple-element.11), channel_id=1, source_target_pairs={{0,1},{1,0},{2,3},{3,2},{4,5},{5,4},{6,7},{7,6},{8,9},{9,8},{10,11... | collective-permute-start | bytes 196616 | tf_op jit(solution)/shard_map/ppermute | solution.py:32
  26.5 0.5 %rest_stress.1 = f32[2,64,128]{2,1,0:T(8,128)S(1)} custom-call(bf16[128,1024]{1,0:T(8,128)(2,1)S(1)} %get-tuple-element.9.other_ref.slip_ref, f32[8,128,2048]{2,1,0:T(8,128)S(1)} %bitcast.22, f32[2,64,128]{2,1,0:T(8,128)S(1)} %get-tuple-element.10.sum_ref), custom_call_target="tpu_custom_call" | custom-call | flops 201326592 | bytes 2097152 | tf_op jit(solution)/shard_map/rest_stress/pallas_call | solution.py:176
  27.0 0.1 collective-permute-start.4
  27.1 0.0 copy-start.1
  27.1 0.0 copy-start.2
  27.1 0.0 copy-start.3
  27.1 0.8 %both_stress.3 = f32[2,64,128]{2,1,0:T(8,128)S(1)} custom-call(bf16[128,1024]{1,0:T(8,128)(2,1)S(1)} %get-tuple-element.7.own_ref, bf16[128,1024]{1,0:T(8,128)(2,1)S(1)} %get-tuple-element.9.other_ref.slip_ref, f32[8,128,2048]{2,1,0:T(8,128)S(1)} %bitcast.23), custom_call_target="tpu_custom_call" | custom-call | flops 201326592 | bytes 2097152 | tf_op jit(solution)/shard_map/both_stress/pallas_call | solution.py:176
  27.9 0.8 %both_stress.2 = f32[2,64,128]{2,1,0:T(8,128)S(1)} custom-call(bf16[128,1024]{1,0:T(8,128)(2,1)S(1)} %get-tuple-element.7.own_ref, bf16[128,1024]{1,0:T(8,128)(2,1)S(1)} %get-tuple-element.9.other_ref.slip_ref, f32[8,128,2048]{2,1,0:T(8,128)S(1)} %bitcast.24), custom_call_target="tpu_custom_call" | custom-call | flops 201326592 | bytes 2097152 | tf_op jit(solution)/shard_map/both_stress/pallas_call | solution.py:176
  28.8 0.6 %collective-permute-done.5 = f32[2,64,128]{2,1,0:T(8,128)S(1)} collective-permute-done((f32[2,64,128]{2,1,0:T(8,128)S(1)}, f32[2,64,128]{2,1,0:T(8,128)S(1)}, u32[]{:S(2)}, u32[]{:S(2)}) %collective-permute-start.5) | collective-permute-done | bytes 65568 | tf_op jit(solution)/shard_map/ppermute | solution.py:32
  29.4 1.2 %collective-permute-start.6 = (f32[64,128]{1,0:T(8,128)S(1)}, f32[64,128]{1,0:T(8,128)S(1)}, u32[]{:S(2)}, u32[]{:S(2)}) collective-permute-start(f32[64,128]{1,0:T(8,128)S(1)} %get-tuple-element.14), channel_id=1, source_target_pairs={{0,6},{1,7},{2,4},{3,5},{4,2},{5,3},{6,0},{7,1},{8,14},{9,15},{10,... | collective-permute-start | bytes 98312 | tf_op jit(solution)/shard_map/ppermute | solution.py:32
  30.6 1.7 %collective-permute-start.7 = (f32[64,128]{1,0:T(8,128)S(1)}, f32[64,128]{1,0:T(8,128)S(1)}, u32[]{:S(2)}, u32[]{:S(2)}) collective-permute-start(f32[64,128]{1,0:T(8,128)S(1)} %get-tuple-element.15), channel_id=1, source_target_pairs={{0,4},{1,5},{2,6},{3,7},{4,0},{5,1},{6,2},{7,3},{8,12},{9,13},{10,... | collective-permute-start | bytes 98312 | tf_op jit(solution)/shard_map/ppermute | solution.py:32
  32.3 0.0 collective-permute-done.4
  32.3 0.7 %collective-permute-start.8 = (f32[64,128]{1,0:T(8,128)S(1)}, f32[64,128]{1,0:T(8,128)S(1)}, u32[]{:S(2)}, u32[]{:S(2)}) collective-permute-start(f32[64,128]{1,0:T(8,128)S(1)} %slice_bitcast_fusion), channel_id=1, source_target_pairs={{0,1},{1,0},{2,3},{3,2},{4,5},{5,4},{6,7},{7,6},{8,9},{9,8},{10,11... | collective-permute-start | bytes 98312 | tf_op jit(solution)/shard_map/ppermute | solution.py:32
  33.0 0.0 copy-done.1
  33.0 0.0 copy-done.2
  33.0 0.0 copy-done.3
  33.0 2.1 %collective-permute-done.6 = f32[64,128]{1,0:T(8,128)S(1)} collective-permute-done((f32[64,128]{1,0:T(8,128)S(1)}, f32[64,128]{1,0:T(8,128)S(1)}, u32[]{:S(2)}, u32[]{:S(2)}) %collective-permute-start.6) | collective-permute-done | bytes 32800 | tf_op jit(solution)/shard_map/ppermute | solution.py:32
  35.2 0.7 %collective-permute-done.7 = f32[64,128]{1,0:T(8,128)S(1)} collective-permute-done((f32[64,128]{1,0:T(8,128)S(1)}, f32[64,128]{1,0:T(8,128)S(1)}, u32[]{:S(2)}, u32[]{:S(2)}) %collective-permute-start.7) | collective-permute-done | bytes 32800 | tf_op jit(solution)/shard_map/ppermute | solution.py:32
  35.8 0.5 %collective-permute-done.8 = f32[64,128]{1,0:T(8,128)S(1)} collective-permute-done((f32[64,128]{1,0:T(8,128)S(1)}, f32[64,128]{1,0:T(8,128)S(1)}, u32[]{:S(2)}, u32[]{:S(2)}) %collective-permute-start.8) | collective-permute-done | bytes 32800 | tf_op jit(solution)/shard_map/ppermute | solution.py:32
  36.3 0.7 %add_bitcast_fusion = (f32[128,64]{0,1:T(8,128)}, f32[64,128]{1,0:T(8,128)}) fusion(f32[128]{0:T(128)S(1)} %get-tuple-element.17, f32[128]{0:T(128)S(1)} %copy-done.1, f32[128]{0:T(128)S(1)} %get-tuple-element.16, f32[64,128]{1,0:T(8,128)S(1)} %collective-permute-done.8, f32[64,128]{1,0:T(8,128)S(1)} %collective-permute-done.7, ...), kind=kLoop, calls=%fused_computation.7 | loop fusion | flops 57344 | bytes 198144 | tf_op jit(solution)/shard_map/transpose | solution.py:217
  (5 shorter events, 0.0 us)
Async XLA Ops:
  0.6 22.3 %copy-start = (f32[1024,2048]{1,0:T(8,128)S(1)}, f32[1024,2048]{1,0:T(8,128)}, u32[]{:S(2)}) copy-start(f32[1024,2048]{1,0:T(8,128)} %param.7) | copy-start | bytes 25165828
  1.6 5.0 %collective-permute-start = (f32[9,8,128]{2,1,0:T(8,128)S(1)}, f32[9,8,128]{2,1,0:T(8,128)S(1)}, u32[]{:S(2)}, u32[]{:S(2)}) collective-permute-start(f32[9,8,128]{2,1,0:T(8,128)S(1)} %pack.1.refs_0_), channel_id=1, source_target_pairs={{0,16},{8,24},{16,0},{24,8},{1,17},{9,25},{17,1},{25,9},{2,18},{10... | collective-permute-start | bytes 110600 | tf_op jit(solution)/shard_map/ppermute | solution.py:32
  4.6 3.5 %collective-permute-start.1 = (f32[9,8,128]{2,1,0:T(8,128)S(1)}, f32[9,8,128]{2,1,0:T(8,128)S(1)}, u32[]{:S(2)}, u32[]{:S(2)}) collective-permute-start(f32[9,8,128]{2,1,0:T(8,128)S(1)} %pack.1.refs_0_), channel_id=1, source_target_pairs={{0,24},{8,16},{16,8},{24,0},{1,25},{9,17},{17,9},{25,1},{2,26},{10... | collective-permute-start | bytes 110600 | tf_op jit(solution)/shard_map/ppermute | solution.py:32
  4.6 3.5 %collective-permute-start.2 = (f32[9,8,128]{2,1,0:T(8,128)S(1)}, f32[9,8,128]{2,1,0:T(8,128)S(1)}, u32[]{:S(2)}, u32[]{:S(2)}) collective-permute-start(f32[9,8,128]{2,1,0:T(8,128)S(1)} %pack.1.refs_0_), channel_id=1, source_target_pairs={{0,8},{8,0},{16,24},{24,16},{1,9},{9,1},{17,25},{25,17},{2,10},{10... | collective-permute-start | bytes 110600 | tf_op jit(solution)/shard_map/ppermute | solution.py:32
  23.0 1.5 %collective-permute-start.3 = (f32[8,8,8,128]{3,2,1,0:T(8,128)S(1)}, f32[8,8,8,128]{3,2,1,0:T(8,128)S(1)}, u32[]{:S(2)}, u32[]{:S(2)}) collective-permute-start(f32[8,8,8,128]{3,2,1,0:T(8,128)S(1)} %all_to_all.5.dense_ref), channel_id=1, source_target_pairs={{0,8},{8,0},{16,24},{24,16},{1,9},{9,1},{17,25},{25,17},{2,10},{10... | collective-permute-start | bytes 786440 | tf_op jit(solution)/shard_map/ppermute | solution.py:32
  25.0 4.3 %collective-permute-start.5 = (f32[2,64,128]{2,1,0:T(8,128)S(1)}, f32[2,64,128]{2,1,0:T(8,128)S(1)}, u32[]{:S(2)}, u32[]{:S(2)}) collective-permute-start(f32[2,64,128]{2,1,0:T(8,128)S(1)} %get-tuple-element.11), channel_id=1, source_target_pairs={{0,1},{1,0},{2,3},{3,2},{4,5},{5,4},{6,7},{7,6},{8,9},{9,8},{10,11... | collective-permute-start | bytes 196616 | tf_op jit(solution)/shard_map/ppermute | solution.py:32
  27.0 5.3 %collective-permute-start.4 = (f32[2,64,128]{2,1,0:T(8,128)S(1)}, f32[2,64,128]{2,1,0:T(8,128)S(1)}, u32[]{:S(2)}, u32[]{:S(2)}) collective-permute-start(f32[2,64,128]{2,1,0:T(8,128)S(1)} %rest_stress.1), channel_id=1, source_target_pairs={{0,2},{1,3},{2,0},{3,1},{4,6},{5,7},{6,4},{7,5},{8,10},{9,11},{10,... | collective-permute-start | bytes 196616 | tf_op jit(solution)/shard_map/ppermute | solution.py:32
  27.1 5.9 %copy-start.1 = (f32[128]{0:T(128)S(1)}, f32[128]{0:T(128)}, u32[]{:S(2)}) copy-start(f32[128]{0:T(128)} %param.11) | copy-start | bytes 1540
  27.1 5.9 %copy-start.2 = (f32[128]{0:T(128)S(1)}, f32[128]{0:T(128)}, u32[]{:S(2)}) copy-start(f32[128]{0:T(128)} %param.12) | copy-start | bytes 1540
  27.1 5.9 %copy-start.3 = (f32[128]{0:T(128)S(1)}, f32[128]{0:T(128)}, u32[]{:S(2)}) copy-start(f32[128]{0:T(128)} %param.13) | copy-start | bytes 1540
  29.4 5.8 %collective-permute-start.6 = (f32[64,128]{1,0:T(8,128)S(1)}, f32[64,128]{1,0:T(8,128)S(1)}, u32[]{:S(2)}, u32[]{:S(2)}) collective-permute-start(f32[64,128]{1,0:T(8,128)S(1)} %get-tuple-element.14), channel_id=1, source_target_pairs={{0,6},{1,7},{2,4},{3,5},{4,2},{5,3},{6,0},{7,1},{8,14},{9,15},{10,... | collective-permute-start | bytes 98312 | tf_op jit(solution)/shard_map/ppermute | solution.py:32
  30.6 5.3 %collective-permute-start.7 = (f32[64,128]{1,0:T(8,128)S(1)}, f32[64,128]{1,0:T(8,128)S(1)}, u32[]{:S(2)}, u32[]{:S(2)}) collective-permute-start(f32[64,128]{1,0:T(8,128)S(1)} %get-tuple-element.15), channel_id=1, source_target_pairs={{0,4},{1,5},{2,6},{3,7},{4,0},{5,1},{6,2},{7,3},{8,12},{9,13},{10,... | collective-permute-start | bytes 98312 | tf_op jit(solution)/shard_map/ppermute | solution.py:32
  32.3 4.0 %collective-permute-start.8 = (f32[64,128]{1,0:T(8,128)S(1)}, f32[64,128]{1,0:T(8,128)S(1)}, u32[]{:S(2)}, u32[]{:S(2)}) collective-permute-start(f32[64,128]{1,0:T(8,128)S(1)} %slice_bitcast_fusion), channel_id=1, source_target_pairs={{0,1},{1,0},{2,3},{3,2},{4,5},{5,4},{6,7},{7,6},{8,9},{9,8},{10,11... | collective-permute-start | bytes 98312 | tf_op jit(solution)/shard_map/ppermute | solution.py:32

commit v20 on v19

--- a/solution.py
+++ b/solution.py
@@ -43,13 +43,12 @@
         copy.start()
     row = lax.axis_index("rows")
     entry = lax.broadcasted_iota(jnp.int32, (events, entries), 1) + row * entries
-    event = lax.broadcasted_iota(jnp.int32, (events, entries), 0)
     ids[...] = jnp.full(ids.shape, -1.0, jnp.float32)
     for copy in copies[:2]:
         copy.wait()
-    count = jnp.zeros((events, entries), jnp.int32)
-    for e in range(events):
-        count = jnp.where(event == e, count_ref[e], count)
+    counts = jnp.broadcast_to(count_ref[...].reshape(1, events), (events, events))
+    diagonal = lax.broadcasted_iota(jnp.int32, counts.shape, 0) == lax.broadcasted_iota(jnp.int32, counts.shape, 1)
+    count = jnp.sum(jnp.where(diagonal, counts, 0), axis=1, keepdims=True)
     ids[0:events, 0:entries] = jnp.where(entry < count, list_ref[...], -1).astype(jnp.float32)
     out_ref[events] = pltpu.roll(ids[...], row * entries, 1)
     copies[2].wait()
@@ -74,7 +73,7 @@
             slips[e, where, :] = ref[e, 0:entries, :]
         slip = slips[e]
         total = jnp.zeros((width * blocks, BLOCK), jnp.float32)
-        for _ in range(3):
+        for _ in range(2):
             piece = slip.astype(jnp.bfloat16)
             slip = slip - piece.astype(jnp.float32)
             total = total + jnp.dot(onehot, piece, preferred_element_type=jnp.float32)
@@ -151,7 +150,7 @@
         out_specs=VMEM_SPEC,
         scratch_shapes=[
             pltpu.VMEM(block_list.shape, jnp.int32),
-            pltpu.SMEM(live_count.shape, jnp.int32),
+            pltpu.VMEM(live_count.shape, jnp.int32),
             pltpu.VMEM((SUB, BLOCK), jnp.float32),
             pltpu.SemaphoreType.DMA((3,)),
         ],

time: 37.2 us -> 37.2 us (level)
  no operation moved by 1% of the time
where the time goes in v20:
time: 37.2 us; the launch traced here: 37 us
  blocking collectives  14.5 us (39%)
  starting transfers between devices  8.45 us (23%)
  waiting for transfers between devices  7.86 us (21%)
  Pallas kernels  4.73 us (13%)
  between operations  0.73 us (2%)
  other arithmetic  0.69 us (2%)
    all_to_all x1, blocking collectives, per_device(): mine = lax.all_to_all(dense, 'cols', 0, 0, tiled=True)  14.5 us
    ppermute x9, starting transfers between devices, send_xor(): lax.ppermute(block, axis, [(r, r ^ k) for r in range(lax.axis_size(axis))])  8.45 us
    ppermute x9, waiting for transfers between devices, send_xor(): lax.ppermute(block, axis, [(r, r ^ k) for r in range(lax.axis_size(axis))])  7.86 us
    pallas_call x5, Pallas kernels, call(): pl.pallas_call(functools.partial(body, targets), out_shape=outs, in_specs...  3.47 us
    pallas_call x1, Pallas kernels, per_device(): pl.pallas_call(pack_body, out_shape=f32(events_here + 1, SUB, BLOCK), in_...  1.03 us
  transfers between devices with their start and end apart: 9, of which 7 were waited for; matrix products, arithmetic and copies ran while one was open for 0% of the time, Pallas kernels for 8%

profile of v20, /device:TPU:0, one launch (start us, length us, event | category | flops | bytes accessed | tf_op | source)
XLA Modules:
  0.0 37.0 jit_solution(8458241892892282210)
XLA Ops:
  0.6 0.0 copy-start
  0.6 1.0 %pack.1.refs_0_ = f32[9,8,128]{2,1,0:T(8,128)S(1)} custom-call(f32[8,8,128]{2,1,0:T(8,128)} %slip_hbm.1, s32[8,8]{1,0:T(8,128)} %list_hbm.1, s32[8]{0:T(128)} %count_hbm.1), custom_call_target="tpu_custom_call" | custom-call | tf_op jit(solution)/shard_map/pack/pallas_call | solution.py:146
  1.7 3.0 %collective-permute-start = (f32[9,8,128]{2,1,0:T(8,128)S(1)}, f32[9,8,128]{2,1,0:T(8,128)S(1)}, u32[]{:S(2)}, u32[]{:S(2)}) collective-permute-start(f32[9,8,128]{2,1,0:T(8,128)S(1)} %pack.1.refs_0_), channel_id=1, source_target_pairs={{0,16},{8,24},{16,0},{24,8},{1,17},{9,25},{17,1},{25,9},{2,18},{10... | collective-permute-start | bytes 110600 | tf_op jit(solution)/shard_map/ppermute | solution.py:32
  4.7 0.0 collective-permute-start.1
  4.7 0.2 collective-permute-start.2
  4.9 1.7 %collective-permute-done.refs_1_ = f32[9,8,128]{2,1,0:T(8,128)S(1)} collective-permute-done((f32[9,8,128]{2,1,0:T(8,128)S(1)}, f32[9,8,128]{2,1,0:T(8,128)S(1)}, u32[]{:S(2)}, u32[]{:S(2)}) %collective-permute-start) | collective-permute-done | bytes 36896 | tf_op jit(solution)/shard_map/ppermute | solution.py:32
  6.6 1.6 %collective-permute-done.1.refs_2_ = f32[9,8,128]{2,1,0:T(8,128)S(1)} collective-permute-done((f32[9,8,128]{2,1,0:T(8,128)S(1)}, f32[9,8,128]{2,1,0:T(8,128)S(1)}, u32[]{:S(2)}, u32[]{:S(2)}) %collective-permute-start.1) | collective-permute-done | bytes 36896 | tf_op jit(solution)/shard_map/ppermute | solution.py:32
  8.2 0.0 collective-permute-done.2.refs_3_
  8.2 0.2 densify.1
  8.5 14.5 %all_to_all.5.dense_ref = f32[8,8,8,128]{3,2,1,0:T(8,128)S(1)} all-to-all(f32[8,8,8,128]{3,2,1,0:T(8,128)S(1)} %densify.1), channel_id=1, replica_groups=mesh['rows'=4,'cols'=8] {'cols'}, dimensions={0} | all-to-all | bytes 524288 | tf_op jit(solution)/shard_map/all_to_all | solution.py:172
  23.0 0.0 collective-permute-start.3
  23.0 0.0 copy-done
  23.0 0.8 %own_stress.1 = (bf16[128,1024]{1,0:T(8,128)(2,1)S(1)}, f32[2,64,128]{2,1,0:T(8,128)S(1)}, f32[2,64,128]{2,1,0:T(8,128)S(1)}) custom-call(f32[8,8,8,128]{3,2,1,0:T(8,128)S(1)} %all_to_all.5.dense_ref, f32[8,128,2048]{2,1,0:T(8,128)S(1)} %bitcast.20), custom_call_target="tpu_custom_call" | custom-call | flops 201326592 | bytes 2097152 | tf_op jit(solution)/shard_map/own_stress/pallas_call | solution.py:175
  23.9 0.7 %collective-permute-done.3.dense_ref = f32[8,8,8,128]{3,2,1,0:T(8,128)S(1)} collective-permute-done((f32[8,8,8,128]{3,2,1,0:T(8,128)S(1)}, f32[8,8,8,128]{3,2,1,0:T(8,128)S(1)}, u32[]{:S(2)}, u32[]{:S(2)}) %collective-permute-start.3) | collective-permute-done | bytes 262176 | tf_op jit(solution)/shard_map/ppermute | solution.py:32
  24.5 0.5 %other_stress.1 = (bf16[128,1024]{1,0:T(8,128)(2,1)S(1)}, f32[2,64,128]{2,1,0:T(8,128)S(1)}) custom-call(f32[8,8,8,128]{3,2,1,0:T(8,128)S(1)} %collective-permute-done.3.dense_ref, f32[8,128,2048]{2,1,0:T(8,128)S(1)} %bitcast.21, f32[2,64,128]{2,1,0:T(8,128)S(1)} %get-tuple-element.8.sum_ref), custom_call_target="tpu_custom_call" | custom-call | flops 201326592 | bytes 2097152 | tf_op jit(solution)/shard_map/other_stress/pallas_call | solution.py:175
  25.0 1.5 %collective-permute-start.5 = (f32[2,64,128]{2,1,0:T(8,128)S(1)}, f32[2,64,128]{2,1,0:T(8,128)S(1)}, u32[]{:S(2)}, u32[]{:S(2)}) collective-permute-start(f32[2,64,128]{2,1,0:T(8,128)S(1)} %get-tuple-element.11), channel_id=1, source_target_pairs={{0,1},{1,0},{2,3},{3,2},{4,5},{5,4},{6,7},{7,6},{8,9},{9,8},{10,11... | collective-permute-start | bytes 196616 | tf_op jit(solution)/shard_map/ppermute | solution.py:32
  26.5 0.5 %rest_stress.1 = f32[2,64,128]{2,1,0:T(8,128)S(1)} custom-call(bf16[128,1024]{1,0:T(8,128)(2,1)S(1)} %get-tuple-element.9.other_ref.slip_ref, f32[8,128,2048]{2,1,0:T(8,128)S(1)} %bitcast.22, f32[2,64,128]{2,1,0:T(8,128)S(1)} %get-tuple-element.10.sum_ref), custom_call_target="tpu_custom_call" | custom-call | flops 201326592 | bytes 2097152 | tf_op jit(solution)/shard_map/rest_stress/pallas_call | solution.py:175
  27.0 0.1 collective-permute-start.4
  27.1 0.0 copy-start.1
  27.1 0.0 copy-start.2
  27.1 0.0 copy-start.3
  27.1 0.8 %both_stress.3 = f32[2,64,128]{2,1,0:T(8,128)S(1)} custom-call(bf16[128,1024]{1,0:T(8,128)(2,1)S(1)} %get-tuple-element.7.own_ref, bf16[128,1024]{1,0:T(8,128)(2,1)S(1)} %get-tuple-element.9.other_ref.slip_ref, f32[8,128,2048]{2,1,0:T(8,128)S(1)} %bitcast.23), custom_call_target="tpu_custom_call" | custom-call | flops 201326592 | bytes 2097152 | tf_op jit(solution)/shard_map/both_stress/pallas_call | solution.py:175
  28.0 0.8 %both_stress.2 = f32[2,64,128]{2,1,0:T(8,128)S(1)} custom-call(bf16[128,1024]{1,0:T(8,128)(2,1)S(1)} %get-tuple-element.7.own_ref, bf16[128,1024]{1,0:T(8,128)(2,1)S(1)} %get-tuple-element.9.other_ref.slip_ref, f32[8,128,2048]{2,1,0:T(8,128)S(1)} %bitcast.24), custom_call_target="tpu_custom_call" | custom-call | flops 201326592 | bytes 2097152 | tf_op jit(solution)/shard_map/both_stress/pallas_call | solution.py:175
  28.8 0.6 %collective-permute-done.5 = f32[2,64,128]{2,1,0:T(8,128)S(1)} collective-permute-done((f32[2,64,128]{2,1,0:T(8,128)S(1)}, f32[2,64,128]{2,1,0:T(8,128)S(1)}, u32[]{:S(2)}, u32[]{:S(2)}) %collective-permute-start.5) | collective-permute-done | bytes 65568 | tf_op jit(solution)/shard_map/ppermute | solution.py:32
  29.4 1.2 %collective-permute-start.6 = (f32[64,128]{1,0:T(8,128)S(1)}, f32[64,128]{1,0:T(8,128)S(1)}, u32[]{:S(2)}, u32[]{:S(2)}) collective-permute-start(f32[64,128]{1,0:T(8,128)S(1)} %get-tuple-element.14), channel_id=1, source_target_pairs={{0,6},{1,7},{2,4},{3,5},{4,2},{5,3},{6,0},{7,1},{8,14},{9,15},{10,... | collective-permute-start | bytes 98312 | tf_op jit(solution)/shard_map/ppermute | solution.py:32
  30.6 1.7 %collective-permute-start.7 = (f32[64,128]{1,0:T(8,128)S(1)}, f32[64,128]{1,0:T(8,128)S(1)}, u32[]{:S(2)}, u32[]{:S(2)}) collective-permute-start(f32[64,128]{1,0:T(8,128)S(1)} %get-tuple-element.15), channel_id=1, source_target_pairs={{0,4},{1,5},{2,6},{3,7},{4,0},{5,1},{6,2},{7,3},{8,12},{9,13},{10,... | collective-permute-start | bytes 98312 | tf_op jit(solution)/shard_map/ppermute | solution.py:32
  32.3 0.0 collective-permute-done.4
  32.4 0.7 %collective-permute-start.8 = (f32[64,128]{1,0:T(8,128)S(1)}, f32[64,128]{1,0:T(8,128)S(1)}, u32[]{:S(2)}, u32[]{:S(2)}) collective-permute-start(f32[64,128]{1,0:T(8,128)S(1)} %slice_bitcast_fusion), channel_id=1, source_target_pairs={{0,1},{1,0},{2,3},{3,2},{4,5},{5,4},{6,7},{7,6},{8,9},{9,8},{10,11... | collective-permute-start | bytes 98312 | tf_op jit(solution)/shard_map/ppermute | solution.py:32
  33.0 0.0 copy-done.1
  33.0 0.0 copy-done.2
  33.0 0.0 copy-done.3
  33.1 2.1 %collective-permute-done.6 = f32[64,128]{1,0:T(8,128)S(1)} collective-permute-done((f32[64,128]{1,0:T(8,128)S(1)}, f32[64,128]{1,0:T(8,128)S(1)}, u32[]{:S(2)}, u32[]{:S(2)}) %collective-permute-start.6) | collective-permute-done | bytes 32800 | tf_op jit(solution)/shard_map/ppermute | solution.py:32
  35.2 0.7 %collective-permute-done.7 = f32[64,128]{1,0:T(8,128)S(1)} collective-permute-done((f32[64,128]{1,0:T(8,128)S(1)}, f32[64,128]{1,0:T(8,128)S(1)}, u32[]{:S(2)}, u32[]{:S(2)}) %collective-permute-start.7) | collective-permute-done | bytes 32800 | tf_op jit(solution)/shard_map/ppermute | solution.py:32
  35.9 0.5 %collective-permute-done.8 = f32[64,128]{1,0:T(8,128)S(1)} collective-permute-done((f32[64,128]{1,0:T(8,128)S(1)}, f32[64,128]{1,0:T(8,128)S(1)}, u32[]{:S(2)}, u32[]{:S(2)}) %collective-permute-start.8) | collective-permute-done | bytes 32800 | tf_op jit(solution)/shard_map/ppermute | solution.py:32
  36.4 0.7 %add_bitcast_fusion = (f32[128,64]{0,1:T(8,128)}, f32[64,128]{1,0:T(8,128)}) fusion(f32[128]{0:T(128)S(1)} %get-tuple-element.17, f32[128]{0:T(128)S(1)} %copy-done.1, f32[128]{0:T(128)S(1)} %get-tuple-element.16, f32[64,128]{1,0:T(8,128)S(1)} %collective-permute-done.8, f32[64,128]{1,0:T(8,128)S(1)} %collective-permute-done.7, ...), kind=kLoop, calls=%fused_computation.7 | loop fusion | flops 57344 | bytes 198144 | tf_op jit(solution)/shard_map/transpose | solution.py:216
  (5 shorter events, 0.0 us)
Async XLA Ops:
  0.6 22.4 %copy-start = (f32[1024,2048]{1,0:T(8,128)S(1)}, f32[1024,2048]{1,0:T(8,128)}, u32[]{:S(2)}) copy-start(f32[1024,2048]{1,0:T(8,128)} %param.7) | copy-start | bytes 25165828
  1.7 5.0 %collective-permute-start = (f32[9,8,128]{2,1,0:T(8,128)S(1)}, f32[9,8,128]{2,1,0:T(8,128)S(1)}, u32[]{:S(2)}, u32[]{:S(2)}) collective-permute-start(f32[9,8,128]{2,1,0:T(8,128)S(1)} %pack.1.refs_0_), channel_id=1, source_target_pairs={{0,16},{8,24},{16,0},{24,8},{1,17},{9,25},{17,1},{25,9},{2,18},{10... | collective-permute-start | bytes 110600 | tf_op jit(solution)/shard_map/ppermute | solution.py:32
  4.7 3.5 %collective-permute-start.1 = (f32[9,8,128]{2,1,0:T(8,128)S(1)}, f32[9,8,128]{2,1,0:T(8,128)S(1)}, u32[]{:S(2)}, u32[]{:S(2)}) collective-permute-start(f32[9,8,128]{2,1,0:T(8,128)S(1)} %pack.1.refs_0_), channel_id=1, source_target_pairs={{0,24},{8,16},{16,8},{24,0},{1,25},{9,17},{17,9},{25,1},{2,26},{10... | collective-permute-start | bytes 110600 | tf_op jit(solution)/shard_map/ppermute | solution.py:32
  4.7 3.5 %collective-permute-start.2 = (f32[9,8,128]{2,1,0:T(8,128)S(1)}, f32[9,8,128]{2,1,0:T(8,128)S(1)}, u32[]{:S(2)}, u32[]{:S(2)}) collective-permute-start(f32[9,8,128]{2,1,0:T(8,128)S(1)} %pack.1.refs_0_), channel_id=1, source_target_pairs={{0,8},{8,0},{16,24},{24,16},{1,9},{9,1},{17,25},{25,17},{2,10},{10... | collective-permute-start | bytes 110600 | tf_op jit(solution)/shard_map/ppermute | solution.py:32
  23.0 1.5 %collective-permute-start.3 = (f32[8,8,8,128]{3,2,1,0:T(8,128)S(1)}, f32[8,8,8,128]{3,2,1,0:T(8,128)S(1)}, u32[]{:S(2)}, u32[]{:S(2)}) collective-permute-start(f32[8,8,8,128]{3,2,1,0:T(8,128)S(1)} %all_to_all.5.dense_ref), channel_id=1, source_target_pairs={{0,8},{8,0},{16,24},{24,16},{1,9},{9,1},{17,25},{25,17},{2,10},{10... | collective-permute-start | bytes 786440 | tf_op jit(solution)/shard_map/ppermute | solution.py:32
  25.0 4.3 %collective-permute-start.5 = (f32[2,64,128]{2,1,0:T(8,128)S(1)}, f32[2,64,128]{2,1,0:T(8,128)S(1)}, u32[]{:S(2)}, u32[]{:S(2)}) collective-permute-start(f32[2,64,128]{2,1,0:T(8,128)S(1)} %get-tuple-element.11), channel_id=1, source_target_pairs={{0,1},{1,0},{2,3},{3,2},{4,5},{5,4},{6,7},{7,6},{8,9},{9,8},{10,11... | collective-permute-start | bytes 196616 | tf_op jit(solution)/shard_map/ppermute | solution.py:32
  27.0 5.3 %collective-permute-start.4 = (f32[2,64,128]{2,1,0:T(8,128)S(1)}, f32[2,64,128]{2,1,0:T(8,128)S(1)}, u32[]{:S(2)}, u32[]{:S(2)}) collective-permute-start(f32[2,64,128]{2,1,0:T(8,128)S(1)} %rest_stress.1), channel_id=1, source_target_pairs={{0,2},{1,3},{2,0},{3,1},{4,6},{5,7},{6,4},{7,5},{8,10},{9,11},{10,... | collective-permute-start | bytes 196616 | tf_op jit(solution)/shard_map/ppermute | solution.py:32
  27.1 5.9 %copy-start.1 = (f32[128]{0:T(128)S(1)}, f32[128]{0:T(128)}, u32[]{:S(2)}) copy-start(f32[128]{0:T(128)} %param.11) | copy-start | bytes 1540
  27.1 5.9 %copy-start.2 = (f32[128]{0:T(128)S(1)}, f32[128]{0:T(128)}, u32[]{:S(2)}) copy-start(f32[128]{0:T(128)} %param.12) | copy-start | bytes 1540
  27.1 5.9 %copy-start.3 = (f32[128]{0:T(128)S(1)}, f32[128]{0:T(128)}, u32[]{:S(2)}) copy-start(f32[128]{0:T(128)} %param.13) | copy-start | bytes 1540
  29.4 5.8 %collective-permute-start.6 = (f32[64,128]{1,0:T(8,128)S(1)}, f32[64,128]{1,0:T(8,128)S(1)}, u32[]{:S(2)}, u32[]{:S(2)}) collective-permute-start(f32[64,128]{1,0:T(8,128)S(1)} %get-tuple-element.14), channel_id=1, source_target_pairs={{0,6},{1,7},{2,4},{3,5},{4,2},{5,3},{6,0},{7,1},{8,14},{9,15},{10,... | collective-permute-start | bytes 98312 | tf_op jit(solution)/shard_map/ppermute | solution.py:32
  30.6 5.3 %collective-permute-start.7 = (f32[64,128]{1,0:T(8,128)S(1)}, f32[64,128]{1,0:T(8,128)S(1)}, u32[]{:S(2)}, u32[]{:S(2)}) collective-permute-start(f32[64,128]{1,0:T(8,128)S(1)} %get-tuple-element.15), channel_id=1, source_target_pairs={{0,4},{1,5},{2,6},{3,7},{4,0},{5,1},{6,2},{7,3},{8,12},{9,13},{10,... | collective-permute-start | bytes 98312 | tf_op jit(solution)/shard_map/ppermute | solution.py:32
  32.4 4.0 %collective-permute-start.8 = (f32[64,128]{1,0:T(8,128)S(1)}, f32[64,128]{1,0:T(8,128)S(1)}, u32[]{:S(2)}, u32[]{:S(2)}) collective-permute-start(f32[64,128]{1,0:T(8,128)S(1)} %slice_bitcast_fusion), channel_id=1, source_target_pairs={{0,1},{1,0},{2,3},{3,2},{4,5},{5,4},{6,7},{7,6},{8,9},{9,8},{10,11... | collective-permute-start | bytes 98312 | tf_op jit(solution)/shard_map/ppermute | solution.py:32

commit v21 on v19

--- a/solution.py
+++ b/solution.py
@@ -10,6 +10,8 @@
 BLOCK = 128
 SUB = 8
 CHUNK = 256
+SLOTS = 24
+STRIDE = 32
 VMEM_SPEC = pl.BlockSpec(memory_space=pltpu.VMEM)
 HBM_SPEC = pl.BlockSpec(memory_space=pltpu.HBM)
 MIB = 1024 * 1024
@@ -55,29 +57,123 @@
     copies[2].wait()
 
 
-def densify_body(entries, sources, *refs):
-    ins, (_, out_ref, slips) = refs[:-3], refs[-3:]
-    events = ins[0].shape[0] - 1
-    width, _, blocks, _ = out_ref.shape
-    live = len(ins) * entries
+def place_slips(sources, ins, slips):
     row = lax.axis_index("rows")
+    events, entries, _ = slips.shape
+    entries //= len(ins)
+    for k, ref in zip(sources, ins):
+        where = pl.ds(pl.multiple_of((row ^ k) * entries, entries), entries)
+        for e in range(events):
+            slips[e, where, :] = ref[e, 0:entries, :]
+
+
+def compact_body(sources, width, blocks, *refs):
+    ins, (_, out_ref, left_ref, slips) = refs[:-4], refs[-4:]
+    events, live, _ = slips.shape
+    place_slips(sources, ins, slips)
+    core = lax.axis_index("rows") % 2
+    ids = ins[0][events]
+    for ref in ins[1:]:
+        ids = jnp.maximum(ids, ref[events])
+    mine = []
+    for h in range(2):
+        for c in range(width):
+            low = ((2 * c + (core ^ h)) * blocks).astype(jnp.float32)
+            mine.append((ids >= low) & (ids < low + blocks))
+    rows = 2 * width * SUB
+    member = jnp.concatenate([m.astype(jnp.float32) for m in mine], axis=0)
+    i, j = (lax.broadcasted_iota(jnp.int32, (BLOCK, BLOCK), d) for d in (0, 1))
+    before = jnp.dot(member.astype(jnp.bfloat16), (i < j).astype(jnp.bfloat16), preferred_element_type=jnp.float32)
+    count = jnp.dot(member.astype(jnp.bfloat16), jnp.ones((BLOCK, BLOCK), jnp.bfloat16), preferred_element_type=jnp.float32)
+    i, j = (lax.broadcasted_iota(jnp.int32, (rows, rows), d) for d in (0, 1))
+    earlier = ((i // SUB == j // SUB) & (j % SUB < i % SUB)).astype(jnp.bfloat16)
+    offset = jnp.dot(earlier, count.astype(jnp.bfloat16), preferred_element_type=jnp.float32)
+    over = jnp.max(offset + count) > SLOTS
+    mark = jnp.where(over, 1.0, 0.0)
+    rank = jnp.where(member > 0, before + offset, -1.0)
+    left = jnp.zeros(ids.shape, jnp.bool_)
+    for c in range(width):
+        left = left | (rank[c * SUB : (c + 1) * SUB] >= SLOTS)
+    left_ref[...] = jnp.where(left, ids, -1.0)
+
+    group = BLOCK // live
+    groups = -(-events // group)
+    event = lax.broadcasted_iota(jnp.int32, ids.shape, 0)
+    code = jnp.maximum(ids, 0.0) - jnp.floor(jnp.maximum(ids, 0.0) / blocks) * blocks + 1.0
+    code = code + (event * blocks).astype(jnp.float32)
+
+    def rows_of(tile):
+        tile = [pltpu.roll(tile[e : e + 1], (e % group) * live, 1) if e % group else tile[e : e + 1] for e in range(events)]
+        lane = lax.broadcasted_iota(jnp.int32, (1, BLOCK), 1) // live
+        out = []
+        for g in range(groups):
+            line = jnp.full((1, BLOCK), -1.0, jnp.float32)
+            for e in range(g * group, min((g + 1) * group, events)):
+                line = jnp.where(lane == e % group, tile[e], line)
+            out.append(line)
+        return out
+
+    codes = rows_of(code)
+    slot = lax.broadcasted_iota(jnp.int32, (STRIDE, BLOCK), 0).astype(jnp.float32)
+    picks = [[] for _ in range(groups)]
+    for c in range(width):
+        for g, line in enumerate(rows_of(rank[c * SUB : (c + 1) * SUB])):
+            line = jnp.where(line < SLOTS, line, -1.0)
+            picks[g].append((slot == jnp.broadcast_to(line, slot.shape)).astype(jnp.bfloat16))
+    data = numbers = 0.0
+    for g in range(groups):
+        pick = jnp.concatenate(picks[g], axis=0)
+        size = min(group, events - g * group) * live
+        slip = slips[g * group : min((g + 1) * group, events)].reshape(size, BLOCK)
+        hi = slip.astype(jnp.bfloat16)
+        lo = (slip - hi.astype(jnp.float32)).astype(jnp.bfloat16)
+        data += jnp.dot(pick[:, :size], hi, preferred_element_type=jnp.float32)
+        data += jnp.dot(pick[:, :size], lo, preferred_element_type=jnp.float32)
+        line = jnp.broadcast_to(codes[g], (SUB, BLOCK)).astype(jnp.bfloat16)
+        numbers += lax.dot_general(line, pick, NT, preferred_element_type=jnp.float32)
+    lane = lax.broadcasted_iota(jnp.int32, (SUB, BLOCK), 1)
+    for c in range(width):
+        out_ref[c, 0:SLOTS, :] = data[c * STRIDE : c * STRIDE + SLOTS]
+        start = c * STRIDE // BLOCK * BLOCK
+        tile = numbers[:, start : start + BLOCK]
+        shift = c * STRIDE - start
+        tile = pltpu.roll(tile, BLOCK - shift, 1) if shift else tile
+        out_ref[c, SLOTS : SLOTS + SUB, :] = jnp.where(lane < STRIDE, tile, mark)
+
+
+def expand_body(in_ref, out_ref, mark_ref):
+    width, events, blocks, _ = out_ref.shape
+    mark = in_ref[0, SLOTS : SLOTS + SUB, :]
+    for c in range(width):
+        info = in_ref[c, SLOTS : SLOTS + SUB, :]
+        mark = jnp.maximum(mark, info)
+        numbers = jnp.broadcast_to(info[0:1, :], (events * blocks, BLOCK))[:, :STRIDE]
+        place = lax.broadcasted_iota(jnp.int32, numbers.shape, 0).astype(jnp.float32) + 1.0
+        pick = (numbers == place).astype(jnp.bfloat16)
+        slip = in_ref[c]
+        hi = slip.astype(jnp.bfloat16)
+        lo = (slip - hi.astype(jnp.float32)).astype(jnp.bfloat16)
+        total = jnp.dot(pick, hi, preferred_element_type=jnp.float32)
+        total += jnp.dot(pick, lo, preferred_element_type=jnp.float32)
+        out_ref[c] = total.reshape(events, blocks, BLOCK)
+    mark_ref[...] = mark
+
+
+def densify_body(sources, *refs):
+    ins, (ids_ref, out_ref, slips) = refs[:-3], refs[-3:]
+    width, events, blocks, _ = out_ref.shape
+    live = slips.shape[1]
+    place_slips(sources, ins, slips)
     line = lax.broadcasted_iota(jnp.int32, (width * blocks, live), 0)
-    number = ((line // blocks * 2 + row % 2) * blocks + line % blocks).astype(jnp.float32)
+    number = ((line // blocks * 2 + lax.axis_index("rows") % 2) * blocks + line % blocks).astype(jnp.float32)
     for e in range(events):
-        ids = jnp.full((1, BLOCK), -1.0, jnp.float32)
-        for ref in ins:
-            ids = jnp.maximum(ids, ref[events, e : e + 1, :])
-        ids = jnp.broadcast_to(ids, (width * blocks, BLOCK))[:, :live]
+        ids = jnp.broadcast_to(ids_ref[e : e + 1, :], (width * blocks, BLOCK))[:, :live]
         onehot = (ids == number).astype(jnp.bfloat16)
-        for k, ref in zip(sources, ins):
-            where = pl.ds(pl.multiple_of((row ^ k) * entries, entries), entries)
-            slips[e, where, :] = ref[e, 0:entries, :]
         slip = slips[e]
-        total = jnp.zeros((width * blocks, BLOCK), jnp.float32)
-        for _ in range(3):
-            piece = slip.astype(jnp.bfloat16)
-            slip = slip - piece.astype(jnp.float32)
-            total = total + jnp.dot(onehot, piece, preferred_element_type=jnp.float32)
+        hi = slip.astype(jnp.bfloat16)
+        lo = (slip - hi.astype(jnp.float32)).astype(jnp.bfloat16)
+        total = jnp.dot(onehot, hi, preferred_element_type=jnp.float32)
+        total += jnp.dot(onehot, lo, preferred_element_type=jnp.float32)
         out_ref[:, e] = total.reshape(width, blocks, BLOCK)
 
 
@@ -161,16 +257,39 @@
     others = sorted(range(1, height), key=lambda k: (k < 2, k))
     came = [send_xor(packed, "rows", k) for k in others]
     blocks_half = blocks_here // 2
-    dense = pl.pallas_call(
-        functools.partial(densify_body, entries, [0] + others),
-        out_shape=f32(width, events_here, blocks_half, BLOCK),
+    sources_of = [0] + others
+    blocks_of = [packed, *came]
+    live = height * entries
+    slips_held = pltpu.VMEM((events_here, live, BLOCK), jnp.float32)
+    message, left = pl.pallas_call(
+        functools.partial(compact_body, sources_of, width, blocks_half),
+        out_shape=[f32(width, SLOTS + SUB, BLOCK), f32(SUB, BLOCK)],
         in_specs=[VMEM_SPEC] * height + [HBM_SPEC],
-        out_specs=VMEM_SPEC,
-        scratch_shapes=[pltpu.VMEM((events_here, height * entries, BLOCK), jnp.float32)],
+        out_specs=[VMEM_SPEC] * 2,
+        scratch_shapes=[slips_held],
+        compiler_params=params(16),
+        name="compact",
+    )(*blocks_of, in_hbm(kernel))
+    mine, mark = pl.pallas_call(
+        expand_body,
+        out_shape=[f32(width, events_here, blocks_half, BLOCK), f32(SUB, BLOCK)],
+        in_specs=[VMEM_SPEC],
+        out_specs=[VMEM_SPEC] * 2,
         compiler_params=params(8),
-        name="densify",
-    )(packed, *came, in_hbm(kernel))
-    mine = lax.all_to_all(dense, "cols", 0, 0, tiled=True)
+        name="expand",
+    )(lax.all_to_all(message, "cols", 0, 0, tiled=True))
+
+    def all_left(kernel, left, *blocks_of):
+        dense = pl.pallas_call(
+            functools.partial(densify_body, sources_of),
+            out_shape=f32(width, events_here, blocks_half, BLOCK),
+            in_specs=[VMEM_SPEC] * (height + 1),
+            out_specs=VMEM_SPEC,
+            scratch_shapes=[slips_held],
+            compiler_params=params(8),
+            name="densify",
+        )(*blocks_of, left)
+        return stress_of(kernel, lax.all_to_all(dense, "cols", 0, 0, tiled=True))
 
     def call(body, targets, outs, *args):
         return pl.pallas_call(
@@ -178,7 +297,7 @@
             out_shape=outs,
             in_specs=[VMEM_SPEC] * len(args),
             out_specs=jax.tree.map(lambda _: VMEM_SPEC, outs),
-            compiler_params=params(8),
+            compiler_params=params(24),
             cost_estimate=pl.CostEstimate(
                 flops=3 * receivers * sources * events // 2,
                 bytes_accessed=receivers * sources,
@@ -192,23 +311,29 @@
     def sums(targets):
         return f32(len(targets), events, share)
 
-    came = send_xor(mine, "rows", 1)
-    own, far_own, near_own = call(
-        own_body, (far_send, near_send), [slips, sums(far_send), sums(near_send)], mine, kernel
+    def stress_of(kernel, mine):
+        came = send_xor(mine, "rows", 1)
+        own, far_own, near_own = call(
+            own_body, (far_send, near_send), [slips, sums(far_send), sums(near_send)], mine, kernel
+        )
+        other, far_sent = call(other_body, far_send, [slips, sums(far_send)], came, kernel, far_own)
+        near_sent = call(rest_body, near_send, sums(near_send), other, kernel, near_own)
+
+        def later(targets):
+            return call(both_body, targets, sums(targets), own, other, kernel)
+
+        far_came = send_xor(far_sent, "cols", 1)
+        near_came = [send_xor(near_sent[j : j + 2], "cols", near_send[j]) for j in range(0, len(near_send), 2)]
+        far = later(far_keep) + far_came
+        near = sum(near_came, later(near_keep))
+        parts = [send_xor(far[j], "cols", k) for j, k in reversed(list(enumerate(far_keep)))]
+        parts.append(send_xor(near[1], "cols", 1))
+        return sum(parts, near[0])
+
+    stress_change = stress_of(kernel, mine)
+    stress_change += lax.cond(
+        jnp.any(mark[0, STRIDE:] > 0), all_left, lambda *_: jnp.zeros_like(stress_change), kernel, left, *blocks_of
     )
-    other, far_sent = call(other_body, far_send, [slips, sums(far_send)], came, kernel, far_own)
-    near_sent = call(rest_body, near_send, sums(near_send), other, kernel, near_own)
-
-    def later(targets):
-        return call(both_body, targets, sums(targets), own, other, kernel)
-
-    far_came = send_xor(far_sent, "cols", 1)
-    near_came = [send_xor(near_sent[j : j + 2], "cols", near_send[j]) for j in range(0, len(near_send), 2)]
-    far = later(far_keep) + far_came
-    near = sum(near_came, later(near_keep))
-    parts = [send_xor(far[j], "cols", k) for j, k in reversed(list(enumerate(far_keep)))]
-    parts.append(send_xor(near[1], "cols", 1))
-    stress_change = sum(parts, near[0])
     scale = direct_effect[None, :]
     growth = jnp.expm1(load_rate * time_before / direct_effect)[None, :]
     log_time = jnp.log(scale / load_rate[None, :]) + jnp.log(

time: 37.2 us -> 43.7 us (1.17)
  Pallas kernels: 4.68 us -> 12.3 us
  waiting for transfers between devices: 7.86 us -> 6.06 us
  blocking collectives: 14.5 us -> 12.9 us
  between operations: 0.73 us -> 1.44 us
  other arithmetic: 0.69 us -> 1.39 us
  starting transfers between devices: 8.45 us -> 9.07 us
    pallas_call x5, Pallas kernels: 3.46 us -> 10.5 us  [call(): pl.pallas_call(functools.partial(body, targets), out_shape=outs, in_specs...]
    ppermute x9, waiting for transfers between devices: 7.86 us -> 6.06 us  [send_xor(): lax.ppermute(block, axis, [(r, r ^ k) for r in range(lax.axis_size(axis))])]
    all_to_all x1, blocking collectives: 14.5 us -> 12.9 us  [per_device(): lax.all_to_all(message, 'cols', 0, 0, tiled=True)]
    reduce_or x0 -> x1, other arithmetic: none -> 0.7 us  [per_device(): jnp.any(mark[0, STRIDE:] > 0)]
    ppermute x9, starting transfers between devices: 8.45 us -> 9.07 us  [send_xor(): lax.ppermute(block, axis, [(r, r ^ k) for r in range(lax.axis_size(axis))])]
    pallas_call x1 -> x2, Pallas kernels: 0.26 us -> 0.83 us  [the longest x1 0.63 us: per_device(): pl.pallas_call(functools.partial(compact_body, sources_of, width, blocks_...]
  transfers between devices with their start and end apart: 9 -> 9, of which waited for: 7 -> 6; matrix products, arithmetic and copies ran while one was open for 0% -> 2% of each run, Pallas kernels for 8% -> 23%
where the time goes in v21:
time: 43.7 us; the launch traced here: 43.5 us
  blocking collectives  12.9 us (30%)
  Pallas kernels  12.3 us (28%)
  starting transfers between devices  9.07 us (21%)
  waiting for transfers between devices  6.06 us (14%)
  between operations  1.44 us (3%)
  other arithmetic  1.39 us (3%)
    all_to_all x1, blocking collectives, per_device(): lax.all_to_all(message, 'cols', 0, 0, tiled=True)  12.9 us
    pallas_call x5, Pallas kernels, call(): pl.pallas_call(functools.partial(body, targets), out_shape=outs, in_specs...  10.5 us
    ppermute x9, starting transfers between devices, send_xor(): lax.ppermute(block, axis, [(r, r ^ k) for r in range(lax.axis_size(axis))])  9.07 us
    ppermute x9, waiting for transfers between devices, send_xor(): lax.ppermute(block, axis, [(r, r ^ k) for r in range(lax.axis_size(axis))])  6.06 us
    pallas_call x1, Pallas kernels, per_device(): pl.pallas_call(pack_body, out_shape=f32(events_here + 1, SUB, BLOCK), in_...  0.96 us
  transfers between devices with their start and end apart: 9, of which 6 were waited for; matrix products, arithmetic and copies ran while one was open for 2% of the time, Pallas kernels for 23%

profile of v21, /device:TPU:0, one launch (start us, length us, event | category | flops | bytes accessed | tf_op | source)
XLA Modules:
  0.0 43.5 jit_solution(10755942346163037603)
XLA Ops:
  0.6 0.0 copy-start
  0.6 1.0 %pack.1.refs_0_ = f32[9,8,128]{2,1,0:T(8,128)S(1)} custom-call(f32[8,8,128]{2,1,0:T(8,128)} %slip_hbm.1, s32[8,8]{1,0:T(8,128)} %list_hbm.1, s32[8]{0:T(128)} %count_hbm.1), custom_call_target="tpu_custom_call" | custom-call | tf_op jit(solution)/shard_map/pack/pallas_call | solution.py:243
  1.6 3.0 %collective-permute-start.6 = (f32[9,8,128]{2,1,0:T(8,128)S(1)}, f32[9,8,128]{2,1,0:T(8,128)S(1)}, u32[]{:S(2)}, u32[]{:S(2)}) collective-permute-start(f32[9,8,128]{2,1,0:T(8,128)S(1)} %pack.1.refs_0_), channel_id=1, source_target_pairs={{0,16},{8,24},{16,0},{24,8},{1,17},{9,25},{17,1},{25,9},{2,18},{10... | collective-permute-start | bytes 110600 | tf_op jit(solution)/shard_map/ppermute | solution.py:34
  4.6 0.0 collective-permute-start.7
  4.6 0.2 collective-permute-start.8
  4.8 1.7 %collective-permute-done.6.refs_1_ = f32[9,8,128]{2,1,0:T(8,128)S(1)} collective-permute-done((f32[9,8,128]{2,1,0:T(8,128)S(1)}, f32[9,8,128]{2,1,0:T(8,128)S(1)}, u32[]{:S(2)}, u32[]{:S(2)}) %collective-permute-start.6) | collective-permute-done | bytes 36896 | tf_op jit(solution)/shard_map/ppermute | solution.py:34
  6.6 1.6 %collective-permute-done.7.refs_2_ = f32[9,8,128]{2,1,0:T(8,128)S(1)} collective-permute-done((f32[9,8,128]{2,1,0:T(8,128)S(1)}, f32[9,8,128]{2,1,0:T(8,128)S(1)}, u32[]{:S(2)}, u32[]{:S(2)}) %collective-permute-start.7) | collective-permute-done | bytes 36896 | tf_op jit(solution)/shard_map/ppermute | solution.py:34
  8.2 0.0 collective-permute-done.8.refs_3_
  8.2 0.6 %compact.1 = (f32[8,32,128]{2,1,0:T(8,128)S(1)}, f32[8,128]{1,0:T(8,128)S(1)}) custom-call(f32[9,8,128]{2,1,0:T(8,128)S(1)} %pack.1.refs_0_, f32[9,8,128]{2,1,0:T(8,128)S(1)} %collective-permute-done.6.refs_1_, f32[9,8,128]{2,1,0:T(8,128)S(1)} %collective-permute-done.7.refs_2_, f32[9,8,128]{2,1,0:T(8,128)S(1)} %collective-permute-done.8.refs_3_, ...), custom_call_target="tpu_custom_call" | custom-call | tf_op jit(solution)/shard_map/compact/pallas_call | solution.py:264
  8.8 12.9 %all_to_all.10.in_ref = f32[8,32,128]{2,1,0:T(8,128)S(1)} all-to-all(f32[8,32,128]{2,1,0:T(8,128)S(1)} %get-tuple-element.37), channel_id=1, replica_groups=mesh['rows'=4,'cols'=8] {'cols'}, dimensions={0} | all-to-all | bytes 262144 | tf_op jit(solution)/shard_map/all_to_all | solution.py:280
  21.7 0.2 expand.1
  21.9 0.1 collective-permute-start.9
  22.0 0.0 copy-done
  22.0 0.8 %own_stress.3 = (bf16[128,1024]{1,0:T(8,128)(2,1)S(1)}, f32[2,64,128]{2,1,0:T(8,128)S(1)}, f32[2,64,128]{2,1,0:T(8,128)S(1)}) custom-call(f32[8,8,8,128]{3,2,1,0:T(8,128)S(1)} %get-tuple-element.38.dense_ref, f32[8,128,2048]{2,1,0:T(8,128)S(1)} %bitcast.39), custom_call_target="tpu_custom_call" | custom-call | flops 201326592 | bytes 2097152 | tf_op jit(solution)/shard_map/own_stress/pallas_call | solution.py:295
  22.9 0.7 %collective-permute-done.9.dense_ref = f32[8,8,8,128]{3,2,1,0:T(8,128)S(1)} collective-permute-done((f32[8,8,8,128]{3,2,1,0:T(8,128)S(1)}, f32[8,8,8,128]{3,2,1,0:T(8,128)S(1)}, u32[]{:S(2)}, u32[]{:S(2)}) %collective-permute-start.9) | collective-permute-done | bytes 262176 | tf_op jit(solution)/shard_map/ppermute | solution.py:34
  23.5 0.5 %other_stress.3 = (bf16[128,1024]{1,0:T(8,128)(2,1)S(1)}, f32[2,64,128]{2,1,0:T(8,128)S(1)}) custom-call(f32[8,8,8,128]{3,2,1,0:T(8,128)S(1)} %collective-permute-done.9.dense_ref, f32[8,128,2048]{2,1,0:T(8,128)S(1)} %bitcast.40, f32[2,64,128]{2,1,0:T(8,128)S(1)} %get-tuple-element.40.sum_ref), custom_call_target="tpu_custom_call" | custom-call | flops 201326592 | bytes 2097152 | tf_op jit(solution)/shard_map/other_stress/pallas_call | solution.py:295
  24.1 0.3 collective-permute-start.11
  24.3 0.7 %compare_reduce_fusion = pred[]{:T(512)} fusion(f32[8,128]{1,0:T(8,128)S(1)} %get-tuple-element.44), kind=kLoop, calls=%fused_computation.16 | loop fusion | flops 191 | bytes 385 | tf_op jit(solution)/shard_map/reduce_or | solution.py:335
  25.7 0.0 slice-start
  25.7 4.0 %rest_stress.3 = f32[2,64,128]{2,1,0:T(8,128)S(1)} custom-call(bf16[128,1024]{1,0:T(8,128)(2,1)S(1)} %get-tuple-element.41.other_ref.slip_ref, f32[8,128,2048]{2,1,0:T(8,128)} %bitcast.37, f32[2,64,128]{2,1,0:T(8,128)S(1)} %get-tuple-element.42.sum_ref), custom_call_target="tpu_custom_call" | custom-call | flops 201326592 | bytes 2097152 | tf_op jit(solution)/shard_map/rest_stress/pallas_call | solution.py:295
  29.8 1.2 %collective-permute-start.10 = (f32[2,64,128]{2,1,0:T(8,128)S(1)}, f32[2,64,128]{2,1,0:T(8,128)S(1)}, u32[]{:S(2)}, u32[]{:S(2)}) collective-permute-start(f32[2,64,128]{2,1,0:T(8,128)S(1)} %rest_stress.3), channel_id=1, source_target_pairs={{0,2},{1,3},{2,0},{3,1},{4,6},{5,7},{6,4},{7,5},{8,10},{9,11},{10,... | collective-permute-start | bytes 196616 | tf_op jit(solution)/shard_map/ppermute | solution.py:34
  30.9 0.0 slice-start.1
  30.9 0.0 copy-start.2
  30.9 0.0 copy-start.3
  30.9 0.0 copy-start.4
  30.9 4.3 %both_stress.7 = f32[2,64,128]{2,1,0:T(8,128)S(1)} custom-call(bf16[128,1024]{1,0:T(8,128)(2,1)S(1)} %get-tuple-element.39.own_ref, bf16[128,1024]{1,0:T(8,128)(2,1)S(1)} %get-tuple-element.41.other_ref.slip_ref, f32[8,128,2048]{2,1,0:T(8,128)} %bitcast.38), custom_call_target="tpu_custom_call" | custom-call | flops 201326592 | bytes 2097152 | tf_op jit(solution)/shard_map/both_stress/pallas_call | solution.py:295
  35.3 0.0 slice-done
  35.3 0.2 slice-done.1
  35.5 0.8 %both_stress.6 = f32[2,64,128]{2,1,0:T(8,128)S(1)} custom-call(bf16[128,1024]{1,0:T(8,128)(2,1)S(1)} %get-tuple-element.39.own_ref, bf16[128,1024]{1,0:T(8,128)(2,1)S(1)} %get-tuple-element.41.other_ref.slip_ref, f32[8,128,2048]{2,1,0:T(8,128)S(1)} %bitcast.43), custom_call_target="tpu_custom_call" | custom-call | flops 201326592 | bytes 2097152 | tf_op jit(solution)/shard_map/both_stress/pallas_call | solution.py:295
  36.3 0.0 collective-permute-done.11
  36.3 0.8 %collective-permute-start.12 = (f32[64,128]{1,0:T(8,128)S(1)}, f32[64,128]{1,0:T(8,128)S(1)}, u32[]{:S(2)}, u32[]{:S(2)}) collective-permute-start(f32[64,128]{1,0:T(8,128)S(1)} %get-tuple-element.50), channel_id=1, source_target_pairs={{0,6},{1,7},{2,4},{3,5},{4,2},{5,3},{6,0},{7,1},{8,14},{9,15},{10,... | collective-permute-start | bytes 98312 | tf_op jit(solution)/shard_map/ppermute | solution.py:34
  37.2 1.6 %collective-permute-start.13 = (f32[64,128]{1,0:T(8,128)S(1)}, f32[64,128]{1,0:T(8,128)S(1)}, u32[]{:S(2)}, u32[]{:S(2)}) collective-permute-start(f32[64,128]{1,0:T(8,128)S(1)} %get-tuple-element.51), channel_id=1, source_target_pairs={{0,4},{1,5},{2,6},{3,7},{4,0},{5,1},{6,2},{7,3},{8,12},{9,13},{10,... | collective-permute-start | bytes 98312 | tf_op jit(solution)/shard_map/ppermute | solution.py:34
  38.8 0.0 collective-permute-done.10
  38.8 1.9 %collective-permute-start.14 = (f32[64,128]{1,0:T(8,128)S(1)}, f32[64,128]{1,0:T(8,128)S(1)}, u32[]{:S(2)}, u32[]{:S(2)}) collective-permute-start(f32[64,128]{1,0:T(8,128)S(1)} %slice_bitcast_fusion.4), channel_id=1, source_target_pairs={{0,1},{1,0},{2,3},{3,2},{4,5},{5,4},{6,7},{7,6},{8,9},{9,8},{10,11... | collective-permute-start | bytes 98312 | tf_op jit(solution)/shard_map/ppermute | solution.py:34
  40.7 0.0 copy-done.2
  40.7 0.0 copy-done.3
  40.7 0.0 copy-done.4
  40.7 1.5 %collective-permute-done.12 = f32[64,128]{1,0:T(8,128)S(1)} collective-permute-done((f32[64,128]{1,0:T(8,128)S(1)}, f32[64,128]{1,0:T(8,128)S(1)}, u32[]{:S(2)}, u32[]{:S(2)}) %collective-permute-start.12) | collective-permute-done | bytes 32800 | tf_op jit(solution)/shard_map/ppermute | solution.py:34
  42.2 0.5 %collective-permute-done.13 = f32[64,128]{1,0:T(8,128)S(1)} collective-permute-done((f32[64,128]{1,0:T(8,128)S(1)}, f32[64,128]{1,0:T(8,128)S(1)}, u32[]{:S(2)}, u32[]{:S(2)}) %collective-permute-start.13) | collective-permute-done | bytes 32800 | tf_op jit(solution)/shard_map/ppermute | solution.py:34
  42.7 0.1 collective-permute-done.14
  42.8 0.7 %add_bitcast_fusion = (f32[128,64]{0,1:T(8,128)}, f32[64,128]{1,0:T(8,128)}) fusion(f32[128]{0:T(128)S(1)} %get-tuple-element.53, f32[128]{0:T(128)S(1)} %copy-done.2, f32[128]{0:T(128)S(1)} %get-tuple-element.52, f32[64,128]{1,0:T(8,128)S(1)} %get-tuple-element.54, f32[64,128]{1,0:T(8,128)S(1)} %collective-permute-done.14, ...), kind=kLoop, calls=%fused_computation.15 | loop fusion | flops 65536 | bytes 230912 | tf_op jit(solution)/shard_map/transpose | solution.py:342
  (8 shorter events, 0.1 us)
Async XLA Ops:
  0.6 21.4 %copy-start = (f32[1024,2048]{1,0:T(8,128)S(1)}, f32[1024,2048]{1,0:T(8,128)}, u32[]{:S(2)}) copy-start(f32[1024,2048]{1,0:T(8,128)} %param.9) | copy-start | bytes 25165828
  1.6 5.0 %collective-permute-start.6 = (f32[9,8,128]{2,1,0:T(8,128)S(1)}, f32[9,8,128]{2,1,0:T(8,128)S(1)}, u32[]{:S(2)}, u32[]{:S(2)}) collective-permute-start(f32[9,8,128]{2,1,0:T(8,128)S(1)} %pack.1.refs_0_), channel_id=1, source_target_pairs={{0,16},{8,24},{16,0},{24,8},{1,17},{9,25},{17,1},{25,9},{2,18},{10... | collective-permute-start | bytes 110600 | tf_op jit(solution)/shard_map/ppermute | solution.py:34
  4.6 3.5 %collective-permute-start.7 = (f32[9,8,128]{2,1,0:T(8,128)S(1)}, f32[9,8,128]{2,1,0:T(8,128)S(1)}, u32[]{:S(2)}, u32[]{:S(2)}) collective-permute-start(f32[9,8,128]{2,1,0:T(8,128)S(1)} %pack.1.refs_0_), channel_id=1, source_target_pairs={{0,24},{8,16},{16,8},{24,0},{1,25},{9,17},{17,9},{25,1},{2,26},{10... | collective-permute-start | bytes 110600 | tf_op jit(solution)/shard_map/ppermute | solution.py:34
  4.6 3.5 %collective-permute-start.8 = (f32[9,8,128]{2,1,0:T(8,128)S(1)}, f32[9,8,128]{2,1,0:T(8,128)S(1)}, u32[]{:S(2)}, u32[]{:S(2)}) collective-permute-start(f32[9,8,128]{2,1,0:T(8,128)S(1)} %pack.1.refs_0_), channel_id=1, source_target_pairs={{0,8},{8,0},{16,24},{24,16},{1,9},{9,1},{17,25},{25,17},{2,10},{10... | collective-permute-start | bytes 110600 | tf_op jit(solution)/shard_map/ppermute | solution.py:34
  21.9 1.6 %collective-permute-start.9 = (f32[8,8,8,128]{3,2,1,0:T(8,128)S(1)}, f32[8,8,8,128]{3,2,1,0:T(8,128)S(1)}, u32[]{:S(2)}, u32[]{:S(2)}) collective-permute-start(f32[8,8,8,128]{3,2,1,0:T(8,128)S(1)} %get-tuple-element.38.dense_ref), channel_id=1, source_target_pairs={{0,8},{8,0},{16,24},{24,16},{1,9},{9,1},{17,25},{25,17},{2,10},{10... | collective-permute-start | bytes 786440 | tf_op jit(solution)/shard_map/ppermute | solution.py:34
  24.1 12.2 %collective-permute-start.11 = (f32[2,64,128]{2,1,0:T(8,128)S(1)}, f32[2,64,128]{2,1,0:T(8,128)S(1)}, u32[]{:S(2)}, u32[]{:S(2)}) collective-permute-start(f32[2,64,128]{2,1,0:T(8,128)S(1)} %get-tuple-element.43), channel_id=1, source_target_pairs={{0,1},{1,0},{2,3},{3,2},{4,5},{5,4},{6,7},{7,6},{8,9},{9,8},{10,11... | collective-permute-start | bytes 196616 | tf_op jit(solution)/shard_map/ppermute | solution.py:34
  25.7 9.5 %slice-start = ((s8[8388608]{0:T(1024)(128)(4,1)}), s8[4194304]{0:T(1024)(128)(4,1)S(1)}, s32[]{:S(2)}) async-start(s8[8388608]{0:T(1024)(128)(4,1)} %bitcast.41), calls=%async_computation.2 | async-start | bytes 8388608
  29.8 9.1 %collective-permute-start.10 = (f32[2,64,128]{2,1,0:T(8,128)S(1)}, f32[2,64,128]{2,1,0:T(8,128)S(1)}, u32[]{:S(2)}, u32[]{:S(2)}) collective-permute-start(f32[2,64,128]{2,1,0:T(8,128)S(1)} %rest_stress.3), channel_id=1, source_target_pairs={{0,2},{1,3},{2,0},{3,1},{4,6},{5,7},{6,4},{7,5},{8,10},{9,11},{10,... | collective-permute-start | bytes 196616 | tf_op jit(solution)/shard_map/ppermute | solution.py:34
  30.9 4.6 %slice-start.1 = ((s8[8388608]{0:T(1024)(128)(4,1)}), s8[4194304]{0:T(1024)(128)(4,1)S(1)}, s32[]{:S(2)}) async-start(s8[8388608]{0:T(1024)(128)(4,1)} %bitcast.41), calls=%async_computation.3 | async-start | bytes 8388608
  30.9 9.8 %copy-start.2 = (f32[128]{0:T(128)S(1)}, f32[128]{0:T(128)}, u32[]{:S(2)}) copy-start(f32[128]{0:T(128)} %param.13) | copy-start | bytes 1540
  30.9 9.8 %copy-start.3 = (f32[128]{0:T(128)S(1)}, f32[128]{0:T(128)}, u32[]{:S(2)}) copy-start(f32[128]{0:T(128)} %param.14) | copy-start | bytes 1540
  30.9 9.8 %copy-start.4 = (f32[128]{0:T(128)S(1)}, f32[128]{0:T(128)}, u32[]{:S(2)}) copy-start(f32[128]{0:T(128)} %param.15) | copy-start | bytes 1540
  36.3 5.9 %collective-permute-start.12 = (f32[64,128]{1,0:T(8,128)S(1)}, f32[64,128]{1,0:T(8,128)S(1)}, u32[]{:S(2)}, u32[]{:S(2)}) collective-permute-start(f32[64,128]{1,0:T(8,128)S(1)} %get-tuple-element.50), channel_id=1, source_target_pairs={{0,6},{1,7},{2,4},{3,5},{4,2},{5,3},{6,0},{7,1},{8,14},{9,15},{10,... | collective-permute-start | bytes 98312 | tf_op jit(solution)/shard_map/ppermute | solution.py:34
  37.2 5.5 %collective-permute-start.13 = (f32[64,128]{1,0:T(8,128)S(1)}, f32[64,128]{1,0:T(8,128)S(1)}, u32[]{:S(2)}, u32[]{:S(2)}) collective-permute-start(f32[64,128]{1,0:T(8,128)S(1)} %get-tuple-element.51), channel_id=1, source_target_pairs={{0,4},{1,5},{2,6},{3,7},{4,0},{5,1},{6,2},{7,3},{8,12},{9,13},{10,... | collective-permute-start | bytes 98312 | tf_op jit(solution)/shard_map/ppermute | solution.py:34
  38.8 4.0 %collective-permute-start.14 = (f32[64,128]{1,0:T(8,128)S(1)}, f32[64,128]{1,0:T(8,128)S(1)}, u32[]{:S(2)}, u32[]{:S(2)}) collective-permute-start(f32[64,128]{1,0:T(8,128)S(1)} %slice_bitcast_fusion.4), channel_id=1, source_target_pairs={{0,1},{1,0},{2,3},{3,2},{4,5},{5,4},{6,7},{7,6},{8,9},{9,8},{10,11... | collective-permute-start | bytes 98312 | tf_op jit(solution)/shard_map/ppermute | solution.py:34

commit v22 on v21

--- a/solution.py
+++ b/solution.py
@@ -289,7 +289,7 @@
             compiler_params=params(8),
             name="densify",
         )(*blocks_of, left)
-        return stress_of(kernel, lax.all_to_all(dense, "cols", 0, 0, tiled=True))
+        return sum(stress_of(kernel, lax.all_to_all(dense, "cols", 0, 0, tiled=True)))
 
     def call(body, targets, outs, *args):
         return pl.pallas_call(
@@ -328,12 +328,14 @@
         near = sum(near_came, later(near_keep))
         parts = [send_xor(far[j], "cols", k) for j, k in reversed(list(enumerate(far_keep)))]
         parts.append(send_xor(near[1], "cols", 1))
-        return sum(parts, near[0])
-
-    stress_change = stress_of(kernel, mine)
-    stress_change += lax.cond(
-        jnp.any(mark[0, STRIDE:] > 0), all_left, lambda *_: jnp.zeros_like(stress_change), kernel, left, *blocks_of
+        return [*parts, near[0]]
+
+    first, *parts = stress_of(kernel, mine)
+    first, left, *blocks_of = lax.optimization_barrier((first, left, *blocks_of))
+    parts.append(
+        lax.cond(jnp.any(mark[0, STRIDE:] > 0), all_left, lambda *_: jnp.zeros_like(first), kernel, left, *blocks_of)
     )
+    stress_change = sum(parts, first)
     scale = direct_effect[None, :]
     growth = jnp.expm1(load_rate * time_before / direct_effect)[None, :]
     log_time = jnp.log(scale / load_rate[None, :]) + jnp.log(

time: 43.7 us -> 36.7 us (0.84)
  Pallas kernels: 12.3 us -> 5.28 us
  waiting for transfers between devices: 6.06 us -> 7.07 us
  starting transfers between devices: 9.07 us -> 8.3 us
    pallas_call x5, Pallas kernels: 10.5 us -> 3.49 us  [call(): pl.pallas_call(functools.partial(body, targets), out_shape=outs, in_specs...]
    ppermute x9, waiting for transfers between devices: 6.06 us -> 7.07 us  [send_xor(): lax.ppermute(block, axis, [(r, r ^ k) for r in range(lax.axis_size(axis))])]
    ppermute x9, starting transfers between devices: 9.07 us -> 8.3 us  [send_xor(): lax.ppermute(block, axis, [(r, r ^ k) for r in range(lax.axis_size(axis))])]
  transfers between devices with their start and end apart: 9 -> 9, of which waited for: 6 -> 6; matrix products, arithmetic and copies ran while one was open for 2% -> 2% of each run, Pallas kernels for 23% -> 7%
where the time goes in v22:
time: 36.7 us; the launch traced here: 36.5 us
  blocking collectives  12.9 us (35%)
  starting transfers between devices  8.3 us (23%)
  waiting for transfers between devices  7.07 us (19%)
  Pallas kernels  5.28 us (14%)
  between operations  1.42 us (4%)
  other arithmetic  1.4 us (4%)
    all_to_all x1, blocking collectives, per_device(): lax.all_to_all(message, 'cols', 0, 0, tiled=True)  12.9 us
    ppermute x9, starting transfers between devices, send_xor(): lax.ppermute(block, axis, [(r, r ^ k) for r in range(lax.axis_size(axis))])  8.3 us
    ppermute x9, waiting for transfers between devices, send_xor(): lax.ppermute(block, axis, [(r, r ^ k) for r in range(lax.axis_size(axis))])  7.07 us
    pallas_call x5, Pallas kernels, call(): pl.pallas_call(functools.partial(body, targets), out_shape=outs, in_specs...  3.49 us
    pallas_call x1, Pallas kernels, per_device(): pl.pallas_call(pack_body, out_shape=f32(events_here + 1, SUB, BLOCK), in_...  0.96 us
  transfers between devices with their start and end apart: 9, of which 6 were waited for; matrix products, arithmetic and copies ran while one was open for 2% of the time, Pallas kernels for 7%

profile of v22, /device:TPU:0, one launch (start us, length us, event | category | flops | bytes accessed | tf_op | source)
XLA Modules:
  0.0 36.5 jit_solution(1226214032821350692)
XLA Ops:
  0.6 0.0 copy-start
  0.6 1.0 %pack.1.refs_0_ = f32[9,8,128]{2,1,0:T(8,128)S(1)} custom-call(f32[8,8,128]{2,1,0:T(8,128)} %slip_hbm.1, s32[8,8]{1,0:T(8,128)} %list_hbm.1, s32[8]{0:T(128)} %count_hbm.1), custom_call_target="tpu_custom_call" | custom-call | tf_op jit(solution)/shard_map/pack/pallas_call | solution.py:243
  1.6 3.0 %collective-permute-start.6 = (f32[9,8,128]{2,1,0:T(8,128)S(1)}, f32[9,8,128]{2,1,0:T(8,128)S(1)}, u32[]{:S(2)}, u32[]{:S(2)}) collective-permute-start(f32[9,8,128]{2,1,0:T(8,128)S(1)} %pack.1.refs_0_), channel_id=1, source_target_pairs={{0,16},{8,24},{16,0},{24,8},{1,17},{9,25},{17,1},{25,9},{2,18},{10... | collective-permute-start | bytes 110600 | tf_op jit(solution)/shard_map/ppermute | solution.py:34
  4.6 0.0 collective-permute-start.7
  4.6 0.2 collective-permute-start.8
  4.8 1.7 %collective-permute-done.6.refs_1_ = f32[9,8,128]{2,1,0:T(8,128)S(1)} collective-permute-done((f32[9,8,128]{2,1,0:T(8,128)S(1)}, f32[9,8,128]{2,1,0:T(8,128)S(1)}, u32[]{:S(2)}, u32[]{:S(2)}) %collective-permute-start.6) | collective-permute-done | bytes 36896 | tf_op jit(solution)/shard_map/ppermute | solution.py:34
  6.6 1.6 %collective-permute-done.7.refs_2_ = f32[9,8,128]{2,1,0:T(8,128)S(1)} collective-permute-done((f32[9,8,128]{2,1,0:T(8,128)S(1)}, f32[9,8,128]{2,1,0:T(8,128)S(1)}, u32[]{:S(2)}, u32[]{:S(2)}) %collective-permute-start.7) | collective-permute-done | bytes 36896 | tf_op jit(solution)/shard_map/ppermute | solution.py:34
  8.2 0.0 collective-permute-done.8.refs_3_
  8.2 0.6 %compact.1 = (f32[8,32,128]{2,1,0:T(8,128)S(1)}, f32[8,128]{1,0:T(8,128)S(1)}) custom-call(f32[9,8,128]{2,1,0:T(8,128)S(1)} %pack.1.refs_0_, f32[9,8,128]{2,1,0:T(8,128)S(1)} %collective-permute-done.6.refs_1_, f32[9,8,128]{2,1,0:T(8,128)S(1)} %collective-permute-done.7.refs_2_, f32[9,8,128]{2,1,0:T(8,128)S(1)} %collective-permute-done.8.refs_3_, ...), custom_call_target="tpu_custom_call" | custom-call | tf_op jit(solution)/shard_map/compact/pallas_call | solution.py:264
  8.8 12.9 %all_to_all.10.in_ref = f32[8,32,128]{2,1,0:T(8,128)S(1)} all-to-all(f32[8,32,128]{2,1,0:T(8,128)S(1)} %get-tuple-element.43), channel_id=1, replica_groups=mesh['rows'=4,'cols'=8] {'cols'}, dimensions={0} | all-to-all | bytes 262144 | tf_op jit(solution)/shard_map/all_to_all | solution.py:280
  21.7 0.2 expand.1
  21.9 0.1 collective-permute-start.9
  22.0 0.0 copy-done
  22.0 0.8 %own_stress.3 = (bf16[128,1024]{1,0:T(8,128)(2,1)S(1)}, f32[2,64,128]{2,1,0:T(8,128)S(1)}, f32[2,64,128]{2,1,0:T(8,128)S(1)}) custom-call(f32[8,8,8,128]{3,2,1,0:T(8,128)S(1)} %get-tuple-element.44.dense_ref, f32[8,128,2048]{2,1,0:T(8,128)S(1)} %bitcast.29), custom_call_target="tpu_custom_call" | custom-call | flops 201326592 | bytes 2097152 | tf_op jit(solution)/shard_map/own_stress/pallas_call | solution.py:295
  22.9 0.7 %collective-permute-done.9.dense_ref = f32[8,8,8,128]{3,2,1,0:T(8,128)S(1)} collective-permute-done((f32[8,8,8,128]{3,2,1,0:T(8,128)S(1)}, f32[8,8,8,128]{3,2,1,0:T(8,128)S(1)}, u32[]{:S(2)}, u32[]{:S(2)}) %collective-permute-start.9) | collective-permute-done | bytes 262176 | tf_op jit(solution)/shard_map/ppermute | solution.py:34
  23.5 0.0 copy-start.2
  23.5 0.0 copy-start.3
  23.5 0.0 copy-start.4
  23.5 0.5 %other_stress.3 = (bf16[128,1024]{1,0:T(8,128)(2,1)S(1)}, f32[2,64,128]{2,1,0:T(8,128)S(1)}) custom-call(f32[8,8,8,128]{3,2,1,0:T(8,128)S(1)} %collective-permute-done.9.dense_ref, f32[8,128,2048]{2,1,0:T(8,128)S(1)} %bitcast.30, f32[2,64,128]{2,1,0:T(8,128)S(1)} %get-tuple-element.46.sum_ref), custom_call_target="tpu_custom_call" | custom-call | flops 201326592 | bytes 2097152 | tf_op jit(solution)/shard_map/other_stress/pallas_call | solution.py:295
  24.1 0.5 %rest_stress.3 = f32[2,64,128]{2,1,0:T(8,128)S(1)} custom-call(bf16[128,1024]{1,0:T(8,128)(2,1)S(1)} %get-tuple-element.47.other_ref.slip_ref, f32[8,128,2048]{2,1,0:T(8,128)S(1)} %bitcast.31, f32[2,64,128]{2,1,0:T(8,128)S(1)} %get-tuple-element.51.sum_ref), custom_call_target="tpu_custom_call" | custom-call | flops 201326592 | bytes 2097152 | tf_op jit(solution)/shard_map/rest_stress/pallas_call | solution.py:295
  24.6 0.1 collective-permute-start.13
  24.7 0.0 copy-done.2
  24.7 0.0 copy-done.3
  24.7 0.0 copy-done.4
  24.7 1.3 %collective-permute-start.10 = (f32[2,64,128]{2,1,0:T(8,128)S(1)}, f32[2,64,128]{2,1,0:T(8,128)S(1)}, u32[]{:S(2)}, u32[]{:S(2)}) collective-permute-start(f32[2,64,128]{2,1,0:T(8,128)S(1)} %get-tuple-element.48), channel_id=1, source_target_pairs={{0,1},{1,0},{2,3},{3,2},{4,5},{5,4},{6,7},{7,6},{8,9},{9,8},{10,11... | collective-permute-start | bytes 196616 | tf_op jit(solution)/shard_map/ppermute | solution.py:34
  26.0 0.8 %both_stress.7 = f32[2,64,128]{2,1,0:T(8,128)S(1)} custom-call(bf16[128,1024]{1,0:T(8,128)(2,1)S(1)} %get-tuple-element.45.own_ref, bf16[128,1024]{1,0:T(8,128)(2,1)S(1)} %get-tuple-element.47.other_ref.slip_ref, f32[8,128,2048]{2,1,0:T(8,128)S(1)} %bitcast.32), custom_call_target="tpu_custom_call" | custom-call | flops 201326592 | bytes 2097152 | tf_op jit(solution)/shard_map/both_stress/pallas_call | solution.py:295
  26.8 0.8 %both_stress.6 = f32[2,64,128]{2,1,0:T(8,128)S(1)} custom-call(bf16[128,1024]{1,0:T(8,128)(2,1)S(1)} %get-tuple-element.45.own_ref, bf16[128,1024]{1,0:T(8,128)(2,1)S(1)} %get-tuple-element.47.other_ref.slip_ref, f32[8,128,2048]{2,1,0:T(8,128)S(1)} %bitcast.33), custom_call_target="tpu_custom_call" | custom-call | flops 201326592 | bytes 2097152 | tf_op jit(solution)/shard_map/both_stress/pallas_call | solution.py:295
  27.7 1.2 %collective-permute-done.13 = f32[2,64,128]{2,1,0:T(8,128)S(1)} collective-permute-done((f32[2,64,128]{2,1,0:T(8,128)S(1)}, f32[2,64,128]{2,1,0:T(8,128)S(1)}, u32[]{:S(2)}, u32[]{:S(2)}) %collective-permute-start.13) | collective-permute-done | bytes 65568 | tf_op jit(solution)/shard_map/ppermute | solution.py:34
  28.9 0.3 collective-permute-start.14
  29.2 0.0 collective-permute-done.10
  29.2 1.7 %collective-permute-start.11 = (f32[64,128]{1,0:T(8,128)S(1)}, f32[64,128]{1,0:T(8,128)S(1)}, u32[]{:S(2)}, u32[]{:S(2)}) collective-permute-start(f32[64,128]{1,0:T(8,128)S(1)} %get-tuple-element.63), channel_id=1, source_target_pairs={{0,6},{1,7},{2,4},{3,5},{4,2},{5,3},{6,0},{7,1},{8,14},{9,15},{10,... | collective-permute-start | bytes 98312 | tf_op jit(solution)/shard_map/ppermute | solution.py:34
  30.9 1.6 %collective-permute-start.12 = (f32[64,128]{1,0:T(8,128)S(1)}, f32[64,128]{1,0:T(8,128)S(1)}, u32[]{:S(2)}, u32[]{:S(2)}) collective-permute-start(f32[64,128]{1,0:T(8,128)S(1)} %get-tuple-element.62), channel_id=1, source_target_pairs={{0,4},{1,5},{2,6},{3,7},{4,0},{5,1},{6,2},{7,3},{8,12},{9,13},{10,... | collective-permute-start | bytes 98312 | tf_op jit(solution)/shard_map/ppermute | solution.py:34
  32.6 0.7 %compare_reduce_fusion = pred[]{:T(512)} fusion(f32[8,128]{1,0:T(8,128)S(1)} %get-tuple-element.52), kind=kLoop, calls=%fused_computation.12 | loop fusion | flops 191 | bytes 385 | tf_op jit(solution)/shard_map/reduce_or | solution.py:336
  33.9 1.1 %collective-permute-done.11 = f32[64,128]{1,0:T(8,128)S(1)} collective-permute-done((f32[64,128]{1,0:T(8,128)S(1)}, f32[64,128]{1,0:T(8,128)S(1)}, u32[]{:S(2)}, u32[]{:S(2)}) %collective-permute-start.11) | collective-permute-done | bytes 32800 | tf_op jit(solution)/shard_map/ppermute | solution.py:34
  35.0 0.0 collective-permute-done.14
  35.0 0.8 %collective-permute-done.12 = f32[64,128]{1,0:T(8,128)S(1)} collective-permute-done((f32[64,128]{1,0:T(8,128)S(1)}, f32[64,128]{1,0:T(8,128)S(1)}, u32[]{:S(2)}, u32[]{:S(2)}) %collective-permute-start.12) | collective-permute-done | bytes 32800 | tf_op jit(solution)/shard_map/ppermute | solution.py:34
  35.8 0.7 %add_bitcast_fusion = (f32[128,64]{0,1:T(8,128)}, f32[64,128]{1,0:T(8,128)}) fusion(f32[128]{0:T(128)S(1)} %get-tuple-element.65, f32[128]{0:T(128)S(1)} %copy-done.2, f32[128]{0:T(128)S(1)} %get-tuple-element.64, f32[64,128]{1,0:T(8,128)S(1)} %get-tuple-element.66, f32[2,64,128]{2,1,0:T(8,128)S(1)} %add.43, f32[64,128]{1,0:T(8,128)S(1)} %collective-permute-done.14, ...), kind=kLoop, calls=%fused_computation.11 | loop fusion | flops 65536 | bytes 230912 | tf_op jit(solution)/shard_map/transpose | solution.py:344
  (7 shorter events, 0.1 us)
Async XLA Ops:
  0.6 21.4 %copy-start = (f32[1024,2048]{1,0:T(8,128)S(1)}, f32[1024,2048]{1,0:T(8,128)}, u32[]{:S(2)}) copy-start(f32[1024,2048]{1,0:T(8,128)} %param.9) | copy-start | bytes 25165828
  1.6 5.0 %collective-permute-start.6 = (f32[9,8,128]{2,1,0:T(8,128)S(1)}, f32[9,8,128]{2,1,0:T(8,128)S(1)}, u32[]{:S(2)}, u32[]{:S(2)}) collective-permute-start(f32[9,8,128]{2,1,0:T(8,128)S(1)} %pack.1.refs_0_), channel_id=1, source_target_pairs={{0,16},{8,24},{16,0},{24,8},{1,17},{9,25},{17,1},{25,9},{2,18},{10... | collective-permute-start | bytes 110600 | tf_op jit(solution)/shard_map/ppermute | solution.py:34
  4.6 3.5 %collective-permute-start.7 = (f32[9,8,128]{2,1,0:T(8,128)S(1)}, f32[9,8,128]{2,1,0:T(8,128)S(1)}, u32[]{:S(2)}, u32[]{:S(2)}) collective-permute-start(f32[9,8,128]{2,1,0:T(8,128)S(1)} %pack.1.refs_0_), channel_id=1, source_target_pairs={{0,24},{8,16},{16,8},{24,0},{1,25},{9,17},{17,9},{25,1},{2,26},{10... | collective-permute-start | bytes 110600 | tf_op jit(solution)/shard_map/ppermute | solution.py:34
  4.6 3.5 %collective-permute-start.8 = (f32[9,8,128]{2,1,0:T(8,128)S(1)}, f32[9,8,128]{2,1,0:T(8,128)S(1)}, u32[]{:S(2)}, u32[]{:S(2)}) collective-permute-start(f32[9,8,128]{2,1,0:T(8,128)S(1)} %pack.1.refs_0_), channel_id=1, source_target_pairs={{0,8},{8,0},{16,24},{24,16},{1,9},{9,1},{17,25},{25,17},{2,10},{10... | collective-permute-start | bytes 110600 | tf_op jit(solution)/shard_map/ppermute | solution.py:34
  21.9 1.6 %collective-permute-start.9 = (f32[8,8,8,128]{3,2,1,0:T(8,128)S(1)}, f32[8,8,8,128]{3,2,1,0:T(8,128)S(1)}, u32[]{:S(2)}, u32[]{:S(2)}) collective-permute-start(f32[8,8,8,128]{3,2,1,0:T(8,128)S(1)} %get-tuple-element.44.dense_ref), channel_id=1, source_target_pairs={{0,8},{8,0},{16,24},{24,16},{1,9},{9,1},{17,25},{25,17},{2,10},{10... | collective-permute-start | bytes 786440 | tf_op jit(solution)/shard_map/ppermute | solution.py:34
  23.5 1.1 %copy-start.2 = (f32[128]{0:T(128)S(1)}, f32[128]{0:T(128)}, u32[]{:S(2)}) copy-start(f32[128]{0:T(128)} %param.13) | copy-start | bytes 1540
  23.5 1.1 %copy-start.3 = (f32[128]{0:T(128)S(1)}, f32[128]{0:T(128)}, u32[]{:S(2)}) copy-start(f32[128]{0:T(128)} %param.14) | copy-start | bytes 1540
  23.5 1.1 %copy-start.4 = (f32[128]{0:T(128)S(1)}, f32[128]{0:T(128)}, u32[]{:S(2)}) copy-start(f32[128]{0:T(128)} %param.15) | copy-start | bytes 1540
  24.6 4.3 %collective-permute-start.13 = (f32[2,64,128]{2,1,0:T(8,128)S(1)}, f32[2,64,128]{2,1,0:T(8,128)S(1)}, u32[]{:S(2)}, u32[]{:S(2)}) collective-permute-start(f32[2,64,128]{2,1,0:T(8,128)S(1)} %rest_stress.3), channel_id=1, source_target_pairs={{0,2},{1,3},{2,0},{3,1},{4,6},{5,7},{6,4},{7,5},{8,10},{9,11},{10,... | collective-permute-start | bytes 196616 | tf_op jit(solution)/shard_map/ppermute | solution.py:34
  24.7 4.5 %collective-permute-start.10 = (f32[2,64,128]{2,1,0:T(8,128)S(1)}, f32[2,64,128]{2,1,0:T(8,128)S(1)}, u32[]{:S(2)}, u32[]{:S(2)}) collective-permute-start(f32[2,64,128]{2,1,0:T(8,128)S(1)} %get-tuple-element.48), channel_id=1, source_target_pairs={{0,1},{1,0},{2,3},{3,2},{4,5},{5,4},{6,7},{7,6},{8,9},{9,8},{10,11... | collective-permute-start | bytes 196616 | tf_op jit(solution)/shard_map/ppermute | solution.py:34
  28.9 6.1 %collective-permute-start.14 = (f32[64,128]{1,0:T(8,128)S(1)}, f32[64,128]{1,0:T(8,128)S(1)}, u32[]{:S(2)}, u32[]{:S(2)}) collective-permute-start(f32[64,128]{1,0:T(8,128)S(1)} %slice_bitcast_fusion.5), channel_id=1, source_target_pairs={{0,1},{1,0},{2,3},{3,2},{4,5},{5,4},{6,7},{7,6},{8,9},{9,8},{10,11... | collective-permute-start | bytes 98312 | tf_op jit(solution)/shard_map/ppermute | solution.py:34
  29.2 5.8 %collective-permute-start.11 = (f32[64,128]{1,0:T(8,128)S(1)}, f32[64,128]{1,0:T(8,128)S(1)}, u32[]{:S(2)}, u32[]{:S(2)}) collective-permute-start(f32[64,128]{1,0:T(8,128)S(1)} %get-tuple-element.63), channel_id=1, source_target_pairs={{0,6},{1,7},{2,4},{3,5},{4,2},{5,3},{6,0},{7,1},{8,14},{9,15},{10,... | collective-permute-start | bytes 98312 | tf_op jit(solution)/shard_map/ppermute | solution.py:34
  30.9 4.9 %collective-permute-start.12 = (f32[64,128]{1,0:T(8,128)S(1)}, f32[64,128]{1,0:T(8,128)S(1)}, u32[]{:S(2)}, u32[]{:S(2)}) collective-permute-start(f32[64,128]{1,0:T(8,128)S(1)} %get-tuple-element.62), channel_id=1, source_target_pairs={{0,4},{1,5},{2,6},{3,7},{4,0},{5,1},{6,2},{7,3},{8,12},{9,13},{10,... | collective-permute-start | bytes 98312 | tf_op jit(solution)/shard_map/ppermute | solution.py:34

commit v23 on v22

--- a/solution.py
+++ b/solution.py
@@ -330,7 +330,8 @@
         parts.append(send_xor(near[1], "cols", 1))
         return [*parts, near[0]]
 
-    first, *parts = stress_of(kernel, mine)
+    *parts, first, mine_part = stress_of(kernel, mine)
+    parts.append(mine_part)
     first, left, *blocks_of = lax.optimization_barrier((first, left, *blocks_of))
     parts.append(
         lax.cond(jnp.any(mark[0, STRIDE:] > 0), all_left, lambda *_: jnp.zeros_like(first), kernel, left, *blocks_of)

time: 36.7 us -> 35.1 us (0.956)
  waiting for transfers between devices: 7.07 us -> 5.43 us
    ppermute x9, waiting for transfers between devices: 7.07 us -> 5.43 us  [send_xor(): lax.ppermute(block, axis, [(r, r ^ k) for r in range(lax.axis_size(axis))])]
  transfers between devices with their start and end apart: 9 -> 9, of which waited for: 6 -> 5; matrix products, arithmetic and copies ran while one was open for 2% -> 2% of each run, Pallas kernels for 7% -> 9%
where the time goes in v23:
time: 35.1 us; the launch traced here: 34.9 us
  blocking collectives  12.9 us (37%)
  starting transfers between devices  8.38 us (24%)
  waiting for transfers between devices  5.43 us (15%)
  Pallas kernels  5.3 us (15%)
  between operations  1.43 us (4%)
  other arithmetic  1.4 us (4%)
    all_to_all x1, blocking collectives, per_device(): lax.all_to_all(message, 'cols', 0, 0, tiled=True)  12.9 us
    ppermute x9, starting transfers between devices, send_xor(): lax.ppermute(block, axis, [(r, r ^ k) for r in range(lax.axis_size(axis))])  8.38 us
    ppermute x9, waiting for transfers between devices, send_xor(): lax.ppermute(block, axis, [(r, r ^ k) for r in range(lax.axis_size(axis))])  5.43 us
    pallas_call x5, Pallas kernels, call(): pl.pallas_call(functools.partial(body, targets), out_shape=outs, in_specs...  3.51 us
    pallas_call x1, Pallas kernels, per_device(): pl.pallas_call(pack_body, out_shape=f32(events_here + 1, SUB, BLOCK), in_...  0.96 us
    reduce_or x1, other arithmetic, per_device(): jnp.any(mark[0, STRIDE:] > 0)  0.7 us
  transfers between devices with their start and end apart: 9, of which 5 were waited for; matrix products, arithmetic and copies ran while one was open for 2% of the time, Pallas kernels for 9%

profile of v23, /device:TPU:0, one launch (start us, length us, event | category | flops | bytes accessed | tf_op | source)
XLA Modules:
  0.0 34.9 jit_solution(16516862888153763397)
XLA Ops:
  0.6 0.0 copy-start
  0.6 1.0 %pack.1.refs_0_ = f32[9,8,128]{2,1,0:T(8,128)S(1)} custom-call(f32[8,8,128]{2,1,0:T(8,128)} %slip_hbm.1, s32[8,8]{1,0:T(8,128)} %list_hbm.1, s32[8]{0:T(128)} %count_hbm.1), custom_call_target="tpu_custom_call" | custom-call | tf_op jit(solution)/shard_map/pack/pallas_call | solution.py:243
  1.6 3.0 %collective-permute-start.6 = (f32[9,8,128]{2,1,0:T(8,128)S(1)}, f32[9,8,128]{2,1,0:T(8,128)S(1)}, u32[]{:S(2)}, u32[]{:S(2)}) collective-permute-start(f32[9,8,128]{2,1,0:T(8,128)S(1)} %pack.1.refs_0_), channel_id=1, source_target_pairs={{0,16},{8,24},{16,0},{24,8},{1,17},{9,25},{17,1},{25,9},{2,18},{10... | collective-permute-start | bytes 110600 | tf_op jit(solution)/shard_map/ppermute | solution.py:34
  4.6 0.0 collective-permute-start.7
  4.6 0.2 collective-permute-start.8
  4.8 1.7 %collective-permute-done.6.refs_1_ = f32[9,8,128]{2,1,0:T(8,128)S(1)} collective-permute-done((f32[9,8,128]{2,1,0:T(8,128)S(1)}, f32[9,8,128]{2,1,0:T(8,128)S(1)}, u32[]{:S(2)}, u32[]{:S(2)}) %collective-permute-start.6) | collective-permute-done | bytes 36896 | tf_op jit(solution)/shard_map/ppermute | solution.py:34
  6.6 1.6 %collective-permute-done.7.refs_2_ = f32[9,8,128]{2,1,0:T(8,128)S(1)} collective-permute-done((f32[9,8,128]{2,1,0:T(8,128)S(1)}, f32[9,8,128]{2,1,0:T(8,128)S(1)}, u32[]{:S(2)}, u32[]{:S(2)}) %collective-permute-start.7) | collective-permute-done | bytes 36896 | tf_op jit(solution)/shard_map/ppermute | solution.py:34
  8.2 0.0 collective-permute-done.8.refs_3_
  8.2 0.6 %compact.1 = (f32[8,32,128]{2,1,0:T(8,128)S(1)}, f32[8,128]{1,0:T(8,128)S(1)}) custom-call(f32[9,8,128]{2,1,0:T(8,128)S(1)} %pack.1.refs_0_, f32[9,8,128]{2,1,0:T(8,128)S(1)} %collective-permute-done.6.refs_1_, f32[9,8,128]{2,1,0:T(8,128)S(1)} %collective-permute-done.7.refs_2_, f32[9,8,128]{2,1,0:T(8,128)S(1)} %collective-permute-done.8.refs_3_, ...), custom_call_target="tpu_custom_call" | custom-call | tf_op jit(solution)/shard_map/compact/pallas_call | solution.py:264
  8.8 12.9 %all_to_all.10.in_ref = f32[8,32,128]{2,1,0:T(8,128)S(1)} all-to-all(f32[8,32,128]{2,1,0:T(8,128)S(1)} %get-tuple-element.43), channel_id=1, replica_groups=mesh['rows'=4,'cols'=8] {'cols'}, dimensions={0} | all-to-all | bytes 262144 | tf_op jit(solution)/shard_map/all_to_all | solution.py:280
  21.7 0.2 expand.1
  21.9 0.0 copy-start.2
  22.0 0.0 copy-start.3
  22.0 0.0 copy-start.4
  22.0 0.1 collective-permute-start.9
  22.1 0.0 copy-done
  22.1 0.9 %own_stress.3 = (bf16[128,1024]{1,0:T(8,128)(2,1)S(1)}, f32[2,64,128]{2,1,0:T(8,128)S(1)}, f32[2,64,128]{2,1,0:T(8,128)S(1)}) custom-call(f32[8,8,8,128]{3,2,1,0:T(8,128)S(1)} %get-tuple-element.44.dense_ref, f32[8,128,2048]{2,1,0:T(8,128)S(1)} %bitcast.29), custom_call_target="tpu_custom_call" | custom-call | flops 201326592 | bytes 2097152 | tf_op jit(solution)/shard_map/own_stress/pallas_call | solution.py:295
  22.9 0.6 %collective-permute-done.9.dense_ref = f32[8,8,8,128]{3,2,1,0:T(8,128)S(1)} collective-permute-done((f32[8,8,8,128]{3,2,1,0:T(8,128)S(1)}, f32[8,8,8,128]{3,2,1,0:T(8,128)S(1)}, u32[]{:S(2)}, u32[]{:S(2)}) %collective-permute-start.9) | collective-permute-done | bytes 262176 | tf_op jit(solution)/shard_map/ppermute | solution.py:34
  23.6 0.5 %other_stress.3 = (bf16[128,1024]{1,0:T(8,128)(2,1)S(1)}, f32[2,64,128]{2,1,0:T(8,128)S(1)}) custom-call(f32[8,8,8,128]{3,2,1,0:T(8,128)S(1)} %collective-permute-done.9.dense_ref, f32[8,128,2048]{2,1,0:T(8,128)S(1)} %bitcast.30, f32[2,64,128]{2,1,0:T(8,128)S(1)} %get-tuple-element.46.sum_ref), custom_call_target="tpu_custom_call" | custom-call | flops 201326592 | bytes 2097152 | tf_op jit(solution)/shard_map/other_stress/pallas_call | solution.py:295
  24.1 0.3 collective-permute-start.12
  24.4 0.0 copy-done.2
  24.4 0.0 copy-done.3
  24.4 0.0 copy-done.4
  24.4 0.5 %rest_stress.3 = f32[2,64,128]{2,1,0:T(8,128)S(1)} custom-call(bf16[128,1024]{1,0:T(8,128)(2,1)S(1)} %get-tuple-element.47.other_ref.slip_ref, f32[8,128,2048]{2,1,0:T(8,128)S(1)} %bitcast.31, f32[2,64,128]{2,1,0:T(8,128)S(1)} %get-tuple-element.48.sum_ref), custom_call_target="tpu_custom_call" | custom-call | flops 201326592 | bytes 2097152 | tf_op jit(solution)/shard_map/rest_stress/pallas_call | solution.py:295
  24.9 1.2 %collective-permute-start.10 = (f32[2,64,128]{2,1,0:T(8,128)S(1)}, f32[2,64,128]{2,1,0:T(8,128)S(1)}, u32[]{:S(2)}, u32[]{:S(2)}) collective-permute-start(f32[2,64,128]{2,1,0:T(8,128)S(1)} %rest_stress.3), channel_id=1, source_target_pairs={{0,2},{1,3},{2,0},{3,1},{4,6},{5,7},{6,4},{7,5},{8,10},{9,11},{10,... | collective-permute-start | bytes 196616 | tf_op jit(solution)/shard_map/ppermute | solution.py:34
  26.1 0.8 %both_stress.7 = f32[2,64,128]{2,1,0:T(8,128)S(1)} custom-call(bf16[128,1024]{1,0:T(8,128)(2,1)S(1)} %get-tuple-element.45.own_ref, bf16[128,1024]{1,0:T(8,128)(2,1)S(1)} %get-tuple-element.47.other_ref.slip_ref, f32[8,128,2048]{2,1,0:T(8,128)S(1)} %bitcast.32), custom_call_target="tpu_custom_call" | custom-call | flops 201326592 | bytes 2097152 | tf_op jit(solution)/shard_map/both_stress/pallas_call | solution.py:295
  26.9 0.8 %both_stress.6 = f32[2,64,128]{2,1,0:T(8,128)S(1)} custom-call(bf16[128,1024]{1,0:T(8,128)(2,1)S(1)} %get-tuple-element.45.own_ref, bf16[128,1024]{1,0:T(8,128)(2,1)S(1)} %get-tuple-element.47.other_ref.slip_ref, f32[8,128,2048]{2,1,0:T(8,128)S(1)} %bitcast.33), custom_call_target="tpu_custom_call" | custom-call | flops 201326592 | bytes 2097152 | tf_op jit(solution)/shard_map/both_stress/pallas_call | solution.py:295
  27.7 0.7 %collective-permute-done.12 = f32[2,64,128]{2,1,0:T(8,128)S(1)} collective-permute-done((f32[2,64,128]{2,1,0:T(8,128)S(1)}, f32[2,64,128]{2,1,0:T(8,128)S(1)}, u32[]{:S(2)}, u32[]{:S(2)}) %collective-permute-start.12) | collective-permute-done | bytes 65568 | tf_op jit(solution)/shard_map/ppermute | solution.py:34
  28.4 0.6 %collective-permute-start.13 = (f32[64,128]{1,0:T(8,128)S(1)}, f32[64,128]{1,0:T(8,128)S(1)}, u32[]{:S(2)}, u32[]{:S(2)}) collective-permute-start(f32[64,128]{1,0:T(8,128)S(1)} %get-tuple-element.62), channel_id=1, source_target_pairs={{0,6},{1,7},{2,4},{3,5},{4,2},{5,3},{6,0},{7,1},{8,14},{9,15},{10,... | collective-permute-start | bytes 98312 | tf_op jit(solution)/shard_map/ppermute | solution.py:34
  29.1 1.1 %collective-permute-start.14 = (f32[64,128]{1,0:T(8,128)S(1)}, f32[64,128]{1,0:T(8,128)S(1)}, u32[]{:S(2)}, u32[]{:S(2)}) collective-permute-start(f32[64,128]{1,0:T(8,128)S(1)} %get-tuple-element.63), channel_id=1, source_target_pairs={{0,4},{1,5},{2,6},{3,7},{4,0},{5,1},{6,2},{7,3},{8,12},{9,13},{10,... | collective-permute-start | bytes 98312 | tf_op jit(solution)/shard_map/ppermute | solution.py:34
  30.2 0.0 collective-permute-done.10
  30.2 1.9 %collective-permute-start.11 = (f32[64,128]{1,0:T(8,128)S(1)}, f32[64,128]{1,0:T(8,128)S(1)}, u32[]{:S(2)}, u32[]{:S(2)}) collective-permute-start(f32[64,128]{1,0:T(8,128)S(1)} %slice_bitcast_fusion.7), channel_id=1, source_target_pairs={{0,1},{1,0},{2,3},{3,2},{4,5},{5,4},{6,7},{7,6},{8,9},{9,8},{10,11... | collective-permute-start | bytes 98312 | tf_op jit(solution)/shard_map/ppermute | solution.py:34
  32.1 0.7 %compare_reduce_fusion = pred[]{:T(512)} fusion(f32[8,128]{1,0:T(8,128)S(1)} %get-tuple-element.52), kind=kLoop, calls=%fused_computation.12 | loop fusion | flops 191 | bytes 385 | tf_op jit(solution)/shard_map/reduce_or | solution.py:337
  33.5 0.7 %collective-permute-done.11 = f32[64,128]{1,0:T(8,128)S(1)} collective-permute-done((f32[64,128]{1,0:T(8,128)S(1)}, f32[64,128]{1,0:T(8,128)S(1)}, u32[]{:S(2)}, u32[]{:S(2)}) %collective-permute-start.11) | collective-permute-done | bytes 32800 | tf_op jit(solution)/shard_map/ppermute | solution.py:34
  34.2 0.0 collective-permute-done.13
  34.2 0.0 collective-permute-done.14
  34.2 0.7 %add_bitcast_fusion = (f32[128,64]{0,1:T(8,128)}, f32[64,128]{1,0:T(8,128)}) fusion(f32[128]{0:T(128)S(1)} %get-tuple-element.65, f32[128]{0:T(128)S(1)} %copy-done.2, f32[128]{0:T(128)S(1)} %get-tuple-element.64, f32[64,128]{1,0:T(8,128)S(1)} %get-tuple-element.66, f32[2,64,128]{2,1,0:T(8,128)S(1)} %add.41, f32[64,128]{1,0:T(8,128)S(1)} %collective-permute-done.14, ...), kind=kLoop, calls=%fused_computation.11 | loop fusion | flops 65536 | bytes 230912 | tf_op jit(solution)/shard_map/transpose | solution.py:345
  (7 shorter events, 0.0 us)
Async XLA Ops:
  0.6 21.4 %copy-start = (f32[1024,2048]{1,0:T(8,128)S(1)}, f32[1024,2048]{1,0:T(8,128)}, u32[]{:S(2)}) copy-start(f32[1024,2048]{1,0:T(8,128)} %param.9) | copy-start | bytes 25165828
  1.6 5.0 %collective-permute-start.6 = (f32[9,8,128]{2,1,0:T(8,128)S(1)}, f32[9,8,128]{2,1,0:T(8,128)S(1)}, u32[]{:S(2)}, u32[]{:S(2)}) collective-permute-start(f32[9,8,128]{2,1,0:T(8,128)S(1)} %pack.1.refs_0_), channel_id=1, source_target_pairs={{0,16},{8,24},{16,0},{24,8},{1,17},{9,25},{17,1},{25,9},{2,18},{10... | collective-permute-start | bytes 110600 | tf_op jit(solution)/shard_map/ppermute | solution.py:34
  4.6 3.5 %collective-permute-start.7 = (f32[9,8,128]{2,1,0:T(8,128)S(1)}, f32[9,8,128]{2,1,0:T(8,128)S(1)}, u32[]{:S(2)}, u32[]{:S(2)}) collective-permute-start(f32[9,8,128]{2,1,0:T(8,128)S(1)} %pack.1.refs_0_), channel_id=1, source_target_pairs={{0,24},{8,16},{16,8},{24,0},{1,25},{9,17},{17,9},{25,1},{2,26},{10... | collective-permute-start | bytes 110600 | tf_op jit(solution)/shard_map/ppermute | solution.py:34
  4.6 3.5 %collective-permute-start.8 = (f32[9,8,128]{2,1,0:T(8,128)S(1)}, f32[9,8,128]{2,1,0:T(8,128)S(1)}, u32[]{:S(2)}, u32[]{:S(2)}) collective-permute-start(f32[9,8,128]{2,1,0:T(8,128)S(1)} %pack.1.refs_0_), channel_id=1, source_target_pairs={{0,8},{8,0},{16,24},{24,16},{1,9},{9,1},{17,25},{25,17},{2,10},{10... | collective-permute-start | bytes 110600 | tf_op jit(solution)/shard_map/ppermute | solution.py:34
  21.9 2.4 %copy-start.2 = (f32[128]{0:T(128)S(1)}, f32[128]{0:T(128)}, u32[]{:S(2)}) copy-start(f32[128]{0:T(128)} %param.13) | copy-start | bytes 1540
  22.0 2.4 %copy-start.3 = (f32[128]{0:T(128)S(1)}, f32[128]{0:T(128)}, u32[]{:S(2)}) copy-start(f32[128]{0:T(128)} %param.14) | copy-start | bytes 1540
  22.0 2.4 %copy-start.4 = (f32[128]{0:T(128)S(1)}, f32[128]{0:T(128)}, u32[]{:S(2)}) copy-start(f32[128]{0:T(128)} %param.15) | copy-start | bytes 1540
  22.0 1.6 %collective-permute-start.9 = (f32[8,8,8,128]{3,2,1,0:T(8,128)S(1)}, f32[8,8,8,128]{3,2,1,0:T(8,128)S(1)}, u32[]{:S(2)}, u32[]{:S(2)}) collective-permute-start(f32[8,8,8,128]{3,2,1,0:T(8,128)S(1)} %get-tuple-element.44.dense_ref), channel_id=1, source_target_pairs={{0,8},{8,0},{16,24},{24,16},{1,9},{9,1},{17,25},{25,17},{2,10},{10... | collective-permute-start | bytes 786440 | tf_op jit(solution)/shard_map/ppermute | solution.py:34
  24.1 4.3 %collective-permute-start.12 = (f32[2,64,128]{2,1,0:T(8,128)S(1)}, f32[2,64,128]{2,1,0:T(8,128)S(1)}, u32[]{:S(2)}, u32[]{:S(2)}) collective-permute-start(f32[2,64,128]{2,1,0:T(8,128)S(1)} %get-tuple-element.51), channel_id=1, source_target_pairs={{0,1},{1,0},{2,3},{3,2},{4,5},{5,4},{6,7},{7,6},{8,9},{9,8},{10,11... | collective-permute-start | bytes 196616 | tf_op jit(solution)/shard_map/ppermute | solution.py:34
  24.9 5.3 %collective-permute-start.10 = (f32[2,64,128]{2,1,0:T(8,128)S(1)}, f32[2,64,128]{2,1,0:T(8,128)S(1)}, u32[]{:S(2)}, u32[]{:S(2)}) collective-permute-start(f32[2,64,128]{2,1,0:T(8,128)S(1)} %rest_stress.3), channel_id=1, source_target_pairs={{0,2},{1,3},{2,0},{3,1},{4,6},{5,7},{6,4},{7,5},{8,10},{9,11},{10,... | collective-permute-start | bytes 196616 | tf_op jit(solution)/shard_map/ppermute | solution.py:34
  28.4 5.8 %collective-permute-start.13 = (f32[64,128]{1,0:T(8,128)S(1)}, f32[64,128]{1,0:T(8,128)S(1)}, u32[]{:S(2)}, u32[]{:S(2)}) collective-permute-start(f32[64,128]{1,0:T(8,128)S(1)} %get-tuple-element.62), channel_id=1, source_target_pairs={{0,6},{1,7},{2,4},{3,5},{4,2},{5,3},{6,0},{7,1},{8,14},{9,15},{10,... | collective-permute-start | bytes 98312 | tf_op jit(solution)/shard_map/ppermute | solution.py:34
  29.1 5.2 %collective-permute-start.14 = (f32[64,128]{1,0:T(8,128)S(1)}, f32[64,128]{1,0:T(8,128)S(1)}, u32[]{:S(2)}, u32[]{:S(2)}) collective-permute-start(f32[64,128]{1,0:T(8,128)S(1)} %get-tuple-element.63), channel_id=1, source_target_pairs={{0,4},{1,5},{2,6},{3,7},{4,0},{5,1},{6,2},{7,3},{8,12},{9,13},{10,... | collective-permute-start | bytes 98312 | tf_op jit(solution)/shard_map/ppermute | solution.py:34
  30.2 4.0 %collective-permute-start.11 = (f32[64,128]{1,0:T(8,128)S(1)}, f32[64,128]{1,0:T(8,128)S(1)}, u32[]{:S(2)}, u32[]{:S(2)}) collective-permute-start(f32[64,128]{1,0:T(8,128)S(1)} %slice_bitcast_fusion.7), channel_id=1, source_target_pairs={{0,1},{1,0},{2,3},{3,2},{4,5},{5,4},{6,7},{7,6},{8,9},{9,8},{10,11... | collective-permute-start | bytes 98312 | tf_op jit(solution)/shard_map/ppermute | solution.py:34

commit v24 on v19

--- a/solution.py
+++ b/solution.py
@@ -10,6 +10,8 @@
 BLOCK = 128
 SUB = 8
 CHUNK = 256
+SLOTS = 15
+STRIDE = 16
 VMEM_SPEC = pl.BlockSpec(memory_space=pltpu.VMEM)
 HBM_SPEC = pl.BlockSpec(memory_space=pltpu.HBM)
 MIB = 1024 * 1024
@@ -32,9 +34,11 @@
     return lax.ppermute(block, axis, [(r, r ^ k) for r in range(lax.axis_size(axis))])
 
 
-def pack_body(slip_hbm, list_hbm, count_hbm, out_ref, list_ref, count_ref, ids, sems):
+def compact_body(
+    width, blocks, slip_hbm, list_hbm, count_hbm, _, out_ref, left_ref, list_ref, count_ref, number, sems
+):
     events, entries = list_ref.shape
-    slips = out_ref.at[pl.ds(0, events), pl.ds(0, entries)]
+    slips = left_ref.at[pl.ds(0, events), pl.ds(0, entries)]
     copies = [
         pltpu.make_async_copy(src, dst, sems.at[j])
         for j, (src, dst) in enumerate(((list_hbm, list_ref), (count_hbm, count_ref), (slip_hbm, slips)))
@@ -44,40 +48,125 @@
     row = lax.axis_index("rows")
     entry = lax.broadcasted_iota(jnp.int32, (events, entries), 1) + row * entries
     event = lax.broadcasted_iota(jnp.int32, (events, entries), 0)
-    ids[...] = jnp.full(ids.shape, -1.0, jnp.float32)
+    number[...] = jnp.full(number.shape, -1.0, jnp.float32)
+    pieces = 2 * width
+    rows = pieces * SUB
+    i, j = (lax.broadcasted_iota(jnp.int32, (BLOCK, BLOCK), d) for d in (0, 1))
+    lanes = jnp.concatenate([i < j, i >= 0], axis=1).astype(jnp.bfloat16)
+    i, j = (lax.broadcasted_iota(jnp.int32, (rows, rows), d) for d in (0, 1))
+    earlier = ((i // SUB == j // SUB) & (j % SUB < i % SUB)).astype(jnp.bfloat16)
     for copy in copies[:2]:
         copy.wait()
     count = jnp.zeros((events, entries), jnp.int32)
     for e in range(events):
         count = jnp.where(event == e, count_ref[e], count)
-    ids[0:events, 0:entries] = jnp.where(entry < count, list_ref[...], -1).astype(jnp.float32)
-    out_ref[events] = pltpu.roll(ids[...], row * entries, 1)
+    number[0:events, 0:entries] = jnp.where(entry < count, list_ref[...], -1).astype(jnp.float32)
+    ids = number[...]
+    member = []
+    for core in range(2):
+        for c in range(width):
+            low = float((2 * c + core) * blocks)
+            member.append(((ids >= low) & (ids < low + blocks)).astype(jnp.float32))
+    member = jnp.concatenate(member, axis=0)
+    within = jnp.dot(member.astype(jnp.bfloat16), lanes, preferred_element_type=jnp.float32)
+    total = within[:, BLOCK:]
+    offset = jnp.dot(earlier, total.astype(jnp.bfloat16), preferred_element_type=jnp.float32)
+    mark = jnp.where(jnp.max(offset + total) > SLOTS, 1.0, 0.0)
+    rank = jnp.where(member > 0, within[:, :BLOCK] + offset, -1.0)
+    left = jnp.zeros(ids.shape, jnp.bool_)
+    for p in range(pieces):
+        left = left | (rank[p * SUB : (p + 1) * SUB] >= SLOTS)
+    left_ref[events] = pltpu.roll(jnp.where(left, ids, -1.0), row * entries, 1)
+
+    lane = lax.broadcasted_iota(jnp.int32, (1, BLOCK), 1) // entries
+
+    def line_of(tile):
+        line = jnp.full((1, BLOCK), -1.0, jnp.float32)
+        for e in range(events):
+            part = pltpu.roll(tile[e : e + 1], e * entries, 1) if e else tile[0:1]
+            line = jnp.where(lane == e, part, line)
+        return line
+
+    known = jnp.maximum(ids, 0.0)
+    code = known - jnp.floor(known / blocks) * blocks + 1.0
+    code += (lax.broadcasted_iota(jnp.int32, ids.shape, 0) * blocks).astype(jnp.float32)
+    codes = jnp.broadcast_to(line_of(code), (SUB, BLOCK)).astype(jnp.bfloat16)
+    slot = lax.broadcasted_iota(jnp.int32, (STRIDE, BLOCK), 0).astype(jnp.float32)
+    picks = []
+    for p in range(pieces):
+        line = line_of(rank[p * SUB : (p + 1) * SUB])
+        line = jnp.where(line < SLOTS, line, -1.0)
+        picks.append((slot == jnp.broadcast_to(line, slot.shape)).astype(jnp.bfloat16))
+    pick = jnp.concatenate(picks, axis=0)
+    numbers = lax.dot_general(codes, pick, NT, preferred_element_type=jnp.float32)
     copies[2].wait()
-
-
-def densify_body(entries, sources, *refs):
-    ins, (_, out_ref, slips) = refs[:-3], refs[-3:]
-    events = ins[0].shape[0] - 1
-    width, _, blocks, _ = out_ref.shape
-    live = len(ins) * entries
+    slip = jnp.concatenate([left_ref[e, 0:entries, :] for e in range(events)], axis=0)
+    hi = slip.astype(jnp.bfloat16)
+    lo = (slip - hi.astype(jnp.float32)).astype(jnp.bfloat16)
+    size = events * entries
+    data = jnp.dot(pick[:, :size], hi, preferred_element_type=jnp.float32)
+    data += jnp.dot(pick[:, :size], lo, preferred_element_type=jnp.float32)
+    last = lax.broadcasted_iota(jnp.int32, (STRIDE, BLOCK), 0) == SLOTS
+    lane = lax.broadcasted_iota(jnp.int32, (1, BLOCK), 1)
+    for p in range(pieces):
+        start = p * STRIDE // BLOCK * BLOCK
+        tile = numbers[0:1, start : start + BLOCK]
+        shift = p * STRIDE - start
+        tile = pltpu.roll(tile, BLOCK - shift, 1) if shift else tile
+        tile = jnp.broadcast_to(jnp.where(lane < STRIDE, tile, mark), (STRIDE, BLOCK))
+        piece = jnp.where(last, tile, data[p * STRIDE : (p + 1) * STRIDE])
+        for other in range(out_ref.shape[0] // pieces):
+            out_ref[other * pieces + p] = piece
+
+
+def expand_body(in_ref, out_ref, mark_ref):
+    width, events, blocks, _ = out_ref.shape
+    height = in_ref.shape[0] // width
+    lane = lax.broadcasted_iota(jnp.int32, (1, BLOCK), 1)
+    mark = jnp.zeros((1, BLOCK), jnp.float32)
+    for c in range(width):
+        numbers = jnp.zeros((1, BLOCK), jnp.float32)
+        slip = []
+        for r in range(height):
+            piece = in_ref[r * width + c]
+            info = piece[SLOTS : SLOTS + 1, :]
+            mark = jnp.maximum(mark, jnp.where(lane >= STRIDE, info, 0.0))
+            info = pltpu.roll(info, r * STRIDE, 1) if r else info
+            numbers = jnp.where(lane // STRIDE == r, info, numbers)
+            slip.append(piece)
+        slip = jnp.concatenate(slip, axis=0)
+        numbers = jnp.broadcast_to(numbers, (events * blocks, BLOCK))[:, : height * STRIDE]
+        place = lax.broadcasted_iota(jnp.int32, numbers.shape, 0).astype(jnp.float32) + 1.0
+        pick = (numbers == place).astype(jnp.bfloat16)
+        hi = slip.astype(jnp.bfloat16)
+        lo = (slip - hi.astype(jnp.float32)).astype(jnp.bfloat16)
+        total = jnp.dot(pick, hi, preferred_element_type=jnp.float32)
+        total += jnp.dot(pick, lo, preferred_element_type=jnp.float32)
+        out_ref[c] = total.reshape(events, blocks, BLOCK)
+    mark_ref[...] = jnp.broadcast_to(mark, mark_ref.shape)
+
+
+def densify_body(sources, *refs):
+    ins, (out_ref, slips) = refs[:-2], refs[-2:]
+    width, events, blocks, _ = out_ref.shape
+    live = slips.shape[1]
+    entries = live // len(ins)
     row = lax.axis_index("rows")
     line = lax.broadcasted_iota(jnp.int32, (width * blocks, live), 0)
     number = ((line // blocks * 2 + row % 2) * blocks + line % blocks).astype(jnp.float32)
     for e in range(events):
         ids = jnp.full((1, BLOCK), -1.0, jnp.float32)
-        for ref in ins:
+        for k, ref in zip(sources, ins):
             ids = jnp.maximum(ids, ref[events, e : e + 1, :])
+            where = pl.ds(pl.multiple_of((row ^ k) * entries, entries), entries)
+            slips[e, where, :] = ref[e, 0:entries, :]
         ids = jnp.broadcast_to(ids, (width * blocks, BLOCK))[:, :live]
         onehot = (ids == number).astype(jnp.bfloat16)
-        for k, ref in zip(sources, ins):
-            where = pl.ds(pl.multiple_of((row ^ k) * entries, entries), entries)
-            slips[e, where, :] = ref[e, 0:entries, :]
         slip = slips[e]
-        total = jnp.zeros((width * blocks, BLOCK), jnp.float32)
-        for _ in range(3):
-            piece = slip.astype(jnp.bfloat16)
-            slip = slip - piece.astype(jnp.float32)
-            total = total + jnp.dot(onehot, piece, preferred_element_type=jnp.float32)
+        hi = slip.astype(jnp.bfloat16)
+        lo = (slip - hi.astype(jnp.float32)).astype(jnp.bfloat16)
+        total = jnp.dot(onehot, hi, preferred_element_type=jnp.float32)
+        total += jnp.dot(onehot, lo, preferred_element_type=jnp.float32)
         out_ref[:, e] = total.reshape(width, blocks, BLOCK)
 
 
@@ -144,33 +233,42 @@
     near_keep, near_send = [0, 1], list(range(2, width // 2))
     in_hbm = functools.partial(pltpu.with_memory_space_constraint, memory_space=pltpu.HBM)
     kernel = kernel.reshape(width, share, sources)
-    packed = pl.pallas_call(
-        pack_body,
-        out_shape=f32(events_here + 1, SUB, BLOCK),
-        in_specs=[HBM_SPEC] * 3,
-        out_specs=VMEM_SPEC,
+    blocks_half = blocks_here // 2
+    message, left = pl.pallas_call(
+        functools.partial(compact_body, width, blocks_half),
+        out_shape=[f32(height * width, STRIDE, BLOCK), f32(events_here + 1, SUB, BLOCK)],
+        in_specs=[HBM_SPEC] * 4,
+        out_specs=[VMEM_SPEC] * 2,
         scratch_shapes=[
             pltpu.VMEM(block_list.shape, jnp.int32),
             pltpu.SMEM(live_count.shape, jnp.int32),
             pltpu.VMEM((SUB, BLOCK), jnp.float32),
             pltpu.SemaphoreType.DMA((3,)),
         ],
-        compiler_params=params(4),
-        name="pack",
-    )(in_hbm(slip_delta), in_hbm(block_list), in_hbm(live_count))
-    others = sorted(range(1, height), key=lambda k: (k < 2, k))
-    came = [send_xor(packed, "rows", k) for k in others]
-    blocks_half = blocks_here // 2
-    dense = pl.pallas_call(
-        functools.partial(densify_body, entries, [0] + others),
-        out_shape=f32(width, events_here, blocks_half, BLOCK),
-        in_specs=[VMEM_SPEC] * height + [HBM_SPEC],
-        out_specs=VMEM_SPEC,
-        scratch_shapes=[pltpu.VMEM((events_here, height * entries, BLOCK), jnp.float32)],
-        compiler_params=params(8),
-        name="densify",
-    )(packed, *came, in_hbm(kernel))
-    mine = lax.all_to_all(dense, "cols", 0, 0, tiled=True)
+        compiler_params=params(16),
+        name="compact",
+    )(in_hbm(slip_delta), in_hbm(block_list), in_hbm(live_count), in_hbm(kernel))
+    mine, mark = pl.pallas_call(
+        expand_body,
+        out_shape=[f32(width, events_here, blocks_half, BLOCK), f32(SUB, BLOCK)],
+        in_specs=[VMEM_SPEC],
+        out_specs=[VMEM_SPEC] * 2,
+        compiler_params=params(16),
+        name="expand",
+    )(lax.all_to_all(message, ("rows", "cols"), 0, 0, tiled=True))
+
+    def all_left(kernel, left):
+        others = sorted(range(1, height), key=lambda k: (k < 2, k))
+        dense = pl.pallas_call(
+            functools.partial(densify_body, [0] + others),
+            out_shape=f32(width, events_here, blocks_half, BLOCK),
+            in_specs=[VMEM_SPEC] * height,
+            out_specs=VMEM_SPEC,
+            scratch_shapes=[pltpu.VMEM((events_here, height * entries, BLOCK), jnp.float32)],
+            compiler_params=params(8),
+            name="densify",
+        )(left, *(send_xor(left, "rows", k) for k in others))
+        return sum(stress_of(kernel, lax.all_to_all(dense, "cols", 0, 0, tiled=True)))
 
     def call(body, targets, outs, *args):
         return pl.pallas_call(
@@ -178,7 +276,7 @@
             out_shape=outs,
             in_specs=[VMEM_SPEC] * len(args),
             out_specs=jax.tree.map(lambda _: VMEM_SPEC, outs),
-            compiler_params=params(8),
+            compiler_params=params(24),
             cost_estimate=pl.CostEstimate(
                 flops=3 * receivers * sources * events // 2,
                 bytes_accessed=receivers * sources,
@@ -192,23 +290,30 @@
     def sums(targets):
         return f32(len(targets), events, share)
 
-    came = send_xor(mine, "rows", 1)
-    own, far_own, near_own = call(
-        own_body, (far_send, near_send), [slips, sums(far_send), sums(near_send)], mine, kernel
-    )
-    other, far_sent = call(other_body, far_send, [slips, sums(far_send)], came, kernel, far_own)
-    near_sent = call(rest_body, near_send, sums(near_send), other, kernel, near_own)
-
-    def later(targets):
-        return call(both_body, targets, sums(targets), own, other, kernel)
-
-    far_came = send_xor(far_sent, "cols", 1)
-    near_came = [send_xor(near_sent[j : j + 2], "cols", near_send[j]) for j in range(0, len(near_send), 2)]
-    far = later(far_keep) + far_came
-    near = sum(near_came, later(near_keep))
-    parts = [send_xor(far[j], "cols", k) for j, k in reversed(list(enumerate(far_keep)))]
-    parts.append(send_xor(near[1], "cols", 1))
-    stress_change = sum(parts, near[0])
+    def stress_of(kernel, mine):
+        came = send_xor(mine, "rows", 1)
+        own, far_own, near_own = call(
+            own_body, (far_send, near_send), [slips, sums(far_send), sums(near_send)], mine, kernel
+        )
+        other, far_sent = call(other_body, far_send, [slips, sums(far_send)], came, kernel, far_own)
+        near_sent = call(rest_body, near_send, sums(near_send), other, kernel, near_own)
+
+        def later(targets):
+            return call(both_body, targets, sums(targets), own, other, kernel)
+
+        far_came = send_xor(far_sent, "cols", 1)
+        near_came = [send_xor(near_sent[j : j + 2], "cols", near_send[j]) for j in range(0, len(near_send), 2)]
+        far = later(far_keep) + far_came
+        near = sum(near_came, later(near_keep))
+        parts = [send_xor(far[j], "cols", k) for j, k in reversed(list(enumerate(far_keep)))]
+        parts.append(send_xor(near[1], "cols", 1))
+        return [*parts, near[0]]
+
+    *parts, first, mine_part = stress_of(kernel, mine)
+    parts.append(mine_part)
+    first, left = lax.optimization_barrier((first, left))
+    parts.append(lax.cond(jnp.any(mark[0, STRIDE:] > 0), all_left, lambda *_: jnp.zeros_like(first), kernel, left))
+    stress_change = sum(parts, first)
     scale = direct_effect[None, :]
     growth = jnp.expm1(load_rate * time_before / direct_effect)[None, :]
     log_time = jnp.log(scale / load_rate[None, :]) + jnp.log(

time: 37.2 us -> 34.3 us (0.922)
  waiting for transfers between devices: 7.86 us -> 3.17 us
  starting transfers between devices: 8.45 us -> 4.88 us
  blocking collectives: 14.5 us -> 17.8 us
  Pallas kernels: 4.68 us -> 5.45 us
  other arithmetic: 0.69 us -> 1.39 us
  between operations: 0.73 us -> 1.43 us
    ppermute x9 -> x6, waiting for transfers between devices: 7.86 us -> 3.17 us  [send_xor(): lax.ppermute(block, axis, [(r, r ^ k) for r in range(lax.axis_size(axis))])]
    ppermute x9 -> x6, starting transfers between devices: 8.45 us -> 4.88 us  [send_xor(): lax.ppermute(block, axis, [(r, r ^ k) for r in range(lax.axis_size(axis))])]
    all_to_all x1, blocking collectives: 14.5 us -> 17.8 us  [per_device(): lax.all_to_all(message, ('rows', 'cols'), 0, 0, tiled=True)]
    pallas_call x2, Pallas kernels: 1.22 us -> 1.93 us  [the longest x1 1.65 us: per_device(): pl.pallas_call(functools.partial(compact_body, width, blocks_half), out_s...]
    reduce_or x0 -> x1, other arithmetic: none -> 0.7 us  [per_device(): jnp.any(mark[0, STRIDE:] > 0)]
  transfers between devices with their start and end apart: 9 -> 6, of which waited for: 7 -> 3; matrix products, arithmetic and copies ran while one was open for 0% -> 2% of each run, Pallas kernels for 8% -> 9%
where the time goes in v24:
time: 34.3 us; the launch traced here: 34.1 us
  blocking collectives  17.8 us (52%)
  Pallas kernels  5.45 us (16%)
  starting transfers between devices  4.88 us (14%)
  waiting for transfers between devices  3.17 us (9%)
  between operations  1.43 us (4%)
  other arithmetic  1.39 us (4%)
    all_to_all x1, blocking collectives, per_device(): lax.all_to_all(message, ('rows', 'cols'), 0, 0, tiled=True)  17.8 us
    ppermute x6, starting transfers between devices, send_xor(): lax.ppermute(block, axis, [(r, r ^ k) for r in range(lax.axis_size(axis))])  4.88 us
    pallas_call x5, Pallas kernels, call(): pl.pallas_call(functools.partial(body, targets), out_shape=outs, in_specs...  3.52 us
    ppermute x6, waiting for transfers between devices, send_xor(): lax.ppermute(block, axis, [(r, r ^ k) for r in range(lax.axis_size(axis))])  3.17 us
    pallas_call x1, Pallas kernels, per_device(): pl.pallas_call(functools.partial(compact_body, width, blocks_half), out_s...  1.65 us
    reduce_or x1, other arithmetic, per_device(): jnp.any(mark[0, STRIDE:] > 0)  0.7 us
  transfers between devices with their start and end apart: 6, of which 3 were waited for; matrix products, arithmetic and copies ran while one was open for 2% of the time, Pallas kernels for 9%

profile of v24, /device:TPU:0, one launch (start us, length us, event | category | flops | bytes accessed | tf_op | source)
XLA Modules:
  0.0 34.1 jit_solution(3556628836269233863)
XLA Ops:
  0.6 0.0 copy-start
  0.6 1.7 %compact.1 = (f32[32,16,128]{2,1,0:T(8,128)S(1)}, f32[9,8,128]{2,1,0:T(8,128)S(1)}) custom-call(f32[8,8,128]{2,1,0:T(8,128)} %slip_hbm.1, s32[8,8]{1,0:T(8,128)} %list_hbm.1, s32[8]{0:T(128)} %count_hbm.1, f32[8,128,2048]{2,1,0:T(8,128)} %bitcast.27), custom_call_target="tpu_custom_call" | custom-call | tf_op jit(solution)/shard_map/compact/pallas_call | solution.py:237
  2.3 17.8 %all_to_all.10.in_ref = f32[32,16,128]{2,1,0:T(8,128)S(1)} all-to-all(f32[32,16,128]{2,1,0:T(8,128)S(1)} %get-tuple-element.27), channel_id=1, replica_groups=mesh['rows'=4,'cols'=8] {'rows','cols'}, dimensions={0} | all-to-all | bytes 524288 | tf_op jit(solution)/shard_map/all_to_all | solution.py:258
  20.1 0.3 expand.1
  20.3 0.0 copy-start.2
  20.4 0.0 copy-start.3
  20.4 0.0 copy-start.4
  20.4 0.1 collective-permute-start.9
  20.5 0.0 copy-done
  20.5 0.9 %own_stress.3 = (bf16[128,1024]{1,0:T(8,128)(2,1)S(1)}, f32[2,64,128]{2,1,0:T(8,128)S(1)}, f32[2,64,128]{2,1,0:T(8,128)S(1)}) custom-call(f32[8,8,8,128]{3,2,1,0:T(8,128)S(1)} %get-tuple-element.28.dense_ref, f32[8,128,2048]{2,1,0:T(8,128)S(1)} %bitcast.29), custom_call_target="tpu_custom_call" | custom-call | flops 201326592 | bytes 2097152 | tf_op jit(solution)/shard_map/own_stress/pallas_call | solution.py:274
  21.3 0.6 %collective-permute-done.9.dense_ref = f32[8,8,8,128]{3,2,1,0:T(8,128)S(1)} collective-permute-done((f32[8,8,8,128]{3,2,1,0:T(8,128)S(1)}, f32[8,8,8,128]{3,2,1,0:T(8,128)S(1)}, u32[]{:S(2)}, u32[]{:S(2)}) %collective-permute-start.9) | collective-permute-done | bytes 262176 | tf_op jit(solution)/shard_map/ppermute | solution.py:34
  22.0 0.5 %other_stress.3 = (bf16[128,1024]{1,0:T(8,128)(2,1)S(1)}, f32[2,64,128]{2,1,0:T(8,128)S(1)}) custom-call(f32[8,8,8,128]{3,2,1,0:T(8,128)S(1)} %collective-permute-done.9.dense_ref, f32[8,128,2048]{2,1,0:T(8,128)S(1)} %bitcast.30, f32[2,64,128]{2,1,0:T(8,128)S(1)} %get-tuple-element.30.sum_ref), custom_call_target="tpu_custom_call" | custom-call | flops 201326592 | bytes 2097152 | tf_op jit(solution)/shard_map/other_stress/pallas_call | solution.py:274
  22.5 1.1 %collective-permute-start.12 = (f32[2,64,128]{2,1,0:T(8,128)S(1)}, f32[2,64,128]{2,1,0:T(8,128)S(1)}, u32[]{:S(2)}, u32[]{:S(2)}) collective-permute-start(f32[2,64,128]{2,1,0:T(8,128)S(1)} %get-tuple-element.35), channel_id=1, source_target_pairs={{0,1},{1,0},{2,3},{3,2},{4,5},{5,4},{6,7},{7,6},{8,9},{9,8},{10,11... | collective-permute-start | bytes 196616 | tf_op jit(solution)/shard_map/ppermute | solution.py:34
  23.6 0.0 copy-done.2
  23.6 0.0 copy-done.3
  23.6 0.0 copy-done.4
  23.6 0.5 %rest_stress.3 = f32[2,64,128]{2,1,0:T(8,128)S(1)} custom-call(bf16[128,1024]{1,0:T(8,128)(2,1)S(1)} %get-tuple-element.31.other_ref.slip_ref, f32[8,128,2048]{2,1,0:T(8,128)S(1)} %bitcast.31, f32[2,64,128]{2,1,0:T(8,128)S(1)} %get-tuple-element.32.sum_ref), custom_call_target="tpu_custom_call" | custom-call | flops 201326592 | bytes 2097152 | tf_op jit(solution)/shard_map/rest_stress/pallas_call | solution.py:274
  24.1 0.1 collective-permute-start.10
  24.2 0.8 %both_stress.7 = f32[2,64,128]{2,1,0:T(8,128)S(1)} custom-call(bf16[128,1024]{1,0:T(8,128)(2,1)S(1)} %get-tuple-element.29.own_ref, bf16[128,1024]{1,0:T(8,128)(2,1)S(1)} %get-tuple-element.31.other_ref.slip_ref, f32[8,128,2048]{2,1,0:T(8,128)S(1)} %bitcast.32), custom_call_target="tpu_custom_call" | custom-call | flops 201326592 | bytes 2097152 | tf_op jit(solution)/shard_map/both_stress/pallas_call | solution.py:274
  25.0 0.8 %both_stress.6 = f32[2,64,128]{2,1,0:T(8,128)S(1)} custom-call(bf16[128,1024]{1,0:T(8,128)(2,1)S(1)} %get-tuple-element.29.own_ref, bf16[128,1024]{1,0:T(8,128)(2,1)S(1)} %get-tuple-element.31.other_ref.slip_ref, f32[8,128,2048]{2,1,0:T(8,128)S(1)} %bitcast.33), custom_call_target="tpu_custom_call" | custom-call | flops 201326592 | bytes 2097152 | tf_op jit(solution)/shard_map/both_stress/pallas_call | solution.py:274
  25.9 1.0 %collective-permute-done.12 = f32[2,64,128]{2,1,0:T(8,128)S(1)} collective-permute-done((f32[2,64,128]{2,1,0:T(8,128)S(1)}, f32[2,64,128]{2,1,0:T(8,128)S(1)}, u32[]{:S(2)}, u32[]{:S(2)}) %collective-permute-start.12) | collective-permute-done | bytes 65568 | tf_op jit(solution)/shard_map/ppermute | solution.py:34
  26.9 1.2 %collective-permute-start.13 = (f32[64,128]{1,0:T(8,128)S(1)}, f32[64,128]{1,0:T(8,128)S(1)}, u32[]{:S(2)}, u32[]{:S(2)}) collective-permute-start(f32[64,128]{1,0:T(8,128)S(1)} %get-tuple-element.42), channel_id=1, source_target_pairs={{0,6},{1,7},{2,4},{3,5},{4,2},{5,3},{6,0},{7,1},{8,14},{9,15},{10,... | collective-permute-start | bytes 98312 | tf_op jit(solution)/shard_map/ppermute | solution.py:34
  28.0 1.4 %collective-permute-start.14 = (f32[64,128]{1,0:T(8,128)S(1)}, f32[64,128]{1,0:T(8,128)S(1)}, u32[]{:S(2)}, u32[]{:S(2)}) collective-permute-start(f32[64,128]{1,0:T(8,128)S(1)} %get-tuple-element.43), channel_id=1, source_target_pairs={{0,4},{1,5},{2,6},{3,7},{4,0},{5,1},{6,2},{7,3},{8,12},{9,13},{10,... | collective-permute-start | bytes 98312 | tf_op jit(solution)/shard_map/ppermute | solution.py:34
  29.4 0.0 collective-permute-done.10
  29.5 1.1 %collective-permute-start.11 = (f32[64,128]{1,0:T(8,128)S(1)}, f32[64,128]{1,0:T(8,128)S(1)}, u32[]{:S(2)}, u32[]{:S(2)}) collective-permute-start(f32[64,128]{1,0:T(8,128)S(1)} %slice_bitcast_fusion.7), channel_id=1, source_target_pairs={{0,1},{1,0},{2,3},{3,2},{4,5},{5,4},{6,7},{7,6},{8,9},{9,8},{10,11... | collective-permute-start | bytes 98312 | tf_op jit(solution)/shard_map/ppermute | solution.py:34
  30.5 0.7 %compare_reduce_fusion = pred[]{:T(512)} fusion(f32[8,128]{1,0:T(8,128)S(1)} %get-tuple-element.36), kind=kLoop, calls=%fused_computation.12 | loop fusion | flops 223 | bytes 449 | tf_op jit(solution)/shard_map/reduce_or | solution.py:315
  31.9 1.6 %collective-permute-done.11 = f32[64,128]{1,0:T(8,128)S(1)} collective-permute-done((f32[64,128]{1,0:T(8,128)S(1)}, f32[64,128]{1,0:T(8,128)S(1)}, u32[]{:S(2)}, u32[]{:S(2)}) %collective-permute-start.11) | collective-permute-done | bytes 32800 | tf_op jit(solution)/shard_map/ppermute | solution.py:34
  33.4 0.0 collective-permute-done.13
  33.4 0.0 collective-permute-done.14
  33.5 0.7 %add_bitcast_fusion = (f32[128,64]{0,1:T(8,128)}, f32[64,128]{1,0:T(8,128)}) fusion(f32[128]{0:T(128)S(1)} %get-tuple-element.45, f32[128]{0:T(128)S(1)} %copy-done.2, f32[128]{0:T(128)S(1)} %get-tuple-element.44, f32[64,128]{1,0:T(8,128)S(1)} %get-tuple-element.46, f32[2,64,128]{2,1,0:T(8,128)S(1)} %add.41, f32[64,128]{1,0:T(8,128)S(1)} %collective-permute-done.14, ...), kind=kLoop, calls=%fused_computation.11 | loop fusion | flops 65536 | bytes 230912 | tf_op jit(solution)/shard_map/transpose | solution.py:322
  (7 shorter events, 0.0 us)
Async XLA Ops:
  0.6 19.8 %copy-start = (f32[1024,2048]{1,0:T(8,128)S(1)}, f32[1024,2048]{1,0:T(8,128)}, u32[]{:S(2)}) copy-start(f32[1024,2048]{1,0:T(8,128)} %param.9) | copy-start | bytes 25165828
  20.3 3.2 %copy-start.2 = (f32[128]{0:T(128)S(1)}, f32[128]{0:T(128)}, u32[]{:S(2)}) copy-start(f32[128]{0:T(128)} %param.13) | copy-start | bytes 1540
  20.4 3.2 %copy-start.3 = (f32[128]{0:T(128)S(1)}, f32[128]{0:T(128)}, u32[]{:S(2)}) copy-start(f32[128]{0:T(128)} %param.14) | copy-start | bytes 1540
  20.4 3.2 %copy-start.4 = (f32[128]{0:T(128)S(1)}, f32[128]{0:T(128)}, u32[]{:S(2)}) copy-start(f32[128]{0:T(128)} %param.15) | copy-start | bytes 1540
  20.4 1.6 %collective-permute-start.9 = (f32[8,8,8,128]{3,2,1,0:T(8,128)S(1)}, f32[8,8,8,128]{3,2,1,0:T(8,128)S(1)}, u32[]{:S(2)}, u32[]{:S(2)}) collective-permute-start(f32[8,8,8,128]{3,2,1,0:T(8,128)S(1)} %get-tuple-element.28.dense_ref), channel_id=1, source_target_pairs={{0,8},{8,0},{16,24},{24,16},{1,9},{9,1},{17,25},{25,17},{2,10},{10... | collective-permute-start | bytes 786440 | tf_op jit(solution)/shard_map/ppermute | solution.py:34
  22.5 4.3 %collective-permute-start.12 = (f32[2,64,128]{2,1,0:T(8,128)S(1)}, f32[2,64,128]{2,1,0:T(8,128)S(1)}, u32[]{:S(2)}, u32[]{:S(2)}) collective-permute-start(f32[2,64,128]{2,1,0:T(8,128)S(1)} %get-tuple-element.35), channel_id=1, source_target_pairs={{0,1},{1,0},{2,3},{3,2},{4,5},{5,4},{6,7},{7,6},{8,9},{9,8},{10,11... | collective-permute-start | bytes 196616 | tf_op jit(solution)/shard_map/ppermute | solution.py:34
  24.1 5.3 %collective-permute-start.10 = (f32[2,64,128]{2,1,0:T(8,128)S(1)}, f32[2,64,128]{2,1,0:T(8,128)S(1)}, u32[]{:S(2)}, u32[]{:S(2)}) collective-permute-start(f32[2,64,128]{2,1,0:T(8,128)S(1)} %rest_stress.3), channel_id=1, source_target_pairs={{0,2},{1,3},{2,0},{3,1},{4,6},{5,7},{6,4},{7,5},{8,10},{9,11},{10,... | collective-permute-start | bytes 196616 | tf_op jit(solution)/shard_map/ppermute | solution.py:34
  26.9 6.6 %collective-permute-start.13 = (f32[64,128]{1,0:T(8,128)S(1)}, f32[64,128]{1,0:T(8,128)S(1)}, u32[]{:S(2)}, u32[]{:S(2)}) collective-permute-start(f32[64,128]{1,0:T(8,128)S(1)} %get-tuple-element.42), channel_id=1, source_target_pairs={{0,6},{1,7},{2,4},{3,5},{4,2},{5,3},{6,0},{7,1},{8,14},{9,15},{10,... | collective-permute-start | bytes 98312 | tf_op jit(solution)/shard_map/ppermute | solution.py:34
  28.0 5.4 %collective-permute-start.14 = (f32[64,128]{1,0:T(8,128)S(1)}, f32[64,128]{1,0:T(8,128)S(1)}, u32[]{:S(2)}, u32[]{:S(2)}) collective-permute-start(f32[64,128]{1,0:T(8,128)S(1)} %get-tuple-element.43), channel_id=1, source_target_pairs={{0,4},{1,5},{2,6},{3,7},{4,0},{5,1},{6,2},{7,3},{8,12},{9,13},{10,... | collective-permute-start | bytes 98312 | tf_op jit(solution)/shard_map/ppermute | solution.py:34
  29.5 4.0 %collective-permute-start.11 = (f32[64,128]{1,0:T(8,128)S(1)}, f32[64,128]{1,0:T(8,128)S(1)}, u32[]{:S(2)}, u32[]{:S(2)}) collective-permute-start(f32[64,128]{1,0:T(8,128)S(1)} %slice_bitcast_fusion.7), channel_id=1, source_target_pairs={{0,1},{1,0},{2,3},{3,2},{4,5},{5,4},{6,7},{7,6},{8,9},{9,8},{10,11... | collective-permute-start | bytes 98312 | tf_op jit(solution)/shard_map/ppermute | solution.py:34

commit v25 on v24

--- a/solution.py
+++ b/solution.py
@@ -78,14 +78,12 @@
         left = left | (rank[p * SUB : (p + 1) * SUB] >= SLOTS)
     left_ref[events] = pltpu.roll(jnp.where(left, ids, -1.0), row * entries, 1)
 
-    lane = lax.broadcasted_iota(jnp.int32, (1, BLOCK), 1) // entries
+    i, j = (lax.broadcasted_iota(jnp.int32, (SUB, BLOCK), d) for d in (0, 1))
+    here = j // entries == i
 
     def line_of(tile):
-        line = jnp.full((1, BLOCK), -1.0, jnp.float32)
-        for e in range(events):
-            part = pltpu.roll(tile[e : e + 1], e * entries, 1) if e else tile[0:1]
-            line = jnp.where(lane == e, part, line)
-        return line
+        moved = pltpu.roll(tile, 0, 1, stride=entries, stride_axis=0)
+        return jnp.max(jnp.where(here, moved, -1.0), axis=0, keepdims=True)
 
     known = jnp.maximum(ids, 0.0)
     code = known - jnp.floor(known / blocks) * blocks + 1.0
@@ -115,8 +113,10 @@
         tile = pltpu.roll(tile, BLOCK - shift, 1) if shift else tile
         tile = jnp.broadcast_to(jnp.where(lane < STRIDE, tile, mark), (STRIDE, BLOCK))
         piece = jnp.where(last, tile, data[p * STRIDE : (p + 1) * STRIDE])
-        for other in range(out_ref.shape[0] // pieces):
-            out_ref[other * pieces + p] = piece
+        core, c = p // width, p % width
+        height = out_ref.shape[0] // width
+        for r in range(core, height, 2):
+            out_ref[c * height + r] = piece
 
 
 def expand_body(in_ref, out_ref, mark_ref):
@@ -128,7 +128,7 @@
         numbers = jnp.zeros((1, BLOCK), jnp.float32)
         slip = []
         for r in range(height):
-            piece = in_ref[r * width + c]
+            piece = in_ref[c * height + r]
             info = piece[SLOTS : SLOTS + 1, :]
             mark = jnp.maximum(mark, jnp.where(lane >= STRIDE, info, 0.0))
             info = pltpu.roll(info, r * STRIDE, 1) if r else info
@@ -255,7 +255,7 @@
         out_specs=[VMEM_SPEC] * 2,
         compiler_params=params(16),
         name="expand",
-    )(lax.all_to_all(message, ("rows", "cols"), 0, 0, tiled=True))
+    )(lax.all_to_all(message, ("cols", "rows"), 0, 0, tiled=True))
 
     def all_left(kernel, left):
         others = sorted(range(1, height), key=lambda k: (k < 2, k))

time: 34.3 us -> 34 us (level)
  waiting for transfers between devices: 3.17 us -> 2.55 us
  starting transfers between devices: 4.88 us -> 5.4 us
    ppermute x6, waiting for transfers between devices: 3.17 us -> 2.55 us  [send_xor(): lax.ppermute(block, axis, [(r, r ^ k) for r in range(lax.axis_size(axis))])]
    ppermute x6, starting transfers between devices: 4.88 us -> 5.4 us  [send_xor(): lax.ppermute(block, axis, [(r, r ^ k) for r in range(lax.axis_size(axis))])]
where the time goes in v25:
time: 34 us; the launch traced here: 33.9 us
  blocking collectives  17.7 us (52%)
  starting transfers between devices  5.4 us (16%)
  Pallas kernels  5.35 us (16%)
  waiting for transfers between devices  2.55 us (7%)
  between operations  1.42 us (4%)
  other arithmetic  1.39 us (4%)
    all_to_all x1, blocking collectives, per_device(): lax.all_to_all(message, ('cols', 'rows'), 0, 0, tiled=True)  17.7 us
    ppermute x6, starting transfers between devices, send_xor(): lax.ppermute(block, axis, [(r, r ^ k) for r in range(lax.axis_size(axis))])  5.4 us
    pallas_call x5, Pallas kernels, call(): pl.pallas_call(functools.partial(body, targets), out_shape=outs, in_specs...  3.5 us
    ppermute x6, waiting for transfers between devices, send_xor(): lax.ppermute(block, axis, [(r, r ^ k) for r in range(lax.axis_size(axis))])  2.55 us
    pallas_call x1, Pallas kernels, per_device(): pl.pallas_call(functools.partial(compact_body, width, blocks_half), out_s...  1.58 us
    reduce_or x1, other arithmetic, per_device(): jnp.any(mark[0, STRIDE:] > 0)  0.7 us
  transfers between devices with their start and end apart: 6, of which 3 were waited for; matrix products, arithmetic and copies ran while one was open for 2% of the time, Pallas kernels for 9%

profile of v25, /device:TPU:0, one launch (start us, length us, event | category | flops | bytes accessed | tf_op | source)
XLA Modules:
  0.0 33.9 jit_solution(4154007409215464115)
XLA Ops:
  0.6 0.0 copy-start
  0.6 1.6 %compact.1 = (f32[32,16,128]{2,1,0:T(8,128)S(1)}, f32[9,8,128]{2,1,0:T(8,128)S(1)}) custom-call(f32[8,8,128]{2,1,0:T(8,128)} %slip_hbm.1, s32[8,8]{1,0:T(8,128)} %list_hbm.1, s32[8]{0:T(128)} %count_hbm.1, f32[8,128,2048]{2,1,0:T(8,128)} %bitcast.27), custom_call_target="tpu_custom_call" | custom-call | tf_op jit(solution)/shard_map/compact/pallas_call | solution.py:237
  2.2 17.7 %all_to_all.10.in_ref = f32[32,16,128]{2,1,0:T(8,128)S(1)} all-to-all(f32[32,16,128]{2,1,0:T(8,128)S(1)} %get-tuple-element.27), channel_id=1, replica_groups=mesh['rows'=4,'cols'=8] {'cols','rows'}, dimensions={0} | all-to-all | bytes 524288 | tf_op jit(solution)/shard_map/all_to_all | solution.py:258
  19.9 0.3 expand.1
  20.2 0.0 copy-start.2
  20.2 0.0 copy-start.3
  20.2 0.0 copy-start.4
  20.2 0.1 collective-permute-start.9
  20.3 0.0 copy-done
  20.3 0.9 %own_stress.3 = (bf16[128,1024]{1,0:T(8,128)(2,1)S(1)}, f32[2,64,128]{2,1,0:T(8,128)S(1)}, f32[2,64,128]{2,1,0:T(8,128)S(1)}) custom-call(f32[8,8,8,128]{3,2,1,0:T(8,128)S(1)} %get-tuple-element.28.dense_ref, f32[8,128,2048]{2,1,0:T(8,128)S(1)} %bitcast.29), custom_call_target="tpu_custom_call" | custom-call | flops 201326592 | bytes 2097152 | tf_op jit(solution)/shard_map/own_stress/pallas_call | solution.py:274
  21.2 0.6 %collective-permute-done.9.dense_ref = f32[8,8,8,128]{3,2,1,0:T(8,128)S(1)} collective-permute-done((f32[8,8,8,128]{3,2,1,0:T(8,128)S(1)}, f32[8,8,8,128]{3,2,1,0:T(8,128)S(1)}, u32[]{:S(2)}, u32[]{:S(2)}) %collective-permute-start.9) | collective-permute-done | bytes 262176 | tf_op jit(solution)/shard_map/ppermute | solution.py:34
  21.8 0.5 %other_stress.3 = (bf16[128,1024]{1,0:T(8,128)(2,1)S(1)}, f32[2,64,128]{2,1,0:T(8,128)S(1)}) custom-call(f32[8,8,8,128]{3,2,1,0:T(8,128)S(1)} %collective-permute-done.9.dense_ref, f32[8,128,2048]{2,1,0:T(8,128)S(1)} %bitcast.30, f32[2,64,128]{2,1,0:T(8,128)S(1)} %get-tuple-element.30.sum_ref), custom_call_target="tpu_custom_call" | custom-call | flops 201326592 | bytes 2097152 | tf_op jit(solution)/shard_map/other_stress/pallas_call | solution.py:274
  22.4 1.0 %collective-permute-start.12 = (f32[2,64,128]{2,1,0:T(8,128)S(1)}, f32[2,64,128]{2,1,0:T(8,128)S(1)}, u32[]{:S(2)}, u32[]{:S(2)}) collective-permute-start(f32[2,64,128]{2,1,0:T(8,128)S(1)} %get-tuple-element.35), channel_id=1, source_target_pairs={{0,1},{1,0},{2,3},{3,2},{4,5},{5,4},{6,7},{7,6},{8,9},{9,8},{10,11... | collective-permute-start | bytes 196616 | tf_op jit(solution)/shard_map/ppermute | solution.py:34
  23.3 0.0 copy-done.2
  23.3 0.0 copy-done.3
  23.3 0.0 copy-done.4
  23.3 0.5 %rest_stress.3 = f32[2,64,128]{2,1,0:T(8,128)S(1)} custom-call(bf16[128,1024]{1,0:T(8,128)(2,1)S(1)} %get-tuple-element.31.other_ref.slip_ref, f32[8,128,2048]{2,1,0:T(8,128)S(1)} %bitcast.31, f32[2,64,128]{2,1,0:T(8,128)S(1)} %get-tuple-element.32.sum_ref), custom_call_target="tpu_custom_call" | custom-call | flops 201326592 | bytes 2097152 | tf_op jit(solution)/shard_map/rest_stress/pallas_call | solution.py:274
  23.9 0.7 %collective-permute-start.10 = (f32[2,64,128]{2,1,0:T(8,128)S(1)}, f32[2,64,128]{2,1,0:T(8,128)S(1)}, u32[]{:S(2)}, u32[]{:S(2)}) collective-permute-start(f32[2,64,128]{2,1,0:T(8,128)S(1)} %rest_stress.3), channel_id=1, source_target_pairs={{0,2},{1,3},{2,0},{3,1},{4,6},{5,7},{6,4},{7,5},{8,10},{9,11},{10,... | collective-permute-start | bytes 196616 | tf_op jit(solution)/shard_map/ppermute | solution.py:34
  24.6 0.8 %both_stress.7 = f32[2,64,128]{2,1,0:T(8,128)S(1)} custom-call(bf16[128,1024]{1,0:T(8,128)(2,1)S(1)} %get-tuple-element.29.own_ref, bf16[128,1024]{1,0:T(8,128)(2,1)S(1)} %get-tuple-element.31.other_ref.slip_ref, f32[8,128,2048]{2,1,0:T(8,128)S(1)} %bitcast.32), custom_call_target="tpu_custom_call" | custom-call | flops 201326592 | bytes 2097152 | tf_op jit(solution)/shard_map/both_stress/pallas_call | solution.py:274
  25.4 0.8 %both_stress.6 = f32[2,64,128]{2,1,0:T(8,128)S(1)} custom-call(bf16[128,1024]{1,0:T(8,128)(2,1)S(1)} %get-tuple-element.29.own_ref, bf16[128,1024]{1,0:T(8,128)(2,1)S(1)} %get-tuple-element.31.other_ref.slip_ref, f32[8,128,2048]{2,1,0:T(8,128)S(1)} %bitcast.33), custom_call_target="tpu_custom_call" | custom-call | flops 201326592 | bytes 2097152 | tf_op jit(solution)/shard_map/both_stress/pallas_call | solution.py:274
  26.2 0.5 %collective-permute-done.12 = f32[2,64,128]{2,1,0:T(8,128)S(1)} collective-permute-done((f32[2,64,128]{2,1,0:T(8,128)S(1)}, f32[2,64,128]{2,1,0:T(8,128)S(1)}, u32[]{:S(2)}, u32[]{:S(2)}) %collective-permute-start.12) | collective-permute-done | bytes 65568 | tf_op jit(solution)/shard_map/ppermute | solution.py:34
  26.7 1.4 %collective-permute-start.13 = (f32[64,128]{1,0:T(8,128)S(1)}, f32[64,128]{1,0:T(8,128)S(1)}, u32[]{:S(2)}, u32[]{:S(2)}) collective-permute-start(f32[64,128]{1,0:T(8,128)S(1)} %get-tuple-element.42), channel_id=1, source_target_pairs={{0,6},{1,7},{2,4},{3,5},{4,2},{5,3},{6,0},{7,1},{8,14},{9,15},{10,... | collective-permute-start | bytes 98312 | tf_op jit(solution)/shard_map/ppermute | solution.py:34
  28.1 1.1 %collective-permute-start.14 = (f32[64,128]{1,0:T(8,128)S(1)}, f32[64,128]{1,0:T(8,128)S(1)}, u32[]{:S(2)}, u32[]{:S(2)}) collective-permute-start(f32[64,128]{1,0:T(8,128)S(1)} %get-tuple-element.43), channel_id=1, source_target_pairs={{0,4},{1,5},{2,6},{3,7},{4,0},{5,1},{6,2},{7,3},{8,12},{9,13},{10,... | collective-permute-start | bytes 98312 | tf_op jit(solution)/shard_map/ppermute | solution.py:34
  29.2 0.0 collective-permute-done.10
  29.2 1.2 %collective-permute-start.11 = (f32[64,128]{1,0:T(8,128)S(1)}, f32[64,128]{1,0:T(8,128)S(1)}, u32[]{:S(2)}, u32[]{:S(2)}) collective-permute-start(f32[64,128]{1,0:T(8,128)S(1)} %slice_bitcast_fusion.7), channel_id=1, source_target_pairs={{0,1},{1,0},{2,3},{3,2},{4,5},{5,4},{6,7},{7,6},{8,9},{9,8},{10,11... | collective-permute-start | bytes 98312 | tf_op jit(solution)/shard_map/ppermute | solution.py:34
  30.4 0.7 %compare_reduce_fusion = pred[]{:T(512)} fusion(f32[8,128]{1,0:T(8,128)S(1)} %get-tuple-element.36), kind=kLoop, calls=%fused_computation.12 | loop fusion | flops 223 | bytes 449 | tf_op jit(solution)/shard_map/reduce_or | solution.py:315
  31.8 1.4 %collective-permute-done.11 = f32[64,128]{1,0:T(8,128)S(1)} collective-permute-done((f32[64,128]{1,0:T(8,128)S(1)}, f32[64,128]{1,0:T(8,128)S(1)}, u32[]{:S(2)}, u32[]{:S(2)}) %collective-permute-start.11) | collective-permute-done | bytes 32800 | tf_op jit(solution)/shard_map/ppermute | solution.py:34
  33.2 0.0 collective-permute-done.13
  33.2 0.0 collective-permute-done.14
  33.2 0.7 %add_bitcast_fusion = (f32[128,64]{0,1:T(8,128)}, f32[64,128]{1,0:T(8,128)}) fusion(f32[128]{0:T(128)S(1)} %get-tuple-element.45, f32[128]{0:T(128)S(1)} %copy-done.2, f32[128]{0:T(128)S(1)} %get-tuple-element.44, f32[64,128]{1,0:T(8,128)S(1)} %get-tuple-element.46, f32[2,64,128]{2,1,0:T(8,128)S(1)} %add.41, f32[64,128]{1,0:T(8,128)S(1)} %collective-permute-done.14, ...), kind=kLoop, calls=%fused_computation.11 | loop fusion | flops 65536 | bytes 230912 | tf_op jit(solution)/shard_map/transpose | solution.py:322
  (7 shorter events, 0.0 us)
Async XLA Ops:
  0.6 19.7 %copy-start = (f32[1024,2048]{1,0:T(8,128)S(1)}, f32[1024,2048]{1,0:T(8,128)}, u32[]{:S(2)}) copy-start(f32[1024,2048]{1,0:T(8,128)} %param.9) | copy-start | bytes 25165828
  20.2 3.1 %copy-start.2 = (f32[128]{0:T(128)S(1)}, f32[128]{0:T(128)}, u32[]{:S(2)}) copy-start(f32[128]{0:T(128)} %param.13) | copy-start | bytes 1540
  20.2 3.1 %copy-start.3 = (f32[128]{0:T(128)S(1)}, f32[128]{0:T(128)}, u32[]{:S(2)}) copy-start(f32[128]{0:T(128)} %param.14) | copy-start | bytes 1540
  20.2 3.1 %copy-start.4 = (f32[128]{0:T(128)S(1)}, f32[128]{0:T(128)}, u32[]{:S(2)}) copy-start(f32[128]{0:T(128)} %param.15) | copy-start | bytes 1540
  20.2 1.6 %collective-permute-start.9 = (f32[8,8,8,128]{3,2,1,0:T(8,128)S(1)}, f32[8,8,8,128]{3,2,1,0:T(8,128)S(1)}, u32[]{:S(2)}, u32[]{:S(2)}) collective-permute-start(f32[8,8,8,128]{3,2,1,0:T(8,128)S(1)} %get-tuple-element.28.dense_ref), channel_id=1, source_target_pairs={{0,8},{8,0},{16,24},{24,16},{1,9},{9,1},{17,25},{25,17},{2,10},{10... | collective-permute-start | bytes 786440 | tf_op jit(solution)/shard_map/ppermute | solution.py:34
  22.4 4.3 %collective-permute-start.12 = (f32[2,64,128]{2,1,0:T(8,128)S(1)}, f32[2,64,128]{2,1,0:T(8,128)S(1)}, u32[]{:S(2)}, u32[]{:S(2)}) collective-permute-start(f32[2,64,128]{2,1,0:T(8,128)S(1)} %get-tuple-element.35), channel_id=1, source_target_pairs={{0,1},{1,0},{2,3},{3,2},{4,5},{5,4},{6,7},{7,6},{8,9},{9,8},{10,11... | collective-permute-start | bytes 196616 | tf_op jit(solution)/shard_map/ppermute | solution.py:34
  23.9 5.3 %collective-permute-start.10 = (f32[2,64,128]{2,1,0:T(8,128)S(1)}, f32[2,64,128]{2,1,0:T(8,128)S(1)}, u32[]{:S(2)}, u32[]{:S(2)}) collective-permute-start(f32[2,64,128]{2,1,0:T(8,128)S(1)} %rest_stress.3), channel_id=1, source_target_pairs={{0,2},{1,3},{2,0},{3,1},{4,6},{5,7},{6,4},{7,5},{8,10},{9,11},{10,... | collective-permute-start | bytes 196616 | tf_op jit(solution)/shard_map/ppermute | solution.py:34
  26.7 6.5 %collective-permute-start.13 = (f32[64,128]{1,0:T(8,128)S(1)}, f32[64,128]{1,0:T(8,128)S(1)}, u32[]{:S(2)}, u32[]{:S(2)}) collective-permute-start(f32[64,128]{1,0:T(8,128)S(1)} %get-tuple-element.42), channel_id=1, source_target_pairs={{0,6},{1,7},{2,4},{3,5},{4,2},{5,3},{6,0},{7,1},{8,14},{9,15},{10,... | collective-permute-start | bytes 98312 | tf_op jit(solution)/shard_map/ppermute | solution.py:34
  28.1 5.1 %collective-permute-start.14 = (f32[64,128]{1,0:T(8,128)S(1)}, f32[64,128]{1,0:T(8,128)S(1)}, u32[]{:S(2)}, u32[]{:S(2)}) collective-permute-start(f32[64,128]{1,0:T(8,128)S(1)} %get-tuple-element.43), channel_id=1, source_target_pairs={{0,4},{1,5},{2,6},{3,7},{4,0},{5,1},{6,2},{7,3},{8,12},{9,13},{10,... | collective-permute-start | bytes 98312 | tf_op jit(solution)/shard_map/ppermute | solution.py:34
  29.2 4.0 %collective-permute-start.11 = (f32[64,128]{1,0:T(8,128)S(1)}, f32[64,128]{1,0:T(8,128)S(1)}, u32[]{:S(2)}, u32[]{:S(2)}) collective-permute-start(f32[64,128]{1,0:T(8,128)S(1)} %slice_bitcast_fusion.7), channel_id=1, source_target_pairs={{0,1},{1,0},{2,3},{3,2},{4,5},{5,4},{6,7},{7,6},{8,9},{9,8},{10,11... | collective-permute-start | bytes 98312 | tf_op jit(solution)/shard_map/ppermute | solution.py:34

commit v26 on v25

--- a/solution.py
+++ b/solution.py
@@ -292,9 +292,8 @@
 
     def stress_of(kernel, mine):
         came = send_xor(mine, "rows", 1)
-        own, far_own, near_own = call(
-            own_body, (far_send, near_send), [slips, sums(far_send), sums(near_send)], mine, kernel
-        )
+        groups = (far_send, near_send, far_keep)
+        own, far_own, near_own, kept_own = call(own_body, groups, [slips, *map(sums, groups)], mine, kernel)
         other, far_sent = call(other_body, far_send, [slips, sums(far_send)], came, kernel, far_own)
         near_sent = call(rest_body, near_send, sums(near_send), other, kernel, near_own)
 
@@ -303,7 +302,7 @@
 
         far_came = send_xor(far_sent, "cols", 1)
         near_came = [send_xor(near_sent[j : j + 2], "cols", near_send[j]) for j in range(0, len(near_send), 2)]
-        far = later(far_keep) + far_came
+        far = call(rest_body, far_keep, sums(far_keep), other, kernel, kept_own) + far_came
         near = sum(near_came, later(near_keep))
         parts = [send_xor(far[j], "cols", k) for j, k in reversed(list(enumerate(far_keep)))]
         parts.append(send_xor(near[1], "cols", 1))

time: 34 us -> 34 us (level)
  no operation moved by 1% of the time
where the time goes in v26:
time: 34 us; the launch traced here: 33.9 us
  blocking collectives  17.7 us (52%)
  Pallas kernels  5.37 us (16%)
  starting transfers between devices  5.07 us (15%)
  waiting for transfers between devices  2.88 us (8%)
  between operations  1.41 us (4%)
  other arithmetic  1.39 us (4%)
    all_to_all x1, blocking collectives, per_device(): lax.all_to_all(message, ('cols', 'rows'), 0, 0, tiled=True)  17.7 us
    ppermute x6, starting transfers between devices, send_xor(): lax.ppermute(block, axis, [(r, r ^ k) for r in range(lax.axis_size(axis))])  5.07 us
    pallas_call x5, Pallas kernels, call(): pl.pallas_call(functools.partial(body, targets), out_shape=outs, in_specs...  3.52 us
    ppermute x6, waiting for transfers between devices, send_xor(): lax.ppermute(block, axis, [(r, r ^ k) for r in range(lax.axis_size(axis))])  2.88 us
    pallas_call x1, Pallas kernels, per_device(): pl.pallas_call(functools.partial(compact_body, width, blocks_half), out_s...  1.58 us
    reduce_or x1, other arithmetic, per_device(): jnp.any(mark[0, STRIDE:] > 0)  0.7 us
  transfers between devices with their start and end apart: 6, of which 3 were waited for; matrix products, arithmetic and copies ran while one was open for 2% of the time, Pallas kernels for 9%

profile of v26, /device:TPU:0, one launch (start us, length us, event | category | flops | bytes accessed | tf_op | source)
XLA Modules:
  0.0 33.9 jit_solution(11788885720567245469)
XLA Ops:
  0.6 0.0 copy-start
  0.6 1.6 %compact.1 = (f32[32,16,128]{2,1,0:T(8,128)S(1)}, f32[9,8,128]{2,1,0:T(8,128)S(1)}) custom-call(f32[8,8,128]{2,1,0:T(8,128)} %slip_hbm.1, s32[8,8]{1,0:T(8,128)} %list_hbm.1, s32[8]{0:T(128)} %count_hbm.1, f32[8,128,2048]{2,1,0:T(8,128)} %bitcast.27), custom_call_target="tpu_custom_call" | custom-call | tf_op jit(solution)/shard_map/compact/pallas_call | solution.py:237
  2.2 17.7 %all_to_all.10.in_ref = f32[32,16,128]{2,1,0:T(8,128)S(1)} all-to-all(f32[32,16,128]{2,1,0:T(8,128)S(1)} %get-tuple-element.29), channel_id=1, replica_groups=mesh['rows'=4,'cols'=8] {'cols','rows'}, dimensions={0} | all-to-all | bytes 524288 | tf_op jit(solution)/shard_map/all_to_all | solution.py:258
  19.9 0.3 expand.1
  20.2 0.0 copy-start.2
  20.2 0.0 copy-start.3
  20.2 0.0 copy-start.4
  20.2 0.1 collective-permute-start.9
  20.3 0.0 copy-done
  20.3 1.2 %own_stress.3 = (bf16[128,1024]{1,0:T(8,128)(2,1)S(1)}, f32[2,64,128]{2,1,0:T(8,128)S(1)}, f32[2,64,128]{2,1,0:T(8,128)S(1)}, f32[2,64,128]{2,1,0:T(8,128)S(1)}) custom-call(f32[8,8,8,128]{3,2,1,0:T(8,128)S(1)} %get-tuple-element.30.dense_ref, f32[8,128,2048]{2,1,0:T(8,128)S(1)} %bitcast.29), custom_call_target="tpu_custom_call" | custom-call | flops 201326592 | bytes 2097152 | tf_op jit(solution)/shard_map/own_stress/pallas_call | solution.py:274
  21.5 0.3 collective-permute-done.9.dense_ref
  21.8 0.5 %other_stress.3 = (bf16[128,1024]{1,0:T(8,128)(2,1)S(1)}, f32[2,64,128]{2,1,0:T(8,128)S(1)}) custom-call(f32[8,8,8,128]{3,2,1,0:T(8,128)S(1)} %collective-permute-done.9.dense_ref, f32[8,128,2048]{2,1,0:T(8,128)S(1)} %bitcast.30, f32[2,64,128]{2,1,0:T(8,128)S(1)} %get-tuple-element.32.sum_ref), custom_call_target="tpu_custom_call" | custom-call | flops 201326592 | bytes 2097152 | tf_op jit(solution)/shard_map/other_stress/pallas_call | solution.py:274
  22.4 1.0 %collective-permute-start.12 = (f32[2,64,128]{2,1,0:T(8,128)S(1)}, f32[2,64,128]{2,1,0:T(8,128)S(1)}, u32[]{:S(2)}, u32[]{:S(2)}) collective-permute-start(f32[2,64,128]{2,1,0:T(8,128)S(1)} %get-tuple-element.38), channel_id=1, source_target_pairs={{0,1},{1,0},{2,3},{3,2},{4,5},{5,4},{6,7},{7,6},{8,9},{9,8},{10,11... | collective-permute-start | bytes 196616 | tf_op jit(solution)/shard_map/ppermute | solution.py:34
  23.3 0.0 copy-done.2
  23.3 0.0 copy-done.3
  23.3 0.0 copy-done.4
  23.4 0.5 %rest_stress.6 = f32[2,64,128]{2,1,0:T(8,128)S(1)} custom-call(bf16[128,1024]{1,0:T(8,128)(2,1)S(1)} %get-tuple-element.33.other_ref.slip_ref, f32[8,128,2048]{2,1,0:T(8,128)S(1)} %bitcast.31, f32[2,64,128]{2,1,0:T(8,128)S(1)} %get-tuple-element.34.sum_ref), custom_call_target="tpu_custom_call" | custom-call | flops 201326592 | bytes 2097152 | tf_op jit(solution)/shard_map/rest_stress/pallas_call | solution.py:274
  23.9 0.7 %collective-permute-start.10 = (f32[2,64,128]{2,1,0:T(8,128)S(1)}, f32[2,64,128]{2,1,0:T(8,128)S(1)}, u32[]{:S(2)}, u32[]{:S(2)}) collective-permute-start(f32[2,64,128]{2,1,0:T(8,128)S(1)} %rest_stress.6), channel_id=1, source_target_pairs={{0,2},{1,3},{2,0},{3,1},{4,6},{5,7},{6,4},{7,5},{8,10},{9,11},{10,... | collective-permute-start | bytes 196616 | tf_op jit(solution)/shard_map/ppermute | solution.py:34
  24.6 0.5 %rest_stress.7 = f32[2,64,128]{2,1,0:T(8,128)S(1)} custom-call(bf16[128,1024]{1,0:T(8,128)(2,1)S(1)} %get-tuple-element.33.other_ref.slip_ref, f32[8,128,2048]{2,1,0:T(8,128)S(1)} %bitcast.32, f32[2,64,128]{2,1,0:T(8,128)S(1)} %get-tuple-element.37.sum_ref), custom_call_target="tpu_custom_call" | custom-call | flops 201326592 | bytes 2097152 | tf_op jit(solution)/shard_map/rest_stress/pallas_call | solution.py:274
  25.1 0.8 %both_stress.3 = f32[2,64,128]{2,1,0:T(8,128)S(1)} custom-call(bf16[128,1024]{1,0:T(8,128)(2,1)S(1)} %get-tuple-element.31.own_ref, bf16[128,1024]{1,0:T(8,128)(2,1)S(1)} %get-tuple-element.33.other_ref.slip_ref, f32[8,128,2048]{2,1,0:T(8,128)S(1)} %bitcast.33), custom_call_target="tpu_custom_call" | custom-call | flops 201326592 | bytes 2097152 | tf_op jit(solution)/shard_map/both_stress/pallas_call | solution.py:274
  25.9 0.8 %collective-permute-done.12 = f32[2,64,128]{2,1,0:T(8,128)S(1)} collective-permute-done((f32[2,64,128]{2,1,0:T(8,128)S(1)}, f32[2,64,128]{2,1,0:T(8,128)S(1)}, u32[]{:S(2)}, u32[]{:S(2)}) %collective-permute-start.12) | collective-permute-done | bytes 65568 | tf_op jit(solution)/shard_map/ppermute | solution.py:34
  26.7 1.4 %collective-permute-start.13 = (f32[64,128]{1,0:T(8,128)S(1)}, f32[64,128]{1,0:T(8,128)S(1)}, u32[]{:S(2)}, u32[]{:S(2)}) collective-permute-start(f32[64,128]{1,0:T(8,128)S(1)} %get-tuple-element.45), channel_id=1, source_target_pairs={{0,6},{1,7},{2,4},{3,5},{4,2},{5,3},{6,0},{7,1},{8,14},{9,15},{10,... | collective-permute-start | bytes 98312 | tf_op jit(solution)/shard_map/ppermute | solution.py:34
  28.1 1.0 %collective-permute-start.14 = (f32[64,128]{1,0:T(8,128)S(1)}, f32[64,128]{1,0:T(8,128)S(1)}, u32[]{:S(2)}, u32[]{:S(2)}) collective-permute-start(f32[64,128]{1,0:T(8,128)S(1)} %get-tuple-element.46), channel_id=1, source_target_pairs={{0,4},{1,5},{2,6},{3,7},{4,0},{5,1},{6,2},{7,3},{8,12},{9,13},{10,... | collective-permute-start | bytes 98312 | tf_op jit(solution)/shard_map/ppermute | solution.py:34
  29.2 0.0 collective-permute-done.10
  29.2 0.9 %collective-permute-start.11 = (f32[64,128]{1,0:T(8,128)S(1)}, f32[64,128]{1,0:T(8,128)S(1)}, u32[]{:S(2)}, u32[]{:S(2)}) collective-permute-start(f32[64,128]{1,0:T(8,128)S(1)} %slice_bitcast_fusion.7), channel_id=1, source_target_pairs={{0,1},{1,0},{2,3},{3,2},{4,5},{5,4},{6,7},{7,6},{8,9},{9,8},{10,11... | collective-permute-start | bytes 98312 | tf_op jit(solution)/shard_map/ppermute | solution.py:34
  30.1 0.7 %compare_reduce_fusion = pred[]{:T(512)} fusion(f32[8,128]{1,0:T(8,128)S(1)} %get-tuple-element.39), kind=kLoop, calls=%fused_computation.12 | loop fusion | flops 223 | bytes 449 | tf_op jit(solution)/shard_map/reduce_or | solution.py:314
  31.4 1.8 %collective-permute-done.11 = f32[64,128]{1,0:T(8,128)S(1)} collective-permute-done((f32[64,128]{1,0:T(8,128)S(1)}, f32[64,128]{1,0:T(8,128)S(1)}, u32[]{:S(2)}, u32[]{:S(2)}) %collective-permute-start.11) | collective-permute-done | bytes 32800 | tf_op jit(solution)/shard_map/ppermute | solution.py:34
  33.2 0.0 collective-permute-done.13
  33.2 0.0 collective-permute-done.14
  33.2 0.7 %add_bitcast_fusion = (f32[128,64]{0,1:T(8,128)}, f32[64,128]{1,0:T(8,128)}) fusion(f32[128]{0:T(128)S(1)} %get-tuple-element.48, f32[128]{0:T(128)S(1)} %copy-done.2, f32[128]{0:T(128)S(1)} %get-tuple-element.47, f32[64,128]{1,0:T(8,128)S(1)} %get-tuple-element.49, f32[2,64,128]{2,1,0:T(8,128)S(1)} %add.41, f32[64,128]{1,0:T(8,128)S(1)} %collective-permute-done.14, ...), kind=kLoop, calls=%fused_computation.11 | loop fusion | flops 65536 | bytes 230912 | tf_op jit(solution)/shard_map/transpose | solution.py:321
  (7 shorter events, 0.0 us)
Async XLA Ops:
  0.6 19.7 %copy-start = (f32[1024,2048]{1,0:T(8,128)S(1)}, f32[1024,2048]{1,0:T(8,128)}, u32[]{:S(2)}) copy-start(f32[1024,2048]{1,0:T(8,128)} %param.9) | copy-start | bytes 25165828
  20.2 3.1 %copy-start.2 = (f32[128]{0:T(128)S(1)}, f32[128]{0:T(128)}, u32[]{:S(2)}) copy-start(f32[128]{0:T(128)} %param.13) | copy-start | bytes 1540
  20.2 3.1 %copy-start.3 = (f32[128]{0:T(128)S(1)}, f32[128]{0:T(128)}, u32[]{:S(2)}) copy-start(f32[128]{0:T(128)} %param.14) | copy-start | bytes 1540
  20.2 3.1 %copy-start.4 = (f32[128]{0:T(128)S(1)}, f32[128]{0:T(128)}, u32[]{:S(2)}) copy-start(f32[128]{0:T(128)} %param.15) | copy-start | bytes 1540
  20.2 1.6 %collective-permute-start.9 = (f32[8,8,8,128]{3,2,1,0:T(8,128)S(1)}, f32[8,8,8,128]{3,2,1,0:T(8,128)S(1)}, u32[]{:S(2)}, u32[]{:S(2)}) collective-permute-start(f32[8,8,8,128]{3,2,1,0:T(8,128)S(1)} %get-tuple-element.30.dense_ref), channel_id=1, source_target_pairs={{0,8},{8,0},{16,24},{24,16},{1,9},{9,1},{17,25},{25,17},{2,10},{10... | collective-permute-start | bytes 786440 | tf_op jit(solution)/shard_map/ppermute | solution.py:34
  22.4 4.3 %collective-permute-start.12 = (f32[2,64,128]{2,1,0:T(8,128)S(1)}, f32[2,64,128]{2,1,0:T(8,128)S(1)}, u32[]{:S(2)}, u32[]{:S(2)}) collective-permute-start(f32[2,64,128]{2,1,0:T(8,128)S(1)} %get-tuple-element.38), channel_id=1, source_target_pairs={{0,1},{1,0},{2,3},{3,2},{4,5},{5,4},{6,7},{7,6},{8,9},{9,8},{10,11... | collective-permute-start | bytes 196616 | tf_op jit(solution)/shard_map/ppermute | solution.py:34
  23.9 5.3 %collective-permute-start.10 = (f32[2,64,128]{2,1,0:T(8,128)S(1)}, f32[2,64,128]{2,1,0:T(8,128)S(1)}, u32[]{:S(2)}, u32[]{:S(2)}) collective-permute-start(f32[2,64,128]{2,1,0:T(8,128)S(1)} %rest_stress.6), channel_id=1, source_target_pairs={{0,2},{1,3},{2,0},{3,1},{4,6},{5,7},{6,4},{7,5},{8,10},{9,11},{10,... | collective-permute-start | bytes 196616 | tf_op jit(solution)/shard_map/ppermute | solution.py:34
  26.7 6.5 %collective-permute-start.13 = (f32[64,128]{1,0:T(8,128)S(1)}, f32[64,128]{1,0:T(8,128)S(1)}, u32[]{:S(2)}, u32[]{:S(2)}) collective-permute-start(f32[64,128]{1,0:T(8,128)S(1)} %get-tuple-element.45), channel_id=1, source_target_pairs={{0,6},{1,7},{2,4},{3,5},{4,2},{5,3},{6,0},{7,1},{8,14},{9,15},{10,... | collective-permute-start | bytes 98312 | tf_op jit(solution)/shard_map/ppermute | solution.py:34
  28.1 5.1 %collective-permute-start.14 = (f32[64,128]{1,0:T(8,128)S(1)}, f32[64,128]{1,0:T(8,128)S(1)}, u32[]{:S(2)}, u32[]{:S(2)}) collective-permute-start(f32[64,128]{1,0:T(8,128)S(1)} %get-tuple-element.46), channel_id=1, source_target_pairs={{0,4},{1,5},{2,6},{3,7},{4,0},{5,1},{6,2},{7,3},{8,12},{9,13},{10,... | collective-permute-start | bytes 98312 | tf_op jit(solution)/shard_map/ppermute | solution.py:34
  29.2 4.0 %collective-permute-start.11 = (f32[64,128]{1,0:T(8,128)S(1)}, f32[64,128]{1,0:T(8,128)S(1)}, u32[]{:S(2)}, u32[]{:S(2)}) collective-permute-start(f32[64,128]{1,0:T(8,128)S(1)} %slice_bitcast_fusion.7), channel_id=1, source_target_pairs={{0,1},{1,0},{2,3},{3,2},{4,5},{5,4},{6,7},{7,6},{8,9},{9,8},{10,11... | collective-permute-start | bytes 98312 | tf_op jit(solution)/shard_map/ppermute | solution.py:34
